TPU v7x, 32 devices: a whole 2x2x4 slice. The times are simulated.
32 devices in a mesh: seq: 8 (over z, x), dp: 2 (over y), domain: 2 (over core).
Axes of the slice: x: 2, y: 2, z: 4, core: 2. Of those that a mesh axis runs over, the one named last changes fastest.
Arguments:
- history: bfloat16 [2, 2, 2048, 1024], P('domain', 'dp', 'seq'), may hold values from -6 to 6
- qkv_weight: bfloat16 [2, 1024, 3072], P('domain', 'seq'), may hold values from -0.375 to 0.375
- norm_gain: float32 [2, 1024], P('domain'), may hold values from 0.1 to 1.9
- pool_gain: float32 [2, 1024], P('domain'), may hold values from 0.1 to 1.9
- lengths: int32 [2, 2], P('domain', 'dp'), may hold values from 256 to 2048, as said below
- positives: int32 [2], replicated, may hold values from 0 to 1, each once
Outputs:
- user_vec: bfloat16 [2, 2, 1024], P('domain', 'dp', 'seq')
- loss: float32 [2, 2], P('domain', 'dp')
Inputs may be any that keep to these rules, and one draw needn't show every extreme that they name: `lengths`: in each domain one user has exactly 2048 valid events and another exactly 256. `positives`: each user of the second domain is named exactly once.
All inputs are finite; a program needn't handle non-finite values.
Results may differ from a plain program's by a relative error of at most 0.0085.
Values may be sent and summed in bfloat16 or wider, within the bound.
No kernel may reach another device: no remote copies, remote signals or barrier semaphores. Data moves between devices by JAX's collectives and lax.ppermute only.
A program may use at most 64 MiB of HBM per device.

v0:
```python
import jax
import jax.numpy as jnp
from jax import lax
from jax.sharding import PartitionSpec as P

HEADS = 8
HEAD_DIM = 128


logit_scale = 20.0
epsilon = 1e-06
highest = lax.Precision.HIGHEST


def carried_in(part, axis, combine, identity):
    place = lax.axis_index(axis)
    gathered = jax.tree.map(lambda a: lax.all_gather(a, axis), part)
    state = jax.tree.map(lambda a, e: jnp.zeros_like(a) + jnp.asarray(e, a.dtype), part, identity)

    def one(hop, state):
        return combine(
            state, jax.tree.map(lambda a: lax.dynamic_index_in_dim(a, hop, 0, False), gathered)
        )

    return lax.fori_loop(0, place, one, state)


def partner_2(block, axis, stride):
    count = lax.axis_size(axis)
    route = []
    for low in range(count):
        high = low | 1 << stride
        if high != low and high < count:
            route += [(low, high), (high, low)]
    return lax.ppermute(block, axis, route)


def feature_map(values):
    return jax.nn.elu(values) + 1.0


def add_pair(earlier, later):
    return (earlier[0] + later[0], earlier[1] + later[1])


def shards(history, qkv_weight, norm_gain, pool_gain, lengths, positives):
    seq_count = lax.axis_size("seq")
    seq_place = lax.axis_index("seq")
    group_place = lax.axis_index("dp")
    domain_place = lax.axis_index("domain")
    events = history[0]
    users_dev, tokens_dev, width = events.shape
    row_count = users_dev * tokens_dev
    wide = events.astype(jnp.float32)
    normed = (
        wide * lax.rsqrt(jnp.mean(wide * wide, -1, keepdims=True) + epsilon) * norm_gain[0]
    ).astype(jnp.bfloat16)
    normed = normed.reshape(row_count, width)
    rows_here = qkv_weight[0]
    projected = jnp.dot(
        normed,
        lax.all_gather(rows_here, "seq", axis=0, tiled=True),
        preferred_element_type=jnp.float32,
    )
    query_raw = projected[:, :width]
    key_raw = projected[:, width : 2 * width]
    value_raw = projected[:, 2 * width :]
    positions = seq_place * tokens_dev + jnp.arange(tokens_dev)
    valid = positions[None, :] < lengths[0][:, None]
    shape_heads = (users_dev, tokens_dev, HEADS, HEAD_DIM)
    queries = feature_map(query_raw).astype(jnp.bfloat16).reshape(shape_heads)
    key_feats = (
        jnp.where(valid.reshape(row_count)[:, None], feature_map(key_raw), 0.0)
        .astype(jnp.bfloat16)
        .reshape(shape_heads)
    )
    val_feats = value_raw.astype(jnp.bfloat16).reshape(shape_heads)
    local_state = jnp.einsum(
        "uthc,uthd->uhcd", key_feats, val_feats, preferred_element_type=jnp.float32
    )
    local_total = jnp.sum(key_feats.astype(jnp.float32), axis=1)
    state_before, total_before = carried_in(
        (local_state, local_total),
        "seq",
        add_pair,
        (jnp.zeros_like(local_state), jnp.zeros_like(local_total)),
    )
    causal = jnp.arange(tokens_dev)[:, None] >= jnp.arange(tokens_dev)[None, :]
    scores = jnp.einsum("uthc,ushc->uhts", queries, key_feats, preferred_element_type=jnp.float32)
    scores = jnp.where(causal, scores, 0.0)
    denominator = jnp.sum(scores, axis=-1) + jnp.einsum(
        "uthc,uhc->uht", queries.astype(jnp.float32), total_before, precision=highest
    )
    numerator = jnp.einsum(
        "uhts,ushc->uthc",
        scores.astype(jnp.bfloat16),
        val_feats,
        preferred_element_type=jnp.float32,
    )
    numerator = numerator + jnp.einsum(
        "uthc,uhcd->uthd",
        queries,
        state_before.astype(jnp.bfloat16),
        preferred_element_type=jnp.float32,
    )
    attended = numerator / jnp.transpose(denominator, (0, 2, 1))[..., None]
    attended = attended.reshape(users_dev, tokens_dev, width)
    partial_value = jnp.sum(jnp.where(valid[..., None], wide + attended, 0.0), axis=1)
    piece_width = width // seq_count
    gain_row = pool_gain[0]
    pooled = lax.psum(partial_value, "seq")
    factor = lax.rsqrt(jnp.mean(pooled * pooled, -1, keepdims=True) + epsilon)
    full_vec = (pooled * factor * gain_row).astype(jnp.bfloat16)
    out_vec = lax.dynamic_slice_in_dim(full_vec, seq_place * piece_width, piece_width, 1)
    group = lax.all_gather(full_vec, "dp", axis=0, tiled=True)
    other = partner_2(group, "domain", 0)
    logits = jnp.einsum("uc,vc->uv", full_vec, other, preferred_element_type=jnp.float32) * (
        logit_scale / width
    )
    users_all = other.shape[0]
    own_index = group_place * users_dev + jnp.arange(users_dev)
    targets = lax.dynamic_slice_in_dim(positives, group_place * users_dev, users_dev)
    forward_pair = targets[:, None] == jnp.arange(users_all)[None, :]
    backward_pair = positives[None, :] == own_index[:, None]
    partner = jnp.where(domain_place == 0, forward_pair, backward_pair)
    loss = jnp.log(jnp.sum(jnp.exp(logits), axis=-1)) - jnp.sum(
        jnp.where(partner, logits, 0.0), axis=-1
    )
    return (out_vec[None], loss[None])


def solution(mesh):
    placed = (
        P("domain", "dp", "seq", None),
        P("domain", "seq", None),
        P("domain", None),
        P("domain", None),
        P("domain", "dp"),
        P(),
    )
    return jax.shard_map(
        shards,
        mesh=mesh,
        in_specs=placed,
        out_specs=(P("domain", "dp", "seq"), P("domain", "dp")),
        check_vma=False,
    )
```

profile of v0, /device:TPU:0, one launch (start us, length us, event | category | flops | bytes accessed | tf_op | source)
XLA Modules:
  0.0 242.5 jit_solution(3652567783507155478)
XLA Ops:
  7.2 0.7 all-gather.6.cloned.1.call-update
  8.6 1.2 fusion.6
  9.8 102.1 %all-gather.6.cloned.1.call-done = bf16[1,1024,3072]{2,1,0:T(8,128)(2,1)} async-done(((bf16[1,128,3072]{2,1,0:T(8,128)(2,1)}), bf16[1,1024,3072]{2,1,0:T(8,128)(2,1)}) %all-gather.6.cloned.1.call-update) | async-done | bytes 6291472 | tf_op jit(solution)/shard_map/all_gather | solution.py:62
  111.9 4.9 %fusion = f32[256,3072]{1,0:T(8,128)S(1)} fusion(bf16[1,1024,3072]{2,1,0:T(8,128)(2,1)} %all-gather.6.cloned.1.call-done, bf16[1,1,256,1024]{3,2,1,0:T(8,128)(2,1)} %param.8, f32[1024]{0:T(1024)} %bitcast.117, f32[256]{0:T(256)S(1)} %add_rsqrt_fusion), kind=kOutput, calls=%fused_computation.2 | convolution fusion | flops 1611661312 | bytes 9966592 | tf_op jit(solution)/shard_map/dot_general | solution.py:60
  116.8 2.0 convert_reduce_fusion
  118.8 2.0 copy.43
  120.8 2.1 fusion.32
  123.0 0.6 dynamic_slice.15
  123.6 30.8 %all_gather.22 = f32[8,1,8,128]{3,2,1,0:T(8,128)S(1)} all-gather(f32[1,1,8,128]{3,2,1,0:T(8,128)S(1)} %bitcast.113), channel_id=1, replica_groups=mesh['seq'=8,'dp'=2,'domain'=2] {'seq'}, dimensions={0}, use_global_device_ids=true | all-gather | bytes 36864 | tf_op jit(solution)/shard_map/all_gather | solution.py:17
  154.5 2.0 select_reduce_fusion
  156.5 1.3 fusion.12
  157.8 37.1 %all-gather.8.cloned.1.call-done = f32[64,128,128]{2,1,0:T(8,128)} async-done(((f32[8,128,128]{2,1,0:T(8,128)}), f32[64,128,128]{2,1,0:T(8,128)}) %all-gather.8.cloned.1.call-update) | async-done | bytes 4194320 | tf_op jit(solution)/shard_map/all_gather | solution.py:17
  195.0 1.0 copy-done.2
  196.0 0.5 fusion.27
  196.6 1.4 fusion.22
  198.0 0.3 copy.37
  198.4 0.2 fusion.8
  198.5 26.3 %psum.7 = f32[1,1024]{1,0:T(1,128)S(1)} all-reduce(f32[1,1024]{1,0:T(1,128)S(1)} %bitcast.114), channel_id=1, replica_groups=mesh['seq'=8,'dp'=2,'domain'=2] {'seq'}, use_global_device_ids=true, to_apply=%region_6.7 | all-reduce | flops 1024 | bytes 8192 | tf_op jit(solution)/shard_map/psum | solution.py:111
  224.9 0.6 multiply_reduce_fusion
  226.2 4.3 %all-gather.2 = bf16[2,1,1024]{2,1,0:T(2,128)(2,1)S(1)} all-gather(bf16[1,1,1024]{2,1,0:T(2,128)(2,1)S(1)} %bitcast.115), channel_id=1, replica_groups=mesh['seq'=8,'dp'=2,'domain'=2] {'dp'}, dimensions={0}, use_global_device_ids=true | all-gather | bytes 6144 | tf_op jit(solution)/shard_map/all_gather | solution.py:115
  230.6 0.1 collective-permute-start
  230.6 0.5 dynamic-slice_bitcast_fusion
  231.2 0.6 collective-permute-done
  231.8 1.4 fusion.45
  (21 shorter events, 0.2 us)
Async XLA Ops:
  7.2 104.8 %all-gather.6.cloned.1.call-start = ((), (), s32[]{:S(2)}) async-start(), calls=%async_computation | async-start | bytes 7077888 | tf_op jit(solution)/shard_map/all_gather | solution.py:62
  7.9 187.0 %all-gather.8.cloned.1.call-start = ((), (), s32[]{:S(2)}) async-start(), calls=%async_computation.1 | async-start | bytes 4718592 | tf_op jit(solution)/shard_map/all_gather | solution.py:17
  116.8 6.2 %copy-start.4 = (s32[2]{0:T(128)S(1)}, s32[2]{0:T(128)}, u32[]{:S(2)}) copy-start(s32[2]{0:T(128)} %param.13) | copy-start | bytes 28
  195.0 1.0 copy-start.2
  195.0 1.5 copy-start.1
  196.5 1.8 copy-start
  196.5 29.6 %copy-start.3 = (f32[1,1024]{1,0:T(1,128)S(1)}, f32[1,1024]{1,0:T(1,128)}, u32[]{:S(2)}) copy-start(f32[1,1024]{1,0:T(1,128)} %param.11) | copy-start | bytes 12292
  230.6 1.2 collective-permute-start
Sparse Core Ops, SparseCore 0:
  10.2 101.7 all-gather.5
  123.1 71.7 all-gather.7
where the time goes:
time: 243 us
  waiting for transfers between devices  141 us (58%)
  blocking collectives  61.5 us (25%)
  between operations  18 us (7%)
  matrix products  13.7 us (6%)
  local copies, waits for them, and re-layouts  4.57 us (2%)
  other arithmetic  4.06 us (2%)
    all_gather x1, waiting for transfers between devices, shards(): lax.all_gather(rows_here, 'seq', axis=0, tiled=True)  102 us
    all_gather x1, waiting for transfers between devices, carried_in(): gathered = jax.tree.map(lambda a: lax.all_gather(a, axis), part)  37.1 us
    all_gather x1, blocking collectives, carried_in(): gathered = jax.tree.map(lambda a: lax.all_gather(a, axis), part)  30.8 us
    psum x1, blocking collectives, shards(): pooled = lax.psum(partial_value, 'seq')  26.3 us
  transfers between devices with their start and end apart: 3, of which 3 were waited for; matrix products, arithmetic and copies ran while one was open for 2% of the time, Pallas kernels for 0%

commit v1 on v0

--- a/solution.py
+++ b/solution.py
@@ -1,6 +1,10 @@
+import functools
+
 import jax
 import jax.numpy as jnp
 from jax import lax
+from jax.experimental import pallas as pl
+from jax.experimental.pallas import tpu as pltpu
 from jax.sharding import PartitionSpec as P
 
 HEADS = 8
@@ -129,6 +133,335 @@
     return (out_vec[None], loss[None])
 
 
+PLANE = 4
+PLANES = 4
+GROUP = 256
+DOT_T = (((0,), (0,)), ((), ()))
+
+
+def places():
+    seq_place = lax.axis_index("seq")
+    return lax.div(seq_place, 2), lax.rem(seq_place, 2), lax.axis_index("dp")
+
+
+def head_sums(a):
+    return [
+        jnp.sum(a[:, h * HEAD_DIM : (h + 1) * HEAD_DIM], axis=1, keepdims=True)
+        for h in range(GROUP // HEAD_DIM)
+    ]
+
+
+def by_head(columns):
+    rows = columns[0].shape[0]
+    return jnp.concatenate([jnp.broadcast_to(c, (rows, HEAD_DIM)) for c in columns], axis=1)
+
+
+def split_two(a):
+    high = a.astype(jnp.bfloat16)
+    return high, (a - high.astype(jnp.float32)).astype(jnp.bfloat16)
+
+
+def project_kernel(lengths, own, near, across, corner, w_own, w_near, *rest):
+    shifted = rest[:6]
+    gain, normed, feats, sums, raw, weights, sems = rest[6:]
+    tokens, width = own.shape
+    wide = 2 * GROUP
+    z, x, u = places()
+    own_long = lengths[0, 0] > tokens
+    long_u = jnp.where(own_long, u, 1 - u)
+    blocks = (own, near, across, corner)
+
+    rows = width // (2 * PLANES)
+    half_at = (x, 1 - x)
+    copies = []
+    for half, ref in enumerate((w_own, w_near)):
+        at = pl.multiple_of((2 * z + half_at[half]) * rows, rows)
+        copies.append((ref.at[:, pl.ds(0, wide)], at))
+    for step in range(1, PLANES):
+        other = lax.rem(z + PLANES - step, PLANES)
+        for half in range(2):
+            at = pl.multiple_of((2 * other + half_at[half]) * rows, rows)
+            copies.append((shifted[2 * (step - 1) + half], at))
+    for i, (ref, at) in enumerate(copies):
+        pltpu.make_async_copy(ref, weights.at[pl.ds(at, rows)], sems.at[3 + i]).start()
+
+    for slot in range(3):
+        from_x = 1 if slot == 1 else 0
+        from_u = 1 - long_u if slot == 2 else long_u
+        pick = jnp.bitwise_xor(x, from_x) + 2 * jnp.bitwise_xor(u, from_u)
+        for j, ref in enumerate(blocks):
+
+            @pl.when(pick == j)
+            def _():
+                pltpu.make_async_copy(ref, raw.at[slot], sems.at[slot]).start()
+
+    for i, (ref, at) in enumerate(copies):
+        pltpu.make_async_copy(ref, weights.at[pl.ds(at, rows)], sems.at[3 + i]).wait()
+    columns = pl.ds(pl.multiple_of((2 * x + u) * GROUP, GROUP), GROUP)
+
+    def one(slot):
+        values = raw[slot].astype(jnp.float32)
+        scale = lax.rsqrt(jnp.mean(values * values, axis=1, keepdims=True) + epsilon)
+        low = (values * scale * gain[...]).astype(jnp.bfloat16)
+        normed[pl.ds(slot * tokens, tokens), :] = low
+        out = jnp.dot(low, weights[...], preferred_element_type=jnp.float32)
+        out = jnp.where(out > 0.0, out + 1.0, jnp.exp(jnp.minimum(out, 0.0))).astype(jnp.bfloat16)
+        feats[pl.ds(slot * tokens, tokens), :] = out
+        key_total = jnp.sum(out[:, GROUP:].astype(jnp.float32), axis=0, keepdims=True)
+        part = raw[slot, :, columns].astype(jnp.float32)
+        return key_total, jnp.sum(part, axis=0, keepdims=True)
+
+    for slot in range(3):
+        pltpu.make_async_copy(own, raw.at[slot], sems.at[slot]).wait()
+    key_one, sum_one = one(0)
+    key_two, sum_two = one(1)
+    sums[0:1, :] = key_one + key_two
+    sums[1:2, :] = sum_one + sum_two
+    sums[2:3, :] = jnp.zeros_like(sum_one)
+
+    @pl.when(z == 0)
+    def _():
+        _, sum_short = one(2)
+        sums[2:3, :] = sum_short
+
+
+def scan_kernel(sums, total_1, total_2, total_3, feats, weight_sum, local):
+    tokens = feats.shape[0] // 3
+    z, _, _ = places()
+    row = lax.broadcasted_iota(jnp.int32, (tokens, tokens), 0)
+    col = lax.broadcasted_iota(jnp.int32, (tokens, tokens), 1)
+    lower = (row >= col).astype(jnp.bfloat16)
+    upper = (row <= col).astype(jnp.bfloat16)
+    before = jnp.zeros((1, GROUP), jnp.float32)
+    for step, ref in enumerate((total_1, total_2, total_3), 1):
+        before = before + jnp.where(z >= step, ref[...], 0.0)
+
+    def block(slot, carry):
+        part = pl.ds(slot * tokens, tokens)
+        query = feats[part, :GROUP].astype(jnp.float32)
+        key = feats[part, GROUP:]
+        prefix = jnp.dot(lower, key, preferred_element_type=jnp.float32) + carry
+        share = query / by_head(head_sums(query * prefix))
+        return share, key, prefix[tokens - 1 : tokens, :]
+
+    def suffix(share):
+        high, low = split_two(share)
+        return jnp.dot(upper, high, preferred_element_type=jnp.float32) + jnp.dot(
+            upper, low, preferred_element_type=jnp.float32
+        )
+
+    def store(slot, key, after):
+        sums_by_head = head_sums(key.astype(jnp.float32) * after)
+        part = pl.ds(slot * tokens, tokens)
+        local[part, :] = jnp.concatenate(
+            [jnp.broadcast_to(c, (tokens, HEAD_DIM // 2)) for c in sums_by_head], axis=1
+        )
+
+    share_one, key_one, carry = block(0, before)
+    share_two, key_two, _ = block(1, carry)
+    after_two = suffix(share_two)
+    after_one = suffix(share_one) + after_two[0:1, :]
+    weight_sum[...] = after_one[0:1, :]
+    store(0, key_one, after_one)
+    store(1, key_two, after_two)
+
+    @pl.when(z == 0)
+    def _():
+        share, key, _ = block(2, jnp.zeros((1, GROUP), jnp.float32))
+        store(2, key, suffix(share))
+
+
+def pool_kernel(
+    lengths, sums, later_1, later_2, later_3, feats, local, normed, v_own, v_near, v_1, v_2, v_3, pooled, values, mixed
+):
+    tokens = feats.shape[0] // 3
+    rows = v_own.shape[0]
+    width = normed.shape[1]
+    z, x, u = places()
+    long_u = jnp.where(lengths[0, 0] > tokens, u, 1 - u)
+    at = [pl.multiple_of((2 * z + half) * rows, rows) for half in (x, 1 - x)]
+    values[pl.ds(at[0], rows), :] = v_own[...]
+    values[pl.ds(at[1], rows), :] = v_near[...]
+    for step, ref in enumerate((v_1, v_2, v_3), 1):
+        other = lax.rem(z + PLANES - step, PLANES)
+        for half, place in enumerate((x, 1 - x)):
+            start = pl.multiple_of((2 * other + place) * rows, rows)
+            values[pl.ds(start, rows), :] = ref[pl.ds(half * rows, rows), :]
+
+    after = jnp.zeros((1, GROUP), jnp.float32)
+    for step, ref in enumerate((later_1, later_2, later_3), 1):
+        after = after + jnp.where(z < step, ref[...], 0.0)
+    lane = lax.broadcasted_iota(jnp.int32, (1, HEAD_DIM), 1)
+
+    def mix(weight, slot, count):
+        high, low = split_two(weight)
+        both = jnp.where(lax.rem(lane, 64) < 32, high.astype(jnp.float32), low.astype(jnp.float32))
+        part = normed[pl.ds(slot * tokens, count), :]
+        return lax.dot_general(both.astype(jnp.bfloat16), part, DOT_T, preferred_element_type=jnp.float32)
+
+    key = feats[0 : 2 * tokens, GROUP:].astype(jnp.float32)
+    extra = jnp.concatenate(
+        [jnp.broadcast_to(c, (2 * tokens, HEAD_DIM // 2)) for c in head_sums(key * after)], axis=1
+    )
+    mixed[0:HEAD_DIM, :] = mix(local[0 : 2 * tokens, :] + extra, 0, 2 * tokens)
+    mixed[HEAD_DIM:, :] = jnp.zeros((HEAD_DIM, width), jnp.float32)
+
+    @pl.when(z == 0)
+    def _():
+        mixed[HEAD_DIM:, :] = mix(local[2 * tokens :, :], 2, tokens)
+
+    picked = [mixed[h : h + 1, :] + mixed[h + 32 : h + 33, :] for h in (0, 64, 128, 192)]
+    high, low = split_two(jnp.concatenate(picked + picked, axis=0))
+    out = jnp.dot(high, values[...], preferred_element_type=jnp.float32) + jnp.dot(
+        low, values[...], preferred_element_type=jnp.float32
+    )
+    half = HEAD_DIM
+    long_row = jnp.concatenate([out[0:1, :half], out[1:2, half:]], axis=1) + sums[1:2, :]
+    short_row = jnp.concatenate([out[2:3, :half], out[3:4, half:]], axis=1) + sums[2:3, :]
+    pooled[0:1, :] = jnp.where(long_u == 0, long_row, short_row)
+    pooled[1:2, :] = jnp.where(long_u == 0, short_row, long_row)
+
+
+def loss_kernel(positives, parts, o_1, o_2, o_3, p_0, p_1, p_2, p_3, gain, gain_other, vec, loss, mine, theirs):
+    z, x, u = places()
+    domain = lax.axis_index("domain")
+    group = 2 * x + u
+    width = gain.shape[1]
+    piece = vec.shape[2]
+
+    def collect(refs, gains, dest):
+        total = jnp.zeros((2, 1), jnp.float32)
+        for move, ref in enumerate(refs):
+            values = ref[...]
+            total = total + jnp.sum(values * values, axis=1, keepdims=True)
+            at = pl.multiple_of(jnp.bitwise_xor(group, move) * GROUP, GROUP)
+            dest[:, pl.ds(at, GROUP)] = values * gains[:, pl.ds(at, GROUP)]
+        factor = lax.rsqrt(total / width + epsilon)
+        return (dest[...] * factor).astype(jnp.bfloat16).astype(jnp.float32)
+
+    own = collect((parts, o_1, o_2, o_3), gain, mine)
+    other = collect((p_0, p_1, p_2, p_3), gain_other, theirs)
+    mine[...] = own
+    start = pl.multiple_of((2 * z + x) * piece, piece)
+    out = mine[:, pl.ds(start, piece)]
+    vec[0] = jnp.where(u == 0, out[0:1], out[1:2]).astype(jnp.bfloat16)
+    this = jnp.where(u == 0, own[0:1], own[1:2])
+    logits = jnp.sum(this * other, axis=1, keepdims=True) * (logit_scale / width)
+    top = jnp.max(logits, axis=0, keepdims=True)
+    spread = jnp.log(jnp.sum(jnp.exp(logits - top), axis=0, keepdims=True)) + top
+    forward = jnp.where(u == 0, positives[0], positives[1])
+    backward = jnp.where(positives[0] == u, 0, 1)
+    partner = jnp.where(domain == 0, forward, backward)
+    rows = lax.broadcasted_iota(jnp.int32, (2, 1), 0)
+    loss[...] = spread - jnp.sum(jnp.where(rows == partner, logits, 0.0), axis=0, keepdims=True)
+
+
+def vmem():
+    return pl.BlockSpec(memory_space=pltpu.VMEM)
+
+
+def anywhere():
+    return pl.BlockSpec(memory_space=pl.ANY)
+
+
+def smem():
+    return pl.BlockSpec(memory_space=pltpu.SMEM)
+
+
+def call(kernel, outs, in_specs, scratch, flops):
+    return pl.pallas_call(
+        kernel,
+        out_shape=outs,
+        in_specs=in_specs,
+        out_specs=jax.tree.map(lambda _: vmem(), outs),
+        scratch_shapes=scratch,
+        compiler_params=pltpu.CompilerParams(vmem_limit_bytes=40 * 1024 * 1024),
+        cost_estimate=pl.CostEstimate(flops=flops, bytes_accessed=2**21, transcendentals=0),
+    )
+
+
+def towers(history, qkv_weight, norm_gain, pool_gain, lengths, positives):
+    events = history[0, 0]
+    tokens, width = events.shape
+    weight = qkv_weight[0]
+    rows = weight.shape[0]
+    f32, bf16 = jnp.float32, jnp.bfloat16
+    shape = jax.ShapeDtypeStruct
+    z, x, u = places()
+    group = 2 * x + u
+    here = PLANE * PLANES
+
+    def plane_hop(a, move):
+        return lax.ppermute(a, ("seq", "dp"), [(i, i ^ move) for i in range(here)])
+
+    def level_hop(a, step):
+        return lax.ppermute(a, ("seq", "dp"), [(i, (i + PLANE * step) % here) for i in range(here)])
+
+    def domain_hop(a, move):
+        pairs = [(i, i ^ (2 * move + 1)) for i in range(2 * here)]
+        return lax.ppermute(a, ("seq", "dp", "domain"), pairs)
+
+    def columns(which):
+        return jnp.concatenate(
+            [lax.dynamic_slice(weight, (0, part * width + which * GROUP), (rows, GROUP)) for part in range(3)],
+            axis=1,
+        )
+
+    near = plane_hop(events, 2)
+    across = plane_hop(events, 1)
+    corner = plane_hop(events, 3)
+    w_own = columns(group)
+    w_near = plane_hop(columns(jnp.bitwise_xor(group, 2)), 2)
+    shifted = []
+    for step in range(1, PLANES):
+        shifted.append(level_hop(w_own[:, : 2 * GROUP], step))
+        shifted.append(level_hop(w_near[:, : 2 * GROUP], step))
+    v_own, v_near = w_own[:, 2 * GROUP :], w_near[:, 2 * GROUP :]
+    v_both = jnp.concatenate([v_own, v_near], axis=0)
+    v_far = [level_hop(v_both, step) for step in range(1, PLANES)]
+    gain_other = domain_hop(pool_gain, 0)
+
+    normed, feats, sums = call(
+        project_kernel,
+        (shape((3 * tokens, width), bf16), shape((3 * tokens, 2 * GROUP), bf16), shape((8, GROUP), f32)),
+        [smem()] + [anywhere()] * 12 + [vmem()],
+        [
+            pltpu.VMEM((3, tokens, width), bf16),
+            pltpu.VMEM((width, 2 * GROUP), bf16),
+            pltpu.SemaphoreType.DMA((3 + 2 * PLANES,)),
+        ],
+        2 * 3 * tokens * width * 2 * GROUP,
+    )(lengths, events, near, across, corner, w_own, w_near, *shifted, norm_gain)
+    key_total = sums[0:1]
+    totals = [level_hop(key_total, step) for step in range(1, PLANES)]
+    weight_sum, local = call(
+        scan_kernel,
+        (shape((1, GROUP), f32), shape((3 * tokens, HEAD_DIM), f32)),
+        [vmem()] * 5,
+        [],
+        2 * 9 * tokens * tokens * GROUP,
+    )(sums, *totals, feats)
+    later = [level_hop(weight_sum, step) for step in range(1, PLANES)]
+    part = call(
+        pool_kernel,
+        shape((2, GROUP), f32),
+        [smem()] + [vmem()] * 12,
+        [pltpu.VMEM((width, GROUP), bf16), pltpu.VMEM((2 * HEAD_DIM, width), f32)],
+        2 * 3 * tokens * width * HEAD_DIM,
+    )(lengths, sums, *later, feats, local, normed, v_own, v_near, *v_far)
+    part = part + level_hop(part, 1) + level_hop(part, 2) + level_hop(part, 3)
+    own = [plane_hop(part, move) for move in range(1, PLANE)]
+    other = [domain_hop(part, move) for move in range(PLANE)]
+    vec, loss = call(
+        loss_kernel,
+        (shape((1, 1, width // 8), bf16), shape((1, 1), f32)),
+        [smem()] + [vmem()] * 10,
+        [pltpu.VMEM((2, width), f32), pltpu.VMEM((2, width), f32)],
+        2**14,
+    )(positives, part, *own, *other, pool_gain, gain_other)
+    return vec, loss
+
+
 def solution(mesh):
     placed = (
         P("domain", "dp", "seq", None),
@@ -138,8 +471,9 @@
         P("domain", "dp"),
         P(),
     )
+    small = mesh.shape["seq"] == 2 * PLANES and mesh.shape["dp"] == 2
     return jax.shard_map(
-        shards,
+        towers if small else shards,
         mesh=mesh,
         in_specs=placed,
         out_specs=(P("domain", "dp", "seq"), P("domain", "dp")),

time: 243 us -> 79.3 us (0.33)
  waiting for transfers between devices: 141 us -> 28.1 us
  blocking collectives: 61.5 us -> 0 us
  starting transfers between devices: 0.14 us -> 41.7 us
  between operations: 18 us -> 1.46 us
  matrix products: 13.7 us -> 0 us
  Pallas kernels: 0 us -> 6.78 us
  other arithmetic: 4.06 us -> 0.05 us
  local copies, waits for them, and re-layouts: 4.57 us -> 1.13 us
    all_gather x2 -> x0, waiting for transfers between devices: 139 us -> none  [the longest x1 102 us: shards(): lax.all_gather(rows_here, 'seq', axis=0, tiled=True)]
    ppermute x1 -> x30, starting transfers between devices: 0.06 us -> 41.7 us  [the longest x18 28.4 us: level_hop(): lax.ppermute(a, ('seq', 'dp'), [(i, (i + PLANE * step) % here) for i in r...]
    all_gather x2 -> x0, blocking collectives: 35.1 us -> none  [the longest x1 30.8 us: carried_in(): gathered = jax.tree.map(lambda a: lax.all_gather(a, axis), part)]
    ppermute x1 -> x30, waiting for transfers between devices: 0.63 us -> 28.1 us  [the longest x18 25.2 us: level_hop(): lax.ppermute(a, ('seq', 'dp'), [(i, (i + PLANE * step) % here) for i in r...]
    psum x1 -> x0, blocking collectives: 26.3 us -> none  [shards(): pooled = lax.psum(partial_value, 'seq')]
    dot_general x7 -> x0, matrix products: 13.7 us -> none  [the longest x1 4.85 us: shards(): jnp.dot(normed, lax.all_gather(rows_here, 'seq', axis=0, tiled=True), pre...]
    pallas_call x0 -> x4, Pallas kernels: none -> 6.78 us  [the longest x1 3.06 us: towers(): call(project_kernel, (shape((3 * tokens, width), bf16), shape((3 * tokens...]
    reduce_sum x4 -> x0, other arithmetic: 4 us -> none  [the longest x1 1.99 us: shards(): local_total = jnp.sum(key_feats.astype(jnp.float32), axis=1)]
  transfers between devices with their start and end apart: 3 -> 30, of which waited for: 3 -> 15; matrix products, arithmetic and copies ran while one was open for 2% -> 0% of each run, Pallas kernels for 0% -> 6%
where the time goes in v1:
time: 79.3 us; the launch traced here: 79.1 us
  starting transfers between devices  41.7 us (53%)
  waiting for transfers between devices  28.1 us (35%)
  Pallas kernels  6.78 us (9%)
  between operations  1.46 us (2%)
  local copies, waits for them, and re-layouts  1.13 us (1%)
    ppermute x18, starting transfers between devices, level_hop(): lax.ppermute(a, ('seq', 'dp'), [(i, (i + PLANE * step) % here) for i in r...  28.4 us
    ppermute x18, waiting for transfers between devices, level_hop(): lax.ppermute(a, ('seq', 'dp'), [(i, (i + PLANE * step) % here) for i in r...  25.2 us
    ppermute x7, starting transfers between devices, plane_hop(): return lax.ppermute(a, ('seq', 'dp'), [(i, i ^ move) for i in range(here)])  9.98 us
    ppermute x5, starting transfers between devices, domain_hop(): return lax.ppermute(a, ('seq', 'dp', 'domain'), pairs)  3.32 us
    pallas_call x1, Pallas kernels, towers(): call(project_kernel, (shape((3 * tokens, width), bf16), shape((3 * tokens...  3.06 us
    ppermute x5, waiting for transfers between devices, domain_hop(): return lax.ppermute(a, ('seq', 'dp', 'domain'), pairs)  2.28 us
  transfers between devices with their start and end apart: 30, of which 15 were waited for; matrix products, arithmetic and copies ran while one was open for 0% of the time, Pallas kernels for 6%

profile of v1, /device:TPU:0, one launch (start us, length us, event | category | flops | bytes accessed | tf_op | source)
XLA Modules:
  0.0 79.1 jit_solution(6820691666531020767)
XLA Ops:
  1.8 3.0 %collective-permute-start.3 = (bf16[128,768]{1,0:T(8,128)(2,1)S(1)}, bf16[128,768]{1,0:T(8,128)(2,1)S(1)}, u32[]{:S(2)}, u32[]{:S(2)}) collective-permute-start(bf16[128,768]{1,0:T(8,128)(2,1)S(1)} %pad_maximum_fusion.1), channel_id=1, source_target_pairs={{0,4},{2,6},{4,0},{6,2},{8,12},{10,14},{12,8},{14,10},{16,20},{18,... | collective-permute-start | bytes 589832 | tf_op jit(solution)/shard_map/ppermute | solution.py:395
  4.9 2.0 %collective-permute-start.1 = (bf16[256,1024]{1,0:T(8,128)(2,1)}, bf16[256,1024]{1,0:T(8,128)(2,1)S(1)}, u32[]{:S(2)}, u32[]{:S(2)}) collective-permute-start(bf16[256,1024]{1,0:T(8,128)(2,1)} %bitcast.14), channel_id=1, source_target_pairs={{0,2},{2,0},{4,6},{6,4},{8,10},{10,8},{12,14},{14,12},{16,18},{18,... | collective-permute-start | bytes 1572872 | tf_op jit(solution)/shard_map/ppermute | solution.py:395
  8.3 1.6 %collective-permute-start.4 = (bf16[128,512]{1,0:T(8,128)(2,1)S(1)}, bf16[128,512]{1,0:T(8,128)(2,1)S(1)}, u32[]{:S(2)}, u32[]{:S(2)}) collective-permute-start(bf16[128,512]{1,0:T(8,128)(2,1)S(1)} %pad_maximum_fusion.2), channel_id=1, source_target_pairs={{0,8},{2,10},{4,12},{6,14},{8,16},{10,18},{12,20},{14,22},{16,24},... | collective-permute-start | bytes 393224 | tf_op jit(solution)/shard_map/ppermute | solution.py:398
  10.5 3.2 %collective-permute-start.6 = (bf16[128,512]{1,0:T(8,128)(2,1)S(1)}, bf16[128,512]{1,0:T(8,128)(2,1)S(1)}, u32[]{:S(2)}, u32[]{:S(2)}) collective-permute-start(bf16[128,512]{1,0:T(8,128)(2,1)S(1)} %pad_maximum_fusion.2), channel_id=1, source_target_pairs={{0,16},{2,18},{4,20},{6,22},{8,24},{10,26},{12,28},{14,30},{16,0},... | collective-permute-start | bytes 393224 | tf_op jit(solution)/shard_map/ppermute | solution.py:398
  13.7 3.0 %collective-permute-done.4.rest_0_ = bf16[128,512]{1,0:T(8,128)(2,1)S(1)} collective-permute-done((bf16[128,512]{1,0:T(8,128)(2,1)S(1)}, bf16[128,512]{1,0:T(8,128)(2,1)S(1)}, u32[]{:S(2)}, u32[]{:S(2)}) %collective-permute-start.4) | collective-permute-done | bytes 131104 | tf_op jit(solution)/shard_map/ppermute | solution.py:398
  17.2 3.4 %collective-permute-done.6.rest_2_ = bf16[128,512]{1,0:T(8,128)(2,1)S(1)} collective-permute-done((bf16[128,512]{1,0:T(8,128)(2,1)S(1)}, bf16[128,512]{1,0:T(8,128)(2,1)S(1)}, u32[]{:S(2)}, u32[]{:S(2)}) %collective-permute-start.6) | collective-permute-done | bytes 131104 | tf_op jit(solution)/shard_map/ppermute | solution.py:398
  20.6 2.8 %collective-permute-start.5 = (bf16[128,512]{1,0:T(8,128)(2,1)S(1)}, bf16[128,512]{1,0:T(8,128)(2,1)S(1)}, u32[]{:S(2)}, u32[]{:S(2)}) collective-permute-start(bf16[128,512]{1,0:T(8,128)(2,1)S(1)} %slice.18), channel_id=1, source_target_pairs={{0,8},{2,10},{4,12},{6,14},{8,16},{10,18},{12,20},{14,22},{16,24},... | collective-permute-start | bytes 393224 | tf_op jit(solution)/shard_map/ppermute | solution.py:398
  23.4 3.4 %collective-permute-start.7 = (bf16[128,512]{1,0:T(8,128)(2,1)S(1)}, bf16[128,512]{1,0:T(8,128)(2,1)S(1)}, u32[]{:S(2)}, u32[]{:S(2)}) collective-permute-start(bf16[128,512]{1,0:T(8,128)(2,1)S(1)} %slice.18), channel_id=1, source_target_pairs={{0,16},{2,18},{4,20},{6,22},{8,24},{10,26},{12,28},{14,30},{16,0},... | collective-permute-start | bytes 393224 | tf_op jit(solution)/shard_map/ppermute | solution.py:398
  26.8 2.8 %collective-permute-done.5.rest_1_ = bf16[128,512]{1,0:T(8,128)(2,1)S(1)} collective-permute-done((bf16[128,512]{1,0:T(8,128)(2,1)S(1)}, bf16[128,512]{1,0:T(8,128)(2,1)S(1)}, u32[]{:S(2)}, u32[]{:S(2)}) %collective-permute-start.5) | collective-permute-done | bytes 131104 | tf_op jit(solution)/shard_map/ppermute | solution.py:398
  29.6 3.0 %collective-permute-start.9 = (bf16[128,512]{1,0:T(8,128)(2,1)S(1)}, bf16[128,512]{1,0:T(8,128)(2,1)S(1)}, u32[]{:S(2)}, u32[]{:S(2)}) collective-permute-start(bf16[128,512]{1,0:T(8,128)(2,1)S(1)} %slice.18), channel_id=1, source_target_pairs={{0,24},{2,26},{4,28},{6,30},{8,0},{10,2},{12,4},{14,6},{16,8},{18,... | collective-permute-start | bytes 393224 | tf_op jit(solution)/shard_map/ppermute | solution.py:398
  33.7 2.3 %collective-permute-done.9.rest_5_ = bf16[128,512]{1,0:T(8,128)(2,1)S(1)} collective-permute-done((bf16[128,512]{1,0:T(8,128)(2,1)S(1)}, bf16[128,512]{1,0:T(8,128)(2,1)S(1)}, u32[]{:S(2)}, u32[]{:S(2)}) %collective-permute-start.9) | collective-permute-done | bytes 131104 | tf_op jit(solution)/shard_map/ppermute | solution.py:398
  36.3 4.0 %collective-permute-start.18 = (bf16[256,256]{1,0:T(8,128)(2,1)S(1)}, bf16[256,256]{1,0:T(8,128)(2,1)S(1)}, u32[]{:S(2)}, u32[]{:S(2)}) collective-permute-start(bf16[256,256]{1,0:T(8,128)(2,1)S(1)} %pad_maximum_fusion.3), channel_id=1, source_target_pairs={{0,24},{2,26},{4,28},{6,30},{8,0},{10,2},{12,4},{14,6},{16,8},{18,... | collective-permute-start | bytes 393224 | tf_op jit(solution)/shard_map/ppermute | solution.py:398
  41.1 3.1 %shard_map.77 = (bf16[768,1024]{1,0:T(8,128)(2,1)S(1)}, bf16[768,512]{1,0:T(8,128)(2,1)S(1)}, f32[8,256]{1,0:T(8,128)S(1)}) custom-call(s32[1,1]{1,0:T(1,128)S(6)} %copy.8.lengths, bf16[256,1024]{1,0:T(8,128)(2,1)S(1)} %bitcast.16, bf16[256,1024]{1,0:T(8,128)(2,1)S(1)} %collective-permute-done.near, bf16[256,1024]{1,0:T(8,128)(2,1)S(1)} %collective-permute-done.1.across, ...), custom_call_target="tpu_custom_call" | custom-call | flops 805306368 | bytes 2097152 | tf_op jit(solution)/shard_map/pallas_call | solution.py:424
  45.6 3.9 %collective-permute-done.10.total_1 = f32[1,256]{1,0:T(1,128)S(1)} collective-permute-done((f32[1,256]{1,0:T(1,128)S(1)}, f32[1,256]{1,0:T(1,128)S(1)}, u32[]{:S(2)}, u32[]{:S(2)}) %collective-permute-start.10) | collective-permute-done | bytes 1056 | tf_op jit(solution)/shard_map/ppermute | solution.py:398
  49.6 3.6 %collective-permute-done.12.total_3 = f32[1,256]{1,0:T(1,128)S(1)} collective-permute-done((f32[1,256]{1,0:T(1,128)S(1)}, f32[1,256]{1,0:T(1,128)S(1)}, u32[]{:S(2)}, u32[]{:S(2)}) %collective-permute-start.12) | collective-permute-done | bytes 1056 | tf_op jit(solution)/shard_map/ppermute | solution.py:398
  54.6 1.8 %collective-permute-start.14 = (f32[1,256]{1,0:T(1,128)S(1)}, f32[1,256]{1,0:T(1,128)S(1)}, u32[]{:S(2)}, u32[]{:S(2)}) collective-permute-start(f32[1,256]{1,0:T(1,128)S(1)} %get-tuple-element.9), channel_id=1, source_target_pairs={{0,16},{2,18},{4,20},{6,22},{8,24},{10,26},{12,28},{14,30},{16,0},... | collective-permute-start | bytes 3080 | tf_op jit(solution)/shard_map/ppermute | solution.py:398
  56.4 2.0 %collective-permute-start.15 = (f32[1,256]{1,0:T(1,128)S(1)}, f32[1,256]{1,0:T(1,128)S(1)}, u32[]{:S(2)}, u32[]{:S(2)}) collective-permute-start(f32[1,256]{1,0:T(1,128)S(1)} %get-tuple-element.9), channel_id=1, source_target_pairs={{0,24},{2,26},{4,28},{6,30},{8,0},{10,2},{12,4},{14,6},{16,8},{18,... | collective-permute-start | bytes 3080 | tf_op jit(solution)/shard_map/ppermute | solution.py:398
  58.4 1.5 %collective-permute-done.13.later_1 = f32[1,256]{1,0:T(1,128)S(1)} collective-permute-done((f32[1,256]{1,0:T(1,128)S(1)}, f32[1,256]{1,0:T(1,128)S(1)}, u32[]{:S(2)}, u32[]{:S(2)}) %collective-permute-start.13) | collective-permute-done | bytes 1056 | tf_op jit(solution)/shard_map/ppermute | solution.py:398
  61.6 1.8 %collective-permute-start.19 = (f32[2,256]{1,0:T(2,128)S(1)}, f32[2,256]{1,0:T(2,128)S(1)}, u32[]{:S(2)}, u32[]{:S(2)}) collective-permute-start(f32[2,256]{1,0:T(2,128)S(1)} %shard_map.79), channel_id=1, source_target_pairs={{0,8},{2,10},{4,12},{6,14},{8,16},{10,18},{12,20},{14,22},{16,24},... | collective-permute-start | bytes 6152 | tf_op jit(solution)/shard_map/ppermute | solution.py:398
  63.4 1.8 %collective-permute-start.20 = (f32[2,256]{1,0:T(2,128)S(1)}, f32[2,256]{1,0:T(2,128)S(1)}, u32[]{:S(2)}, u32[]{:S(2)}) collective-permute-start(f32[2,256]{1,0:T(2,128)S(1)} %shard_map.79), channel_id=1, source_target_pairs={{0,16},{2,18},{4,20},{6,22},{8,24},{10,26},{12,28},{14,30},{16,0},... | collective-permute-start | bytes 6152 | tf_op jit(solution)/shard_map/ppermute | solution.py:398
  68.7 1.5 %collective-permute-start.22 = (f32[2,256]{1,0:T(2,128)S(1)}, f32[2,256]{1,0:T(2,128)S(1)}, u32[]{:S(2)}, u32[]{:S(2)}) collective-permute-start(f32[2,256]{1,0:T(2,128)S(1)} %add_add_fusion.parts), channel_id=1, source_target_pairs={{0,2},{2,0},{4,6},{6,4},{8,10},{10,8},{12,14},{14,12},{16,18},{18,... | collective-permute-start | bytes 6152 | tf_op jit(solution)/shard_map/ppermute | solution.py:395
  70.3 2.0 %collective-permute-start.24 = (f32[2,256]{1,0:T(2,128)S(1)}, f32[2,256]{1,0:T(2,128)S(1)}, u32[]{:S(2)}, u32[]{:S(2)}) collective-permute-start(f32[2,256]{1,0:T(2,128)S(1)} %add_add_fusion.parts), channel_id=1, source_target_pairs={{0,6},{2,4},{4,2},{6,0},{8,14},{10,12},{12,10},{14,8},{16,22},{18,... | collective-permute-start | bytes 6152 | tf_op jit(solution)/shard_map/ppermute | solution.py:395
  72.2 1.6 %collective-permute-start.26 = (f32[2,256]{1,0:T(2,128)S(1)}, f32[2,256]{1,0:T(2,128)S(1)}, u32[]{:S(2)}, u32[]{:S(2)}) collective-permute-start(f32[2,256]{1,0:T(2,128)S(1)} %add_add_fusion.parts), channel_id=1, source_target_pairs={{0,3},{1,2},{2,1},{3,0},{4,7},{5,6},{6,5},{7,4},{8,11},{9,10},{10,... | collective-permute-start | bytes 6152 | tf_op jit(solution)/shard_map/ppermute | solution.py:402
  73.9 1.7 %collective-permute-start.28 = (f32[2,256]{1,0:T(2,128)S(1)}, f32[2,256]{1,0:T(2,128)S(1)}, u32[]{:S(2)}, u32[]{:S(2)}) collective-permute-start(f32[2,256]{1,0:T(2,128)S(1)} %add_add_fusion.parts), channel_id=1, source_target_pairs={{0,7},{1,6},{2,5},{3,4},{4,3},{5,2},{6,1},{7,0},{8,15},{9,14},{10,... | collective-permute-start | bytes 6152 | tf_op jit(solution)/shard_map/ppermute | solution.py:402
  (57 shorter events, 17.0 us)
Async XLA Ops:
  1.8 8.7 %collective-permute-start.3 = (bf16[128,768]{1,0:T(8,128)(2,1)S(1)}, bf16[128,768]{1,0:T(8,128)(2,1)S(1)}, u32[]{:S(2)}, u32[]{:S(2)}) collective-permute-start(bf16[128,768]{1,0:T(8,128)(2,1)S(1)} %pad_maximum_fusion.1), channel_id=1, source_target_pairs={{0,4},{2,6},{4,0},{6,2},{8,12},{10,14},{12,8},{14,10},{16,20},{18,... | collective-permute-start | bytes 589832 | tf_op jit(solution)/shard_map/ppermute | solution.py:395
  4.8 31.5 %collective-permute-start = (bf16[256,1024]{1,0:T(8,128)(2,1)}, bf16[256,1024]{1,0:T(8,128)(2,1)S(1)}, u32[]{:S(2)}, u32[]{:S(2)}) collective-permute-start(bf16[256,1024]{1,0:T(8,128)(2,1)} %bitcast.13), channel_id=1, source_target_pairs={{0,4},{2,6},{4,0},{6,2},{8,12},{10,14},{12,8},{14,10},{16,20},{18,... | collective-permute-start | bytes 1572872 | tf_op jit(solution)/shard_map/ppermute | solution.py:395
  4.9 36.1 %collective-permute-start.1 = (bf16[256,1024]{1,0:T(8,128)(2,1)}, bf16[256,1024]{1,0:T(8,128)(2,1)S(1)}, u32[]{:S(2)}, u32[]{:S(2)}) collective-permute-start(bf16[256,1024]{1,0:T(8,128)(2,1)} %bitcast.14), channel_id=1, source_target_pairs={{0,2},{2,0},{4,6},{6,4},{8,10},{10,8},{12,14},{14,12},{16,18},{18,... | collective-permute-start | bytes 1572872 | tf_op jit(solution)/shard_map/ppermute | solution.py:395
  6.9 34.2 %collective-permute-start.2 = (bf16[256,1024]{1,0:T(8,128)(2,1)}, bf16[256,1024]{1,0:T(8,128)(2,1)S(1)}, u32[]{:S(2)}, u32[]{:S(2)}) collective-permute-start(bf16[256,1024]{1,0:T(8,128)(2,1)} %bitcast.15), channel_id=1, source_target_pairs={{0,6},{2,4},{4,2},{6,0},{8,14},{10,12},{12,10},{14,8},{16,22},{18,... | collective-permute-start | bytes 1572872 | tf_op jit(solution)/shard_map/ppermute | solution.py:395
  8.3 8.4 %collective-permute-start.4 = (bf16[128,512]{1,0:T(8,128)(2,1)S(1)}, bf16[128,512]{1,0:T(8,128)(2,1)S(1)}, u32[]{:S(2)}, u32[]{:S(2)}) collective-permute-start(bf16[128,512]{1,0:T(8,128)(2,1)S(1)} %pad_maximum_fusion.2), channel_id=1, source_target_pairs={{0,8},{2,10},{4,12},{6,14},{8,16},{10,18},{12,20},{14,22},{16,24},... | collective-permute-start | bytes 393224 | tf_op jit(solution)/shard_map/ppermute | solution.py:398
  10.5 10.1 %collective-permute-start.6 = (bf16[128,512]{1,0:T(8,128)(2,1)S(1)}, bf16[128,512]{1,0:T(8,128)(2,1)S(1)}, u32[]{:S(2)}, u32[]{:S(2)}) collective-permute-start(bf16[128,512]{1,0:T(8,128)(2,1)S(1)} %pad_maximum_fusion.2), channel_id=1, source_target_pairs={{0,16},{2,18},{4,20},{6,22},{8,24},{10,26},{12,28},{14,30},{16,0},... | collective-permute-start | bytes 393224 | tf_op jit(solution)/shard_map/ppermute | solution.py:398
  16.7 6.7 %collective-permute-start.8 = (bf16[128,512]{1,0:T(8,128)(2,1)S(1)}, bf16[128,512]{1,0:T(8,128)(2,1)S(1)}, u32[]{:S(2)}, u32[]{:S(2)}) collective-permute-start(bf16[128,512]{1,0:T(8,128)(2,1)S(1)} %pad_maximum_fusion.2), channel_id=1, source_target_pairs={{0,24},{2,26},{4,28},{6,30},{8,0},{10,2},{12,4},{14,6},{16,8},{18,... | collective-permute-start | bytes 393224 | tf_op jit(solution)/shard_map/ppermute | solution.py:398
  20.6 8.9 %collective-permute-start.5 = (bf16[128,512]{1,0:T(8,128)(2,1)S(1)}, bf16[128,512]{1,0:T(8,128)(2,1)S(1)}, u32[]{:S(2)}, u32[]{:S(2)}) collective-permute-start(bf16[128,512]{1,0:T(8,128)(2,1)S(1)} %slice.18), channel_id=1, source_target_pairs={{0,8},{2,10},{4,12},{6,14},{8,16},{10,18},{12,20},{14,22},{16,24},... | collective-permute-start | bytes 393224 | tf_op jit(solution)/shard_map/ppermute | solution.py:398
  23.4 10.3 %collective-permute-start.7 = (bf16[128,512]{1,0:T(8,128)(2,1)S(1)}, bf16[128,512]{1,0:T(8,128)(2,1)S(1)}, u32[]{:S(2)}, u32[]{:S(2)}) collective-permute-start(bf16[128,512]{1,0:T(8,128)(2,1)S(1)} %slice.18), channel_id=1, source_target_pairs={{0,16},{2,18},{4,20},{6,22},{8,24},{10,26},{12,28},{14,30},{16,0},... | collective-permute-start | bytes 393224 | tf_op jit(solution)/shard_map/ppermute | solution.py:398
  29.6 6.5 %collective-permute-start.9 = (bf16[128,512]{1,0:T(8,128)(2,1)S(1)}, bf16[128,512]{1,0:T(8,128)(2,1)S(1)}, u32[]{:S(2)}, u32[]{:S(2)}) collective-permute-start(bf16[128,512]{1,0:T(8,128)(2,1)S(1)} %slice.18), channel_id=1, source_target_pairs={{0,24},{2,26},{4,28},{6,30},{8,0},{10,2},{12,4},{14,6},{16,8},{18,... | collective-permute-start | bytes 393224 | tf_op jit(solution)/shard_map/ppermute | solution.py:398
  33.7 22.7 %collective-permute-start.16 = (bf16[256,256]{1,0:T(8,128)(2,1)S(1)}, bf16[256,256]{1,0:T(8,128)(2,1)S(1)}, u32[]{:S(2)}, u32[]{:S(2)}) collective-permute-start(bf16[256,256]{1,0:T(8,128)(2,1)S(1)} %pad_maximum_fusion.3), channel_id=1, source_target_pairs={{0,8},{2,10},{4,12},{6,14},{8,16},{10,18},{12,20},{14,22},{16,24},... | collective-permute-start | bytes 393224 | tf_op jit(solution)/shard_map/ppermute | solution.py:398
  36.1 22.4 %collective-permute-start.17 = (bf16[256,256]{1,0:T(8,128)(2,1)S(1)}, bf16[256,256]{1,0:T(8,128)(2,1)S(1)}, u32[]{:S(2)}, u32[]{:S(2)}) collective-permute-start(bf16[256,256]{1,0:T(8,128)(2,1)S(1)} %pad_maximum_fusion.3), channel_id=1, source_target_pairs={{0,16},{2,18},{4,20},{6,22},{8,24},{10,26},{12,28},{14,30},{16,0},... | collective-permute-start | bytes 393224 | tf_op jit(solution)/shard_map/ppermute | solution.py:398
  36.3 22.1 %collective-permute-start.18 = (bf16[256,256]{1,0:T(8,128)(2,1)S(1)}, bf16[256,256]{1,0:T(8,128)(2,1)S(1)}, u32[]{:S(2)}, u32[]{:S(2)}) collective-permute-start(bf16[256,256]{1,0:T(8,128)(2,1)S(1)} %pad_maximum_fusion.3), channel_id=1, source_target_pairs={{0,24},{2,26},{4,28},{6,30},{8,0},{10,2},{12,4},{14,6},{16,8},{18,... | collective-permute-start | bytes 393224 | tf_op jit(solution)/shard_map/ppermute | solution.py:398
  44.1 5.4 %collective-permute-start.10 = (f32[1,256]{1,0:T(1,128)S(1)}, f32[1,256]{1,0:T(1,128)S(1)}, u32[]{:S(2)}, u32[]{:S(2)}) collective-permute-start(f32[1,256]{1,0:T(1,128)S(1)} %slice.16), channel_id=1, source_target_pairs={{0,8},{2,10},{4,12},{6,14},{8,16},{10,18},{12,20},{14,22},{16,24},... | collective-permute-start | bytes 3080 | tf_op jit(solution)/shard_map/ppermute | solution.py:398
  44.2 5.4 %collective-permute-start.11 = (f32[1,256]{1,0:T(1,128)S(1)}, f32[1,256]{1,0:T(1,128)S(1)}, u32[]{:S(2)}, u32[]{:S(2)}) collective-permute-start(f32[1,256]{1,0:T(1,128)S(1)} %slice.16), channel_id=1, source_target_pairs={{0,16},{2,18},{4,20},{6,22},{8,24},{10,26},{12,28},{14,30},{16,0},... | collective-permute-start | bytes 3080 | tf_op jit(solution)/shard_map/ppermute | solution.py:398
  54.5 5.4 %collective-permute-start.13 = (f32[1,256]{1,0:T(1,128)S(1)}, f32[1,256]{1,0:T(1,128)S(1)}, u32[]{:S(2)}, u32[]{:S(2)}) collective-permute-start(f32[1,256]{1,0:T(1,128)S(1)} %get-tuple-element.9), channel_id=1, source_target_pairs={{0,8},{2,10},{4,12},{6,14},{8,16},{10,18},{12,20},{14,22},{16,24},... | collective-permute-start | bytes 3080 | tf_op jit(solution)/shard_map/ppermute | solution.py:398
  54.6 5.4 %collective-permute-start.14 = (f32[1,256]{1,0:T(1,128)S(1)}, f32[1,256]{1,0:T(1,128)S(1)}, u32[]{:S(2)}, u32[]{:S(2)}) collective-permute-start(f32[1,256]{1,0:T(1,128)S(1)} %get-tuple-element.9), channel_id=1, source_target_pairs={{0,16},{2,18},{4,20},{6,22},{8,24},{10,26},{12,28},{14,30},{16,0},... | collective-permute-start | bytes 3080 | tf_op jit(solution)/shard_map/ppermute | solution.py:398
  56.4 4.2 %collective-permute-start.15 = (f32[1,256]{1,0:T(1,128)S(1)}, f32[1,256]{1,0:T(1,128)S(1)}, u32[]{:S(2)}, u32[]{:S(2)}) collective-permute-start(f32[1,256]{1,0:T(1,128)S(1)} %get-tuple-element.9), channel_id=1, source_target_pairs={{0,24},{2,26},{4,28},{6,30},{8,0},{10,2},{12,4},{14,6},{16,8},{18,... | collective-permute-start | bytes 3080 | tf_op jit(solution)/shard_map/ppermute | solution.py:398
  61.6 5.4 %collective-permute-start.19 = (f32[2,256]{1,0:T(2,128)S(1)}, f32[2,256]{1,0:T(2,128)S(1)}, u32[]{:S(2)}, u32[]{:S(2)}) collective-permute-start(f32[2,256]{1,0:T(2,128)S(1)} %shard_map.79), channel_id=1, source_target_pairs={{0,8},{2,10},{4,12},{6,14},{8,16},{10,18},{12,20},{14,22},{16,24},... | collective-permute-start | bytes 6152 | tf_op jit(solution)/shard_map/ppermute | solution.py:398
  63.4 4.5 %collective-permute-start.20 = (f32[2,256]{1,0:T(2,128)S(1)}, f32[2,256]{1,0:T(2,128)S(1)}, u32[]{:S(2)}, u32[]{:S(2)}) collective-permute-start(f32[2,256]{1,0:T(2,128)S(1)} %shard_map.79), channel_id=1, source_target_pairs={{0,16},{2,18},{4,20},{6,22},{8,24},{10,26},{12,28},{14,30},{16,0},... | collective-permute-start | bytes 6152 | tf_op jit(solution)/shard_map/ppermute | solution.py:398
  65.8 6.5 %collective-permute-start.29 = (f32[1,1024]{1,0:T(1,128)S(1)}, f32[1,1024]{1,0:T(1,128)S(1)}, u32[]{:S(2)}, u32[]{:S(2)}) collective-permute-start(f32[1,1024]{1,0:T(1,128)S(1)} %copy-done.2), channel_id=1, source_target_pairs={{0,1},{1,0},{2,3},{3,2},{4,5},{5,4},{6,7},{7,6},{8,9},{9,8},{10,11... | collective-permute-start | bytes 12296 | tf_op jit(solution)/shard_map/ppermute | solution.py:402
  68.7 5.1 %collective-permute-start.22 = (f32[2,256]{1,0:T(2,128)S(1)}, f32[2,256]{1,0:T(2,128)S(1)}, u32[]{:S(2)}, u32[]{:S(2)}) collective-permute-start(f32[2,256]{1,0:T(2,128)S(1)} %add_add_fusion.parts), channel_id=1, source_target_pairs={{0,2},{2,0},{4,6},{6,4},{8,10},{10,8},{12,14},{14,12},{16,18},{18,... | collective-permute-start | bytes 6152 | tf_op jit(solution)/shard_map/ppermute | solution.py:395
  70.3 5.3 %collective-permute-start.24 = (f32[2,256]{1,0:T(2,128)S(1)}, f32[2,256]{1,0:T(2,128)S(1)}, u32[]{:S(2)}, u32[]{:S(2)}) collective-permute-start(f32[2,256]{1,0:T(2,128)S(1)} %add_add_fusion.parts), channel_id=1, source_target_pairs={{0,6},{2,4},{4,2},{6,0},{8,14},{10,12},{12,10},{14,8},{16,22},{18,... | collective-permute-start | bytes 6152 | tf_op jit(solution)/shard_map/ppermute | solution.py:395
  73.9 4.0 %collective-permute-start.28 = (f32[2,256]{1,0:T(2,128)S(1)}, f32[2,256]{1,0:T(2,128)S(1)}, u32[]{:S(2)}, u32[]{:S(2)}) collective-permute-start(f32[2,256]{1,0:T(2,128)S(1)} %add_add_fusion.parts), channel_id=1, source_target_pairs={{0,7},{1,6},{2,5},{3,4},{4,3},{5,2},{6,1},{7,0},{8,15},{9,14},{10,... | collective-permute-start | bytes 6152 | tf_op jit(solution)/shard_map/ppermute | solution.py:402
  (10 other events, 123.9 us)

commit v2 on v1

--- a/solution.py
+++ b/solution.py
@@ -163,7 +163,7 @@
 
 def project_kernel(lengths, own, near, across, corner, w_own, w_near, *rest):
     shifted = rest[:6]
-    gain, normed, feats, sums, raw, weights, sems = rest[6:]
+    gain, normed, feats, totals, sums, raw, weights, sems = rest[6:]
     tokens, width = own.shape
     wide = 2 * GROUP
     z, x, u = places()
@@ -215,17 +215,17 @@
         pltpu.make_async_copy(own, raw.at[slot], sems.at[slot]).wait()
     key_one, sum_one = one(0)
     key_two, sum_two = one(1)
-    sums[0:1, :] = key_one + key_two
-    sums[1:2, :] = sum_one + sum_two
-    sums[2:3, :] = jnp.zeros_like(sum_one)
+    totals[...] = jnp.broadcast_to((key_one + key_two)[None], totals.shape)
+    sums[0:1, :] = sum_one + sum_two
+    sums[1:2, :] = jnp.zeros_like(sum_one)
 
     @pl.when(z == 0)
     def _():
         _, sum_short = one(2)
-        sums[2:3, :] = sum_short
-
-
-def scan_kernel(sums, total_1, total_2, total_3, feats, weight_sum, local):
+        sums[1:2, :] = sum_short
+
+
+def scan_kernel(totals, feats, weight_sum, local):
     tokens = feats.shape[0] // 3
     z, _, _ = places()
     row = lax.broadcasted_iota(jnp.int32, (tokens, tokens), 0)
@@ -233,8 +233,8 @@
     lower = (row >= col).astype(jnp.bfloat16)
     upper = (row <= col).astype(jnp.bfloat16)
     before = jnp.zeros((1, GROUP), jnp.float32)
-    for step, ref in enumerate((total_1, total_2, total_3), 1):
-        before = before + jnp.where(z >= step, ref[...], 0.0)
+    for plane in range(PLANES - 1):
+        before = before + jnp.where(plane < z, totals[plane], 0.0)
 
     def block(slot, carry):
         part = pl.ds(slot * tokens, tokens)
@@ -261,7 +261,7 @@
     share_two, key_two, _ = block(1, carry)
     after_two = suffix(share_two)
     after_one = suffix(share_one) + after_two[0:1, :]
-    weight_sum[...] = after_one[0:1, :]
+    weight_sum[...] = jnp.broadcast_to(after_one[0:1, :][None], weight_sum.shape)
     store(0, key_one, after_one)
     store(1, key_two, after_two)
 
@@ -271,76 +271,79 @@
         store(2, key, suffix(share))
 
 
-def pool_kernel(
-    lengths, sums, later_1, later_2, later_3, feats, local, normed, v_own, v_near, v_1, v_2, v_3, pooled, values, mixed
-):
+def mix_kernel(later, feats, local, normed, mixed):
     tokens = feats.shape[0] // 3
-    rows = v_own.shape[0]
-    width = normed.shape[1]
-    z, x, u = places()
-    long_u = jnp.where(lengths[0, 0] > tokens, u, 1 - u)
-    at = [pl.multiple_of((2 * z + half) * rows, rows) for half in (x, 1 - x)]
-    values[pl.ds(at[0], rows), :] = v_own[...]
-    values[pl.ds(at[1], rows), :] = v_near[...]
-    for step, ref in enumerate((v_1, v_2, v_3), 1):
-        other = lax.rem(z + PLANES - step, PLANES)
-        for half, place in enumerate((x, 1 - x)):
-            start = pl.multiple_of((2 * other + place) * rows, rows)
-            values[pl.ds(start, rows), :] = ref[pl.ds(half * rows, rows), :]
-
+    z, _, _ = places()
     after = jnp.zeros((1, GROUP), jnp.float32)
-    for step, ref in enumerate((later_1, later_2, later_3), 1):
-        after = after + jnp.where(z < step, ref[...], 0.0)
+    for plane in range(1, PLANES):
+        after = after + jnp.where(plane > z, later[plane], 0.0)
     lane = lax.broadcasted_iota(jnp.int32, (1, HEAD_DIM), 1)
 
     def mix(weight, slot, count):
         high, low = split_two(weight)
         both = jnp.where(lax.rem(lane, 64) < 32, high.astype(jnp.float32), low.astype(jnp.float32))
         part = normed[pl.ds(slot * tokens, count), :]
-        return lax.dot_general(both.astype(jnp.bfloat16), part, DOT_T, preferred_element_type=jnp.float32)
+        out = lax.dot_general(both.astype(jnp.bfloat16), part, DOT_T, preferred_element_type=jnp.float32)
+        return [out[h : h + 1, :] + out[h + 32 : h + 33, :] for h in (0, 64)]
+
+    def store(row, values):
+        for plane in range(PLANES):
+            mixed[plane, row : row + 1, :] = values[:, plane * GROUP : (plane + 1) * GROUP]
 
     key = feats[0 : 2 * tokens, GROUP:].astype(jnp.float32)
     extra = jnp.concatenate(
         [jnp.broadcast_to(c, (2 * tokens, HEAD_DIM // 2)) for c in head_sums(key * after)], axis=1
     )
-    mixed[0:HEAD_DIM, :] = mix(local[0 : 2 * tokens, :] + extra, 0, 2 * tokens)
-    mixed[HEAD_DIM:, :] = jnp.zeros((HEAD_DIM, width), jnp.float32)
+    for row, values in enumerate(mix(local[0 : 2 * tokens, :] + extra, 0, 2 * tokens)):
+        store(row, values)
+    mixed[:, 2:, :] = jnp.zeros((PLANES, 2, GROUP), jnp.float32)
 
     @pl.when(z == 0)
     def _():
-        mixed[HEAD_DIM:, :] = mix(local[2 * tokens :, :], 2, tokens)
-
-    picked = [mixed[h : h + 1, :] + mixed[h + 32 : h + 33, :] for h in (0, 64, 128, 192)]
-    high, low = split_two(jnp.concatenate(picked + picked, axis=0))
+        for row, values in enumerate(mix(local[2 * tokens :, :], 2, tokens)):
+            store(2 + row, values)
+
+
+def pool_kernel(lengths, tokens, sums, mixed, v_own, v_near, gain, part, values):
+    rows = v_own.shape[0]
+    _, x, u = places()
+    long_u = jnp.where(lengths[0, 0] > tokens, u, 1 - u)
+    for half, ref in ((x, v_own), (1 - x, v_near)):
+        values[pl.ds(pl.multiple_of(half * rows, rows), rows), :] = ref[...]
+    total = (mixed[0] + mixed[1]) + (mixed[2] + mixed[3])
+    high, low = split_two(jnp.concatenate([total, total], axis=0))
     out = jnp.dot(high, values[...], preferred_element_type=jnp.float32) + jnp.dot(
         low, values[...], preferred_element_type=jnp.float32
     )
     half = HEAD_DIM
-    long_row = jnp.concatenate([out[0:1, :half], out[1:2, half:]], axis=1) + sums[1:2, :]
-    short_row = jnp.concatenate([out[2:3, :half], out[3:4, half:]], axis=1) + sums[2:3, :]
-    pooled[0:1, :] = jnp.where(long_u == 0, long_row, short_row)
-    pooled[1:2, :] = jnp.where(long_u == 0, short_row, long_row)
-
-
-def loss_kernel(positives, parts, o_1, o_2, o_3, p_0, p_1, p_2, p_3, gain, gain_other, vec, loss, mine, theirs):
+    long_row = jnp.concatenate([out[0:1, :half], out[1:2, half:]], axis=1) + sums[0:1, :]
+    short_row = jnp.concatenate([out[2:3, :half], out[3:4, half:]], axis=1) + sums[1:2, :]
+    first = jnp.where(long_u == 0, long_row, short_row)
+    second = jnp.where(long_u == 0, short_row, long_row)
+    columns = pl.ds(pl.multiple_of((2 * x + u) * GROUP, GROUP), GROUP)
+    own_gain = gain[:, columns]
+    block = jnp.concatenate([first, second, own_gain, own_gain], axis=0)
+    part[...] = jnp.broadcast_to(block[None], part.shape)
+
+
+def loss_kernel(positives, parts, vec, loss, mine, theirs):
     z, x, u = places()
     domain = lax.axis_index("domain")
-    group = 2 * x + u
-    width = gain.shape[1]
+    width = mine.shape[1]
     piece = vec.shape[2]
 
-    def collect(refs, gains, dest):
+    def collect(place, dest):
         total = jnp.zeros((2, 1), jnp.float32)
-        for move, ref in enumerate(refs):
-            values = ref[...]
+        for group in range(PLANE):
+            blocks = [parts[2 * (PLANE * plane + group) + place] for plane in range(PLANES)]
+            values = (blocks[0][:2] + blocks[1][:2]) + (blocks[2][:2] + blocks[3][:2])
             total = total + jnp.sum(values * values, axis=1, keepdims=True)
-            at = pl.multiple_of(jnp.bitwise_xor(group, move) * GROUP, GROUP)
-            dest[:, pl.ds(at, GROUP)] = values * gains[:, pl.ds(at, GROUP)]
+            dest[:, group * GROUP : (group + 1) * GROUP] = values * blocks[0][2:3]
         factor = lax.rsqrt(total / width + epsilon)
         return (dest[...] * factor).astype(jnp.bfloat16).astype(jnp.float32)
 
-    own = collect((parts, o_1, o_2, o_3), gain, mine)
-    other = collect((p_0, p_1, p_2, p_3), gain_other, theirs)
+    own = collect(domain, mine)
+    other = collect(1 - domain, theirs)
     mine[...] = own
     start = pl.multiple_of((2 * z + x) * piece, piece)
     out = mine[:, pl.ds(start, piece)]
@@ -397,9 +400,10 @@
     def level_hop(a, step):
         return lax.ppermute(a, ("seq", "dp"), [(i, (i + PLANE * step) % here) for i in range(here)])
 
-    def domain_hop(a, move):
-        pairs = [(i, i ^ (2 * move + 1)) for i in range(2 * here)]
-        return lax.ppermute(a, ("seq", "dp", "domain"), pairs)
+    def swap(a, axes, groups=None):
+        return lax.all_to_all(a, axes, 0, 0, axis_index_groups=groups, tiled=True)
+
+    levels = [[2 * plane + half for plane in range(PLANES)] for half in range(2)]
 
     def columns(which):
         return jnp.concatenate(
@@ -417,13 +421,15 @@
         shifted.append(level_hop(w_own[:, : 2 * GROUP], step))
         shifted.append(level_hop(w_near[:, : 2 * GROUP], step))
     v_own, v_near = w_own[:, 2 * GROUP :], w_near[:, 2 * GROUP :]
-    v_both = jnp.concatenate([v_own, v_near], axis=0)
-    v_far = [level_hop(v_both, step) for step in range(1, PLANES)]
-    gain_other = domain_hop(pool_gain, 0)
-
-    normed, feats, sums = call(
+
+    normed, feats, totals, sums = call(
         project_kernel,
-        (shape((3 * tokens, width), bf16), shape((3 * tokens, 2 * GROUP), bf16), shape((8, GROUP), f32)),
+        (
+            shape((3 * tokens, width), bf16),
+            shape((3 * tokens, 2 * GROUP), bf16),
+            shape((PLANES, 1, GROUP), f32),
+            shape((2, GROUP), f32),
+        ),
         [smem()] + [anywhere()] * 12 + [vmem()],
         [
             pltpu.VMEM((3, tokens, width), bf16),
@@ -432,33 +438,38 @@
         ],
         2 * 3 * tokens * width * 2 * GROUP,
     )(lengths, events, near, across, corner, w_own, w_near, *shifted, norm_gain)
-    key_total = sums[0:1]
-    totals = [level_hop(key_total, step) for step in range(1, PLANES)]
+    totals = swap(totals, "seq", levels)
     weight_sum, local = call(
         scan_kernel,
-        (shape((1, GROUP), f32), shape((3 * tokens, HEAD_DIM), f32)),
-        [vmem()] * 5,
+        (shape((PLANES, 1, GROUP), f32), shape((3 * tokens, HEAD_DIM), f32)),
+        [vmem()] * 2,
         [],
         2 * 9 * tokens * tokens * GROUP,
-    )(sums, *totals, feats)
-    later = [level_hop(weight_sum, step) for step in range(1, PLANES)]
+    )(totals, feats)
+    later = swap(weight_sum, "seq", levels)
+    mixed = call(
+        mix_kernel,
+        shape((PLANES, 4, GROUP), f32),
+        [vmem()] * 4,
+        [],
+        2 * 3 * tokens * width * HEAD_DIM,
+    )(later, feats, local, normed)
+    mixed = swap(mixed, "seq", levels)
     part = call(
-        pool_kernel,
-        shape((2, GROUP), f32),
-        [smem()] + [vmem()] * 12,
-        [pltpu.VMEM((width, GROUP), bf16), pltpu.VMEM((2 * HEAD_DIM, width), f32)],
-        2 * 3 * tokens * width * HEAD_DIM,
-    )(lengths, sums, *later, feats, local, normed, v_own, v_near, *v_far)
-    part = part + level_hop(part, 1) + level_hop(part, 2) + level_hop(part, 3)
-    own = [plane_hop(part, move) for move in range(1, PLANE)]
-    other = [domain_hop(part, move) for move in range(PLANE)]
+        lambda lengths, *refs: pool_kernel(lengths, tokens, *refs),
+        shape((2 * here, 4, GROUP), f32),
+        [smem()] + [vmem()] * 5,
+        [pltpu.VMEM((GROUP, GROUP), bf16)],
+        2 * 8 * GROUP * GROUP,
+    )(lengths, sums, mixed, v_own, v_near, pool_gain)
+    parts = swap(part, ("seq", "dp", "domain"))
     vec, loss = call(
         loss_kernel,
         (shape((1, 1, width // 8), bf16), shape((1, 1), f32)),
-        [smem()] + [vmem()] * 10,
+        [smem(), vmem()],
         [pltpu.VMEM((2, width), f32), pltpu.VMEM((2, width), f32)],
         2**14,
-    )(positives, part, *own, *other, pool_gain, gain_other)
+    )(positives, parts)
     return vec, loss
 
 

time: 79.3 us -> 79.7 us (level)
  blocking collectives: 0 us -> 28.2 us
  starting transfers between devices: 41.7 us -> 24.2 us
  waiting for transfers between devices: 28.1 us -> 17.1 us
    all_to_all x0 -> x3, blocking collectives: none -> 28.2 us  [swap(): return lax.all_to_all(a, axes, 0, 0, axis_index_groups=groups, tiled=True)]
    ppermute x18 -> x6, waiting for transfers between devices: 25.2 us -> 11 us  [level_hop(): lax.ppermute(a, ('seq', 'dp'), [(i, (i + PLANE * step) % here) for i in r...]
    ppermute x18 -> x6, starting transfers between devices: 28.4 us -> 14.5 us  [level_hop(): lax.ppermute(a, ('seq', 'dp'), [(i, (i + PLANE * step) % here) for i in r...]
    all_to_all x0 -> x1, waiting for transfers between devices: none -> 5.56 us  [swap(): return lax.all_to_all(a, axes, 0, 0, axis_index_groups=groups, tiled=True)]
    ppermute x7 -> x4, starting transfers between devices: 9.98 us -> 6.49 us  [plane_hop(): return lax.ppermute(a, ('seq', 'dp'), [(i, i ^ move) for i in range(here)])]
    ppermute x5 -> x0, starting transfers between devices: 3.32 us -> none  [domain_hop(): return lax.ppermute(a, ('seq', 'dp', 'domain'), pairs)]
    all_to_all x0 -> x1, starting transfers between devices: none -> 3.24 us  [swap(): return lax.all_to_all(a, axes, 0, 0, axis_index_groups=groups, tiled=True)]
    ppermute x5 -> x0, waiting for transfers between devices: 2.28 us -> none  [domain_hop(): return lax.ppermute(a, ('seq', 'dp', 'domain'), pairs)]
  transfers between devices with their start and end apart: 30 -> 11, of which waited for: 15 -> 7; matrix products, arithmetic and copies ran while one was open for 0% -> 0% of each run, Pallas kernels for 6% -> 0%
where the time goes in v2:
time: 79.7 us; the launch traced here: 79.4 us
  blocking collectives  28.2 us (35%)
  starting transfers between devices  24.2 us (30%)
  waiting for transfers between devices  17.1 us (21%)
  Pallas kernels  7.29 us (9%)
  between operations  1.43 us (2%)
  local copies, waits for them, and re-layouts  1.13 us (1%)
    all_to_all x3, blocking collectives, swap(): return lax.all_to_all(a, axes, 0, 0, axis_index_groups=groups, tiled=True)  28.2 us
    ppermute x6, starting transfers between devices, level_hop(): lax.ppermute(a, ('seq', 'dp'), [(i, (i + PLANE * step) % here) for i in r...  14.5 us
    ppermute x6, waiting for transfers between devices, level_hop(): lax.ppermute(a, ('seq', 'dp'), [(i, (i + PLANE * step) % here) for i in r...  11 us
    ppermute x4, starting transfers between devices, plane_hop(): return lax.ppermute(a, ('seq', 'dp'), [(i, i ^ move) for i in range(here)])  6.49 us
    all_to_all x1, waiting for transfers between devices, swap(): return lax.all_to_all(a, axes, 0, 0, axis_index_groups=groups, tiled=True)  5.56 us
    all_to_all x1, starting transfers between devices, swap(): return lax.all_to_all(a, axes, 0, 0, axis_index_groups=groups, tiled=True)  3.24 us
    pallas_call x1, Pallas kernels, towers(): call(project_kernel, (shape((3 * tokens, width), bf16), shape((3 * tokens...  3.05 us
  transfers between devices with their start and end apart: 11, of which 7 were waited for; matrix products, arithmetic and copies ran while one was open for 0% of the time, Pallas kernels for 0%

profile of v2, /device:TPU:0, one launch (start us, length us, event | category | flops | bytes accessed | tf_op | source)
XLA Modules:
  0.0 79.4 jit_solution(5229904631085615391)
XLA Ops:
  0.7 1.1 %dynamic-slice_bitcast_fusion.2 = (bf16[128,256]{1,0:T(8,128)(2,1)S(1)}, bf16[128,256]{1,0:T(8,128)(2,1)S(1)}, bf16[128,256]{1,0:T(8,128)(2,1)S(1)}, bf16[128,25...) fusion(bf16[1,128,3072]{2,1,0:T(8,128)(2,1)} %param.7, s32[]{:T(128)S(6)} %select_n.21, ...), kind=kLoop, calls=%fused_computation.5 | loop fusion | bytes 786456 | tf_op jit(solution)/shard_map/dynamic_slice | solution.py:410
  1.8 3.0 %collective-permute-start.3 = (bf16[128,768]{1,0:T(8,128)(2,1)S(1)}, bf16[128,768]{1,0:T(8,128)(2,1)S(1)}, u32[]{:S(2)}, u32[]{:S(2)}) collective-permute-start(bf16[128,768]{1,0:T(8,128)(2,1)S(1)} %pad_maximum_fusion.1), channel_id=1, source_target_pairs={{0,4},{2,6},{4,0},{6,2},{8,12},{10,14},{12,8},{14,10},{16,20},{18,... | collective-permute-start | bytes 589832 | tf_op jit(solution)/shard_map/ppermute | solution.py:398
  4.9 2.0 %collective-permute-start.1 = (bf16[256,1024]{1,0:T(8,128)(2,1)}, bf16[256,1024]{1,0:T(8,128)(2,1)S(1)}, u32[]{:S(2)}, u32[]{:S(2)}) collective-permute-start(bf16[256,1024]{1,0:T(8,128)(2,1)} %bitcast.14), channel_id=1, source_target_pairs={{0,2},{2,0},{4,6},{6,4},{8,10},{10,8},{12,14},{14,12},{16,18},{18,... | collective-permute-start | bytes 1572872 | tf_op jit(solution)/shard_map/ppermute | solution.py:398
  6.9 1.4 %collective-permute-start.2 = (bf16[256,1024]{1,0:T(8,128)(2,1)}, bf16[256,1024]{1,0:T(8,128)(2,1)S(1)}, u32[]{:S(2)}, u32[]{:S(2)}) collective-permute-start(bf16[256,1024]{1,0:T(8,128)(2,1)} %bitcast.15), channel_id=1, source_target_pairs={{0,6},{2,4},{4,2},{6,0},{8,14},{10,12},{12,10},{14,8},{16,22},{18,... | collective-permute-start | bytes 1572872 | tf_op jit(solution)/shard_map/ppermute | solution.py:398
  8.3 1.6 %collective-permute-start.4 = (bf16[128,512]{1,0:T(8,128)(2,1)S(1)}, bf16[128,512]{1,0:T(8,128)(2,1)S(1)}, u32[]{:S(2)}, u32[]{:S(2)}) collective-permute-start(bf16[128,512]{1,0:T(8,128)(2,1)S(1)} %pad_maximum_fusion.2), channel_id=1, source_target_pairs={{0,8},{2,10},{4,12},{6,14},{8,16},{10,18},{12,20},{14,22},{16,24},... | collective-permute-start | bytes 393224 | tf_op jit(solution)/shard_map/ppermute | solution.py:401
  9.9 0.6 collective-permute-done.3.w_near
  10.5 3.2 %collective-permute-start.6 = (bf16[128,512]{1,0:T(8,128)(2,1)S(1)}, bf16[128,512]{1,0:T(8,128)(2,1)S(1)}, u32[]{:S(2)}, u32[]{:S(2)}) collective-permute-start(bf16[128,512]{1,0:T(8,128)(2,1)S(1)} %pad_maximum_fusion.2), channel_id=1, source_target_pairs={{0,16},{2,18},{4,20},{6,22},{8,24},{10,26},{12,28},{14,30},{16,0},... | collective-permute-start | bytes 393224 | tf_op jit(solution)/shard_map/ppermute | solution.py:401
  13.7 3.0 %collective-permute-done.4.rest_0_ = bf16[128,512]{1,0:T(8,128)(2,1)S(1)} collective-permute-done((bf16[128,512]{1,0:T(8,128)(2,1)S(1)}, bf16[128,512]{1,0:T(8,128)(2,1)S(1)}, u32[]{:S(2)}, u32[]{:S(2)}) %collective-permute-start.4) | collective-permute-done | bytes 131104 | tf_op jit(solution)/shard_map/ppermute | solution.py:401
  16.7 0.5 collective-permute-start.8
  17.2 3.4 %collective-permute-done.6.rest_2_ = bf16[128,512]{1,0:T(8,128)(2,1)S(1)} collective-permute-done((bf16[128,512]{1,0:T(8,128)(2,1)S(1)}, bf16[128,512]{1,0:T(8,128)(2,1)S(1)}, u32[]{:S(2)}, u32[]{:S(2)}) %collective-permute-start.6) | collective-permute-done | bytes 131104 | tf_op jit(solution)/shard_map/ppermute | solution.py:401
  20.6 2.8 %collective-permute-start.5 = (bf16[128,512]{1,0:T(8,128)(2,1)S(1)}, bf16[128,512]{1,0:T(8,128)(2,1)S(1)}, u32[]{:S(2)}, u32[]{:S(2)}) collective-permute-start(bf16[128,512]{1,0:T(8,128)(2,1)S(1)} %slice.14), channel_id=1, source_target_pairs={{0,8},{2,10},{4,12},{6,14},{8,16},{10,18},{12,20},{14,22},{16,24},... | collective-permute-start | bytes 393224 | tf_op jit(solution)/shard_map/ppermute | solution.py:401
  23.4 3.4 %collective-permute-start.7 = (bf16[128,512]{1,0:T(8,128)(2,1)S(1)}, bf16[128,512]{1,0:T(8,128)(2,1)S(1)}, u32[]{:S(2)}, u32[]{:S(2)}) collective-permute-start(bf16[128,512]{1,0:T(8,128)(2,1)S(1)} %slice.14), channel_id=1, source_target_pairs={{0,16},{2,18},{4,20},{6,22},{8,24},{10,26},{12,28},{14,30},{16,0},... | collective-permute-start | bytes 393224 | tf_op jit(solution)/shard_map/ppermute | solution.py:401
  26.8 2.8 %collective-permute-done.5.rest_1_ = bf16[128,512]{1,0:T(8,128)(2,1)S(1)} collective-permute-done((bf16[128,512]{1,0:T(8,128)(2,1)S(1)}, bf16[128,512]{1,0:T(8,128)(2,1)S(1)}, u32[]{:S(2)}, u32[]{:S(2)}) %collective-permute-start.5) | collective-permute-done | bytes 131104 | tf_op jit(solution)/shard_map/ppermute | solution.py:401
  29.6 3.0 %collective-permute-start.9 = (bf16[128,512]{1,0:T(8,128)(2,1)S(1)}, bf16[128,512]{1,0:T(8,128)(2,1)S(1)}, u32[]{:S(2)}, u32[]{:S(2)}) collective-permute-start(bf16[128,512]{1,0:T(8,128)(2,1)S(1)} %slice.14), channel_id=1, source_target_pairs={{0,24},{2,26},{4,28},{6,30},{8,0},{10,2},{12,4},{14,6},{16,8},{18,... | collective-permute-start | bytes 393224 | tf_op jit(solution)/shard_map/ppermute | solution.py:401
  33.7 1.3 %collective-permute-done.9.rest_5_ = bf16[128,512]{1,0:T(8,128)(2,1)S(1)} collective-permute-done((bf16[128,512]{1,0:T(8,128)(2,1)S(1)}, bf16[128,512]{1,0:T(8,128)(2,1)S(1)}, u32[]{:S(2)}, u32[]{:S(2)}) %collective-permute-start.9) | collective-permute-done | bytes 131104 | tf_op jit(solution)/shard_map/ppermute | solution.py:401
  35.1 3.1 %shard_map.77 = (bf16[768,1024]{1,0:T(8,128)(2,1)S(1)}, bf16[768,512]{1,0:T(8,128)(2,1)S(1)}, f32[4,1,256]{2,1,0:T(1,128)S(1)}, f32[2,256]{1,0:T(2,128)S(1)}) custom-call(s32[1,1]{1,0:T(1,128)S(6)} %copy.8.lengths, bf16[256,1024]{1,0:T(8,128)(2,1)S(1)} %bitcast.16, bf16[256,1024]{1,0:T(8,128)(2,1)S(1)} %collective-permute-done.near, ...), custom_call_target="tpu_custom_call" | custom-call | flops 805306368 | bytes 2097152 | tf_op jit(solution)/shard_map/pallas_call | solution.py:425
  38.1 10.3 %all_to_all.20.totals = f32[4,1,256]{2,1,0:T(1,128)S(1)} all-to-all(f32[4,1,256]{2,1,0:T(1,128)S(1)} %get-tuple-element.9), channel_id=1, replica_groups={{0,8,16,24},{4,12,20,28},{1,9,17,25},{5,13,21,29},{2,10,18,26},{6,14,22..., dimensions={0} | all-to-all | bytes 8192 | tf_op jit(solution)/shard_map/all_to_all | solution.py:404
  48.4 1.4 %shard_map.78 = (f32[4,1,256]{2,1,0:T(1,128)S(1)}, f32[768,128]{1,0:T(8,128)S(1)}) custom-call(f32[4,1,256]{2,1,0:T(1,128)S(1)} %all_to_all.20.totals, bf16[768,512]{1,0:T(8,128)(2,1)S(1)} %get-tuple-element.10.feats), custom_call_target="tpu_custom_call" | custom-call | flops 301989888 | bytes 2097152 | tf_op jit(solution)/shard_map/pallas_call | solution.py:442
  49.8 7.9 %all_to_all.21.later = f32[4,1,256]{2,1,0:T(1,128)S(1)} all-to-all(f32[4,1,256]{2,1,0:T(1,128)S(1)} %get-tuple-element.11), channel_id=1, replica_groups={{0,8,16,24},{4,12,20,28},{1,9,17,25},{5,13,21,29},{2,10,18,26},{6,14,22..., dimensions={0} | all-to-all | bytes 8192 | tf_op jit(solution)/shard_map/all_to_all | solution.py:404
  57.7 1.4 %shard_map.79 = f32[4,4,256]{2,1,0:T(4,128)} custom-call(f32[4,1,256]{2,1,0:T(1,128)S(1)} %all_to_all.21.later, bf16[768,512]{1,0:T(8,128)(2,1)S(1)} %get-tuple-element.10.feats, f32[768,128]{1,0:T(8,128)S(1)} %get-tuple-element.12.local, bf16[768,1024]{1,0:T(8,128)(2,1)S(1)} %get-tuple-element.13.normed), custom_call_target="tpu_custom_call" | custom-call | flops 201326592 | bytes 2097152 | tf_op jit(solution)/shard_map/pallas_call | solution.py:450
  59.1 3.2 %all-to-all-start.2 = ((f32[4,4,256]{2,1,0:T(4,128)}), f32[4,4,256]{2,1,0:T(4,128)S(1)}, u32[]{:S(2)}, u32[]{:S(2)}) async-start(f32[4,4,256]{2,1,0:T(4,128)} %shard_map.79), calls=%async_computation.2 | async-start | bytes 32768 | tf_op jit(solution)/shard_map/all_to_all | solution.py:404
  62.4 5.6 %all-to-all-done.2.refs_1_ = f32[4,4,256]{2,1,0:T(4,128)S(1)} async-done(((f32[4,4,256]{2,1,0:T(4,128)}), f32[4,4,256]{2,1,0:T(4,128)S(1)}, u32[]{:S(2)}, u32[]{:S(2)}) %all-to-all-start.2) | async-done | bytes 16416 | tf_op jit(solution)/shard_map/all_to_all | solution.py:404
  68.1 10.0 %all_to_all.22.parts = f32[32,4,256]{2,1,0:T(4,128)S(1)} all-to-all(f32[32,4,256]{2,1,0:T(4,128)S(1)} %shard_map.80), channel_id=1, replica_groups=mesh['seq'=8,'dp'=2,'domain'=2] {'seq','dp','domain'}, dimensions={0} | all-to-all | bytes 262144 | tf_op jit(solution)/shard_map/all_to_all | solution.py:404
  78.1 1.3 %shard_map.81 = (bf16[1,1,128]{2,1,0:T(2,128)(2,1)}, f32[1,1]{1,0:T(1,128)}) custom-call(s32[2]{0:T(128)S(1)} %copy-done.3, f32[32,4,256]{2,1,0:T(4,128)S(1)} %all_to_all.22.parts), custom_call_target="tpu_custom_call" | custom-call | flops 16384 | bytes 2097152 | tf_op jit(solution)/shard_map/pallas_call | solution.py:466
  (20 shorter events, 0.9 us)
Async XLA Ops:
  0.6 34.4 %copy-start = (bf16[1,1,256,1024]{3,2,1,0:T(8,128)(2,1)S(1)}, bf16[1,1,256,1024]{3,2,1,0:T(8,128)(2,1)}, u32[]{:S(2)}) copy-start(bf16[1,1,256,1024]{3,2,1,0:T(8,128)(2,1)} %param.6) | copy-start | bytes 1572868
  0.6 34.4 %copy-start.1 = (f32[1,1024]{1,0:T(1,128)S(1)}, f32[1,1024]{1,0:T(1,128)}, u32[]{:S(2)}) copy-start(f32[1,1024]{1,0:T(1,128)} %rest_6_.1) | copy-start | bytes 12292
  1.8 8.7 %collective-permute-start.3 = (bf16[128,768]{1,0:T(8,128)(2,1)S(1)}, bf16[128,768]{1,0:T(8,128)(2,1)S(1)}, u32[]{:S(2)}, u32[]{:S(2)}) collective-permute-start(bf16[128,768]{1,0:T(8,128)(2,1)S(1)} %pad_maximum_fusion.1), channel_id=1, source_target_pairs={{0,4},{2,6},{4,0},{6,2},{8,12},{10,14},{12,8},{14,10},{16,20},{18,... | collective-permute-start | bytes 589832 | tf_op jit(solution)/shard_map/ppermute | solution.py:398
  4.8 30.3 %collective-permute-start = (bf16[256,1024]{1,0:T(8,128)(2,1)}, bf16[256,1024]{1,0:T(8,128)(2,1)S(1)}, u32[]{:S(2)}, u32[]{:S(2)}) collective-permute-start(bf16[256,1024]{1,0:T(8,128)(2,1)} %bitcast.13), channel_id=1, source_target_pairs={{0,4},{2,6},{4,0},{6,2},{8,12},{10,14},{12,8},{14,10},{16,20},{18,... | collective-permute-start | bytes 1572872 | tf_op jit(solution)/shard_map/ppermute | solution.py:398
  4.9 30.2 %collective-permute-start.1 = (bf16[256,1024]{1,0:T(8,128)(2,1)}, bf16[256,1024]{1,0:T(8,128)(2,1)S(1)}, u32[]{:S(2)}, u32[]{:S(2)}) collective-permute-start(bf16[256,1024]{1,0:T(8,128)(2,1)} %bitcast.14), channel_id=1, source_target_pairs={{0,2},{2,0},{4,6},{6,4},{8,10},{10,8},{12,14},{14,12},{16,18},{18,... | collective-permute-start | bytes 1572872 | tf_op jit(solution)/shard_map/ppermute | solution.py:398
  6.9 28.2 %collective-permute-start.2 = (bf16[256,1024]{1,0:T(8,128)(2,1)}, bf16[256,1024]{1,0:T(8,128)(2,1)S(1)}, u32[]{:S(2)}, u32[]{:S(2)}) collective-permute-start(bf16[256,1024]{1,0:T(8,128)(2,1)} %bitcast.15), channel_id=1, source_target_pairs={{0,6},{2,4},{4,2},{6,0},{8,14},{10,12},{12,10},{14,8},{16,22},{18,... | collective-permute-start | bytes 1572872 | tf_op jit(solution)/shard_map/ppermute | solution.py:398
  8.3 8.4 %collective-permute-start.4 = (bf16[128,512]{1,0:T(8,128)(2,1)S(1)}, bf16[128,512]{1,0:T(8,128)(2,1)S(1)}, u32[]{:S(2)}, u32[]{:S(2)}) collective-permute-start(bf16[128,512]{1,0:T(8,128)(2,1)S(1)} %pad_maximum_fusion.2), channel_id=1, source_target_pairs={{0,8},{2,10},{4,12},{6,14},{8,16},{10,18},{12,20},{14,22},{16,24},... | collective-permute-start | bytes 393224 | tf_op jit(solution)/shard_map/ppermute | solution.py:401
  10.5 10.1 %collective-permute-start.6 = (bf16[128,512]{1,0:T(8,128)(2,1)S(1)}, bf16[128,512]{1,0:T(8,128)(2,1)S(1)}, u32[]{:S(2)}, u32[]{:S(2)}) collective-permute-start(bf16[128,512]{1,0:T(8,128)(2,1)S(1)} %pad_maximum_fusion.2), channel_id=1, source_target_pairs={{0,16},{2,18},{4,20},{6,22},{8,24},{10,26},{12,28},{14,30},{16,0},... | collective-permute-start | bytes 393224 | tf_op jit(solution)/shard_map/ppermute | solution.py:401
  16.7 6.7 %collective-permute-start.8 = (bf16[128,512]{1,0:T(8,128)(2,1)S(1)}, bf16[128,512]{1,0:T(8,128)(2,1)S(1)}, u32[]{:S(2)}, u32[]{:S(2)}) collective-permute-start(bf16[128,512]{1,0:T(8,128)(2,1)S(1)} %pad_maximum_fusion.2), channel_id=1, source_target_pairs={{0,24},{2,26},{4,28},{6,30},{8,0},{10,2},{12,4},{14,6},{16,8},{18,... | collective-permute-start | bytes 393224 | tf_op jit(solution)/shard_map/ppermute | solution.py:401
  20.6 8.9 %collective-permute-start.5 = (bf16[128,512]{1,0:T(8,128)(2,1)S(1)}, bf16[128,512]{1,0:T(8,128)(2,1)S(1)}, u32[]{:S(2)}, u32[]{:S(2)}) collective-permute-start(bf16[128,512]{1,0:T(8,128)(2,1)S(1)} %slice.14), channel_id=1, source_target_pairs={{0,8},{2,10},{4,12},{6,14},{8,16},{10,18},{12,20},{14,22},{16,24},... | collective-permute-start | bytes 393224 | tf_op jit(solution)/shard_map/ppermute | solution.py:401
  23.4 10.3 %collective-permute-start.7 = (bf16[128,512]{1,0:T(8,128)(2,1)S(1)}, bf16[128,512]{1,0:T(8,128)(2,1)S(1)}, u32[]{:S(2)}, u32[]{:S(2)}) collective-permute-start(bf16[128,512]{1,0:T(8,128)(2,1)S(1)} %slice.14), channel_id=1, source_target_pairs={{0,16},{2,18},{4,20},{6,22},{8,24},{10,26},{12,28},{14,30},{16,0},... | collective-permute-start | bytes 393224 | tf_op jit(solution)/shard_map/ppermute | solution.py:401
  29.6 5.5 %collective-permute-start.9 = (bf16[128,512]{1,0:T(8,128)(2,1)S(1)}, bf16[128,512]{1,0:T(8,128)(2,1)S(1)}, u32[]{:S(2)}, u32[]{:S(2)}) collective-permute-start(bf16[128,512]{1,0:T(8,128)(2,1)S(1)} %slice.14), channel_id=1, source_target_pairs={{0,24},{2,26},{4,28},{6,30},{8,0},{10,2},{12,4},{14,6},{16,8},{18,... | collective-permute-start | bytes 393224 | tf_op jit(solution)/shard_map/ppermute | solution.py:401
  49.8 18.1 %copy-start.2 = (f32[1,1024]{1,0:T(1,128)S(1)}, f32[1,1024]{1,0:T(1,128)}, u32[]{:S(2)}) copy-start(f32[1,1024]{1,0:T(1,128)} %refs_4_.1) | copy-start | bytes 12292
  57.7 20.4 %copy-start.3 = (s32[2]{0:T(128)S(1)}, s32[2]{0:T(128)}, u32[]{:S(2)}) copy-start(s32[2]{0:T(128)} %positives.1) | copy-start | bytes 28
  59.1 8.8 %all-to-all-start.2 = ((f32[4,4,256]{2,1,0:T(4,128)}), f32[4,4,256]{2,1,0:T(4,128)S(1)}, u32[]{:S(2)}, u32[]{:S(2)}) async-start(f32[4,4,256]{2,1,0:T(4,128)} %shard_map.79), calls=%async_computation.2 | async-start | bytes 32768 | tf_op jit(solution)/shard_map/all_to_all | solution.py:404

commit v3 on v1

--- a/solution.py
+++ b/solution.py
@@ -161,80 +161,106 @@
     return high, (a - high.astype(jnp.float32)).astype(jnp.bfloat16)
 
 
-def project_kernel(lengths, own, near, across, corner, w_own, w_near, *rest):
-    shifted = rest[:6]
-    gain, normed, feats, sums, raw, weights, sems = rest[6:]
-    tokens, width = own.shape
-    wide = 2 * GROUP
+def norm_kernel(lengths, own, near, across, corner_a, corner_b, gain, normed, sums, raw, sems):
+    tokens = own.shape[0]
+    half = corner_a.shape[0]
     z, x, u = places()
-    own_long = lengths[0, 0] > tokens
-    long_u = jnp.where(own_long, u, 1 - u)
-    blocks = (own, near, across, corner)
-
-    rows = width // (2 * PLANES)
-    half_at = (x, 1 - x)
-    copies = []
-    for half, ref in enumerate((w_own, w_near)):
-        at = pl.multiple_of((2 * z + half_at[half]) * rows, rows)
-        copies.append((ref.at[:, pl.ds(0, wide)], at))
-    for step in range(1, PLANES):
-        other = lax.rem(z + PLANES - step, PLANES)
-        for half in range(2):
-            at = pl.multiple_of((2 * other + half_at[half]) * rows, rows)
-            copies.append((shifted[2 * (step - 1) + half], at))
-    for i, (ref, at) in enumerate(copies):
-        pltpu.make_async_copy(ref, weights.at[pl.ds(at, rows)], sems.at[3 + i]).start()
+    long_u = jnp.where(lengths[0, 0] > tokens, u, 1 - u)
+
+    def fetch(slot, pick):
+        for j, ref in enumerate((own, near, across)):
+
+            @pl.when(pick == j)
+            def _():
+                pltpu.make_async_copy(ref.at[pl.ds(0, half)], raw.at[slot, pl.ds(0, half)], sems.at[slot, 0]).start()
+                pltpu.make_async_copy(ref.at[pl.ds(half, half)], raw.at[slot, pl.ds(half, half)], sems.at[slot, 1]).start()
+
+        @pl.when(pick == 3)
+        def _():
+            pltpu.make_async_copy(corner_a, raw.at[slot, pl.ds(0, half)], sems.at[slot, 0]).start()
+            pltpu.make_async_copy(corner_b, raw.at[slot, pl.ds(half, half)], sems.at[slot, 1]).start()
 
     for slot in range(3):
         from_x = 1 if slot == 1 else 0
         from_u = 1 - long_u if slot == 2 else long_u
-        pick = jnp.bitwise_xor(x, from_x) + 2 * jnp.bitwise_xor(u, from_u)
-        for j, ref in enumerate(blocks):
-
-            @pl.when(pick == j)
-            def _():
-                pltpu.make_async_copy(ref, raw.at[slot], sems.at[slot]).start()
-
-    for i, (ref, at) in enumerate(copies):
-        pltpu.make_async_copy(ref, weights.at[pl.ds(at, rows)], sems.at[3 + i]).wait()
+        fetch(slot, jnp.bitwise_xor(x, from_x) + 2 * jnp.bitwise_xor(u, from_u))
     columns = pl.ds(pl.multiple_of((2 * x + u) * GROUP, GROUP), GROUP)
 
     def one(slot):
         values = raw[slot].astype(jnp.float32)
         scale = lax.rsqrt(jnp.mean(values * values, axis=1, keepdims=True) + epsilon)
-        low = (values * scale * gain[...]).astype(jnp.bfloat16)
-        normed[pl.ds(slot * tokens, tokens), :] = low
-        out = jnp.dot(low, weights[...], preferred_element_type=jnp.float32)
-        out = jnp.where(out > 0.0, out + 1.0, jnp.exp(jnp.minimum(out, 0.0))).astype(jnp.bfloat16)
-        feats[pl.ds(slot * tokens, tokens), :] = out
-        key_total = jnp.sum(out[:, GROUP:].astype(jnp.float32), axis=0, keepdims=True)
-        part = raw[slot, :, columns].astype(jnp.float32)
-        return key_total, jnp.sum(part, axis=0, keepdims=True)
+        normed[pl.ds(slot * tokens, tokens), :] = (values * scale * gain[...]).astype(jnp.bfloat16)
+        return jnp.sum(raw[slot, :, columns].astype(jnp.float32), axis=0, keepdims=True)
 
     for slot in range(3):
-        pltpu.make_async_copy(own, raw.at[slot], sems.at[slot]).wait()
-    key_one, sum_one = one(0)
-    key_two, sum_two = one(1)
-    sums[0:1, :] = key_one + key_two
-    sums[1:2, :] = sum_one + sum_two
-    sums[2:3, :] = jnp.zeros_like(sum_one)
+        for part in range(2):
+            at = pl.ds(part * half, half)
+            pltpu.make_async_copy(own.at[at], raw.at[slot, at], sems.at[slot, part]).wait()
+    sums[0:1, :] = one(0) + one(1)
+    sums[1:2, :] = jnp.zeros((1, GROUP), jnp.float32)
 
     @pl.when(z == 0)
     def _():
-        _, sum_short = one(2)
-        sums[2:3, :] = sum_short
-
-
-def scan_kernel(sums, total_1, total_2, total_3, feats, weight_sum, local):
+        sums[1:2, :] = one(2)
+
+
+def gather_rows(z, x, parts, dest):
+    rows = parts[0].shape[0] // 2
+    for j, ref in enumerate(parts):
+        plane = jnp.bitwise_xor(z, j)
+        for half, place in enumerate((x, 1 - x)):
+            start = pl.multiple_of((2 * plane + place) * rows, rows)
+            dest[pl.ds(start, rows), :] = ref[pl.ds(half * rows, rows), :]
+
+
+def project_kernel(normed, own, one_away, two_own, two_near, next_plane, far, feats, totals, weights):
+    tokens = normed.shape[0] // 3
+    rows = two_own.shape[0]
+    z, x, _ = places()
+
+    def put(plane, place, values):
+        weights[pl.ds(pl.multiple_of((2 * plane + place) * rows, rows), rows), :] = values
+
+    def put_both(plane, ref):
+        put(plane, x, ref[:rows, :])
+        put(plane, 1 - x, ref[rows:, :])
+
+    put_both(z, own)
+    put_both(jnp.bitwise_xor(z, 1), one_away)
+    put(jnp.bitwise_xor(z, 2), x, two_own[...])
+    put(jnp.bitwise_xor(z, 2), 1 - x, two_near[...])
+    inner = jnp.logical_or(z == 1, z == 2)
+
+    @pl.when(inner)
+    def _():
+        put_both(3 - z, next_plane)
+
+    @pl.when(jnp.logical_not(inner))
+    def _():
+        put_both(3 - z, far)
+
+    def one(slot, count):
+        part = pl.ds(slot * tokens, count)
+        out = jnp.dot(normed[part, :], weights[...], preferred_element_type=jnp.float32)
+        out = jnp.where(out > 0.0, out + 1.0, jnp.exp(jnp.minimum(out, 0.0))).astype(jnp.bfloat16)
+        feats[part, :] = out
+        return jnp.sum(out[:, GROUP:].astype(jnp.float32), axis=0, keepdims=True)
+
+    totals[...] = one(0, tokens) + one(1, tokens)
+
+    @pl.when(z == 0)
+    def _():
+        one(2, tokens)
+
+
+def scan_kernel(before_1, before_2, before_3, feats, weight_sum, local):
     tokens = feats.shape[0] // 3
     z, _, _ = places()
     row = lax.broadcasted_iota(jnp.int32, (tokens, tokens), 0)
     col = lax.broadcasted_iota(jnp.int32, (tokens, tokens), 1)
     lower = (row >= col).astype(jnp.bfloat16)
     upper = (row <= col).astype(jnp.bfloat16)
-    before = jnp.zeros((1, GROUP), jnp.float32)
-    for step, ref in enumerate((total_1, total_2, total_3), 1):
-        before = before + jnp.where(z >= step, ref[...], 0.0)
+    before = before_1[...] + before_2[...] + before_3[...]
 
     def block(slot, carry):
         part = pl.ds(slot * tokens, tokens)
@@ -272,32 +298,21 @@
 
 
 def pool_kernel(
-    lengths, sums, later_1, later_2, later_3, feats, local, normed, v_own, v_near, v_1, v_2, v_3, pooled, values, mixed
+    lengths, later_1, later_2, later_3, sums, feats, local, normed, v_own, v_1, v_2, v_3, gain, part, values, mixed
 ):
     tokens = feats.shape[0] // 3
-    rows = v_own.shape[0]
     width = normed.shape[1]
     z, x, u = places()
     long_u = jnp.where(lengths[0, 0] > tokens, u, 1 - u)
-    at = [pl.multiple_of((2 * z + half) * rows, rows) for half in (x, 1 - x)]
-    values[pl.ds(at[0], rows), :] = v_own[...]
-    values[pl.ds(at[1], rows), :] = v_near[...]
-    for step, ref in enumerate((v_1, v_2, v_3), 1):
-        other = lax.rem(z + PLANES - step, PLANES)
-        for half, place in enumerate((x, 1 - x)):
-            start = pl.multiple_of((2 * other + place) * rows, rows)
-            values[pl.ds(start, rows), :] = ref[pl.ds(half * rows, rows), :]
-
-    after = jnp.zeros((1, GROUP), jnp.float32)
-    for step, ref in enumerate((later_1, later_2, later_3), 1):
-        after = after + jnp.where(z < step, ref[...], 0.0)
+    gather_rows(z, x, (v_own, v_1, v_2, v_3), values)
+    after = later_1[...] + later_2[...] + later_3[...]
     lane = lax.broadcasted_iota(jnp.int32, (1, HEAD_DIM), 1)
 
     def mix(weight, slot, count):
         high, low = split_two(weight)
         both = jnp.where(lax.rem(lane, 64) < 32, high.astype(jnp.float32), low.astype(jnp.float32))
-        part = normed[pl.ds(slot * tokens, count), :]
-        return lax.dot_general(both.astype(jnp.bfloat16), part, DOT_T, preferred_element_type=jnp.float32)
+        rows = normed[pl.ds(slot * tokens, count), :]
+        return lax.dot_general(both.astype(jnp.bfloat16), rows, DOT_T, preferred_element_type=jnp.float32)
 
     key = feats[0 : 2 * tokens, GROUP:].astype(jnp.float32)
     extra = jnp.concatenate(
@@ -316,31 +331,33 @@
         low, values[...], preferred_element_type=jnp.float32
     )
     half = HEAD_DIM
-    long_row = jnp.concatenate([out[0:1, :half], out[1:2, half:]], axis=1) + sums[1:2, :]
-    short_row = jnp.concatenate([out[2:3, :half], out[3:4, half:]], axis=1) + sums[2:3, :]
-    pooled[0:1, :] = jnp.where(long_u == 0, long_row, short_row)
-    pooled[1:2, :] = jnp.where(long_u == 0, short_row, long_row)
-
-
-def loss_kernel(positives, parts, o_1, o_2, o_3, p_0, p_1, p_2, p_3, gain, gain_other, vec, loss, mine, theirs):
+    long_row = jnp.concatenate([out[0:1, :half], out[1:2, half:]], axis=1) + sums[0:1, :]
+    short_row = jnp.concatenate([out[2:3, :half], out[3:4, half:]], axis=1) + sums[1:2, :]
+    first = jnp.where(long_u == 0, long_row, short_row)
+    second = jnp.where(long_u == 0, short_row, long_row)
+    own_gain = gain[:, pl.ds(pl.multiple_of((2 * x + u) * GROUP, GROUP), GROUP)]
+    block = jnp.concatenate([first, second, own_gain, own_gain], axis=0)
+    part[...] = jnp.broadcast_to(block[None], part.shape)
+
+
+def loss_kernel(positives, parts, vec, loss, mine, theirs):
     z, x, u = places()
     domain = lax.axis_index("domain")
-    group = 2 * x + u
-    width = gain.shape[1]
+    width = mine.shape[1]
     piece = vec.shape[2]
 
-    def collect(refs, gains, dest):
+    def collect(place, dest):
         total = jnp.zeros((2, 1), jnp.float32)
-        for move, ref in enumerate(refs):
-            values = ref[...]
+        for group in range(PLANE):
+            blocks = [parts[2 * (PLANE * plane + group) + place] for plane in range(PLANES)]
+            values = (blocks[0][:2] + blocks[1][:2]) + (blocks[2][:2] + blocks[3][:2])
             total = total + jnp.sum(values * values, axis=1, keepdims=True)
-            at = pl.multiple_of(jnp.bitwise_xor(group, move) * GROUP, GROUP)
-            dest[:, pl.ds(at, GROUP)] = values * gains[:, pl.ds(at, GROUP)]
+            dest[:, group * GROUP : (group + 1) * GROUP] = values * blocks[0][2:3]
         factor = lax.rsqrt(total / width + epsilon)
         return (dest[...] * factor).astype(jnp.bfloat16).astype(jnp.float32)
 
-    own = collect((parts, o_1, o_2, o_3), gain, mine)
-    other = collect((p_0, p_1, p_2, p_3), gain_other, theirs)
+    own = collect(domain, mine)
+    other = collect(1 - domain, theirs)
     mine[...] = own
     start = pl.multiple_of((2 * z + x) * piece, piece)
     out = mine[:, pl.ds(start, piece)]
@@ -391,15 +408,12 @@
     group = 2 * x + u
     here = PLANE * PLANES
 
+    def hop(a, target):
+        pairs = [(i, target(i // PLANE) * PLANE + i % PLANE) for i in range(here) if target(i // PLANE) is not None]
+        return lax.ppermute(a, ("seq", "dp"), pairs)
+
     def plane_hop(a, move):
         return lax.ppermute(a, ("seq", "dp"), [(i, i ^ move) for i in range(here)])
-
-    def level_hop(a, step):
-        return lax.ppermute(a, ("seq", "dp"), [(i, (i + PLANE * step) % here) for i in range(here)])
-
-    def domain_hop(a, move):
-        pairs = [(i, i ^ (2 * move + 1)) for i in range(2 * here)]
-        return lax.ppermute(a, ("seq", "dp", "domain"), pairs)
 
     def columns(which):
         return jnp.concatenate(
@@ -407,58 +421,66 @@
             axis=1,
         )
 
+    def upward(a):
+        return [hop(a, lambda p: p + step if p + step < PLANES else None) for step in (3, 2, 1)]
+
+    def downward(a):
+        return [hop(a, lambda p: p - step if p >= step else None) for step in (3, 2, 1)]
+
+    wide = 2 * GROUP
+    events, w_sent = lax.optimization_barrier((events, columns(jnp.bitwise_xor(group, 2))))
+    w_near = plane_hop(w_sent, 2)
+    w_own = columns(group)
+    qk_own, qk_near = w_own[:, :wide], w_near[:, :wide]
+    two_own = hop(qk_own, lambda p: p ^ 2)
+    across = plane_hop(events, 1)
     near = plane_hop(events, 2)
-    across = plane_hop(events, 1)
-    corner = plane_hop(events, 3)
-    w_own = columns(group)
-    w_near = plane_hop(columns(jnp.bitwise_xor(group, 2)), 2)
-    shifted = []
-    for step in range(1, PLANES):
-        shifted.append(level_hop(w_own[:, : 2 * GROUP], step))
-        shifted.append(level_hop(w_near[:, : 2 * GROUP], step))
-    v_own, v_near = w_own[:, 2 * GROUP :], w_near[:, 2 * GROUP :]
-    v_both = jnp.concatenate([v_own, v_near], axis=0)
-    v_far = [level_hop(v_both, step) for step in range(1, PLANES)]
-    gain_other = domain_hop(pool_gain, 0)
-
-    normed, feats, sums = call(
+    two_near = hop(qk_near, lambda p: p ^ 2)
+    qk = jnp.concatenate([qk_own, qk_near], axis=0)
+    one_away = hop(qk, lambda p: p ^ 1)
+    next_plane = hop(qk, lambda p: 3 - p if p in (1, 2) else None)
+    corner_a = plane_hop(across[: tokens // 2], 2)
+    corner_b = plane_hop(near[tokens // 2 :], 1)
+    far = hop(jnp.concatenate([two_own, two_near], axis=0), lambda p: {1: 0, 2: 3}.get(p))
+    v_own = jnp.concatenate([w_own[:, wide:], w_near[:, wide:]], axis=0)
+    v_far = [hop(v_own, lambda p: p ^ j) for j in (1, 2, 3)]
+
+    normed, sums = call(
+        norm_kernel,
+        (shape((3 * tokens, width), bf16), shape((2, GROUP), f32)),
+        [smem()] + [anywhere()] * 5 + [vmem()],
+        [pltpu.VMEM((3, tokens, width), bf16), pltpu.SemaphoreType.DMA((3, 2))],
+        2 * 3 * tokens * width,
+    )(lengths, events, near, across, corner_a, corner_b, norm_gain)
+    feats, totals = call(
         project_kernel,
-        (shape((3 * tokens, width), bf16), shape((3 * tokens, 2 * GROUP), bf16), shape((8, GROUP), f32)),
-        [smem()] + [anywhere()] * 12 + [vmem()],
-        [
-            pltpu.VMEM((3, tokens, width), bf16),
-            pltpu.VMEM((width, 2 * GROUP), bf16),
-            pltpu.SemaphoreType.DMA((3 + 2 * PLANES,)),
-        ],
-        2 * 3 * tokens * width * 2 * GROUP,
-    )(lengths, events, near, across, corner, w_own, w_near, *shifted, norm_gain)
-    key_total = sums[0:1]
-    totals = [level_hop(key_total, step) for step in range(1, PLANES)]
+        (shape((3 * tokens, wide), bf16), shape((1, GROUP), f32)),
+        [vmem()] * 7,
+        [pltpu.VMEM((width, wide), bf16)],
+        2 * 3 * tokens * width * wide,
+    )(normed, qk, one_away, two_own, two_near, next_plane, far)
     weight_sum, local = call(
         scan_kernel,
         (shape((1, GROUP), f32), shape((3 * tokens, HEAD_DIM), f32)),
-        [vmem()] * 5,
+        [vmem()] * 4,
         [],
         2 * 9 * tokens * tokens * GROUP,
-    )(sums, *totals, feats)
-    later = [level_hop(weight_sum, step) for step in range(1, PLANES)]
+    )(*upward(totals), feats)
     part = call(
         pool_kernel,
-        shape((2, GROUP), f32),
+        shape((2 * here, 4, GROUP), f32),
         [smem()] + [vmem()] * 12,
         [pltpu.VMEM((width, GROUP), bf16), pltpu.VMEM((2 * HEAD_DIM, width), f32)],
         2 * 3 * tokens * width * HEAD_DIM,
-    )(lengths, sums, *later, feats, local, normed, v_own, v_near, *v_far)
-    part = part + level_hop(part, 1) + level_hop(part, 2) + level_hop(part, 3)
-    own = [plane_hop(part, move) for move in range(1, PLANE)]
-    other = [domain_hop(part, move) for move in range(PLANE)]
+    )(lengths, *downward(weight_sum), sums, feats, local, normed, v_own, *v_far, pool_gain)
+    parts = lax.all_to_all(part, ("seq", "dp", "domain"), 0, 0, tiled=True)
     vec, loss = call(
         loss_kernel,
         (shape((1, 1, width // 8), bf16), shape((1, 1), f32)),
-        [smem()] + [vmem()] * 10,
+        [smem(), vmem()],
         [pltpu.VMEM((2, width), f32), pltpu.VMEM((2, width), f32)],
         2**14,
-    )(positives, part, *own, *other, pool_gain, gain_other)
+    )(positives, parts)
     return vec, loss
 
 

time: 79.3 us -> 82.2 us (1.037)
  blocking collectives: 0 us -> 12.6 us
  starting transfers between devices: 41.7 us -> 33.2 us
  waiting for transfers between devices: 28.1 us -> 27.1 us
    ppermute x23 -> x14, waiting for transfers between devices: 27.4 us -> 14 us  [hop(): return lax.ppermute(a, ('seq', 'dp'), pairs)]
    all_to_all x0 -> x1, blocking collectives: none -> 12.6 us  [towers(): parts = lax.all_to_all(part, ('seq', 'dp', 'domain'), 0, 0, tiled=True)]
    ppermute x7 -> x5, waiting for transfers between devices: 0.61 us -> 13.1 us  [plane_hop(): return lax.ppermute(a, ('seq', 'dp'), [(i, i ^ move) for i in range(here)])]
    ppermute x23 -> x14, starting transfers between devices: 31.7 us -> 26 us  [hop(): return lax.ppermute(a, ('seq', 'dp'), pairs)]
    ppermute x7 -> x5, starting transfers between devices: 9.98 us -> 7.19 us  [plane_hop(): return lax.ppermute(a, ('seq', 'dp'), [(i, i ^ move) for i in range(here)])]
    pallas_call x2 -> x3, Pallas kernels: 4.1 us -> 3.44 us  [the longest x1 1.45 us: towers(): call(project_kernel, (shape((3 * tokens, wide), bf16), shape((1, GROUP),...]
  transfers between devices with their start and end apart: 30 -> 19, of which waited for: 15 -> 7; matrix products, arithmetic and copies ran while one was open for 0% -> 0% of each run, Pallas kernels for 6% -> 5%
where the time goes in v3:
time: 82.2 us; the launch traced here: 81.8 us
  starting transfers between devices  33.2 us (40%)
  waiting for transfers between devices  27.1 us (33%)
  blocking collectives  12.6 us (15%)
  Pallas kernels  6.14 us (7%)
  between operations  1.57 us (2%)
  local copies, waits for them, and re-layouts  1.12 us (1%)
    ppermute x14, starting transfers between devices, hop(): return lax.ppermute(a, ('seq', 'dp'), pairs)  26 us
    ppermute x14, waiting for transfers between devices, hop(): return lax.ppermute(a, ('seq', 'dp'), pairs)  14 us
    ppermute x5, waiting for transfers between devices, plane_hop(): return lax.ppermute(a, ('seq', 'dp'), [(i, i ^ move) for i in range(here)])  13.1 us
    all_to_all x1, blocking collectives, towers(): parts = lax.all_to_all(part, ('seq', 'dp', 'domain'), 0, 0, tiled=True)  12.6 us
    ppermute x5, starting transfers between devices, plane_hop(): return lax.ppermute(a, ('seq', 'dp'), [(i, i ^ move) for i in range(here)])  7.19 us
  transfers between devices with their start and end apart: 19, of which 7 were waited for; matrix products, arithmetic and copies ran while one was open for 0% of the time, Pallas kernels for 5%

profile of v3, /device:TPU:0, one launch (start us, length us, event | category | flops | bytes accessed | tf_op | source)
XLA Modules:
  0.0 81.8 jit_solution(11256646405636263355)
XLA Ops:
  1.8 3.0 %collective-permute-start.1 = (bf16[256,1024]{1,0:T(8,128)(2,1)}, bf16[256,1024]{1,0:T(8,128)(2,1)S(1)}, u32[]{:S(2)}, u32[]{:S(2)}) collective-permute-start(bf16[256,1024]{1,0:T(8,128)(2,1)} %bitcast.13), channel_id=1, source_target_pairs={{0,2},{2,0},{4,6},{6,4},{8,10},{10,8},{12,14},{14,12},{16,18},{18,... | collective-permute-start | bytes 1572872 | tf_op jit(solution)/shard_map/ppermute | solution.py:416
  4.8 1.5 %collective-permute-start = (bf16[256,1024]{1,0:T(8,128)(2,1)}, bf16[256,1024]{1,0:T(8,128)(2,1)S(1)}, u32[]{:S(2)}, u32[]{:S(2)}) collective-permute-start(bf16[256,1024]{1,0:T(8,128)(2,1)} %bitcast.14), channel_id=1, source_target_pairs={{0,4},{2,6},{4,0},{6,2},{8,12},{10,14},{12,8},{14,10},{16,20},{18,... | collective-permute-start | bytes 1572872 | tf_op jit(solution)/shard_map/ppermute | solution.py:416
  6.8 2.7 %collective-permute-start.6 = (bf16[128,512]{1,0:T(8,128)(2,1)S(1)}, bf16[128,512]{1,0:T(8,128)(2,1)S(1)}, u32[]{:S(2)}, u32[]{:S(2)}) collective-permute-start(bf16[128,512]{1,0:T(8,128)(2,1)S(1)} %pad_maximum_fusion.3), channel_id=1, source_target_pairs={{0,16},{2,18},{4,20},{6,22},{8,24},{10,26},{12,28},{14,30},{16,0},... | collective-permute-start | bytes 393224 | tf_op jit(solution)/shard_map/ppermute | solution.py:413
  9.5 13.1 %collective-permute-done.4 = bf16[128,768]{1,0:T(8,128)(2,1)S(1)} collective-permute-done((bf16[128,768]{1,0:T(8,128)(2,1)S(1)}, bf16[128,768]{1,0:T(8,128)(2,1)S(1)}, u32[]{:S(2)}, u32[]{:S(2)}) %collective-permute-start.4) | collective-permute-done | bytes 196640 | tf_op jit(solution)/shard_map/ppermute | solution.py:416
  22.6 2.7 %collective-permute-start.7 = (bf16[128,512]{1,0:T(8,128)(2,1)S(1)}, bf16[128,512]{1,0:T(8,128)(2,1)S(1)}, u32[]{:S(2)}, u32[]{:S(2)}) collective-permute-start(bf16[128,512]{1,0:T(8,128)(2,1)S(1)} %slice.18), channel_id=1, source_target_pairs={{0,16},{2,18},{4,20},{6,22},{8,24},{10,26},{12,28},{14,30},{16,0},... | collective-permute-start | bytes 393224 | tf_op jit(solution)/shard_map/ppermute | solution.py:413
  25.3 1.6 %collective-permute-start.5 = (bf16[256,512]{1,0:T(8,128)(2,1)S(1)}, bf16[256,512]{1,0:T(8,128)(2,1)S(1)}, u32[]{:S(2)}, u32[]{:S(2)}) collective-permute-start(bf16[256,512]{1,0:T(8,128)(2,1)S(1)} %pad_maximum_fusion.own), channel_id=1, source_target_pairs={{0,8},{2,10},{4,12},{6,14},{8,0},{10,2},{12,4},{14,6},{16,24},{18,... | collective-permute-start | bytes 786440 | tf_op jit(solution)/shard_map/ppermute | solution.py:413
  27.6 1.6 %collective-permute-start.2 = (bf16[128,1024]{1,0:T(8,128)(2,1)S(1)}, bf16[128,1024]{1,0:T(8,128)(2,1)S(1)}, u32[]{:S(2)}, u32[]{:S(2)}) collective-permute-start(bf16[128,1024]{1,0:T(8,128)(2,1)S(1)} %slice.16), channel_id=1, source_target_pairs={{0,4},{2,6},{4,0},{6,2},{8,12},{10,14},{12,8},{14,10},{16,20},{18,... | collective-permute-start | bytes 786440 | tf_op jit(solution)/shard_map/ppermute | solution.py:416
  30.2 1.3 %collective-permute-start.9 = (bf16[256,512]{1,0:T(8,128)(2,1)S(1)}, bf16[256,512]{1,0:T(8,128)(2,1)S(1)}, u32[]{:S(2)}, u32[]{:S(2)}) collective-permute-start(bf16[256,512]{1,0:T(8,128)(2,1)S(1)} %pad_maximum_fusion.1), channel_id=1, source_target_pairs={{8,0},{10,2},{12,4},{14,6},{16,24},{18,26},{20,28},{22,30},{9,1},{... | collective-permute-start | bytes 786440 | tf_op jit(solution)/shard_map/ppermute | solution.py:413
  31.5 3.2 %collective-permute-done.5.one_away = bf16[256,512]{1,0:T(8,128)(2,1)S(1)} collective-permute-done((bf16[256,512]{1,0:T(8,128)(2,1)S(1)}, bf16[256,512]{1,0:T(8,128)(2,1)S(1)}, u32[]{:S(2)}, u32[]{:S(2)}) %collective-permute-start.5) | collective-permute-done | bytes 262176 | tf_op jit(solution)/shard_map/ppermute | solution.py:413
  34.9 2.8 %collective-permute-start.17 = (bf16[256,256]{1,0:T(8,128)(2,1)S(1)}, bf16[256,256]{1,0:T(8,128)(2,1)S(1)}, u32[]{:S(2)}, u32[]{:S(2)}) collective-permute-start(bf16[256,256]{1,0:T(8,128)(2,1)S(1)} %pad_maximum_fusion.4.v_own), channel_id=1, source_target_pairs={{0,16},{2,18},{4,20},{6,22},{8,24},{10,26},{12,28},{14,30},{16,0},... | collective-permute-start | bytes 393224 | tf_op jit(solution)/shard_map/ppermute | solution.py:413
  37.7 1.4 %collective-permute-start.18 = (bf16[256,256]{1,0:T(8,128)(2,1)S(1)}, bf16[256,256]{1,0:T(8,128)(2,1)S(1)}, u32[]{:S(2)}, u32[]{:S(2)}) collective-permute-start(bf16[256,256]{1,0:T(8,128)(2,1)S(1)} %pad_maximum_fusion.4.v_own), channel_id=1, source_target_pairs={{0,24},{2,26},{4,28},{6,30},{8,16},{10,18},{12,20},{14,22},{16,8},... | collective-permute-start | bytes 393224 | tf_op jit(solution)/shard_map/ppermute | solution.py:413
  40.8 5.0 %collective-permute-done.9.far = bf16[256,512]{1,0:T(8,128)(2,1)S(1)} collective-permute-done((bf16[256,512]{1,0:T(8,128)(2,1)S(1)}, bf16[256,512]{1,0:T(8,128)(2,1)S(1)}, u32[]{:S(2)}, u32[]{:S(2)}) %collective-permute-start.9) | collective-permute-done | bytes 262176 | tf_op jit(solution)/shard_map/ppermute | solution.py:413
  45.8 1.4 %shard_map.78 = (bf16[768,512]{1,0:T(8,128)(2,1)S(1)}, f32[1,256]{1,0:T(1,128)S(1)}) custom-call(bf16[768,1024]{1,0:T(8,128)(2,1)S(1)} %get-tuple-element.11.normed, bf16[256,512]{1,0:T(8,128)(2,1)S(1)} %pad_maximum_fusion.own, bf16[256,512]{1,0:T(8,128)(2,1)S(1)} %collective-permute-done.5.one_away, bf16[128,512]{1,0:T(8,128)(2,1)S(1)} %collective-permute-done.6.two_own, ...), custom_call_target="tpu_custom_call" | custom-call | flops 805306368 | bytes 2097152 | tf_op jit(solution)/shard_map/pallas_call | solution.py:455
  47.3 5.0 %collective-permute-start.10 = (f32[1,256]{1,0:T(1,128)S(1)}, f32[1,256]{1,0:T(1,128)S(1)}, u32[]{:S(2)}, u32[]{:S(2)}) collective-permute-start(f32[1,256]{1,0:T(1,128)S(1)} %get-tuple-element.13), channel_id=1, source_target_pairs={{0,24},{2,26},{4,28},{6,30},{1,25},{3,27},{5,29},{7,31}} | collective-permute-start | bytes 3080 | tf_op jit(solution)/shard_map/ppermute | solution.py:413
  52.3 1.3 %collective-permute-start.11 = (f32[1,256]{1,0:T(1,128)S(1)}, f32[1,256]{1,0:T(1,128)S(1)}, u32[]{:S(2)}, u32[]{:S(2)}) collective-permute-start(f32[1,256]{1,0:T(1,128)S(1)} %get-tuple-element.13), channel_id=1, source_target_pairs={{0,16},{2,18},{4,20},{6,22},{8,24},{10,26},{12,28},{14,30},{1,17},... | collective-permute-start | bytes 3080 | tf_op jit(solution)/shard_map/ppermute | solution.py:413
  53.6 2.5 %collective-permute-start.12 = (f32[1,256]{1,0:T(1,128)S(1)}, f32[1,256]{1,0:T(1,128)S(1)}, u32[]{:S(2)}, u32[]{:S(2)}) collective-permute-start(f32[1,256]{1,0:T(1,128)S(1)} %get-tuple-element.13), channel_id=1, source_target_pairs={{0,8},{2,10},{4,12},{6,14},{8,16},{10,18},{12,20},{14,22},{16,24},... | collective-permute-start | bytes 3080 | tf_op jit(solution)/shard_map/ppermute | solution.py:413
  56.1 1.3 %collective-permute-done.12.before_3 = f32[1,256]{1,0:T(1,128)S(1)} collective-permute-done((f32[1,256]{1,0:T(1,128)S(1)}, f32[1,256]{1,0:T(1,128)S(1)}, u32[]{:S(2)}, u32[]{:S(2)}) %collective-permute-start.12) | collective-permute-done | bytes 1056 | tf_op jit(solution)/shard_map/ppermute | solution.py:413
  57.4 1.4 %shard_map.79 = (f32[1,256]{1,0:T(1,128)S(1)}, f32[768,128]{1,0:T(8,128)S(1)}) custom-call(f32[1,256]{1,0:T(1,128)S(1)} %collective-permute-done.10.before_1, f32[1,256]{1,0:T(1,128)S(1)} %collective-permute-done.11.before_2, f32[1,256]{1,0:T(1,128)S(1)} %collective-permute-done.12.before_3, bf16[768,512]{1,0:T(8,128)(2,1)S(1)} %get-tuple-element.14.feats), custom_call_target="tpu_custom_call" | custom-call | flops 301989888 | bytes 2097152 | tf_op jit(solution)/shard_map/pallas_call | solution.py:462
  58.8 1.3 %collective-permute-start.13 = (f32[1,256]{1,0:T(1,128)S(1)}, f32[1,256]{1,0:T(1,128)S(1)}, u32[]{:S(2)}, u32[]{:S(2)}) collective-permute-start(f32[1,256]{1,0:T(1,128)S(1)} %get-tuple-element.15), channel_id=1, source_target_pairs={{24,0},{26,2},{28,4},{30,6},{25,1},{27,3},{29,5},{31,7}} | collective-permute-start | bytes 3080 | tf_op jit(solution)/shard_map/ppermute | solution.py:413
  60.1 1.3 %collective-permute-start.14 = (f32[1,256]{1,0:T(1,128)S(1)}, f32[1,256]{1,0:T(1,128)S(1)}, u32[]{:S(2)}, u32[]{:S(2)}) collective-permute-start(f32[1,256]{1,0:T(1,128)S(1)} %get-tuple-element.15), channel_id=1, source_target_pairs={{16,0},{18,2},{20,4},{22,6},{24,8},{26,10},{28,12},{30,14},{17,1},... | collective-permute-start | bytes 3080 | tf_op jit(solution)/shard_map/ppermute | solution.py:413
  61.4 1.3 %collective-permute-start.15 = (f32[1,256]{1,0:T(1,128)S(1)}, f32[1,256]{1,0:T(1,128)S(1)}, u32[]{:S(2)}, u32[]{:S(2)}) collective-permute-start(f32[1,256]{1,0:T(1,128)S(1)} %get-tuple-element.15), channel_id=1, source_target_pairs={{8,0},{10,2},{12,4},{14,6},{16,8},{18,10},{20,12},{22,14},{24,16},... | collective-permute-start | bytes 3080 | tf_op jit(solution)/shard_map/ppermute | solution.py:413
  62.7 4.0 %collective-permute-done.13.later_1 = f32[1,256]{1,0:T(1,128)S(1)} collective-permute-done((f32[1,256]{1,0:T(1,128)S(1)}, f32[1,256]{1,0:T(1,128)S(1)}, u32[]{:S(2)}, u32[]{:S(2)}) %collective-permute-start.13) | collective-permute-done | bytes 1056 | tf_op jit(solution)/shard_map/ppermute | solution.py:413
  67.9 12.6 %all_to_all.5.parts = f32[32,4,256]{2,1,0:T(4,128)S(1)} all-to-all(f32[32,4,256]{2,1,0:T(4,128)S(1)} %shard_map.80), channel_id=1, replica_groups=mesh['seq'=8,'dp'=2,'domain'=2] {'seq','dp','domain'}, dimensions={0} | all-to-all | bytes 262144 | tf_op jit(solution)/shard_map/all_to_all | solution.py:476
  80.6 1.3 %shard_map.81 = (bf16[1,1,128]{2,1,0:T(2,128)(2,1)}, f32[1,1]{1,0:T(1,128)}) custom-call(s32[2]{0:T(128)S(1)} %copy-done.3, f32[32,4,256]{2,1,0:T(4,128)S(1)} %all_to_all.5.parts), custom_call_target="tpu_custom_call" | custom-call | flops 16384 | bytes 2097152 | tf_op jit(solution)/shard_map/pallas_call | solution.py:477
  (38 shorter events, 5.7 us)
Async XLA Ops:
  1.7 38.1 %copy-start = (bf16[1,1,256,1024]{3,2,1,0:T(8,128)(2,1)S(1)}, bf16[1,1,256,1024]{3,2,1,0:T(8,128)(2,1)}, u32[]{:S(2)}) copy-start(bf16[1,1,256,1024]{3,2,1,0:T(8,128)(2,1)} %param.6) | copy-start | bytes 1572868
  1.7 38.1 %copy-start.1 = (f32[1,1024]{1,0:T(1,128)S(1)}, f32[1,1024]{1,0:T(1,128)}, u32[]{:S(2)}) copy-start(f32[1,1024]{1,0:T(1,128)} %gain.2) | copy-start | bytes 12292
  1.8 25.2 %collective-permute-start.1 = (bf16[256,1024]{1,0:T(8,128)(2,1)}, bf16[256,1024]{1,0:T(8,128)(2,1)S(1)}, u32[]{:S(2)}, u32[]{:S(2)}) collective-permute-start(bf16[256,1024]{1,0:T(8,128)(2,1)} %bitcast.13), channel_id=1, source_target_pairs={{0,2},{2,0},{4,6},{6,4},{8,10},{10,8},{12,14},{14,12},{16,18},{18,... | collective-permute-start | bytes 1572872 | tf_op jit(solution)/shard_map/ppermute | solution.py:416
  4.8 22.8 %collective-permute-start = (bf16[256,1024]{1,0:T(8,128)(2,1)}, bf16[256,1024]{1,0:T(8,128)(2,1)S(1)}, u32[]{:S(2)}, u32[]{:S(2)}) collective-permute-start(bf16[256,1024]{1,0:T(8,128)(2,1)} %bitcast.14), channel_id=1, source_target_pairs={{0,4},{2,6},{4,0},{6,2},{8,12},{10,14},{12,8},{14,10},{16,20},{18,... | collective-permute-start | bytes 1572872 | tf_op jit(solution)/shard_map/ppermute | solution.py:416
  6.3 16.3 %collective-permute-start.4 = (bf16[128,768]{1,0:T(8,128)(2,1)S(1)}, bf16[128,768]{1,0:T(8,128)(2,1)S(1)}, u32[]{:S(2)}, u32[]{:S(2)}) collective-permute-start(bf16[128,768]{1,0:T(8,128)(2,1)S(1)} %pad_maximum_fusion.2), channel_id=1, source_target_pairs={{0,4},{2,6},{4,0},{6,2},{8,12},{10,14},{12,8},{14,10},{16,20},{18,... | collective-permute-start | bytes 589832 | tf_op jit(solution)/shard_map/ppermute | solution.py:416
  6.8 22.4 %collective-permute-start.6 = (bf16[128,512]{1,0:T(8,128)(2,1)S(1)}, bf16[128,512]{1,0:T(8,128)(2,1)S(1)}, u32[]{:S(2)}, u32[]{:S(2)}) collective-permute-start(bf16[128,512]{1,0:T(8,128)(2,1)S(1)} %pad_maximum_fusion.3), channel_id=1, source_target_pairs={{0,16},{2,18},{4,20},{6,22},{8,24},{10,26},{12,28},{14,30},{16,0},... | collective-permute-start | bytes 393224 | tf_op jit(solution)/shard_map/ppermute | solution.py:413
  22.6 7.5 %collective-permute-start.7 = (bf16[128,512]{1,0:T(8,128)(2,1)S(1)}, bf16[128,512]{1,0:T(8,128)(2,1)S(1)}, u32[]{:S(2)}, u32[]{:S(2)}) collective-permute-start(bf16[128,512]{1,0:T(8,128)(2,1)S(1)} %slice.18), channel_id=1, source_target_pairs={{0,16},{2,18},{4,20},{6,22},{8,24},{10,26},{12,28},{14,30},{16,0},... | collective-permute-start | bytes 393224 | tf_op jit(solution)/shard_map/ppermute | solution.py:413
  25.3 9.4 %collective-permute-start.5 = (bf16[256,512]{1,0:T(8,128)(2,1)S(1)}, bf16[256,512]{1,0:T(8,128)(2,1)S(1)}, u32[]{:S(2)}, u32[]{:S(2)}) collective-permute-start(bf16[256,512]{1,0:T(8,128)(2,1)S(1)} %pad_maximum_fusion.own), channel_id=1, source_target_pairs={{0,8},{2,10},{4,12},{6,14},{8,0},{10,2},{12,4},{14,6},{16,24},{18,... | collective-permute-start | bytes 786440 | tf_op jit(solution)/shard_map/ppermute | solution.py:413
  26.9 13.9 %collective-permute-start.8 = (bf16[256,512]{1,0:T(8,128)(2,1)S(1)}, bf16[256,512]{1,0:T(8,128)(2,1)S(1)}, u32[]{:S(2)}, u32[]{:S(2)}) collective-permute-start(bf16[256,512]{1,0:T(8,128)(2,1)S(1)} %pad_maximum_fusion.own), channel_id=1, source_target_pairs={{8,16},{10,18},{12,20},{14,22},{16,8},{18,10},{20,12},{22,14},{9,1... | collective-permute-start | bytes 786440 | tf_op jit(solution)/shard_map/ppermute | solution.py:413
  27.6 7.3 %collective-permute-start.2 = (bf16[128,1024]{1,0:T(8,128)(2,1)S(1)}, bf16[128,1024]{1,0:T(8,128)(2,1)S(1)}, u32[]{:S(2)}, u32[]{:S(2)}) collective-permute-start(bf16[128,1024]{1,0:T(8,128)(2,1)S(1)} %slice.16), channel_id=1, source_target_pairs={{0,4},{2,6},{4,0},{6,2},{8,12},{10,14},{12,8},{14,10},{16,20},{18,... | collective-permute-start | bytes 786440 | tf_op jit(solution)/shard_map/ppermute | solution.py:416
  29.2 8.5 %collective-permute-start.3 = (bf16[128,1024]{1,0:T(8,128)(2,1)S(1)}, bf16[128,1024]{1,0:T(8,128)(2,1)S(1)}, u32[]{:S(2)}, u32[]{:S(2)}) collective-permute-start(bf16[128,1024]{1,0:T(8,128)(2,1)S(1)} %slice.17), channel_id=1, source_target_pairs={{0,2},{2,0},{4,6},{6,4},{8,10},{10,8},{12,14},{14,12},{16,18},{18,... | collective-permute-start | bytes 786440 | tf_op jit(solution)/shard_map/ppermute | solution.py:416
  30.2 15.7 %collective-permute-start.9 = (bf16[256,512]{1,0:T(8,128)(2,1)S(1)}, bf16[256,512]{1,0:T(8,128)(2,1)S(1)}, u32[]{:S(2)}, u32[]{:S(2)}) collective-permute-start(bf16[256,512]{1,0:T(8,128)(2,1)S(1)} %pad_maximum_fusion.1), channel_id=1, source_target_pairs={{8,0},{10,2},{12,4},{14,6},{16,24},{18,26},{20,28},{22,30},{9,1},{... | collective-permute-start | bytes 786440 | tf_op jit(solution)/shard_map/ppermute | solution.py:413
  34.7 26.7 %collective-permute-start.16 = (bf16[256,256]{1,0:T(8,128)(2,1)S(1)}, bf16[256,256]{1,0:T(8,128)(2,1)S(1)}, u32[]{:S(2)}, u32[]{:S(2)}) collective-permute-start(bf16[256,256]{1,0:T(8,128)(2,1)S(1)} %pad_maximum_fusion.4.v_own), channel_id=1, source_target_pairs={{0,8},{2,10},{4,12},{6,14},{8,0},{10,2},{12,4},{14,6},{16,24},{18,... | collective-permute-start | bytes 393224 | tf_op jit(solution)/shard_map/ppermute | solution.py:413
  34.9 27.8 %collective-permute-start.17 = (bf16[256,256]{1,0:T(8,128)(2,1)S(1)}, bf16[256,256]{1,0:T(8,128)(2,1)S(1)}, u32[]{:S(2)}, u32[]{:S(2)}) collective-permute-start(bf16[256,256]{1,0:T(8,128)(2,1)S(1)} %pad_maximum_fusion.4.v_own), channel_id=1, source_target_pairs={{0,16},{2,18},{4,20},{6,22},{8,24},{10,26},{12,28},{14,30},{16,0},... | collective-permute-start | bytes 393224 | tf_op jit(solution)/shard_map/ppermute | solution.py:413
  37.7 25.0 %collective-permute-start.18 = (bf16[256,256]{1,0:T(8,128)(2,1)S(1)}, bf16[256,256]{1,0:T(8,128)(2,1)S(1)}, u32[]{:S(2)}, u32[]{:S(2)}) collective-permute-start(bf16[256,256]{1,0:T(8,128)(2,1)S(1)} %pad_maximum_fusion.4.v_own), channel_id=1, source_target_pairs={{0,24},{2,26},{4,28},{6,30},{8,16},{10,18},{12,20},{14,22},{16,8},... | collective-permute-start | bytes 393224 | tf_op jit(solution)/shard_map/ppermute | solution.py:413
  45.8 21.0 %copy-start.2 = (f32[1,1024]{1,0:T(1,128)S(1)}, f32[1,1024]{1,0:T(1,128)}, u32[]{:S(2)}) copy-start(f32[1,1024]{1,0:T(1,128)} %gain.3) | copy-start | bytes 12292
  47.3 6.3 %collective-permute-start.10 = (f32[1,256]{1,0:T(1,128)S(1)}, f32[1,256]{1,0:T(1,128)S(1)}, u32[]{:S(2)}, u32[]{:S(2)}) collective-permute-start(f32[1,256]{1,0:T(1,128)S(1)} %get-tuple-element.13), channel_id=1, source_target_pairs={{0,24},{2,26},{4,28},{6,30},{1,25},{3,27},{5,29},{7,31}} | collective-permute-start | bytes 3080 | tf_op jit(solution)/shard_map/ppermute | solution.py:413
  52.3 3.8 %collective-permute-start.11 = (f32[1,256]{1,0:T(1,128)S(1)}, f32[1,256]{1,0:T(1,128)S(1)}, u32[]{:S(2)}, u32[]{:S(2)}) collective-permute-start(f32[1,256]{1,0:T(1,128)S(1)} %get-tuple-element.13), channel_id=1, source_target_pairs={{0,16},{2,18},{4,20},{6,22},{8,24},{10,26},{12,28},{14,30},{1,17},... | collective-permute-start | bytes 3080 | tf_op jit(solution)/shard_map/ppermute | solution.py:413
  53.6 3.8 %collective-permute-start.12 = (f32[1,256]{1,0:T(1,128)S(1)}, f32[1,256]{1,0:T(1,128)S(1)}, u32[]{:S(2)}, u32[]{:S(2)}) collective-permute-start(f32[1,256]{1,0:T(1,128)S(1)} %get-tuple-element.13), channel_id=1, source_target_pairs={{0,8},{2,10},{4,12},{6,14},{8,16},{10,18},{12,20},{14,22},{16,24},... | collective-permute-start | bytes 3080 | tf_op jit(solution)/shard_map/ppermute | solution.py:413
  58.8 8.0 %collective-permute-start.13 = (f32[1,256]{1,0:T(1,128)S(1)}, f32[1,256]{1,0:T(1,128)S(1)}, u32[]{:S(2)}, u32[]{:S(2)}) collective-permute-start(f32[1,256]{1,0:T(1,128)S(1)} %get-tuple-element.15), channel_id=1, source_target_pairs={{24,0},{26,2},{28,4},{30,6},{25,1},{27,3},{29,5},{31,7}} | collective-permute-start | bytes 3080 | tf_op jit(solution)/shard_map/ppermute | solution.py:413
  60.1 6.7 %collective-permute-start.14 = (f32[1,256]{1,0:T(1,128)S(1)}, f32[1,256]{1,0:T(1,128)S(1)}, u32[]{:S(2)}, u32[]{:S(2)}) collective-permute-start(f32[1,256]{1,0:T(1,128)S(1)} %get-tuple-element.15), channel_id=1, source_target_pairs={{16,0},{18,2},{20,4},{22,6},{24,8},{26,10},{28,12},{30,14},{17,1},... | collective-permute-start | bytes 3080 | tf_op jit(solution)/shard_map/ppermute | solution.py:413
  61.4 5.5 %collective-permute-start.15 = (f32[1,256]{1,0:T(1,128)S(1)}, f32[1,256]{1,0:T(1,128)S(1)}, u32[]{:S(2)}, u32[]{:S(2)}) collective-permute-start(f32[1,256]{1,0:T(1,128)S(1)} %get-tuple-element.15), channel_id=1, source_target_pairs={{8,0},{10,2},{12,4},{14,6},{16,8},{18,10},{20,12},{22,14},{24,16},... | collective-permute-start | bytes 3080 | tf_op jit(solution)/shard_map/ppermute | solution.py:413
  66.9 13.7 %copy-start.3 = (s32[2]{0:T(128)S(1)}, s32[2]{0:T(128)}, u32[]{:S(2)}) copy-start(s32[2]{0:T(128)} %positives.1) | copy-start | bytes 28

commit v4 on v3

--- a/solution.py
+++ b/solution.py
@@ -161,6 +161,32 @@
     return high, (a - high.astype(jnp.float32)).astype(jnp.bfloat16)
 
 
+def pack_kernel(weight, qk_own, v_own, qk_sent, v_sent, sems):
+    _, x, u = places()
+    width = weight.shape[1] // 3
+    copies = []
+    for move, qk, v in ((2, qk_sent, v_sent), (0, qk_own, v_own)):
+        group = jnp.bitwise_xor(2 * x + u, move)
+        for part, (ref, at) in enumerate(((qk, 0), (qk, GROUP), (v, 0))):
+            start = pl.multiple_of(part * width + group * GROUP, GROUP)
+            copies.append(
+                pltpu.make_async_copy(
+                    weight.at[:, pl.ds(start, GROUP)], ref.at[:, pl.ds(at, GROUP)], sems.at[len(copies)]
+                )
+            )
+    for copy in copies:
+        copy.start()
+    for copy in copies:
+        copy.wait()
+
+
+def relay_kernel(events, after, out, sem):
+    del after
+    copy = pltpu.make_async_copy(events, out, sem)
+    copy.start()
+    copy.wait()
+
+
 def norm_kernel(lengths, own, near, across, corner_a, corner_b, gain, normed, sums, raw, sems):
     tokens = own.shape[0]
     half = corner_a.shape[0]
@@ -204,15 +230,6 @@
         sums[1:2, :] = one(2)
 
 
-def gather_rows(z, x, parts, dest):
-    rows = parts[0].shape[0] // 2
-    for j, ref in enumerate(parts):
-        plane = jnp.bitwise_xor(z, j)
-        for half, place in enumerate((x, 1 - x)):
-            start = pl.multiple_of((2 * plane + place) * rows, rows)
-            dest[pl.ds(start, rows), :] = ref[pl.ds(half * rows, rows), :]
-
-
 def project_kernel(normed, own, one_away, two_own, two_near, next_plane, far, feats, totals, weights):
     tokens = normed.shape[0] // 3
     rows = two_own.shape[0]
@@ -253,14 +270,16 @@
         one(2, tokens)
 
 
-def scan_kernel(before_1, before_2, before_3, feats, weight_sum, local):
+def scan_kernel(total_1, total_2, total_3, feats, weight_sum, local):
     tokens = feats.shape[0] // 3
     z, _, _ = places()
     row = lax.broadcasted_iota(jnp.int32, (tokens, tokens), 0)
     col = lax.broadcasted_iota(jnp.int32, (tokens, tokens), 1)
     lower = (row >= col).astype(jnp.bfloat16)
     upper = (row <= col).astype(jnp.bfloat16)
-    before = before_1[...] + before_2[...] + before_3[...]
+    before = jnp.zeros((1, GROUP), jnp.float32)
+    for j, ref in enumerate((total_1, total_2, total_3), 1):
+        before = before + jnp.where(jnp.bitwise_xor(z, j) < z, ref[...], 0.0)
 
     def block(slot, carry):
         part = pl.ds(slot * tokens, tokens)
@@ -297,36 +316,45 @@
         store(2, key, suffix(share))
 
 
-def pool_kernel(
-    lengths, later_1, later_2, later_3, sums, feats, local, normed, v_own, v_1, v_2, v_3, gain, part, values, mixed
-):
+def mix_kernel(sum_1, sum_2, sum_3, feats, local, normed, to_0, to_1, to_2, to_3, mixed):
     tokens = feats.shape[0] // 3
-    width = normed.shape[1]
-    z, x, u = places()
-    long_u = jnp.where(lengths[0, 0] > tokens, u, 1 - u)
-    gather_rows(z, x, (v_own, v_1, v_2, v_3), values)
-    after = later_1[...] + later_2[...] + later_3[...]
+    z, _, _ = places()
+    after = jnp.zeros((1, GROUP), jnp.float32)
+    for j, ref in enumerate((sum_1, sum_2, sum_3), 1):
+        after = after + jnp.where(jnp.bitwise_xor(z, j) > z, ref[...], 0.0)
     lane = lax.broadcasted_iota(jnp.int32, (1, HEAD_DIM), 1)
 
     def mix(weight, slot, count):
         high, low = split_two(weight)
         both = jnp.where(lax.rem(lane, 64) < 32, high.astype(jnp.float32), low.astype(jnp.float32))
         rows = normed[pl.ds(slot * tokens, count), :]
-        return lax.dot_general(both.astype(jnp.bfloat16), rows, DOT_T, preferred_element_type=jnp.float32)
+        out = lax.dot_general(both.astype(jnp.bfloat16), rows, DOT_T, preferred_element_type=jnp.float32)
+        return [out[h : h + 1, :] + out[h + 32 : h + 33, :] for h in (0, 64)]
 
     key = feats[0 : 2 * tokens, GROUP:].astype(jnp.float32)
     extra = jnp.concatenate(
         [jnp.broadcast_to(c, (2 * tokens, HEAD_DIM // 2)) for c in head_sums(key * after)], axis=1
     )
-    mixed[0:HEAD_DIM, :] = mix(local[0 : 2 * tokens, :] + extra, 0, 2 * tokens)
-    mixed[HEAD_DIM:, :] = jnp.zeros((HEAD_DIM, width), jnp.float32)
+    mixed[0:2, :] = jnp.concatenate(mix(local[0 : 2 * tokens, :] + extra, 0, 2 * tokens), axis=0)
+    mixed[2:4, :] = jnp.zeros((2, mixed.shape[1]), jnp.float32)
 
     @pl.when(z == 0)
     def _():
-        mixed[HEAD_DIM:, :] = mix(local[2 * tokens :, :], 2, tokens)
-
-    picked = [mixed[h : h + 1, :] + mixed[h + 32 : h + 33, :] for h in (0, 64, 128, 192)]
-    high, low = split_two(jnp.concatenate(picked + picked, axis=0))
+        mixed[2:4, :] = jnp.concatenate(mix(local[2 * tokens :, :], 2, tokens), axis=0)
+
+    for j, ref in enumerate((to_0, to_1, to_2, to_3)):
+        start = pl.multiple_of(jnp.bitwise_xor(z, j) * GROUP, GROUP)
+        ref[...] = mixed[:, pl.ds(start, GROUP)]
+
+
+def pool_kernel(lengths, tokens, sums, from_0, from_1, from_2, from_3, v_own, v_near, gain, part, values):
+    rows = v_own.shape[0]
+    _, x, u = places()
+    long_u = jnp.where(lengths[0, 0] > tokens, u, 1 - u)
+    for half, ref in ((x, v_own), (1 - x, v_near)):
+        values[pl.ds(pl.multiple_of(half * rows, rows), rows), :] = ref[...]
+    total = (from_0[...] + from_1[...]) + (from_2[...] + from_3[...])
+    high, low = split_two(jnp.concatenate([total, total], axis=0))
     out = jnp.dot(high, values[...], preferred_element_type=jnp.float32) + jnp.dot(
         low, values[...], preferred_element_type=jnp.float32
     )
@@ -381,6 +409,10 @@
     return pl.BlockSpec(memory_space=pl.ANY)
 
 
+def hbm():
+    return pl.BlockSpec(memory_space=pltpu.HBM)
+
+
 def smem():
     return pl.BlockSpec(memory_space=pltpu.SMEM)
 
@@ -404,8 +436,6 @@
     rows = weight.shape[0]
     f32, bf16 = jnp.float32, jnp.bfloat16
     shape = jax.ShapeDtypeStruct
-    z, x, u = places()
-    group = 2 * x + u
     here = PLANE * PLANES
 
     def hop(a, target):
@@ -415,26 +445,25 @@
     def plane_hop(a, move):
         return lax.ppermute(a, ("seq", "dp"), [(i, i ^ move) for i in range(here)])
 
-    def columns(which):
-        return jnp.concatenate(
-            [lax.dynamic_slice(weight, (0, part * width + which * GROUP), (rows, GROUP)) for part in range(3)],
-            axis=1,
-        )
-
-    def upward(a):
-        return [hop(a, lambda p: p + step if p + step < PLANES else None) for step in (3, 2, 1)]
-
-    def downward(a):
-        return [hop(a, lambda p: p - step if p >= step else None) for step in (3, 2, 1)]
+    def each(a):
+        return [hop(a, lambda p: p ^ j) for j in range(1, PLANES)]
 
     wide = 2 * GROUP
-    events, w_sent = lax.optimization_barrier((events, columns(jnp.bitwise_xor(group, 2))))
-    w_near = plane_hop(w_sent, 2)
-    w_own = columns(group)
-    qk_own, qk_near = w_own[:, :wide], w_near[:, :wide]
+
+    qk_own, v_own, qk_sent, v_sent = call(
+        pack_kernel,
+        (shape((rows, wide), bf16), shape((rows, GROUP), bf16)) * 2,
+        [hbm()],
+        [pltpu.SemaphoreType.DMA((6,))],
+        0,
+    )(weight)
+    qk_near = plane_hop(qk_sent, 2)
+    across = plane_hop(events, 1)
     two_own = hop(qk_own, lambda p: p ^ 2)
-    across = plane_hop(events, 1)
-    near = plane_hop(events, 2)
+    own = call(
+        relay_kernel, shape((tokens, width), bf16), [hbm(), anywhere()], [pltpu.SemaphoreType.DMA(())], 0
+    )(events, qk_near)
+    near = plane_hop(own, 2)
     two_near = hop(qk_near, lambda p: p ^ 2)
     qk = jnp.concatenate([qk_own, qk_near], axis=0)
     one_away = hop(qk, lambda p: p ^ 1)
@@ -442,8 +471,7 @@
     corner_a = plane_hop(across[: tokens // 2], 2)
     corner_b = plane_hop(near[tokens // 2 :], 1)
     far = hop(jnp.concatenate([two_own, two_near], axis=0), lambda p: {1: 0, 2: 3}.get(p))
-    v_own = jnp.concatenate([w_own[:, wide:], w_near[:, wide:]], axis=0)
-    v_far = [hop(v_own, lambda p: p ^ j) for j in (1, 2, 3)]
+    v_near = plane_hop(v_sent, 2)
 
     normed, sums = call(
         norm_kernel,
@@ -451,7 +479,7 @@
         [smem()] + [anywhere()] * 5 + [vmem()],
         [pltpu.VMEM((3, tokens, width), bf16), pltpu.SemaphoreType.DMA((3, 2))],
         2 * 3 * tokens * width,
-    )(lengths, events, near, across, corner_a, corner_b, norm_gain)
+    )(lengths, own, near, across, corner_a, corner_b, norm_gain)
     feats, totals = call(
         project_kernel,
         (shape((3 * tokens, wide), bf16), shape((1, GROUP), f32)),
@@ -465,14 +493,22 @@
         [vmem()] * 4,
         [],
         2 * 9 * tokens * tokens * GROUP,
-    )(*upward(totals), feats)
+    )(*each(totals), feats)
+    mixed = call(
+        mix_kernel,
+        tuple(shape((4, GROUP), f32) for _ in range(PLANES)),
+        [vmem()] * 6,
+        [pltpu.VMEM((4, width), f32)],
+        2 * 3 * tokens * width * HEAD_DIM,
+    )(*each(weight_sum), feats, local, normed)
+    moved = [hop(mixed[j], lambda p: p ^ j) for j in range(1, PLANES)]
     part = call(
-        pool_kernel,
+        lambda lengths, *refs: pool_kernel(lengths, tokens, *refs),
         shape((2 * here, 4, GROUP), f32),
-        [smem()] + [vmem()] * 12,
-        [pltpu.VMEM((width, GROUP), bf16), pltpu.VMEM((2 * HEAD_DIM, width), f32)],
-        2 * 3 * tokens * width * HEAD_DIM,
-    )(lengths, *downward(weight_sum), sums, feats, local, normed, v_own, *v_far, pool_gain)
+        [smem()] + [vmem()] * 8,
+        [pltpu.VMEM((GROUP, GROUP), bf16)],
+        2 * 8 * GROUP * GROUP,
+    )(lengths, sums, mixed[0], *moved, v_own, v_near, pool_gain)
     parts = lax.all_to_all(part, ("seq", "dp", "domain"), 0, 0, tiled=True)
     vec, loss = call(
         loss_kernel,

time: 82.2 us -> 74.8 us (0.910)
  waiting for transfers between devices: 27.1 us -> 23.9 us
  blocking collectives: 12.6 us -> 9.95 us
  starting transfers between devices: 33.2 us -> 30.9 us
  local copies, waits for them, and re-layouts: 1.12 us -> 2.24 us
    ppermute x14, starting transfers between devices: 26 us -> 19.9 us  [hop(): return lax.ppermute(a, ('seq', 'dp'), pairs)]
    ppermute x5 -> x6, starting transfers between devices: 7.19 us -> 11 us  [plane_hop(): return lax.ppermute(a, ('seq', 'dp'), [(i, i ^ move) for i in range(here)])]
    ppermute x5 -> x6, waiting for transfers between devices: 13.1 us -> 9.39 us  [plane_hop(): return lax.ppermute(a, ('seq', 'dp'), [(i, i ^ move) for i in range(here)])]
    all_to_all x1, blocking collectives: 12.6 us -> 9.95 us  [towers(): parts = lax.all_to_all(part, ('seq', 'dp', 'domain'), 0, 0, tiled=True)]
    unnamed x8 -> x11, local copies, waits for them, and re-layouts: 0.02 us -> 2.19 us
    dynamic_slice x1 -> x0, local copies, waits for them, and re-layouts: 1.04 us -> none  [columns(): lax.dynamic_slice(weight, (0, part * width + which * GROUP), (rows, GROUP))]
  transfers between devices with their start and end apart: 19 -> 20, of which waited for: 7 -> 12; matrix products, arithmetic and copies ran while one was open for 0% -> 0% of each run, Pallas kernels for 5% -> 6%
where the time goes in v4:
time: 74.8 us; the launch traced here: 74.6 us
  starting transfers between devices  30.9 us (41%)
  waiting for transfers between devices  23.9 us (32%)
  blocking collectives  9.95 us (13%)
  Pallas kernels  6.15 us (8%)
  local copies, waits for them, and re-layouts  2.24 us (3%)
  between operations  1.45 us (2%)
    ppermute x14, starting transfers between devices, hop(): return lax.ppermute(a, ('seq', 'dp'), pairs)  19.9 us
    ppermute x14, waiting for transfers between devices, hop(): return lax.ppermute(a, ('seq', 'dp'), pairs)  14.5 us
    ppermute x6, starting transfers between devices, plane_hop(): return lax.ppermute(a, ('seq', 'dp'), [(i, i ^ move) for i in range(here)])  11 us
    all_to_all x1, blocking collectives, towers(): parts = lax.all_to_all(part, ('seq', 'dp', 'domain'), 0, 0, tiled=True)  9.95 us
    ppermute x6, waiting for transfers between devices, plane_hop(): return lax.ppermute(a, ('seq', 'dp'), [(i, i ^ move) for i in range(here)])  9.39 us
    unnamed x11, local copies, waits for them, and re-layouts  2.19 us
  transfers between devices with their start and end apart: 20, of which 12 were waited for; matrix products, arithmetic and copies ran while one was open for 0% of the time, Pallas kernels for 6%

profile of v4, /device:TPU:0, one launch (start us, length us, event | category | flops | bytes accessed | tf_op | source)
XLA Modules:
  0.0 74.6 jit_solution(13767228716367583492)
XLA Ops:
  1.9 3.0 %collective-permute-start = (bf16[128,512]{1,0:T(8,128)(2,1)S(1)}, bf16[128,512]{1,0:T(8,128)(2,1)S(1)}, u32[]{:S(2)}, u32[]{:S(2)}) collective-permute-start(bf16[128,512]{1,0:T(8,128)(2,1)S(1)} %get-tuple-element.16), channel_id=1, source_target_pairs={{0,4},{2,6},{4,0},{6,2},{8,12},{10,14},{12,8},{14,10},{16,20},{18,... | collective-permute-start | bytes 393224 | tf_op jit(solution)/shard_map/ppermute | solution.py:446
  4.9 1.5 %collective-permute-start.2 = (bf16[256,1024]{1,0:T(8,128)(2,1)}, bf16[256,1024]{1,0:T(8,128)(2,1)S(1)}, u32[]{:S(2)}, u32[]{:S(2)}) collective-permute-start(bf16[256,1024]{1,0:T(8,128)(2,1)} %bitcast.3), channel_id=1, source_target_pairs={{0,2},{2,0},{4,6},{6,4},{8,10},{10,8},{12,14},{14,12},{16,18},{18,... | collective-permute-start | bytes 1572872 | tf_op jit(solution)/shard_map/ppermute | solution.py:446
  6.4 2.0 %collective-permute-done.after = bf16[128,512]{1,0:T(8,128)(2,1)S(1)} collective-permute-done((bf16[128,512]{1,0:T(8,128)(2,1)S(1)}, bf16[128,512]{1,0:T(8,128)(2,1)S(1)}, u32[]{:S(2)}, u32[]{:S(2)}) %collective-permute-start) | collective-permute-done | bytes 131104 | tf_op jit(solution)/shard_map/ppermute | solution.py:446
  9.5 1.8 %collective-permute-start.1 = (bf16[256,1024]{1,0:T(8,128)(2,1)S(1)}, bf16[256,1024]{1,0:T(8,128)(2,1)S(1)}, u32[]{:S(2)}, u32[]{:S(2)}) collective-permute-start(bf16[256,1024]{1,0:T(8,128)(2,1)S(1)} %shard_map.78.own), channel_id=1, source_target_pairs={{0,4},{2,6},{4,0},{6,2},{8,12},{10,14},{12,8},{14,10},{16,20},{18,... | collective-permute-start | bytes 1572872 | tf_op jit(solution)/shard_map/ppermute | solution.py:446
  11.3 2.6 %collective-permute-start.6 = (bf16[128,512]{1,0:T(8,128)(2,1)S(1)}, bf16[128,512]{1,0:T(8,128)(2,1)S(1)}, u32[]{:S(2)}, u32[]{:S(2)}) collective-permute-start(bf16[128,512]{1,0:T(8,128)(2,1)S(1)} %get-tuple-element.19), channel_id=1, source_target_pairs={{0,16},{2,18},{4,20},{6,22},{8,24},{10,26},{12,28},{14,30},{16,0},... | collective-permute-start | bytes 393224 | tf_op jit(solution)/shard_map/ppermute | solution.py:443
  14.3 1.6 %collective-permute-start.5 = (bf16[256,512]{1,0:T(8,128)(2,1)S(1)}, bf16[256,512]{1,0:T(8,128)(2,1)S(1)}, u32[]{:S(2)}, u32[]{:S(2)}) collective-permute-start(bf16[256,512]{1,0:T(8,128)(2,1)S(1)} %constant_dynamic-update-slice_fusion.own), channel_id=1, source_target_pairs={{0,8},{2,10},{4,12},{6,14},{8,0},{10,2},{12,4},{14,6},{16,24},{18,... | collective-permute-start | bytes 786440 | tf_op jit(solution)/shard_map/ppermute | solution.py:443
  15.9 2.6 %collective-permute-done.2.across = bf16[256,1024]{1,0:T(8,128)(2,1)S(1)} collective-permute-done((bf16[256,1024]{1,0:T(8,128)(2,1)}, bf16[256,1024]{1,0:T(8,128)(2,1)S(1)}, u32[]{:S(2)}, u32[]{:S(2)}) %collective-permute-start.2) | collective-permute-done | bytes 524320 | tf_op jit(solution)/shard_map/ppermute | solution.py:446
  19.2 3.5 %collective-permute-done.1.near = bf16[256,1024]{1,0:T(8,128)(2,1)S(1)} collective-permute-done((bf16[256,1024]{1,0:T(8,128)(2,1)S(1)}, bf16[256,1024]{1,0:T(8,128)(2,1)S(1)}, u32[]{:S(2)}, u32[]{:S(2)}) %collective-permute-start.1) | collective-permute-done | bytes 524320 | tf_op jit(solution)/shard_map/ppermute | solution.py:446
  22.7 1.4 %collective-permute-start.3 = (bf16[128,1024]{1,0:T(8,128)(2,1)S(1)}, bf16[128,1024]{1,0:T(8,128)(2,1)S(1)}, u32[]{:S(2)}, u32[]{:S(2)}) collective-permute-start(bf16[128,1024]{1,0:T(8,128)(2,1)S(1)} %slice.8), channel_id=1, source_target_pairs={{0,4},{2,6},{4,0},{6,2},{8,12},{10,14},{12,8},{14,10},{16,20},{18,... | collective-permute-start | bytes 786440 | tf_op jit(solution)/shard_map/ppermute | solution.py:446
  24.1 1.6 %collective-permute-start.4 = (bf16[128,1024]{1,0:T(8,128)(2,1)S(1)}, bf16[128,1024]{1,0:T(8,128)(2,1)S(1)}, u32[]{:S(2)}, u32[]{:S(2)}) collective-permute-start(bf16[128,1024]{1,0:T(8,128)(2,1)S(1)} %slice.9), channel_id=1, source_target_pairs={{0,2},{2,0},{4,6},{6,4},{8,10},{10,8},{12,14},{14,12},{16,18},{18,... | collective-permute-start | bytes 786440 | tf_op jit(solution)/shard_map/ppermute | solution.py:446
  27.9 1.3 %collective-permute-done.3.corner_a = bf16[128,1024]{1,0:T(8,128)(2,1)S(1)} collective-permute-done((bf16[128,1024]{1,0:T(8,128)(2,1)S(1)}, bf16[128,1024]{1,0:T(8,128)(2,1)S(1)}, u32[]{:S(2)}, u32[]{:S(2)}) %collective-permute-start.3) | collective-permute-done | bytes 262176 | tf_op jit(solution)/shard_map/ppermute | solution.py:446
  29.2 1.7 %collective-permute-start.19 = (bf16[128,256]{1,0:T(8,128)(2,1)S(1)}, bf16[128,256]{1,0:T(8,128)(2,1)S(1)}, u32[]{:S(2)}, u32[]{:S(2)}) collective-permute-start(bf16[128,256]{1,0:T(8,128)(2,1)S(1)} %get-tuple-element.29), channel_id=1, source_target_pairs={{0,4},{2,6},{4,0},{6,2},{8,12},{10,14},{12,8},{14,10},{16,20},{18,... | collective-permute-start | bytes 196616 | tf_op jit(solution)/shard_map/ppermute | solution.py:446
  31.9 2.4 %collective-permute-done.9.far = bf16[256,512]{1,0:T(8,128)(2,1)S(1)} collective-permute-done((bf16[256,512]{1,0:T(8,128)(2,1)S(1)}, bf16[256,512]{1,0:T(8,128)(2,1)S(1)}, u32[]{:S(2)}, u32[]{:S(2)}) %collective-permute-start.9) | collective-permute-done | bytes 262176 | tf_op jit(solution)/shard_map/ppermute | solution.py:443
  34.2 1.4 %shard_map.80 = (bf16[768,512]{1,0:T(8,128)(2,1)S(1)}, f32[1,256]{1,0:T(1,128)S(1)}) custom-call(bf16[768,1024]{1,0:T(8,128)(2,1)S(1)} %get-tuple-element.18.normed, bf16[256,512]{1,0:T(8,128)(2,1)S(1)} %constant_dynamic-update-slice_fusion.own, bf16[256,512]{1,0:T(8,128)(2,1)S(1)} %collective-permute-done.5.one_away, ...), custom_call_target="tpu_custom_call" | custom-call | flops 805306368 | bytes 2097152 | tf_op jit(solution)/shard_map/pallas_call | solution.py:483
  35.7 4.2 %collective-permute-start.11 = (f32[1,256]{1,0:T(1,128)S(1)}, f32[1,256]{1,0:T(1,128)S(1)}, u32[]{:S(2)}, u32[]{:S(2)}) collective-permute-start(f32[1,256]{1,0:T(1,128)S(1)} %get-tuple-element.20), channel_id=1, source_target_pairs={{0,16},{2,18},{4,20},{6,22},{8,24},{10,26},{12,28},{14,30},{16,0},... | collective-permute-start | bytes 3080 | tf_op jit(solution)/shard_map/ppermute | solution.py:443
  40.1 1.4 %collective-permute-done.11.total_2 = f32[1,256]{1,0:T(1,128)S(1)} collective-permute-done((f32[1,256]{1,0:T(1,128)S(1)}, f32[1,256]{1,0:T(1,128)S(1)}, u32[]{:S(2)}, u32[]{:S(2)}) %collective-permute-start.11) | collective-permute-done | bytes 1056 | tf_op jit(solution)/shard_map/ppermute | solution.py:443
  41.5 3.8 %collective-permute-done.12.total_3 = f32[1,256]{1,0:T(1,128)S(1)} collective-permute-done((f32[1,256]{1,0:T(1,128)S(1)}, f32[1,256]{1,0:T(1,128)S(1)}, u32[]{:S(2)}, u32[]{:S(2)}) %collective-permute-start.12) | collective-permute-done | bytes 1056 | tf_op jit(solution)/shard_map/ppermute | solution.py:443
  45.3 1.4 %shard_map.81 = (f32[1,256]{1,0:T(1,128)S(1)}, f32[768,128]{1,0:T(8,128)S(1)}) custom-call(f32[1,256]{1,0:T(1,128)S(1)} %collective-permute-done.10.total_1, f32[1,256]{1,0:T(1,128)S(1)} %collective-permute-done.11.total_2, f32[1,256]{1,0:T(1,128)S(1)} %collective-permute-done.12.total_3, bf16[768,512]{1,0:T(8,128)(2,1)S(1)} %get-tuple-element.21.feats), custom_call_target="tpu_custom_call" | custom-call | flops 301989888 | bytes 2097152 | tf_op jit(solution)/shard_map/pallas_call | solution.py:490
  46.9 4.3 %collective-permute-start.15 = (f32[1,256]{1,0:T(1,128)S(1)}, f32[1,256]{1,0:T(1,128)S(1)}, u32[]{:S(2)}, u32[]{:S(2)}) collective-permute-start(f32[1,256]{1,0:T(1,128)S(1)} %get-tuple-element.22), channel_id=1, source_target_pairs={{0,24},{2,26},{4,28},{6,30},{8,16},{10,18},{12,20},{14,22},{16,8},... | collective-permute-start | bytes 3080 | tf_op jit(solution)/shard_map/ppermute | solution.py:443
  51.4 1.4 %collective-permute-done.15.sum_3 = f32[1,256]{1,0:T(1,128)S(1)} collective-permute-done((f32[1,256]{1,0:T(1,128)S(1)}, f32[1,256]{1,0:T(1,128)S(1)}, u32[]{:S(2)}, u32[]{:S(2)}) %collective-permute-start.15) | collective-permute-done | bytes 1056 | tf_op jit(solution)/shard_map/ppermute | solution.py:443
  53.9 3.8 %collective-permute-start.17 = (f32[4,256]{1,0:T(4,128)S(1)}, f32[4,256]{1,0:T(4,128)S(1)}, u32[]{:S(2)}, u32[]{:S(2)}) collective-permute-start(f32[4,256]{1,0:T(4,128)S(1)} %get-tuple-element.26), channel_id=1, source_target_pairs={{0,16},{2,18},{4,20},{6,22},{8,24},{10,26},{12,28},{14,30},{16,0},... | collective-permute-start | bytes 12296 | tf_op jit(solution)/shard_map/ppermute | solution.py:443
  58.0 1.3 %collective-permute-done.17.refs_3_ = f32[4,256]{1,0:T(4,128)S(1)} collective-permute-done((f32[4,256]{1,0:T(4,128)S(1)}, f32[4,256]{1,0:T(4,128)S(1)}, u32[]{:S(2)}, u32[]{:S(2)}) %collective-permute-start.17) | collective-permute-done | bytes 4128 | tf_op jit(solution)/shard_map/ppermute | solution.py:443
  59.3 3.8 %collective-permute-done.18.refs_4_ = f32[4,256]{1,0:T(4,128)S(1)} collective-permute-done((f32[4,256]{1,0:T(4,128)S(1)}, f32[4,256]{1,0:T(4,128)S(1)}, u32[]{:S(2)}, u32[]{:S(2)}) %collective-permute-start.18) | collective-permute-done | bytes 4128 | tf_op jit(solution)/shard_map/ppermute | solution.py:443
  63.3 9.9 %all_to_all.5.parts = f32[32,4,256]{2,1,0:T(4,128)S(1)} all-to-all(f32[32,4,256]{2,1,0:T(4,128)S(1)} %shard_map.83), channel_id=1, replica_groups=mesh['seq'=8,'dp'=2,'domain'=2] {'seq','dp','domain'}, dimensions={0} | all-to-all | bytes 262144 | tf_op jit(solution)/shard_map/all_to_all | solution.py:512
  (40 shorter events, 9.3 us)
Async XLA Ops:
  0.6 1.1 %copy-start = (bf16[1,128,3072]{2,1,0:T(8,128)(2,1)S(1)}, bf16[1,128,3072]{2,1,0:T(8,128)(2,1)}, u32[]{:S(2)}) copy-start(bf16[1,128,3072]{2,1,0:T(8,128)(2,1)} %param.7) | copy-start | bytes 2359300
  1.9 6.5 %collective-permute-start = (bf16[128,512]{1,0:T(8,128)(2,1)S(1)}, bf16[128,512]{1,0:T(8,128)(2,1)S(1)}, u32[]{:S(2)}, u32[]{:S(2)}) collective-permute-start(bf16[128,512]{1,0:T(8,128)(2,1)S(1)} %get-tuple-element.16), channel_id=1, source_target_pairs={{0,4},{2,6},{4,0},{6,2},{8,12},{10,14},{12,8},{14,10},{16,20},{18,... | collective-permute-start | bytes 393224 | tf_op jit(solution)/shard_map/ppermute | solution.py:446
  4.9 13.6 %collective-permute-start.2 = (bf16[256,1024]{1,0:T(8,128)(2,1)}, bf16[256,1024]{1,0:T(8,128)(2,1)S(1)}, u32[]{:S(2)}, u32[]{:S(2)}) collective-permute-start(bf16[256,1024]{1,0:T(8,128)(2,1)} %bitcast.3), channel_id=1, source_target_pairs={{0,2},{2,0},{4,6},{6,4},{8,10},{10,8},{12,14},{14,12},{16,18},{18,... | collective-permute-start | bytes 1572872 | tf_op jit(solution)/shard_map/ppermute | solution.py:446
  9.4 21.5 %copy-start.2 = (f32[1,1024]{1,0:T(1,128)S(1)}, f32[1,1024]{1,0:T(1,128)}, u32[]{:S(2)}) copy-start(f32[1,1024]{1,0:T(1,128)} %gain.1) | copy-start | bytes 12292
  9.5 13.2 %collective-permute-start.1 = (bf16[256,1024]{1,0:T(8,128)(2,1)S(1)}, bf16[256,1024]{1,0:T(8,128)(2,1)S(1)}, u32[]{:S(2)}, u32[]{:S(2)}) collective-permute-start(bf16[256,1024]{1,0:T(8,128)(2,1)S(1)} %shard_map.78.own), channel_id=1, source_target_pairs={{0,4},{2,6},{4,0},{6,2},{8,12},{10,14},{12,8},{14,10},{16,20},{18,... | collective-permute-start | bytes 1572872 | tf_op jit(solution)/shard_map/ppermute | solution.py:446
  11.3 12.8 %collective-permute-start.6 = (bf16[128,512]{1,0:T(8,128)(2,1)S(1)}, bf16[128,512]{1,0:T(8,128)(2,1)S(1)}, u32[]{:S(2)}, u32[]{:S(2)}) collective-permute-start(bf16[128,512]{1,0:T(8,128)(2,1)S(1)} %get-tuple-element.19), channel_id=1, source_target_pairs={{0,16},{2,18},{4,20},{6,22},{8,24},{10,26},{12,28},{14,30},{16,0},... | collective-permute-start | bytes 393224 | tf_op jit(solution)/shard_map/ppermute | solution.py:443
  13.9 12.0 %collective-permute-start.7 = (bf16[128,512]{1,0:T(8,128)(2,1)S(1)}, bf16[128,512]{1,0:T(8,128)(2,1)S(1)}, u32[]{:S(2)}, u32[]{:S(2)}) collective-permute-start(bf16[128,512]{1,0:T(8,128)(2,1)S(1)} %collective-permute-done.after), channel_id=1, source_target_pairs={{0,16},{2,18},{4,20},{6,22},{8,24},{10,26},{12,28},{14,30},{16,0},... | collective-permute-start | bytes 393224 | tf_op jit(solution)/shard_map/ppermute | solution.py:443
  14.3 17.6 %collective-permute-start.5 = (bf16[256,512]{1,0:T(8,128)(2,1)S(1)}, bf16[256,512]{1,0:T(8,128)(2,1)S(1)}, u32[]{:S(2)}, u32[]{:S(2)}) collective-permute-start(bf16[256,512]{1,0:T(8,128)(2,1)S(1)} %constant_dynamic-update-slice_fusion.own), channel_id=1, source_target_pairs={{0,8},{2,10},{4,12},{6,14},{8,0},{10,2},{12,4},{14,6},{16,24},{18,... | collective-permute-start | bytes 786440 | tf_op jit(solution)/shard_map/ppermute | solution.py:443
  18.5 13.4 %collective-permute-start.8 = (bf16[256,512]{1,0:T(8,128)(2,1)S(1)}, bf16[256,512]{1,0:T(8,128)(2,1)S(1)}, u32[]{:S(2)}, u32[]{:S(2)}) collective-permute-start(bf16[256,512]{1,0:T(8,128)(2,1)S(1)} %constant_dynamic-update-slice_fusion.own), channel_id=1, source_target_pairs={{8,16},{10,18},{12,20},{14,22},{16,8},{18,10},{20,12},{22,14},{9,1... | collective-permute-start | bytes 786440 | tf_op jit(solution)/shard_map/ppermute | solution.py:443
  22.7 6.6 %collective-permute-start.3 = (bf16[128,1024]{1,0:T(8,128)(2,1)S(1)}, bf16[128,1024]{1,0:T(8,128)(2,1)S(1)}, u32[]{:S(2)}, u32[]{:S(2)}) collective-permute-start(bf16[128,1024]{1,0:T(8,128)(2,1)S(1)} %slice.8), channel_id=1, source_target_pairs={{0,4},{2,6},{4,0},{6,2},{8,12},{10,14},{12,8},{14,10},{16,20},{18,... | collective-permute-start | bytes 786440 | tf_op jit(solution)/shard_map/ppermute | solution.py:446
  24.1 6.8 %collective-permute-start.4 = (bf16[128,1024]{1,0:T(8,128)(2,1)S(1)}, bf16[128,1024]{1,0:T(8,128)(2,1)S(1)}, u32[]{:S(2)}, u32[]{:S(2)}) collective-permute-start(bf16[128,1024]{1,0:T(8,128)(2,1)S(1)} %slice.9), channel_id=1, source_target_pairs={{0,2},{2,0},{4,6},{6,4},{8,10},{10,8},{12,14},{14,12},{16,18},{18,... | collective-permute-start | bytes 786440 | tf_op jit(solution)/shard_map/ppermute | solution.py:446
  26.0 8.3 %collective-permute-start.9 = (bf16[256,512]{1,0:T(8,128)(2,1)S(1)}, bf16[256,512]{1,0:T(8,128)(2,1)S(1)}, u32[]{:S(2)}, u32[]{:S(2)}) collective-permute-start(bf16[256,512]{1,0:T(8,128)(2,1)S(1)} %pad_maximum_fusion), channel_id=1, source_target_pairs={{8,0},{10,2},{12,4},{14,6},{16,24},{18,26},{20,28},{22,30},{9,1},{... | collective-permute-start | bytes 786440 | tf_op jit(solution)/shard_map/ppermute | solution.py:443
  29.2 28.8 %collective-permute-start.19 = (bf16[128,256]{1,0:T(8,128)(2,1)S(1)}, bf16[128,256]{1,0:T(8,128)(2,1)S(1)}, u32[]{:S(2)}, u32[]{:S(2)}) collective-permute-start(bf16[128,256]{1,0:T(8,128)(2,1)S(1)} %get-tuple-element.29), channel_id=1, source_target_pairs={{0,4},{2,6},{4,0},{6,2},{8,12},{10,14},{12,8},{14,10},{16,20},{18,... | collective-permute-start | bytes 196616 | tf_op jit(solution)/shard_map/ppermute | solution.py:446
  35.7 4.5 %collective-permute-start.10 = (f32[1,256]{1,0:T(1,128)S(1)}, f32[1,256]{1,0:T(1,128)S(1)}, u32[]{:S(2)}, u32[]{:S(2)}) collective-permute-start(f32[1,256]{1,0:T(1,128)S(1)} %get-tuple-element.20), channel_id=1, source_target_pairs={{0,8},{2,10},{4,12},{6,14},{8,0},{10,2},{12,4},{14,6},{16,24},{18,... | collective-permute-start | bytes 3080 | tf_op jit(solution)/shard_map/ppermute | solution.py:443
  35.7 5.8 %collective-permute-start.11 = (f32[1,256]{1,0:T(1,128)S(1)}, f32[1,256]{1,0:T(1,128)S(1)}, u32[]{:S(2)}, u32[]{:S(2)}) collective-permute-start(f32[1,256]{1,0:T(1,128)S(1)} %get-tuple-element.20), channel_id=1, source_target_pairs={{0,16},{2,18},{4,20},{6,22},{8,24},{10,26},{12,28},{14,30},{16,0},... | collective-permute-start | bytes 3080 | tf_op jit(solution)/shard_map/ppermute | solution.py:443
  40.0 5.4 %collective-permute-start.12 = (f32[1,256]{1,0:T(1,128)S(1)}, f32[1,256]{1,0:T(1,128)S(1)}, u32[]{:S(2)}, u32[]{:S(2)}) collective-permute-start(f32[1,256]{1,0:T(1,128)S(1)} %get-tuple-element.20), channel_id=1, source_target_pairs={{0,24},{2,26},{4,28},{6,30},{8,16},{10,18},{12,20},{14,22},{16,8},... | collective-permute-start | bytes 3080 | tf_op jit(solution)/shard_map/ppermute | solution.py:443
  46.7 16.4 %copy-start.3 = (f32[1,1024]{1,0:T(1,128)S(1)}, f32[1,1024]{1,0:T(1,128)}, u32[]{:S(2)}) copy-start(f32[1,1024]{1,0:T(1,128)} %refs_7_.1) | copy-start | bytes 12292
  46.8 4.5 %collective-permute-start.13 = (f32[1,256]{1,0:T(1,128)S(1)}, f32[1,256]{1,0:T(1,128)S(1)}, u32[]{:S(2)}, u32[]{:S(2)}) collective-permute-start(f32[1,256]{1,0:T(1,128)S(1)} %get-tuple-element.22), channel_id=1, source_target_pairs={{0,8},{2,10},{4,12},{6,14},{8,0},{10,2},{12,4},{14,6},{16,24},{18,... | collective-permute-start | bytes 3080 | tf_op jit(solution)/shard_map/ppermute | solution.py:443
  46.8 4.5 %collective-permute-start.14 = (f32[1,256]{1,0:T(1,128)S(1)}, f32[1,256]{1,0:T(1,128)S(1)}, u32[]{:S(2)}, u32[]{:S(2)}) collective-permute-start(f32[1,256]{1,0:T(1,128)S(1)} %get-tuple-element.22), channel_id=1, source_target_pairs={{0,16},{2,18},{4,20},{6,22},{8,24},{10,26},{12,28},{14,30},{16,0},... | collective-permute-start | bytes 3080 | tf_op jit(solution)/shard_map/ppermute | solution.py:443
  46.9 5.8 %collective-permute-start.15 = (f32[1,256]{1,0:T(1,128)S(1)}, f32[1,256]{1,0:T(1,128)S(1)}, u32[]{:S(2)}, u32[]{:S(2)}) collective-permute-start(f32[1,256]{1,0:T(1,128)S(1)} %get-tuple-element.22), channel_id=1, source_target_pairs={{0,24},{2,26},{4,28},{6,30},{8,16},{10,18},{12,20},{14,22},{16,8},... | collective-permute-start | bytes 3080 | tf_op jit(solution)/shard_map/ppermute | solution.py:443
  52.8 20.5 %copy-start.4 = (s32[2]{0:T(128)S(1)}, s32[2]{0:T(128)}, u32[]{:S(2)}) copy-start(s32[2]{0:T(128)} %positives.1) | copy-start | bytes 28
  53.5 4.5 %collective-permute-start.16 = (f32[4,256]{1,0:T(4,128)S(1)}, f32[4,256]{1,0:T(4,128)S(1)}, u32[]{:S(2)}, u32[]{:S(2)}) collective-permute-start(f32[4,256]{1,0:T(4,128)S(1)} %get-tuple-element.25), channel_id=1, source_target_pairs={{0,8},{2,10},{4,12},{6,14},{8,0},{10,2},{12,4},{14,6},{16,24},{18,... | collective-permute-start | bytes 12296 | tf_op jit(solution)/shard_map/ppermute | solution.py:443
  53.9 5.4 %collective-permute-start.17 = (f32[4,256]{1,0:T(4,128)S(1)}, f32[4,256]{1,0:T(4,128)S(1)}, u32[]{:S(2)}, u32[]{:S(2)}) collective-permute-start(f32[4,256]{1,0:T(4,128)S(1)} %get-tuple-element.26), channel_id=1, source_target_pairs={{0,16},{2,18},{4,20},{6,22},{8,24},{10,26},{12,28},{14,30},{16,0},... | collective-permute-start | bytes 12296 | tf_op jit(solution)/shard_map/ppermute | solution.py:443
  57.7 5.4 %collective-permute-start.18 = (f32[4,256]{1,0:T(4,128)S(1)}, f32[4,256]{1,0:T(4,128)S(1)}, u32[]{:S(2)}, u32[]{:S(2)}) collective-permute-start(f32[4,256]{1,0:T(4,128)S(1)} %get-tuple-element.27), channel_id=1, source_target_pairs={{0,24},{2,26},{4,28},{6,30},{8,16},{10,18},{12,20},{14,22},{16,8},... | collective-permute-start | bytes 12296 | tf_op jit(solution)/shard_map/ppermute | solution.py:443
  (1 other events, 1.0 us)

commit v5 on v3

--- a/solution.py
+++ b/solution.py
@@ -137,6 +137,7 @@
 PLANES = 4
 GROUP = 256
 DOT_T = (((0,), (0,)), ((), ()))
+MESSAGE = GROUP + 16
 
 
 def places():
@@ -161,29 +162,41 @@
     return high, (a - high.astype(jnp.float32)).astype(jnp.bfloat16)
 
 
-def norm_kernel(lengths, own, near, across, corner_a, corner_b, gain, normed, sums, raw, sems):
+def pack_kernel(weight, out, sems):
+    _, _, u = places()
+    width = weight.shape[1] // 3
+    copies = []
+    for place in range(out.shape[0]):
+        group = 2 * (place % 2) + u
+        for part in range(3):
+            start = pl.multiple_of(part * width + group * GROUP, GROUP)
+            copies.append(
+                pltpu.make_async_copy(
+                    weight.at[:, pl.ds(start, GROUP)],
+                    out.at[place, :, pl.ds(part * GROUP, GROUP)],
+                    sems.at[len(copies)],
+                )
+            )
+    for copy in copies:
+        copy.start()
+    for copy in copies:
+        copy.wait()
+
+
+def norm_kernel(lengths, own, near, across, corner, gain, normed, sums, raw, sems):
     tokens = own.shape[0]
-    half = corner_a.shape[0]
     z, x, u = places()
     long_u = jnp.where(lengths[0, 0] > tokens, u, 1 - u)
-
-    def fetch(slot, pick):
-        for j, ref in enumerate((own, near, across)):
-
-            @pl.when(pick == j)
-            def _():
-                pltpu.make_async_copy(ref.at[pl.ds(0, half)], raw.at[slot, pl.ds(0, half)], sems.at[slot, 0]).start()
-                pltpu.make_async_copy(ref.at[pl.ds(half, half)], raw.at[slot, pl.ds(half, half)], sems.at[slot, 1]).start()
-
-        @pl.when(pick == 3)
-        def _():
-            pltpu.make_async_copy(corner_a, raw.at[slot, pl.ds(0, half)], sems.at[slot, 0]).start()
-            pltpu.make_async_copy(corner_b, raw.at[slot, pl.ds(half, half)], sems.at[slot, 1]).start()
-
     for slot in range(3):
         from_x = 1 if slot == 1 else 0
         from_u = 1 - long_u if slot == 2 else long_u
-        fetch(slot, jnp.bitwise_xor(x, from_x) + 2 * jnp.bitwise_xor(u, from_u))
+        pick = jnp.bitwise_xor(x, from_x) + 2 * jnp.bitwise_xor(u, from_u)
+        for j, ref in enumerate((own, near, across, corner)):
+
+            @pl.when(pick == j)
+            def _():
+                pltpu.make_async_copy(ref, raw.at[slot], sems.at[slot]).start()
+
     columns = pl.ds(pl.multiple_of((2 * x + u) * GROUP, GROUP), GROUP)
 
     def one(slot):
@@ -193,9 +206,7 @@
         return jnp.sum(raw[slot, :, columns].astype(jnp.float32), axis=0, keepdims=True)
 
     for slot in range(3):
-        for part in range(2):
-            at = pl.ds(part * half, half)
-            pltpu.make_async_copy(own.at[at], raw.at[slot, at], sems.at[slot, part]).wait()
+        pltpu.make_async_copy(own, raw.at[slot], sems.at[slot]).wait()
     sums[0:1, :] = one(0) + one(1)
     sums[1:2, :] = jnp.zeros((1, GROUP), jnp.float32)
 
@@ -204,68 +215,54 @@
         sums[1:2, :] = one(2)
 
 
-def gather_rows(z, x, parts, dest):
-    rows = parts[0].shape[0] // 2
-    for j, ref in enumerate(parts):
-        plane = jnp.bitwise_xor(z, j)
-        for half, place in enumerate((x, 1 - x)):
-            start = pl.multiple_of((2 * plane + place) * rows, rows)
-            dest[pl.ds(start, rows), :] = ref[pl.ds(half * rows, rows), :]
-
-
-def project_kernel(normed, own, one_away, two_own, two_near, next_plane, far, feats, totals, weights):
+def project_kernel(normed, weights, feats, message):
     tokens = normed.shape[0] // 3
-    rows = two_own.shape[0]
-    z, x, _ = places()
-
-    def put(plane, place, values):
-        weights[pl.ds(pl.multiple_of((2 * plane + place) * rows, rows), rows), :] = values
-
-    def put_both(plane, ref):
-        put(plane, x, ref[:rows, :])
-        put(plane, 1 - x, ref[rows:, :])
-
-    put_both(z, own)
-    put_both(jnp.bitwise_xor(z, 1), one_away)
-    put(jnp.bitwise_xor(z, 2), x, two_own[...])
-    put(jnp.bitwise_xor(z, 2), 1 - x, two_near[...])
-    inner = jnp.logical_or(z == 1, z == 2)
-
-    @pl.when(inner)
-    def _():
-        put_both(3 - z, next_plane)
-
-    @pl.when(jnp.logical_not(inner))
-    def _():
-        put_both(3 - z, far)
+    z, _, _ = places()
+    wide = 2 * GROUP
 
     def one(slot, count):
         part = pl.ds(slot * tokens, count)
         out = jnp.dot(normed[part, :], weights[...], preferred_element_type=jnp.float32)
-        out = jnp.where(out > 0.0, out + 1.0, jnp.exp(jnp.minimum(out, 0.0))).astype(jnp.bfloat16)
-        feats[part, :] = out
-        return jnp.sum(out[:, GROUP:].astype(jnp.float32), axis=0, keepdims=True)
-
-    totals[...] = one(0, tokens) + one(1, tokens)
+        raw = out[:, :wide]
+        low = jnp.where(raw > 0.0, raw + 1.0, jnp.exp(jnp.minimum(raw, 0.0))).astype(jnp.bfloat16)
+        feats[part, :wide] = low
+        feats[part, wide:] = out[:, wide:].astype(jnp.bfloat16)
+        return jnp.sum(low[:, GROUP:].astype(jnp.float32), axis=0, keepdims=True)
+
+    high, low = split_two(one(0, tokens) + one(1, tokens))
+    for h in range(GROUP // HEAD_DIM):
+        at = h * HEAD_DIM
+        key = feats[0 : 2 * tokens, GROUP + at : GROUP + at + HEAD_DIM]
+        value = feats[0 : 2 * tokens, wide + at : wide + at + HEAD_DIM]
+        state = lax.dot_general(key, value, DOT_T, preferred_element_type=jnp.float32)
+        message[at : at + HEAD_DIM, :] = state.astype(jnp.bfloat16)
+    total_rows = [high[:, :HEAD_DIM], high[:, HEAD_DIM:], low[:, :HEAD_DIM], low[:, HEAD_DIM:]]
+    message[GROUP:, :] = jnp.concatenate(total_rows * 4, axis=0)
 
     @pl.when(z == 0)
     def _():
         one(2, tokens)
 
 
-def scan_kernel(before_1, before_2, before_3, feats, weight_sum, local):
+def pool_kernel(lengths, state_1, state_2, state_3, feats, sums, gain, part, short):
     tokens = feats.shape[0] // 3
-    z, _, _ = places()
+    z, x, u = places()
+    long_u = jnp.where(lengths[0, 0] > tokens, u, 1 - u)
     row = lax.broadcasted_iota(jnp.int32, (tokens, tokens), 0)
     col = lax.broadcasted_iota(jnp.int32, (tokens, tokens), 1)
     lower = (row >= col).astype(jnp.bfloat16)
     upper = (row <= col).astype(jnp.bfloat16)
-    before = before_1[...] + before_2[...] + before_3[...]
+    states = [(jnp.bitwise_xor(z, j) < z, ref) for j, ref in enumerate((state_1, state_2, state_3), 1)]
+    before = jnp.zeros((1, GROUP), jnp.float32)
+    for earlier, ref in states:
+        rows = ref[GROUP : GROUP + 16, :].astype(jnp.float32)
+        total = jnp.concatenate([rows[0:1] + rows[2:3], rows[1:2] + rows[3:4]], axis=1)
+        before = before + jnp.where(earlier, total, 0.0)
 
     def block(slot, carry):
-        part = pl.ds(slot * tokens, tokens)
-        query = feats[part, :GROUP].astype(jnp.float32)
-        key = feats[part, GROUP:]
+        at = pl.ds(slot * tokens, tokens)
+        query = feats[at, :GROUP].astype(jnp.float32)
+        key = feats[at, GROUP : 2 * GROUP]
         prefix = jnp.dot(lower, key, preferred_element_type=jnp.float32) + carry
         share = query / by_head(head_sums(query * prefix))
         return share, key, prefix[tokens - 1 : tokens, :]
@@ -276,68 +273,40 @@
             upper, low, preferred_element_type=jnp.float32
         )
 
-    def store(slot, key, after):
-        sums_by_head = head_sums(key.astype(jnp.float32) * after)
-        part = pl.ds(slot * tokens, tokens)
-        local[part, :] = jnp.concatenate(
-            [jnp.broadcast_to(c, (tokens, HEAD_DIM // 2)) for c in sums_by_head], axis=1
-        )
+    def pooled(slot, key, after):
+        weight = by_head(head_sums(key.astype(jnp.float32) * after))
+        value = feats[pl.ds(slot * tokens, tokens), 2 * GROUP :].astype(jnp.float32)
+        return jnp.sum(weight * value, axis=0, keepdims=True)
 
     share_one, key_one, carry = block(0, before)
     share_two, key_two, _ = block(1, carry)
     after_two = suffix(share_two)
     after_one = suffix(share_one) + after_two[0:1, :]
-    weight_sum[...] = after_one[0:1, :]
-    store(0, key_one, after_one)
-    store(1, key_two, after_two)
+    long_row = pooled(0, key_one, after_one) + pooled(1, key_two, after_two) + sums[0:1, :]
+    weight = after_one[0:1, :]
+    for earlier, ref in states:
+        high, low = split_two(jnp.where(earlier, weight, 0.0))
+        products = []
+        for h in range(GROUP // HEAD_DIM):
+            at = h * HEAD_DIM
+            both = jnp.concatenate([high[:, at : at + HEAD_DIM]] * 8 + [low[:, at : at + HEAD_DIM]] * 8, axis=0)
+            out = jnp.dot(both, ref[at : at + HEAD_DIM, :], preferred_element_type=jnp.float32)
+            products.append(out[0:1] + out[8:9])
+        long_row = long_row + jnp.concatenate(products, axis=1)
+
+    short[...] = sums[1:2, :]
 
     @pl.when(z == 0)
     def _():
         share, key, _ = block(2, jnp.zeros((1, GROUP), jnp.float32))
-        store(2, key, suffix(share))
-
-
-def pool_kernel(
-    lengths, later_1, later_2, later_3, sums, feats, local, normed, v_own, v_1, v_2, v_3, gain, part, values, mixed
-):
-    tokens = feats.shape[0] // 3
-    width = normed.shape[1]
-    z, x, u = places()
-    long_u = jnp.where(lengths[0, 0] > tokens, u, 1 - u)
-    gather_rows(z, x, (v_own, v_1, v_2, v_3), values)
-    after = later_1[...] + later_2[...] + later_3[...]
-    lane = lax.broadcasted_iota(jnp.int32, (1, HEAD_DIM), 1)
-
-    def mix(weight, slot, count):
-        high, low = split_two(weight)
-        both = jnp.where(lax.rem(lane, 64) < 32, high.astype(jnp.float32), low.astype(jnp.float32))
-        rows = normed[pl.ds(slot * tokens, count), :]
-        return lax.dot_general(both.astype(jnp.bfloat16), rows, DOT_T, preferred_element_type=jnp.float32)
-
-    key = feats[0 : 2 * tokens, GROUP:].astype(jnp.float32)
-    extra = jnp.concatenate(
-        [jnp.broadcast_to(c, (2 * tokens, HEAD_DIM // 2)) for c in head_sums(key * after)], axis=1
-    )
-    mixed[0:HEAD_DIM, :] = mix(local[0 : 2 * tokens, :] + extra, 0, 2 * tokens)
-    mixed[HEAD_DIM:, :] = jnp.zeros((HEAD_DIM, width), jnp.float32)
-
-    @pl.when(z == 0)
-    def _():
-        mixed[HEAD_DIM:, :] = mix(local[2 * tokens :, :], 2, tokens)
-
-    picked = [mixed[h : h + 1, :] + mixed[h + 32 : h + 33, :] for h in (0, 64, 128, 192)]
-    high, low = split_two(jnp.concatenate(picked + picked, axis=0))
-    out = jnp.dot(high, values[...], preferred_element_type=jnp.float32) + jnp.dot(
-        low, values[...], preferred_element_type=jnp.float32
-    )
-    half = HEAD_DIM
-    long_row = jnp.concatenate([out[0:1, :half], out[1:2, half:]], axis=1) + sums[0:1, :]
-    short_row = jnp.concatenate([out[2:3, :half], out[3:4, half:]], axis=1) + sums[1:2, :]
+        short[...] = sums[1:2, :] + pooled(2, key, suffix(share))
+
+    short_row = short[...]
     first = jnp.where(long_u == 0, long_row, short_row)
     second = jnp.where(long_u == 0, short_row, long_row)
     own_gain = gain[:, pl.ds(pl.multiple_of((2 * x + u) * GROUP, GROUP), GROUP)]
-    block = jnp.concatenate([first, second, own_gain, own_gain], axis=0)
-    part[...] = jnp.broadcast_to(block[None], part.shape)
+    rows = jnp.concatenate([first, second, own_gain, own_gain], axis=0)
+    part[...] = jnp.broadcast_to(rows[None], part.shape)
 
 
 def loss_kernel(positives, parts, vec, loss, mine, theirs):
@@ -381,6 +350,10 @@
     return pl.BlockSpec(memory_space=pl.ANY)
 
 
+def hbm():
+    return pl.BlockSpec(memory_space=pltpu.HBM)
+
+
 def smem():
     return pl.BlockSpec(memory_space=pltpu.SMEM)
 
@@ -404,8 +377,6 @@
     rows = weight.shape[0]
     f32, bf16 = jnp.float32, jnp.bfloat16
     shape = jax.ShapeDtypeStruct
-    z, x, u = places()
-    group = 2 * x + u
     here = PLANE * PLANES
 
     def hop(a, target):
@@ -415,64 +386,39 @@
     def plane_hop(a, move):
         return lax.ppermute(a, ("seq", "dp"), [(i, i ^ move) for i in range(here)])
 
-    def columns(which):
-        return jnp.concatenate(
-            [lax.dynamic_slice(weight, (0, part * width + which * GROUP), (rows, GROUP)) for part in range(3)],
-            axis=1,
-        )
-
-    def upward(a):
-        return [hop(a, lambda p: p + step if p + step < PLANES else None) for step in (3, 2, 1)]
-
-    def downward(a):
-        return [hop(a, lambda p: p - step if p >= step else None) for step in (3, 2, 1)]
-
-    wide = 2 * GROUP
-    events, w_sent = lax.optimization_barrier((events, columns(jnp.bitwise_xor(group, 2))))
-    w_near = plane_hop(w_sent, 2)
-    w_own = columns(group)
-    qk_own, qk_near = w_own[:, :wide], w_near[:, :wide]
-    two_own = hop(qk_own, lambda p: p ^ 2)
+    def each(a):
+        return [hop(a, lambda p: p ^ j) for j in range(1, PLANES)]
+
+    wide = 3 * GROUP
+    sent = call(
+        pack_kernel, shape((2 * PLANES, rows, wide), bf16), [hbm()], [pltpu.SemaphoreType.DMA((6 * PLANES,))], 0
+    )(weight)
+    weights = lax.all_to_all(sent, "seq", 0, 0, tiled=True).reshape(width, wide)
+    near = plane_hop(events, 2)
     across = plane_hop(events, 1)
-    near = plane_hop(events, 2)
-    two_near = hop(qk_near, lambda p: p ^ 2)
-    qk = jnp.concatenate([qk_own, qk_near], axis=0)
-    one_away = hop(qk, lambda p: p ^ 1)
-    next_plane = hop(qk, lambda p: 3 - p if p in (1, 2) else None)
-    corner_a = plane_hop(across[: tokens // 2], 2)
-    corner_b = plane_hop(near[tokens // 2 :], 1)
-    far = hop(jnp.concatenate([two_own, two_near], axis=0), lambda p: {1: 0, 2: 3}.get(p))
-    v_own = jnp.concatenate([w_own[:, wide:], w_near[:, wide:]], axis=0)
-    v_far = [hop(v_own, lambda p: p ^ j) for j in (1, 2, 3)]
+    corner = plane_hop(events, 3)
 
     normed, sums = call(
         norm_kernel,
         (shape((3 * tokens, width), bf16), shape((2, GROUP), f32)),
-        [smem()] + [anywhere()] * 5 + [vmem()],
-        [pltpu.VMEM((3, tokens, width), bf16), pltpu.SemaphoreType.DMA((3, 2))],
+        [smem()] + [anywhere()] * 4 + [vmem()],
+        [pltpu.VMEM((3, tokens, width), bf16), pltpu.SemaphoreType.DMA((3,))],
         2 * 3 * tokens * width,
-    )(lengths, events, near, across, corner_a, corner_b, norm_gain)
-    feats, totals = call(
+    )(lengths, events, near, across, corner, norm_gain)
+    feats, message = call(
         project_kernel,
-        (shape((3 * tokens, wide), bf16), shape((1, GROUP), f32)),
-        [vmem()] * 7,
-        [pltpu.VMEM((width, wide), bf16)],
+        (shape((3 * tokens, wide), bf16), shape((MESSAGE, HEAD_DIM), bf16)),
+        [vmem()] * 2,
+        [],
         2 * 3 * tokens * width * wide,
-    )(normed, qk, one_away, two_own, two_near, next_plane, far)
-    weight_sum, local = call(
-        scan_kernel,
-        (shape((1, GROUP), f32), shape((3 * tokens, HEAD_DIM), f32)),
-        [vmem()] * 4,
-        [],
-        2 * 9 * tokens * tokens * GROUP,
-    )(*upward(totals), feats)
+    )(normed, weights)
     part = call(
         pool_kernel,
         shape((2 * here, 4, GROUP), f32),
-        [smem()] + [vmem()] * 12,
-        [pltpu.VMEM((width, GROUP), bf16), pltpu.VMEM((2 * HEAD_DIM, width), f32)],
-        2 * 3 * tokens * width * HEAD_DIM,
-    )(lengths, *downward(weight_sum), sums, feats, local, normed, v_own, *v_far, pool_gain)
+        [smem()] + [vmem()] * 6,
+        [pltpu.VMEM((1, GROUP), f32)],
+        2 * 9 * tokens * tokens * GROUP,
+    )(lengths, *each(message), feats, sums, pool_gain)
     parts = lax.all_to_all(part, ("seq", "dp", "domain"), 0, 0, tiled=True)
     vec, loss = call(
         loss_kernel,

time: 82.2 us -> 80.8 us (0.983)
  starting transfers between devices: 33.2 us -> 15.5 us
  waiting for transfers between devices: 27.1 us -> 41.4 us
  local copies, waits for them, and re-layouts: 1.12 us -> 3.73 us
  blocking collectives: 12.6 us -> 11.4 us
  Pallas kernels: 6.14 us -> 7.18 us
    ppermute x5 -> x3, waiting for transfers between devices: 13.1 us -> 37.4 us  [plane_hop(): return lax.ppermute(a, ('seq', 'dp'), [(i, i ^ move) for i in range(here)])]
    ppermute x14 -> x3, starting transfers between devices: 26 us -> 4.45 us  [hop(): return lax.ppermute(a, ('seq', 'dp'), pairs)]
    ppermute x14 -> x3, waiting for transfers between devices: 14 us -> 3.97 us  [hop(): return lax.ppermute(a, ('seq', 'dp'), pairs)]
    all_to_all x0 -> x1, starting transfers between devices: none -> 7.4 us  [towers(): weights = lax.all_to_all(sent, 'seq', 0, 0, tiled=True).reshape(width, wide)]
    unnamed x8 -> x14, local copies, waits for them, and re-layouts: 0.02 us -> 3.73 us
    ppermute x5 -> x3, starting transfers between devices: 7.19 us -> 3.61 us  [plane_hop(): return lax.ppermute(a, ('seq', 'dp'), [(i, i ^ move) for i in range(here)])]
    all_to_all x1, blocking collectives: 12.6 us -> 11.4 us  [towers(): parts = lax.all_to_all(part, ('seq', 'dp', 'domain'), 0, 0, tiled=True)]
    dynamic_slice x1 -> x0, local copies, waits for them, and re-layouts: 1.04 us -> none  [columns(): lax.dynamic_slice(weight, (0, part * width + which * GROUP), (rows, GROUP))]
  transfers between devices with their start and end apart: 19 -> 7, of which waited for: 7 -> 4; matrix products, arithmetic and copies ran while one was open for 0% -> 0% of each run, Pallas kernels for 5% -> 1%
where the time goes in v5:
time: 80.8 us; the launch traced here: 80.5 us
  waiting for transfers between devices  41.4 us (51%)
  starting transfers between devices  15.5 us (19%)
  blocking collectives  11.4 us (14%)
  Pallas kernels  7.18 us (9%)
  local copies, waits for them, and re-layouts  3.73 us (5%)
  between operations  1.37 us (2%)
    ppermute x3, waiting for transfers between devices, plane_hop(): return lax.ppermute(a, ('seq', 'dp'), [(i, i ^ move) for i in range(here)])  37.4 us
    all_to_all x1, blocking collectives, towers(): parts = lax.all_to_all(part, ('seq', 'dp', 'domain'), 0, 0, tiled=True)  11.4 us
    all_to_all x1, starting transfers between devices, towers(): weights = lax.all_to_all(sent, 'seq', 0, 0, tiled=True).reshape(width, wide)  7.4 us
    ppermute x3, starting transfers between devices, hop(): return lax.ppermute(a, ('seq', 'dp'), pairs)  4.45 us
    ppermute x3, waiting for transfers between devices, hop(): return lax.ppermute(a, ('seq', 'dp'), pairs)  3.97 us
    unnamed x14, local copies, waits for them, and re-layouts  3.73 us
    ppermute x3, starting transfers between devices, plane_hop(): return lax.ppermute(a, ('seq', 'dp'), [(i, i ^ move) for i in range(here)])  3.61 us
    pallas_call x1, Pallas kernels, towers(): call(project_kernel, (shape((3 * tokens, wide), bf16), shape((MESSAGE, HE...  1.87 us
  transfers between devices with their start and end apart: 7, of which 4 were waited for; matrix products, arithmetic and copies ran while one was open for 0% of the time, Pallas kernels for 1%

profile of v5, /device:TPU:0, one launch (start us, length us, event | category | flops | bytes accessed | tf_op | source)
XLA Modules:
  0.0 80.5 jit_solution(2821351329679738782)
XLA Ops:
  0.6 1.1 %copy-done = bf16[1,128,3072]{2,1,0:T(8,128)(2,1)S(1)} copy-done((bf16[1,128,3072]{2,1,0:T(8,128)(2,1)S(1)}, bf16[1,128,3072]{2,1,0:T(8,128)(2,1)}, u32[]{:S(2)}) %copy-start) | copy-done | bytes 786456
  1.8 1.6 %shard_map.78 = bf16[8,128,768]{2,1,0:T(8,128)(2,1)} custom-call(bf16[128,3072]{1,0:T(8,128)(2,1)S(1)} %bitcast.4), custom_call_target="tpu_custom_call" | custom-call | bytes 2097152 | tf_op jit(solution)/shard_map/pallas_call | solution.py:393
  3.4 0.0 copy-start.1
  3.4 0.0 copy-start.2
  3.4 7.4 %all-to-all-start = ((bf16[8,128,768]{2,1,0:T(8,128)(2,1)}), bf16[8,128,768]{2,1,0:T(8,128)(2,1)S(1)}, u32[]{:S(2)}, u32[]{:S(2)}) async-start(bf16[8,128,768]{2,1,0:T(8,128)(2,1)} %shard_map.78), calls=%async_computation | async-start | bytes 3145728 | tf_op jit(solution)/shard_map/all_to_all | solution.py:396
  10.8 3.0 %collective-permute-start.2 = (bf16[256,1024]{1,0:T(8,128)(2,1)S(1)}, bf16[256,1024]{1,0:T(8,128)(2,1)S(1)}, u32[]{:S(2)}, u32[]{:S(2)}) collective-permute-start(bf16[256,1024]{1,0:T(8,128)(2,1)S(1)} %bitcast.5), channel_id=1, source_target_pairs={{0,6},{2,4},{4,2},{6,0},{8,14},{10,12},{12,10},{14,8},{16,22},{18,... | collective-permute-start | bytes 1572872 | tf_op jit(solution)/shard_map/ppermute | solution.py:387
  13.8 0.5 collective-permute-start.1
  14.3 0.1 collective-permute-start
  15.1 28.6 %collective-permute-done.2.corner = bf16[256,1024]{1,0:T(8,128)(2,1)S(1)} collective-permute-done((bf16[256,1024]{1,0:T(8,128)(2,1)S(1)}, bf16[256,1024]{1,0:T(8,128)(2,1)S(1)}, u32[]{:S(2)}, u32[]{:S(2)}) %collective-permute-start.2) | collective-permute-done | bytes 524320 | tf_op jit(solution)/shard_map/ppermute | solution.py:387
  43.7 8.8 %collective-permute-done.near = bf16[256,1024]{1,0:T(8,128)(2,1)S(1)} collective-permute-done((bf16[256,1024]{1,0:T(8,128)(2,1)S(1)}, bf16[256,1024]{1,0:T(8,128)(2,1)S(1)}, u32[]{:S(2)}, u32[]{:S(2)}) %collective-permute-start) | collective-permute-done | bytes 524320 | tf_op jit(solution)/shard_map/ppermute | solution.py:387
  52.5 0.9 %shard_map.77 = (bf16[768,1024]{1,0:T(8,128)(2,1)S(1)}, f32[2,256]{1,0:T(2,128)S(1)}) custom-call(s32[1,1]{1,0:T(1,128)S(6)} %copy.8.lengths, bf16[256,1024]{1,0:T(8,128)(2,1)S(1)} %bitcast.8, bf16[256,1024]{1,0:T(8,128)(2,1)S(1)} %collective-permute-done.near, bf16[256,1024]{1,0:T(8,128)(2,1)S(1)} %collective-permute-done.1.across, ...), custom_call_target="tpu_custom_call" | custom-call | flops 1572864 | bytes 2097152 | tf_op jit(solution)/shard_map/pallas_call | solution.py:401
  53.4 1.2 %copy-done.5 = bf16[768,1024]{1,0:T(8,128)(2,1)} copy-done((bf16[768,1024]{1,0:T(8,128)(2,1)}, bf16[768,1024]{1,0:T(8,128)(2,1)S(1)}, u32[]{:S(2)}) %copy-start.5) | copy-done | bytes 1572888
  54.6 0.0 all-to-all-done
  54.6 1.4 %copy-done.6 = bf16[768,1024]{1,0:T(8,128)(2,1)S(1)} copy-done((bf16[768,1024]{1,0:T(8,128)(2,1)S(1)}, bf16[768,1024]{1,0:T(8,128)(2,1)}, u32[]{:S(2)}) %copy-start.6) | copy-done | bytes 1572888
  56.0 1.9 %shard_map.79 = (bf16[768,768]{1,0:T(8,128)(2,1)S(1)}, bf16[272,128]{1,0:T(8,128)(2,1)S(1)}) custom-call(bf16[768,1024]{1,0:T(8,128)(2,1)S(1)} %copy-done.6, bf16[1024,768]{1,0:T(8,128)(2,1)S(1)} %bitcast.3), custom_call_target="tpu_custom_call" | custom-call | flops 1207959552 | bytes 2097152 | tf_op jit(solution)/shard_map/pallas_call | solution.py:408
  57.9 0.0 copy-start.4
  57.9 2.5 %collective-permute-start.5 = (bf16[272,128]{1,0:T(8,128)(2,1)S(1)}, bf16[272,128]{1,0:T(8,128)(2,1)S(1)}, u32[]{:S(2)}, u32[]{:S(2)}) collective-permute-start(bf16[272,128]{1,0:T(8,128)(2,1)S(1)} %get-tuple-element.7), channel_id=1, source_target_pairs={{0,24},{2,26},{4,28},{6,30},{8,16},{10,18},{12,20},{14,22},{16,8},... | collective-permute-start | bytes 208904 | tf_op jit(solution)/shard_map/ppermute | solution.py:384
  60.4 0.0 collective-permute-start.4
  60.4 2.0 %collective-permute-start.3 = (bf16[272,128]{1,0:T(8,128)(2,1)S(1)}, bf16[272,128]{1,0:T(8,128)(2,1)S(1)}, u32[]{:S(2)}, u32[]{:S(2)}) collective-permute-start(bf16[272,128]{1,0:T(8,128)(2,1)S(1)} %get-tuple-element.7), channel_id=1, source_target_pairs={{0,8},{2,10},{4,12},{6,14},{8,0},{10,2},{12,4},{14,6},{16,24},{18,... | collective-permute-start | bytes 208904 | tf_op jit(solution)/shard_map/ppermute | solution.py:384
  62.3 2.5 %collective-permute-done.5.state_3 = bf16[272,128]{1,0:T(8,128)(2,1)S(1)} collective-permute-done((bf16[272,128]{1,0:T(8,128)(2,1)S(1)}, bf16[272,128]{1,0:T(8,128)(2,1)S(1)}, u32[]{:S(2)}, u32[]{:S(2)}) %collective-permute-start.5) | collective-permute-done | bytes 69664 | tf_op jit(solution)/shard_map/ppermute | solution.py:384
  64.9 1.4 %collective-permute-done.4.state_2 = bf16[272,128]{1,0:T(8,128)(2,1)S(1)} collective-permute-done((bf16[272,128]{1,0:T(8,128)(2,1)S(1)}, bf16[272,128]{1,0:T(8,128)(2,1)S(1)}, u32[]{:S(2)}, u32[]{:S(2)}) %collective-permute-start.4) | collective-permute-done | bytes 69664 | tf_op jit(solution)/shard_map/ppermute | solution.py:384
  66.3 1.5 %shard_map.80 = f32[32,4,256]{2,1,0:T(4,128)S(1)} custom-call(s32[1,1]{1,0:T(1,128)S(6)} %copy.8.lengths, bf16[272,128]{1,0:T(8,128)(2,1)S(1)} %collective-permute-done.3.state_1, bf16[272,128]{1,0:T(8,128)(2,1)S(1)} %collective-permute-done.4.state_2, bf16[272,128]{1,0:T(8,128)(2,1)S(1)} %collective-permute-done.5.state_3, ...), custom_call_target="tpu_custom_call" | custom-call | flops 301989888 | bytes 2097152 | tf_op jit(solution)/shard_map/pallas_call | solution.py:415
  67.8 11.4 %all_to_all.10.parts = f32[32,4,256]{2,1,0:T(4,128)S(1)} all-to-all(f32[32,4,256]{2,1,0:T(4,128)S(1)} %shard_map.80), channel_id=1, replica_groups=mesh['seq'=8,'dp'=2,'domain'=2] {'seq','dp','domain'}, dimensions={0} | all-to-all | bytes 262144 | tf_op jit(solution)/shard_map/all_to_all | solution.py:422
  79.2 1.3 %shard_map.81 = (bf16[1,1,128]{2,1,0:T(2,128)(2,1)}, f32[1,1]{1,0:T(1,128)}) custom-call(s32[2]{0:T(128)S(1)} %copy-done.4, f32[32,4,256]{2,1,0:T(4,128)S(1)} %all_to_all.10.parts), custom_call_target="tpu_custom_call" | custom-call | flops 16384 | bytes 2097152 | tf_op jit(solution)/shard_map/pallas_call | solution.py:423
  (10 shorter events, 0.0 us)
Async XLA Ops:
  0.6 1.1 %copy-start = (bf16[1,128,3072]{2,1,0:T(8,128)(2,1)S(1)}, bf16[1,128,3072]{2,1,0:T(8,128)(2,1)}, u32[]{:S(2)}) copy-start(bf16[1,128,3072]{2,1,0:T(8,128)(2,1)} %param.7) | copy-start | bytes 2359300
  3.4 7.4 %copy-start.1 = (bf16[1,1,256,1024]{3,2,1,0:T(8,128)(2,1)S(1)}, bf16[1,1,256,1024]{3,2,1,0:T(8,128)(2,1)}, u32[]{:S(2)}) copy-start(bf16[1,1,256,1024]{3,2,1,0:T(8,128)(2,1)} %param.6) | copy-start | bytes 1572868
  3.4 49.1 %copy-start.2 = (f32[1,1024]{1,0:T(1,128)S(1)}, f32[1,1024]{1,0:T(1,128)}, u32[]{:S(2)}) copy-start(f32[1,1024]{1,0:T(1,128)} %gain.2) | copy-start | bytes 12292
  3.4 51.1 %all-to-all-start = ((bf16[8,128,768]{2,1,0:T(8,128)(2,1)}), bf16[8,128,768]{2,1,0:T(8,128)(2,1)S(1)}, u32[]{:S(2)}, u32[]{:S(2)}) async-start(bf16[8,128,768]{2,1,0:T(8,128)(2,1)} %shard_map.78), calls=%async_computation | async-start | bytes 3145728 | tf_op jit(solution)/shard_map/all_to_all | solution.py:396
  10.8 32.9 %collective-permute-start.2 = (bf16[256,1024]{1,0:T(8,128)(2,1)S(1)}, bf16[256,1024]{1,0:T(8,128)(2,1)S(1)}, u32[]{:S(2)}, u32[]{:S(2)}) collective-permute-start(bf16[256,1024]{1,0:T(8,128)(2,1)S(1)} %bitcast.5), channel_id=1, source_target_pairs={{0,6},{2,4},{4,2},{6,0},{8,14},{10,12},{12,10},{14,8},{16,22},{18,... | collective-permute-start | bytes 1572872 | tf_op jit(solution)/shard_map/ppermute | solution.py:387
  13.8 29.9 %collective-permute-start.1 = (bf16[256,1024]{1,0:T(8,128)(2,1)S(1)}, bf16[256,1024]{1,0:T(8,128)(2,1)S(1)}, u32[]{:S(2)}, u32[]{:S(2)}) collective-permute-start(bf16[256,1024]{1,0:T(8,128)(2,1)S(1)} %bitcast.6), channel_id=1, source_target_pairs={{0,2},{2,0},{4,6},{6,4},{8,10},{10,8},{12,14},{14,12},{16,18},{18,... | collective-permute-start | bytes 1572872 | tf_op jit(solution)/shard_map/ppermute | solution.py:387
  14.3 38.2 %collective-permute-start = (bf16[256,1024]{1,0:T(8,128)(2,1)S(1)}, bf16[256,1024]{1,0:T(8,128)(2,1)S(1)}, u32[]{:S(2)}, u32[]{:S(2)}) collective-permute-start(bf16[256,1024]{1,0:T(8,128)(2,1)S(1)} %bitcast.7), channel_id=1, source_target_pairs={{0,4},{2,6},{4,0},{6,2},{8,12},{10,14},{12,8},{14,10},{16,20},{18,... | collective-permute-start | bytes 1572872 | tf_op jit(solution)/shard_map/ppermute | solution.py:387
  53.4 1.2 %copy-start.5 = (bf16[768,1024]{1,0:T(8,128)(2,1)}, bf16[768,1024]{1,0:T(8,128)(2,1)S(1)}, u32[]{:S(2)}) copy-start(bf16[768,1024]{1,0:T(8,128)(2,1)S(1)} %get-tuple-element.6.normed) | copy-start | bytes 4718596
  54.6 1.4 %copy-start.6 = (bf16[768,1024]{1,0:T(8,128)(2,1)S(1)}, bf16[768,1024]{1,0:T(8,128)(2,1)}, u32[]{:S(2)}) copy-start(bf16[768,1024]{1,0:T(8,128)(2,1)} %copy-done.5) | copy-start | bytes 4718596
  56.0 10.3 %copy-start.3 = (f32[1,1024]{1,0:T(1,128)S(1)}, f32[1,1024]{1,0:T(1,128)}, u32[]{:S(2)}) copy-start(f32[1,1024]{1,0:T(1,128)} %gain.3) | copy-start | bytes 12292
  57.9 21.3 %copy-start.4 = (s32[2]{0:T(128)S(1)}, s32[2]{0:T(128)}, u32[]{:S(2)}) copy-start(s32[2]{0:T(128)} %positives.1) | copy-start | bytes 28
  57.9 7.0 %collective-permute-start.5 = (bf16[272,128]{1,0:T(8,128)(2,1)S(1)}, bf16[272,128]{1,0:T(8,128)(2,1)S(1)}, u32[]{:S(2)}, u32[]{:S(2)}) collective-permute-start(bf16[272,128]{1,0:T(8,128)(2,1)S(1)} %get-tuple-element.7), channel_id=1, source_target_pairs={{0,24},{2,26},{4,28},{6,30},{8,16},{10,18},{12,20},{14,22},{16,8},... | collective-permute-start | bytes 208904 | tf_op jit(solution)/shard_map/ppermute | solution.py:384
  60.4 5.9 %collective-permute-start.4 = (bf16[272,128]{1,0:T(8,128)(2,1)S(1)}, bf16[272,128]{1,0:T(8,128)(2,1)S(1)}, u32[]{:S(2)}, u32[]{:S(2)}) collective-permute-start(bf16[272,128]{1,0:T(8,128)(2,1)S(1)} %get-tuple-element.7), channel_id=1, source_target_pairs={{0,16},{2,18},{4,20},{6,22},{8,24},{10,26},{12,28},{14,30},{16,0},... | collective-permute-start | bytes 208904 | tf_op jit(solution)/shard_map/ppermute | solution.py:384
  60.4 5.9 %collective-permute-start.3 = (bf16[272,128]{1,0:T(8,128)(2,1)S(1)}, bf16[272,128]{1,0:T(8,128)(2,1)S(1)}, u32[]{:S(2)}, u32[]{:S(2)}) collective-permute-start(bf16[272,128]{1,0:T(8,128)(2,1)S(1)} %get-tuple-element.7), channel_id=1, source_target_pairs={{0,8},{2,10},{4,12},{6,14},{8,0},{10,2},{12,4},{14,6},{16,24},{18,... | collective-permute-start | bytes 208904 | tf_op jit(solution)/shard_map/ppermute | solution.py:384

commit v6 on v5

--- a/solution.py
+++ b/solution.py
@@ -162,19 +162,17 @@
     return high, (a - high.astype(jnp.float32)).astype(jnp.bfloat16)
 
 
-def pack_kernel(weight, out, sems):
-    _, _, u = places()
+def pack_kernel(weight, own, sent, sems):
+    _, x, u = places()
     width = weight.shape[1] // 3
     copies = []
-    for place in range(out.shape[0]):
-        group = 2 * (place % 2) + u
+    for move, out in ((2, sent), (0, own)):
+        group = jnp.bitwise_xor(2 * x + u, move)
         for part in range(3):
             start = pl.multiple_of(part * width + group * GROUP, GROUP)
             copies.append(
                 pltpu.make_async_copy(
-                    weight.at[:, pl.ds(start, GROUP)],
-                    out.at[place, :, pl.ds(part * GROUP, GROUP)],
-                    sems.at[len(copies)],
+                    weight.at[:, pl.ds(start, GROUP)], out.at[:, pl.ds(part * GROUP, GROUP)], sems.at[len(copies)]
                 )
             )
     for copy in copies:
@@ -183,20 +181,38 @@
         copy.wait()
 
 
-def norm_kernel(lengths, own, near, across, corner, gain, normed, sums, raw, sems):
+def relay_kernel(events, w_own, w_near, out, both, sem):
+    rows = w_own.shape[0]
+    copy = pltpu.make_async_copy(events, out, sem)
+    copy.start()
+    both[:rows, :] = w_own[...]
+    both[rows:, :] = w_near[...]
+    copy.wait()
+
+
+def norm_kernel(lengths, own, near, across, corner_a, corner_b, gain, normed, sums, raw, sems):
     tokens = own.shape[0]
+    half = corner_a.shape[0]
     z, x, u = places()
     long_u = jnp.where(lengths[0, 0] > tokens, u, 1 - u)
+
+    def fetch(slot, pick):
+        for j, ref in enumerate((own, near, across)):
+
+            @pl.when(pick == j)
+            def _():
+                pltpu.make_async_copy(ref.at[pl.ds(0, half)], raw.at[slot, pl.ds(0, half)], sems.at[slot, 0]).start()
+                pltpu.make_async_copy(ref.at[pl.ds(half, half)], raw.at[slot, pl.ds(half, half)], sems.at[slot, 1]).start()
+
+        @pl.when(pick == 3)
+        def _():
+            pltpu.make_async_copy(corner_a, raw.at[slot, pl.ds(0, half)], sems.at[slot, 0]).start()
+            pltpu.make_async_copy(corner_b, raw.at[slot, pl.ds(half, half)], sems.at[slot, 1]).start()
+
     for slot in range(3):
         from_x = 1 if slot == 1 else 0
         from_u = 1 - long_u if slot == 2 else long_u
-        pick = jnp.bitwise_xor(x, from_x) + 2 * jnp.bitwise_xor(u, from_u)
-        for j, ref in enumerate((own, near, across, corner)):
-
-            @pl.when(pick == j)
-            def _():
-                pltpu.make_async_copy(ref, raw.at[slot], sems.at[slot]).start()
-
+        fetch(slot, jnp.bitwise_xor(x, from_x) + 2 * jnp.bitwise_xor(u, from_u))
     columns = pl.ds(pl.multiple_of((2 * x + u) * GROUP, GROUP), GROUP)
 
     def one(slot):
@@ -206,7 +222,9 @@
         return jnp.sum(raw[slot, :, columns].astype(jnp.float32), axis=0, keepdims=True)
 
     for slot in range(3):
-        pltpu.make_async_copy(own, raw.at[slot], sems.at[slot]).wait()
+        for part in range(2):
+            at = pl.ds(part * half, half)
+            pltpu.make_async_copy(own.at[at], raw.at[slot, at], sems.at[slot, part]).wait()
     sums[0:1, :] = one(0) + one(1)
     sums[1:2, :] = jnp.zeros((1, GROUP), jnp.float32)
 
@@ -215,9 +233,28 @@
         sums[1:2, :] = one(2)
 
 
-def project_kernel(normed, weights, feats, message):
+def project_kernel(normed, both, one, two_own, two_near, next_both, far_own, far_near, feats, message, weights):
     tokens = normed.shape[0] // 3
-    z, _, _ = places()
+    rows = two_own.shape[0]
+    z, x, _ = places()
+
+    def put(plane, own, near):
+        for place, values in ((x, own), (1 - x, near)):
+            weights[pl.ds(pl.multiple_of((2 * plane + place) * rows, rows), rows), :] = values
+
+    put(z, both[:rows, :], both[rows:, :])
+    put(jnp.bitwise_xor(z, 1), one[:rows, :], one[rows:, :])
+    put(jnp.bitwise_xor(z, 2), two_own[...], two_near[...])
+    inner = jnp.logical_or(z == 1, z == 2)
+
+    @pl.when(inner)
+    def _():
+        put(3 - z, next_both[:rows, :], next_both[rows:, :])
+
+    @pl.when(jnp.logical_not(inner))
+    def _():
+        put(3 - z, far_own[...], far_near[...])
+
     wide = 2 * GROUP
 
     def one(slot, count):
@@ -390,28 +427,42 @@
         return [hop(a, lambda p: p ^ j) for j in range(1, PLANES)]
 
     wide = 3 * GROUP
-    sent = call(
-        pack_kernel, shape((2 * PLANES, rows, wide), bf16), [hbm()], [pltpu.SemaphoreType.DMA((6 * PLANES,))], 0
+    w_own, w_sent = call(
+        pack_kernel, (shape((rows, wide), bf16),) * 2, [hbm()], [pltpu.SemaphoreType.DMA((6,))], 0
     )(weight)
-    weights = lax.all_to_all(sent, "seq", 0, 0, tiled=True).reshape(width, wide)
-    near = plane_hop(events, 2)
+    w_near = plane_hop(w_sent, 2)
     across = plane_hop(events, 1)
-    corner = plane_hop(events, 3)
+    two_own = hop(w_own, lambda p: p ^ 2)
+    own, both = call(
+        relay_kernel,
+        (shape((tokens, width), bf16), shape((2 * rows, wide), bf16)),
+        [hbm(), vmem(), vmem()],
+        [pltpu.SemaphoreType.DMA(())],
+        0,
+    )(events, w_own, w_near)
+    two_near = hop(w_near, lambda p: p ^ 2)
+    next_both = hop(both, lambda p: 3 - p if p in (1, 2) else None)
+    one = hop(both, lambda p: p ^ 1)
+    near = plane_hop(own, 2)
+    far_own = hop(two_own, lambda p: {1: 0, 2: 3}.get(p))
+    far_near = hop(two_near, lambda p: {1: 0, 2: 3}.get(p))
+    corner_a = plane_hop(across[: tokens // 2], 2)
+    corner_b = plane_hop(near[tokens // 2 :], 1)
 
     normed, sums = call(
         norm_kernel,
         (shape((3 * tokens, width), bf16), shape((2, GROUP), f32)),
-        [smem()] + [anywhere()] * 4 + [vmem()],
-        [pltpu.VMEM((3, tokens, width), bf16), pltpu.SemaphoreType.DMA((3,))],
+        [smem()] + [anywhere()] * 5 + [vmem()],
+        [pltpu.VMEM((3, tokens, width), bf16), pltpu.SemaphoreType.DMA((3, 2))],
         2 * 3 * tokens * width,
-    )(lengths, events, near, across, corner, norm_gain)
+    )(lengths, own, near, across, corner_a, corner_b, norm_gain)
     feats, message = call(
         project_kernel,
         (shape((3 * tokens, wide), bf16), shape((MESSAGE, HEAD_DIM), bf16)),
-        [vmem()] * 2,
-        [],
+        [vmem()] * 8,
+        [pltpu.VMEM((width, wide), bf16)],
         2 * 3 * tokens * width * wide,
-    )(normed, weights)
+    )(normed, both, one, two_own, two_near, next_both, far_own, far_near)
     part = call(
         pool_kernel,
         shape((2 * here, 4, GROUP), f32),

time: 80.8 us -> 69.3 us (0.86)
  waiting for transfers between devices: 41.4 us -> 26.6 us
  starting transfers between devices: 15.5 us -> 22.9 us
  local copies, waits for them, and re-layouts: 3.73 us -> 2.22 us
  blocking collectives: 11.4 us -> 9.93 us
  Pallas kernels: 7.18 us -> 5.95 us
    ppermute x3 -> x5, waiting for transfers between devices: 37.4 us -> 9.13 us  [plane_hop(): return lax.ppermute(a, ('seq', 'dp'), [(i, i ^ move) for i in range(here)])]
    ppermute x3 -> x9, waiting for transfers between devices: 3.97 us -> 17.5 us  [hop(): return lax.ppermute(a, ('seq', 'dp'), pairs)]
    ppermute x3 -> x9, starting transfers between devices: 4.45 us -> 14.6 us  [hop(): return lax.ppermute(a, ('seq', 'dp'), pairs)]
    all_to_all x1 -> x0, starting transfers between devices: 7.4 us -> none  [towers(): weights = lax.all_to_all(sent, 'seq', 0, 0, tiled=True).reshape(width, wide)]
    ppermute x3 -> x5, starting transfers between devices: 3.61 us -> 8.27 us  [plane_hop(): return lax.ppermute(a, ('seq', 'dp'), [(i, i ^ move) for i in range(here)])]
    unnamed x14 -> x10, local copies, waits for them, and re-layouts: 3.73 us -> 2.18 us
    pallas_call x1 -> x2, Pallas kernels: 1.64 us -> 0.19 us  [the longest x1 0.12 us: towers(): call(pack_kernel, (shape((rows, wide), bf16),) * 2, [hbm()], [pltpu.Semap...]
    all_to_all x1, blocking collectives: 11.4 us -> 9.93 us  [towers(): parts = lax.all_to_all(part, ('seq', 'dp', 'domain'), 0, 0, tiled=True)]
  transfers between devices with their start and end apart: 7 -> 14, of which waited for: 4 -> 10; matrix products, arithmetic and copies ran while one was open for 0% -> 0% of each run, Pallas kernels for 1% -> 1%
where the time goes in v6:
time: 69.3 us; the launch traced here: 69 us
  waiting for transfers between devices  26.6 us (38%)
  starting transfers between devices  22.9 us (33%)
  blocking collectives  9.93 us (14%)
  Pallas kernels  5.95 us (9%)
  local copies, waits for them, and re-layouts  2.22 us (3%)
  between operations  1.41 us (2%)
    ppermute x9, waiting for transfers between devices, hop(): return lax.ppermute(a, ('seq', 'dp'), pairs)  17.5 us
    ppermute x9, starting transfers between devices, hop(): return lax.ppermute(a, ('seq', 'dp'), pairs)  14.6 us
    all_to_all x1, blocking collectives, towers(): parts = lax.all_to_all(part, ('seq', 'dp', 'domain'), 0, 0, tiled=True)  9.93 us
    ppermute x5, waiting for transfers between devices, plane_hop(): return lax.ppermute(a, ('seq', 'dp'), [(i, i ^ move) for i in range(here)])  9.13 us
    ppermute x5, starting transfers between devices, plane_hop(): return lax.ppermute(a, ('seq', 'dp'), [(i, i ^ move) for i in range(here)])  8.27 us
    unnamed x10, local copies, waits for them, and re-layouts  2.18 us
    pallas_call x1, Pallas kernels, towers(): call(project_kernel, (shape((3 * tokens, wide), bf16), shape((MESSAGE, HE...  2.02 us
    pallas_call x1, Pallas kernels, towers(): call(pool_kernel, shape((2 * here, 4, GROUP), f32), [smem()] + [vmem()] *...  1.5 us
  transfers between devices with their start and end apart: 14, of which 10 were waited for; matrix products, arithmetic and copies ran while one was open for 0% of the time, Pallas kernels for 1%

profile of v6, /device:TPU:0, one launch (start us, length us, event | category | flops | bytes accessed | tf_op | source)
XLA Modules:
  0.0 69.0 jit_solution(9903240872758998818)
XLA Ops:
  0.6 1.1 %copy-done = bf16[1,128,3072]{2,1,0:T(8,128)(2,1)S(1)} copy-done((bf16[1,128,3072]{2,1,0:T(8,128)(2,1)S(1)}, bf16[1,128,3072]{2,1,0:T(8,128)(2,1)}, u32[]{:S(2)}) %copy-start) | copy-done | bytes 786456
  1.9 3.0 %collective-permute-start = (bf16[128,768]{1,0:T(8,128)(2,1)S(1)}, bf16[128,768]{1,0:T(8,128)(2,1)S(1)}, u32[]{:S(2)}, u32[]{:S(2)}) collective-permute-start(bf16[128,768]{1,0:T(8,128)(2,1)S(1)} %get-tuple-element.11), channel_id=1, source_target_pairs={{0,4},{2,6},{4,0},{6,2},{8,12},{10,14},{12,8},{14,10},{16,20},{18,... | collective-permute-start | bytes 589832 | tf_op jit(solution)/shard_map/ppermute | solution.py:424
  4.9 1.5 %collective-permute-start.2 = (bf16[256,1024]{1,0:T(8,128)(2,1)}, bf16[256,1024]{1,0:T(8,128)(2,1)S(1)}, u32[]{:S(2)}, u32[]{:S(2)}) collective-permute-start(bf16[256,1024]{1,0:T(8,128)(2,1)} %bitcast.3), channel_id=1, source_target_pairs={{0,2},{2,0},{4,6},{6,4},{8,10},{10,8},{12,14},{14,12},{16,18},{18,... | collective-permute-start | bytes 1572872 | tf_op jit(solution)/shard_map/ppermute | solution.py:424
  6.4 3.4 %collective-permute-done.w_near = bf16[128,768]{1,0:T(8,128)(2,1)S(1)} collective-permute-done((bf16[128,768]{1,0:T(8,128)(2,1)S(1)}, bf16[128,768]{1,0:T(8,128)(2,1)S(1)}, u32[]{:S(2)}, u32[]{:S(2)}) %collective-permute-start) | collective-permute-done | bytes 196640 | tf_op jit(solution)/shard_map/ppermute | solution.py:424
  10.9 1.8 %collective-permute-start.1 = (bf16[256,1024]{1,0:T(8,128)(2,1)S(1)}, bf16[256,1024]{1,0:T(8,128)(2,1)S(1)}, u32[]{:S(2)}, u32[]{:S(2)}) collective-permute-start(bf16[256,1024]{1,0:T(8,128)(2,1)S(1)} %get-tuple-element.12.own), channel_id=1, source_target_pairs={{0,4},{2,6},{4,0},{6,2},{8,12},{10,14},{12,8},{14,10},{16,20},{18,... | collective-permute-start | bytes 1572872 | tf_op jit(solution)/shard_map/ppermute | solution.py:424
  12.7 2.6 %collective-permute-start.6 = (bf16[128,768]{1,0:T(8,128)(2,1)S(1)}, bf16[128,768]{1,0:T(8,128)(2,1)S(1)}, u32[]{:S(2)}, u32[]{:S(2)}) collective-permute-start(bf16[128,768]{1,0:T(8,128)(2,1)S(1)} %get-tuple-element.10.w_own), channel_id=1, source_target_pairs={{0,16},{2,18},{4,20},{6,22},{8,24},{10,26},{12,28},{14,30},{16,0},... | collective-permute-start | bytes 589832 | tf_op jit(solution)/shard_map/ppermute | solution.py:421
  15.3 3.2 %collective-permute-done.2.across = bf16[256,1024]{1,0:T(8,128)(2,1)S(1)} collective-permute-done((bf16[256,1024]{1,0:T(8,128)(2,1)}, bf16[256,1024]{1,0:T(8,128)(2,1)S(1)}, u32[]{:S(2)}, u32[]{:S(2)}) %collective-permute-start.2) | collective-permute-done | bytes 524320 | tf_op jit(solution)/shard_map/ppermute | solution.py:424
  18.9 2.8 %collective-permute-start.7 = (bf16[128,768]{1,0:T(8,128)(2,1)S(1)}, bf16[128,768]{1,0:T(8,128)(2,1)S(1)}, u32[]{:S(2)}, u32[]{:S(2)}) collective-permute-start(bf16[128,768]{1,0:T(8,128)(2,1)S(1)} %collective-permute-done.w_near), channel_id=1, source_target_pairs={{0,16},{2,18},{4,20},{6,22},{8,24},{10,26},{12,28},{14,30},{16,0},... | collective-permute-start | bytes 589832 | tf_op jit(solution)/shard_map/ppermute | solution.py:421
  21.7 1.6 %collective-permute-start.5 = (bf16[256,768]{1,0:T(8,128)(2,1)S(1)}, bf16[256,768]{1,0:T(8,128)(2,1)S(1)}, u32[]{:S(2)}, u32[]{:S(2)}) collective-permute-start(bf16[256,768]{1,0:T(8,128)(2,1)S(1)} %get-tuple-element.14.both), channel_id=1, source_target_pairs={{0,8},{2,10},{4,12},{6,14},{8,0},{10,2},{12,4},{14,6},{16,24},{18,... | collective-permute-start | bytes 1179656 | tf_op jit(solution)/shard_map/ppermute | solution.py:421
  23.3 2.6 %collective-permute-done.1.near = bf16[256,1024]{1,0:T(8,128)(2,1)S(1)} collective-permute-done((bf16[256,1024]{1,0:T(8,128)(2,1)S(1)}, bf16[256,1024]{1,0:T(8,128)(2,1)S(1)}, u32[]{:S(2)}, u32[]{:S(2)}) %collective-permute-start.1) | collective-permute-done | bytes 524320 | tf_op jit(solution)/shard_map/ppermute | solution.py:424
  26.6 2.0 %collective-permute-done.6.two_own = bf16[128,768]{1,0:T(8,128)(2,1)S(1)} collective-permute-done((bf16[128,768]{1,0:T(8,128)(2,1)S(1)}, bf16[128,768]{1,0:T(8,128)(2,1)S(1)}, u32[]{:S(2)}, u32[]{:S(2)}) %collective-permute-start.6) | collective-permute-done | bytes 196640 | tf_op jit(solution)/shard_map/ppermute | solution.py:421
  28.6 1.5 %collective-permute-start.4 = (bf16[128,1024]{1,0:T(8,128)(2,1)S(1)}, bf16[128,1024]{1,0:T(8,128)(2,1)S(1)}, u32[]{:S(2)}, u32[]{:S(2)}) collective-permute-start(bf16[128,1024]{1,0:T(8,128)(2,1)S(1)} %slice.9), channel_id=1, source_target_pairs={{0,2},{2,0},{4,6},{6,4},{8,10},{10,8},{12,14},{14,12},{16,18},{18,... | collective-permute-start | bytes 786440 | tf_op jit(solution)/shard_map/ppermute | solution.py:424
  30.1 2.8 %collective-permute-done.7.two_near = bf16[128,768]{1,0:T(8,128)(2,1)S(1)} collective-permute-done((bf16[128,768]{1,0:T(8,128)(2,1)S(1)}, bf16[128,768]{1,0:T(8,128)(2,1)S(1)}, u32[]{:S(2)}, u32[]{:S(2)}) %collective-permute-start.7) | collective-permute-done | bytes 196640 | tf_op jit(solution)/shard_map/ppermute | solution.py:421
  32.9 1.3 %collective-permute-start.9 = (bf16[128,768]{1,0:T(8,128)(2,1)S(1)}, bf16[128,768]{1,0:T(8,128)(2,1)S(1)}, u32[]{:S(2)}, u32[]{:S(2)}) collective-permute-start(bf16[128,768]{1,0:T(8,128)(2,1)S(1)} %collective-permute-done.6.two_own), channel_id=1, source_target_pairs={{8,0},{10,2},{12,4},{14,6},{16,24},{18,26},{20,28},{22,30},{9,1},{... | collective-permute-start | bytes 589832 | tf_op jit(solution)/shard_map/ppermute | solution.py:421
  34.2 1.3 %collective-permute-start.10 = (bf16[128,768]{1,0:T(8,128)(2,1)S(1)}, bf16[128,768]{1,0:T(8,128)(2,1)S(1)}, u32[]{:S(2)}, u32[]{:S(2)}) collective-permute-start(bf16[128,768]{1,0:T(8,128)(2,1)S(1)} %collective-permute-done.7.two_near), channel_id=1, source_target_pairs={{8,0},{10,2},{12,4},{14,6},{16,24},{18,26},{20,28},{22,30},{9,1},{... | collective-permute-start | bytes 589832 | tf_op jit(solution)/shard_map/ppermute | solution.py:421
  37.2 5.4 %collective-permute-done.9.far_own = bf16[128,768]{1,0:T(8,128)(2,1)S(1)} collective-permute-done((bf16[128,768]{1,0:T(8,128)(2,1)S(1)}, bf16[128,768]{1,0:T(8,128)(2,1)S(1)}, u32[]{:S(2)}, u32[]{:S(2)}) %collective-permute-start.9) | collective-permute-done | bytes 196640 | tf_op jit(solution)/shard_map/ppermute | solution.py:421
  42.6 2.1 %collective-permute-done.10.far_near = bf16[128,768]{1,0:T(8,128)(2,1)S(1)} collective-permute-done((bf16[128,768]{1,0:T(8,128)(2,1)S(1)}, bf16[128,768]{1,0:T(8,128)(2,1)S(1)}, u32[]{:S(2)}, u32[]{:S(2)}) %collective-permute-start.10) | collective-permute-done | bytes 196640 | tf_op jit(solution)/shard_map/ppermute | solution.py:421
  44.7 2.0 %shard_map.80 = (bf16[768,768]{1,0:T(8,128)(2,1)S(1)}, bf16[272,128]{1,0:T(8,128)(2,1)S(1)}) custom-call(bf16[768,1024]{1,0:T(8,128)(2,1)S(1)} %get-tuple-element.13.normed, bf16[256,768]{1,0:T(8,128)(2,1)S(1)} %get-tuple-element.14.both, bf16[256,768]{1,0:T(8,128)(2,1)S(1)} %collective-permute-done.5.one, ...), custom_call_target="tpu_custom_call" | custom-call | flops 1207959552 | bytes 2097152 | tf_op jit(solution)/shard_map/pallas_call | solution.py:459
  46.8 3.3 %collective-permute-start.12 = (bf16[272,128]{1,0:T(8,128)(2,1)S(1)}, bf16[272,128]{1,0:T(8,128)(2,1)S(1)}, u32[]{:S(2)}, u32[]{:S(2)}) collective-permute-start(bf16[272,128]{1,0:T(8,128)(2,1)S(1)} %get-tuple-element.15), channel_id=1, source_target_pairs={{0,16},{2,18},{4,20},{6,22},{8,24},{10,26},{12,28},{14,30},{16,0},... | collective-permute-start | bytes 208904 | tf_op jit(solution)/shard_map/ppermute | solution.py:421
  51.3 1.3 %collective-permute-done.12.state_2 = bf16[272,128]{1,0:T(8,128)(2,1)S(1)} collective-permute-done((bf16[272,128]{1,0:T(8,128)(2,1)S(1)}, bf16[272,128]{1,0:T(8,128)(2,1)S(1)}, u32[]{:S(2)}, u32[]{:S(2)}) %collective-permute-start.12) | collective-permute-done | bytes 69664 | tf_op jit(solution)/shard_map/ppermute | solution.py:421
  52.6 3.7 %collective-permute-done.13.state_3 = bf16[272,128]{1,0:T(8,128)(2,1)S(1)} collective-permute-done((bf16[272,128]{1,0:T(8,128)(2,1)S(1)}, bf16[272,128]{1,0:T(8,128)(2,1)S(1)}, u32[]{:S(2)}, u32[]{:S(2)}) %collective-permute-start.13) | collective-permute-done | bytes 69664 | tf_op jit(solution)/shard_map/ppermute | solution.py:421
  56.3 1.5 %shard_map.81 = f32[32,4,256]{2,1,0:T(4,128)S(1)} custom-call(s32[1,1]{1,0:T(1,128)S(6)} %copy.8.lengths, bf16[272,128]{1,0:T(8,128)(2,1)S(1)} %collective-permute-done.11.state_1, bf16[272,128]{1,0:T(8,128)(2,1)S(1)} %collective-permute-done.12.state_2, bf16[272,128]{1,0:T(8,128)(2,1)S(1)} %collective-permute-done.13.state_3, ...), custom_call_target="tpu_custom_call" | custom-call | flops 301989888 | bytes 2097152 | tf_op jit(solution)/shard_map/pallas_call | solution.py:466
  57.8 9.9 %all_to_all.5.parts = f32[32,4,256]{2,1,0:T(4,128)S(1)} all-to-all(f32[32,4,256]{2,1,0:T(4,128)S(1)} %shard_map.81), channel_id=1, replica_groups=mesh['seq'=8,'dp'=2,'domain'=2] {'seq','dp','domain'}, dimensions={0} | all-to-all | bytes 262144 | tf_op jit(solution)/shard_map/all_to_all | solution.py:473
  67.7 1.3 %shard_map.82 = (bf16[1,1,128]{2,1,0:T(2,128)(2,1)}, f32[1,1]{1,0:T(1,128)}) custom-call(s32[2]{0:T(128)S(1)} %copy-done.4, f32[32,4,256]{2,1,0:T(4,128)S(1)} %all_to_all.5.parts), custom_call_target="tpu_custom_call" | custom-call | flops 16384 | bytes 2097152 | tf_op jit(solution)/shard_map/pallas_call | solution.py:474
  (23 shorter events, 4.5 us)
Async XLA Ops:
  0.6 1.1 %copy-start = (bf16[1,128,3072]{2,1,0:T(8,128)(2,1)S(1)}, bf16[1,128,3072]{2,1,0:T(8,128)(2,1)}, u32[]{:S(2)}) copy-start(bf16[1,128,3072]{2,1,0:T(8,128)(2,1)} %param.7) | copy-start | bytes 2359300
  1.8 34.4 %copy-start.2 = (f32[1,1024]{1,0:T(1,128)S(1)}, f32[1,1024]{1,0:T(1,128)}, u32[]{:S(2)}) copy-start(f32[1,1024]{1,0:T(1,128)} %gain.2) | copy-start | bytes 12292
  1.9 7.9 %collective-permute-start = (bf16[128,768]{1,0:T(8,128)(2,1)S(1)}, bf16[128,768]{1,0:T(8,128)(2,1)S(1)}, u32[]{:S(2)}, u32[]{:S(2)}) collective-permute-start(bf16[128,768]{1,0:T(8,128)(2,1)S(1)} %get-tuple-element.11), channel_id=1, source_target_pairs={{0,4},{2,6},{4,0},{6,2},{8,12},{10,14},{12,8},{14,10},{16,20},{18,... | collective-permute-start | bytes 589832 | tf_op jit(solution)/shard_map/ppermute | solution.py:424
  4.9 13.6 %collective-permute-start.2 = (bf16[256,1024]{1,0:T(8,128)(2,1)}, bf16[256,1024]{1,0:T(8,128)(2,1)S(1)}, u32[]{:S(2)}, u32[]{:S(2)}) collective-permute-start(bf16[256,1024]{1,0:T(8,128)(2,1)} %bitcast.3), channel_id=1, source_target_pairs={{0,2},{2,0},{4,6},{6,4},{8,10},{10,8},{12,14},{14,12},{16,18},{18,... | collective-permute-start | bytes 1572872 | tf_op jit(solution)/shard_map/ppermute | solution.py:424
  9.8 1.0 %copy-start.1 = (bf16[1,1,256,1024]{3,2,1,0:T(8,128)(2,1)S(1)}, bf16[1,1,256,1024]{3,2,1,0:T(8,128)(2,1)}, u32[]{:S(2)}) copy-start(bf16[1,1,256,1024]{3,2,1,0:T(8,128)(2,1)} %param.6) | copy-start | bytes 1572868
  10.9 14.9 %collective-permute-start.1 = (bf16[256,1024]{1,0:T(8,128)(2,1)S(1)}, bf16[256,1024]{1,0:T(8,128)(2,1)S(1)}, u32[]{:S(2)}, u32[]{:S(2)}) collective-permute-start(bf16[256,1024]{1,0:T(8,128)(2,1)S(1)} %get-tuple-element.12.own), channel_id=1, source_target_pairs={{0,4},{2,6},{4,0},{6,2},{8,12},{10,14},{12,8},{14,10},{16,20},{18,... | collective-permute-start | bytes 1572872 | tf_op jit(solution)/shard_map/ppermute | solution.py:424
  12.7 15.8 %collective-permute-start.6 = (bf16[128,768]{1,0:T(8,128)(2,1)S(1)}, bf16[128,768]{1,0:T(8,128)(2,1)S(1)}, u32[]{:S(2)}, u32[]{:S(2)}) collective-permute-start(bf16[128,768]{1,0:T(8,128)(2,1)S(1)} %get-tuple-element.10.w_own), channel_id=1, source_target_pairs={{0,16},{2,18},{4,20},{6,22},{8,24},{10,26},{12,28},{14,30},{16,0},... | collective-permute-start | bytes 589832 | tf_op jit(solution)/shard_map/ppermute | solution.py:421
  18.5 15.7 %collective-permute-start.3 = (bf16[128,1024]{1,0:T(8,128)(2,1)S(1)}, bf16[128,1024]{1,0:T(8,128)(2,1)S(1)}, u32[]{:S(2)}, u32[]{:S(2)}) collective-permute-start(bf16[128,1024]{1,0:T(8,128)(2,1)S(1)} %slice.8), channel_id=1, source_target_pairs={{0,4},{2,6},{4,0},{6,2},{8,12},{10,14},{12,8},{14,10},{16,20},{18,... | collective-permute-start | bytes 786440 | tf_op jit(solution)/shard_map/ppermute | solution.py:424
  18.9 14.0 %collective-permute-start.7 = (bf16[128,768]{1,0:T(8,128)(2,1)S(1)}, bf16[128,768]{1,0:T(8,128)(2,1)S(1)}, u32[]{:S(2)}, u32[]{:S(2)}) collective-permute-start(bf16[128,768]{1,0:T(8,128)(2,1)S(1)} %collective-permute-done.w_near), channel_id=1, source_target_pairs={{0,16},{2,18},{4,20},{6,22},{8,24},{10,26},{12,28},{14,30},{16,0},... | collective-permute-start | bytes 589832 | tf_op jit(solution)/shard_map/ppermute | solution.py:421
  21.7 20.9 %collective-permute-start.5 = (bf16[256,768]{1,0:T(8,128)(2,1)S(1)}, bf16[256,768]{1,0:T(8,128)(2,1)S(1)}, u32[]{:S(2)}, u32[]{:S(2)}) collective-permute-start(bf16[256,768]{1,0:T(8,128)(2,1)S(1)} %get-tuple-element.14.both), channel_id=1, source_target_pairs={{0,8},{2,10},{4,12},{6,14},{8,0},{10,2},{12,4},{14,6},{16,24},{18,... | collective-permute-start | bytes 1179656 | tf_op jit(solution)/shard_map/ppermute | solution.py:421
  25.9 16.7 %collective-permute-start.8 = (bf16[256,768]{1,0:T(8,128)(2,1)S(1)}, bf16[256,768]{1,0:T(8,128)(2,1)S(1)}, u32[]{:S(2)}, u32[]{:S(2)}) collective-permute-start(bf16[256,768]{1,0:T(8,128)(2,1)S(1)} %get-tuple-element.14.both), channel_id=1, source_target_pairs={{8,16},{10,18},{12,20},{14,22},{16,8},{18,10},{20,12},{22,14},{9,1... | collective-permute-start | bytes 1179656 | tf_op jit(solution)/shard_map/ppermute | solution.py:421
  28.6 7.6 %collective-permute-start.4 = (bf16[128,1024]{1,0:T(8,128)(2,1)S(1)}, bf16[128,1024]{1,0:T(8,128)(2,1)S(1)}, u32[]{:S(2)}, u32[]{:S(2)}) collective-permute-start(bf16[128,1024]{1,0:T(8,128)(2,1)S(1)} %slice.9), channel_id=1, source_target_pairs={{0,2},{2,0},{4,6},{6,4},{8,10},{10,8},{12,14},{14,12},{16,18},{18,... | collective-permute-start | bytes 786440 | tf_op jit(solution)/shard_map/ppermute | solution.py:424
  32.9 9.7 %collective-permute-start.9 = (bf16[128,768]{1,0:T(8,128)(2,1)S(1)}, bf16[128,768]{1,0:T(8,128)(2,1)S(1)}, u32[]{:S(2)}, u32[]{:S(2)}) collective-permute-start(bf16[128,768]{1,0:T(8,128)(2,1)S(1)} %collective-permute-done.6.two_own), channel_id=1, source_target_pairs={{8,0},{10,2},{12,4},{14,6},{16,24},{18,26},{20,28},{22,30},{9,1},{... | collective-permute-start | bytes 589832 | tf_op jit(solution)/shard_map/ppermute | solution.py:421
  34.2 10.5 %collective-permute-start.10 = (bf16[128,768]{1,0:T(8,128)(2,1)S(1)}, bf16[128,768]{1,0:T(8,128)(2,1)S(1)}, u32[]{:S(2)}, u32[]{:S(2)}) collective-permute-start(bf16[128,768]{1,0:T(8,128)(2,1)S(1)} %collective-permute-done.7.two_near), channel_id=1, source_target_pairs={{8,0},{10,2},{12,4},{14,6},{16,24},{18,26},{20,28},{22,30},{9,1},{... | collective-permute-start | bytes 589832 | tf_op jit(solution)/shard_map/ppermute | solution.py:421
  44.7 11.6 %copy-start.3 = (f32[1,1024]{1,0:T(1,128)S(1)}, f32[1,1024]{1,0:T(1,128)}, u32[]{:S(2)}) copy-start(f32[1,1024]{1,0:T(1,128)} %gain.3) | copy-start | bytes 12292
  46.7 21.0 %copy-start.4 = (s32[2]{0:T(128)S(1)}, s32[2]{0:T(128)}, u32[]{:S(2)}) copy-start(s32[2]{0:T(128)} %positives.1) | copy-start | bytes 28
  46.7 4.6 %collective-permute-start.11 = (bf16[272,128]{1,0:T(8,128)(2,1)S(1)}, bf16[272,128]{1,0:T(8,128)(2,1)S(1)}, u32[]{:S(2)}, u32[]{:S(2)}) collective-permute-start(bf16[272,128]{1,0:T(8,128)(2,1)S(1)} %get-tuple-element.15), channel_id=1, source_target_pairs={{0,8},{2,10},{4,12},{6,14},{8,0},{10,2},{12,4},{14,6},{16,24},{18,... | collective-permute-start | bytes 208904 | tf_op jit(solution)/shard_map/ppermute | solution.py:421
  46.8 5.8 %collective-permute-start.12 = (bf16[272,128]{1,0:T(8,128)(2,1)S(1)}, bf16[272,128]{1,0:T(8,128)(2,1)S(1)}, u32[]{:S(2)}, u32[]{:S(2)}) collective-permute-start(bf16[272,128]{1,0:T(8,128)(2,1)S(1)} %get-tuple-element.15), channel_id=1, source_target_pairs={{0,16},{2,18},{4,20},{6,22},{8,24},{10,26},{12,28},{14,30},{16,0},... | collective-permute-start | bytes 208904 | tf_op jit(solution)/shard_map/ppermute | solution.py:421
  50.2 6.1 %collective-permute-start.13 = (bf16[272,128]{1,0:T(8,128)(2,1)S(1)}, bf16[272,128]{1,0:T(8,128)(2,1)S(1)}, u32[]{:S(2)}, u32[]{:S(2)}) collective-permute-start(bf16[272,128]{1,0:T(8,128)(2,1)S(1)} %get-tuple-element.15), channel_id=1, source_target_pairs={{0,24},{2,26},{4,28},{6,30},{8,16},{10,18},{12,20},{14,22},{16,8},... | collective-permute-start | bytes 208904 | tf_op jit(solution)/shard_map/ppermute | solution.py:421

commit v7 on v5

--- a/solution.py
+++ b/solution.py
@@ -162,19 +162,17 @@
     return high, (a - high.astype(jnp.float32)).astype(jnp.bfloat16)
 
 
-def pack_kernel(weight, out, sems):
-    _, _, u = places()
+def pack_kernel(weight, own, sent, sems):
+    _, x, u = places()
     width = weight.shape[1] // 3
     copies = []
-    for place in range(out.shape[0]):
-        group = 2 * (place % 2) + u
+    for move, out in ((2, sent), (0, own)):
+        group = jnp.bitwise_xor(2 * x + u, move)
         for part in range(3):
             start = pl.multiple_of(part * width + group * GROUP, GROUP)
             copies.append(
                 pltpu.make_async_copy(
-                    weight.at[:, pl.ds(start, GROUP)],
-                    out.at[place, :, pl.ds(part * GROUP, GROUP)],
-                    sems.at[len(copies)],
+                    weight.at[:, pl.ds(start, GROUP)], out.at[:, pl.ds(part * GROUP, GROUP)], sems.at[len(copies)]
                 )
             )
     for copy in copies:
@@ -183,75 +181,133 @@
         copy.wait()
 
 
-def norm_kernel(lengths, own, near, across, corner, gain, normed, sums, raw, sems):
+def gate_kernel(values, after, out):
+    del after
+    out[...] = values[...]
+
+
+def normalise(values, gain):
+    wide = values.astype(jnp.float32)
+    scale = lax.rsqrt(jnp.mean(wide * wide, axis=1, keepdims=True) + epsilon)
+    return (wide * scale * gain).astype(jnp.bfloat16)
+
+
+def features(normed, weights):
+    out = jnp.dot(normed, weights, preferred_element_type=jnp.float32)
+    raw = out[:, : 2 * GROUP]
+    low = jnp.where(raw > 0.0, raw + 1.0, jnp.exp(jnp.minimum(raw, 0.0))).astype(jnp.bfloat16)
+    return low[:, :GROUP], low[:, GROUP:], out[:, 2 * GROUP :].astype(jnp.bfloat16)
+
+
+def norm_kernel(lengths, own, near, across, corner, gain, normed, sums, short, raw, sems):
     tokens = own.shape[0]
-    z, x, u = places()
+    _, x, u = places()
     long_u = jnp.where(lengths[0, 0] > tokens, u, 1 - u)
     for slot in range(3):
         from_x = 1 if slot == 1 else 0
         from_u = 1 - long_u if slot == 2 else long_u
         pick = jnp.bitwise_xor(x, from_x) + 2 * jnp.bitwise_xor(u, from_u)
+        dest = short if slot == 2 else raw.at[slot]
         for j, ref in enumerate((own, near, across, corner)):
 
             @pl.when(pick == j)
             def _():
-                pltpu.make_async_copy(ref, raw.at[slot], sems.at[slot]).start()
+                pltpu.make_async_copy(ref, dest, sems.at[slot]).start()
 
     columns = pl.ds(pl.multiple_of((2 * x + u) * GROUP, GROUP), GROUP)
-
-    def one(slot):
-        values = raw[slot].astype(jnp.float32)
-        scale = lax.rsqrt(jnp.mean(values * values, axis=1, keepdims=True) + epsilon)
-        normed[pl.ds(slot * tokens, tokens), :] = (values * scale * gain[...]).astype(jnp.bfloat16)
-        return jnp.sum(raw[slot, :, columns].astype(jnp.float32), axis=0, keepdims=True)
-
-    for slot in range(3):
+    total = jnp.zeros((1, GROUP), jnp.float32)
+    for slot in range(2):
         pltpu.make_async_copy(own, raw.at[slot], sems.at[slot]).wait()
-    sums[0:1, :] = one(0) + one(1)
-    sums[1:2, :] = jnp.zeros((1, GROUP), jnp.float32)
-
-    @pl.when(z == 0)
+        normed[pl.ds(slot * tokens, tokens), :] = normalise(raw[slot], gain[...])
+        total = total + jnp.sum(raw[slot, :, columns].astype(jnp.float32), axis=0, keepdims=True)
+    sums[...] = total
+    pltpu.make_async_copy(own, short, sems.at[2]).wait()
+
+
+def project_kernel(normed, both, one, two_own, two_near, next_both, far_own, far_near, feats, message, weights):
+    tokens = normed.shape[0]
+    rows = two_own.shape[0]
+    z, x, _ = places()
+
+    def put(plane, own, near):
+        for place, values in ((x, own), (1 - x, near)):
+            weights[pl.ds(pl.multiple_of((2 * plane + place) * rows, rows), rows), :] = values
+
+    put(z, both[:rows, :], both[rows:, :])
+    put(jnp.bitwise_xor(z, 1), one[:rows, :], one[rows:, :])
+    put(jnp.bitwise_xor(z, 2), two_own[...], two_near[...])
+    inner = jnp.logical_or(z == 1, z == 2)
+
+    @pl.when(inner)
     def _():
-        sums[1:2, :] = one(2)
-
-
-def project_kernel(normed, weights, feats, message):
-    tokens = normed.shape[0] // 3
-    z, _, _ = places()
-    wide = 2 * GROUP
-
-    def one(slot, count):
-        part = pl.ds(slot * tokens, count)
-        out = jnp.dot(normed[part, :], weights[...], preferred_element_type=jnp.float32)
-        raw = out[:, :wide]
-        low = jnp.where(raw > 0.0, raw + 1.0, jnp.exp(jnp.minimum(raw, 0.0))).astype(jnp.bfloat16)
-        feats[part, :wide] = low
-        feats[part, wide:] = out[:, wide:].astype(jnp.bfloat16)
-        return jnp.sum(low[:, GROUP:].astype(jnp.float32), axis=0, keepdims=True)
-
-    high, low = split_two(one(0, tokens) + one(1, tokens))
+        put(3 - z, next_both[:rows, :], next_both[rows:, :])
+
+    @pl.when(jnp.logical_not(inner))
+    def _():
+        put(3 - z, far_own[...], far_near[...])
+
+    half = tokens // 2
+    total = jnp.zeros((1, GROUP), jnp.float32)
+    for part in range(2):
+        at = pl.ds(part * half, half)
+        query, key, value = features(normed[at, :], weights[...])
+        feats[at, :GROUP] = query
+        feats[at, GROUP : 2 * GROUP] = key
+        feats[at, 2 * GROUP :] = value
+        total = total + jnp.sum(key.astype(jnp.float32), axis=0, keepdims=True)
+    high, low = split_two(total)
     for h in range(GROUP // HEAD_DIM):
         at = h * HEAD_DIM
-        key = feats[0 : 2 * tokens, GROUP + at : GROUP + at + HEAD_DIM]
-        value = feats[0 : 2 * tokens, wide + at : wide + at + HEAD_DIM]
+        key = feats[:, GROUP + at : GROUP + at + HEAD_DIM]
+        value = feats[:, 2 * GROUP + at : 2 * GROUP + at + HEAD_DIM]
         state = lax.dot_general(key, value, DOT_T, preferred_element_type=jnp.float32)
         message[at : at + HEAD_DIM, :] = state.astype(jnp.bfloat16)
     total_rows = [high[:, :HEAD_DIM], high[:, HEAD_DIM:], low[:, :HEAD_DIM], low[:, HEAD_DIM:]]
     message[GROUP:, :] = jnp.concatenate(total_rows * 4, axis=0)
 
+
+def triangle(tokens, upper):
+    row = lax.broadcasted_iota(jnp.int32, (tokens, tokens), 0)
+    col = lax.broadcasted_iota(jnp.int32, (tokens, tokens), 1)
+    return (row <= col if upper else row >= col).astype(jnp.bfloat16)
+
+
+def shares(query, key, carry):
+    prefix = jnp.dot(triangle(key.shape[0], False), key, preferred_element_type=jnp.float32) + carry
+    wide = query.astype(jnp.float32)
+    return wide / by_head(head_sums(wide * prefix)), prefix[key.shape[0] - 1 :, :]
+
+
+def suffix(share):
+    upper = triangle(share.shape[0], True)
+    high, low = split_two(share)
+    return jnp.dot(upper, high, preferred_element_type=jnp.float32) + jnp.dot(
+        upper, low, preferred_element_type=jnp.float32
+    )
+
+
+def weighted(key, value, after):
+    weight = by_head(head_sums(key.astype(jnp.float32) * after))
+    return jnp.sum(weight * value.astype(jnp.float32), axis=0, keepdims=True)
+
+
+def short_kernel(raw, weights, gain, out):
+    z, x, u = places()
+    out[...] = jnp.zeros(out.shape, jnp.float32)
+
     @pl.when(z == 0)
     def _():
-        one(2, tokens)
-
-
-def pool_kernel(lengths, state_1, state_2, state_3, feats, sums, gain, part, short):
-    tokens = feats.shape[0] // 3
+        query, key, value = features(normalise(raw[...], gain[...]), weights[...])
+        share, _ = shares(query, key, jnp.zeros((1, GROUP), jnp.float32))
+        columns = pl.ds(pl.multiple_of((2 * x + u) * GROUP, GROUP), GROUP)
+        own = jnp.sum(raw[:, columns].astype(jnp.float32), axis=0, keepdims=True)
+        out[...] = own + weighted(key, value, suffix(share))
+
+
+def pool_kernel(lengths, state_1, state_2, state_3, feats, sums, short, gain, part):
+    tokens = feats.shape[0] // 2
     z, x, u = places()
     long_u = jnp.where(lengths[0, 0] > tokens, u, 1 - u)
-    row = lax.broadcasted_iota(jnp.int32, (tokens, tokens), 0)
-    col = lax.broadcasted_iota(jnp.int32, (tokens, tokens), 1)
-    lower = (row >= col).astype(jnp.bfloat16)
-    upper = (row <= col).astype(jnp.bfloat16)
     states = [(jnp.bitwise_xor(z, j) < z, ref) for j, ref in enumerate((state_1, state_2, state_3), 1)]
     before = jnp.zeros((1, GROUP), jnp.float32)
     for earlier, ref in states:
@@ -259,30 +315,17 @@
         total = jnp.concatenate([rows[0:1] + rows[2:3], rows[1:2] + rows[3:4]], axis=1)
         before = before + jnp.where(earlier, total, 0.0)
 
-    def block(slot, carry):
+    def block(slot):
         at = pl.ds(slot * tokens, tokens)
-        query = feats[at, :GROUP].astype(jnp.float32)
-        key = feats[at, GROUP : 2 * GROUP]
-        prefix = jnp.dot(lower, key, preferred_element_type=jnp.float32) + carry
-        share = query / by_head(head_sums(query * prefix))
-        return share, key, prefix[tokens - 1 : tokens, :]
-
-    def suffix(share):
-        high, low = split_two(share)
-        return jnp.dot(upper, high, preferred_element_type=jnp.float32) + jnp.dot(
-            upper, low, preferred_element_type=jnp.float32
-        )
-
-    def pooled(slot, key, after):
-        weight = by_head(head_sums(key.astype(jnp.float32) * after))
-        value = feats[pl.ds(slot * tokens, tokens), 2 * GROUP :].astype(jnp.float32)
-        return jnp.sum(weight * value, axis=0, keepdims=True)
-
-    share_one, key_one, carry = block(0, before)
-    share_two, key_two, _ = block(1, carry)
+        return feats[at, :GROUP], feats[at, GROUP : 2 * GROUP], feats[at, 2 * GROUP :]
+
+    query_one, key_one, value_one = block(0)
+    query_two, key_two, value_two = block(1)
+    share_one, carry = shares(query_one, key_one, before)
+    share_two, _ = shares(query_two, key_two, carry)
     after_two = suffix(share_two)
     after_one = suffix(share_one) + after_two[0:1, :]
-    long_row = pooled(0, key_one, after_one) + pooled(1, key_two, after_two) + sums[0:1, :]
+    long_row = weighted(key_one, value_one, after_one) + weighted(key_two, value_two, after_two) + sums[...]
     weight = after_one[0:1, :]
     for earlier, ref in states:
         high, low = split_two(jnp.where(earlier, weight, 0.0))
@@ -293,13 +336,6 @@
             out = jnp.dot(both, ref[at : at + HEAD_DIM, :], preferred_element_type=jnp.float32)
             products.append(out[0:1] + out[8:9])
         long_row = long_row + jnp.concatenate(products, axis=1)
-
-    short[...] = sums[1:2, :]
-
-    @pl.when(z == 0)
-    def _():
-        share, key, _ = block(2, jnp.zeros((1, GROUP), jnp.float32))
-        short[...] = sums[1:2, :] + pooled(2, key, suffix(share))
 
     short_row = short[...]
     first = jnp.where(long_u == 0, long_row, short_row)
@@ -390,35 +426,47 @@
         return [hop(a, lambda p: p ^ j) for j in range(1, PLANES)]
 
     wide = 3 * GROUP
-    sent = call(
-        pack_kernel, shape((2 * PLANES, rows, wide), bf16), [hbm()], [pltpu.SemaphoreType.DMA((6 * PLANES,))], 0
+    w_own, w_sent = call(
+        pack_kernel, (shape((rows, wide), bf16),) * 2, [hbm()], [pltpu.SemaphoreType.DMA((6,))], 0
     )(weight)
-    weights = lax.all_to_all(sent, "seq", 0, 0, tiled=True).reshape(width, wide)
     near = plane_hop(events, 2)
     across = plane_hop(events, 1)
     corner = plane_hop(events, 3)
-
-    normed, sums = call(
+    w_near = plane_hop(w_sent, 2)
+    two_own = hop(w_own, lambda p: p ^ 2)
+    two_near = hop(w_near, lambda p: p ^ 2)
+    both = jnp.concatenate([w_own, w_near], axis=0)
+    one_own = hop(w_own, lambda p: p ^ 1)
+    one_near = hop(w_near, lambda p: p ^ 1)
+    one = jnp.concatenate([one_own, one_near], axis=0)
+    next_both = hop(both, lambda p: 3 - p if p in (1, 2) else None)
+    far_own = hop(two_own, lambda p: {1: 0, 2: 3}.get(p))
+    far_near = hop(two_near, lambda p: {1: 0, 2: 3}.get(p))
+
+    normed, sums, raw_short = call(
         norm_kernel,
-        (shape((3 * tokens, width), bf16), shape((2, GROUP), f32)),
+        (shape((2 * tokens, width), bf16), shape((1, GROUP), f32), shape((tokens, width), bf16)),
         [smem()] + [anywhere()] * 4 + [vmem()],
-        [pltpu.VMEM((3, tokens, width), bf16), pltpu.SemaphoreType.DMA((3,))],
+        [pltpu.VMEM((2, tokens, width), bf16), pltpu.SemaphoreType.DMA((3,))],
         2 * 3 * tokens * width,
     )(lengths, events, near, across, corner, norm_gain)
-    feats, message = call(
+    feats, message, weights = call(
         project_kernel,
-        (shape((3 * tokens, wide), bf16), shape((MESSAGE, HEAD_DIM), bf16)),
-        [vmem()] * 2,
+        (shape((2 * tokens, wide), bf16), shape((MESSAGE, HEAD_DIM), bf16), shape((width, wide), bf16)),
+        [vmem()] * 8,
         [],
-        2 * 3 * tokens * width * wide,
-    )(normed, weights)
+        2 * 2 * tokens * width * wide,
+    )(normed, both, one, two_own, two_near, next_both, far_own, far_near)
+    short = call(
+        short_kernel, shape((1, GROUP), f32), [vmem()] * 3, [], 2 * tokens * width * wide
+    )(raw_short, weights, norm_gain)
     part = call(
         pool_kernel,
         shape((2 * here, 4, GROUP), f32),
-        [smem()] + [vmem()] * 6,
-        [pltpu.VMEM((1, GROUP), f32)],
+        [smem()] + [vmem()] * 7,
+        [],
         2 * 9 * tokens * tokens * GROUP,
-    )(lengths, *each(message), feats, sums, pool_gain)
+    )(lengths, *each(message), feats, sums, short, pool_gain)
     parts = lax.all_to_all(part, ("seq", "dp", "domain"), 0, 0, tiled=True)
     vec, loss = call(
         loss_kernel,

time: 80.8 us -> 63.6 us (0.79)
  waiting for transfers between devices: 41.4 us -> 21.4 us
  starting transfers between devices: 15.5 us -> 22.2 us
  local copies, waits for them, and re-layouts: 3.73 us -> 1.17 us
  Pallas kernels: 7.18 us -> 5.6 us
    ppermute x3 -> x4, waiting for transfers between devices: 37.4 us -> 2.15 us  [plane_hop(): return lax.ppermute(a, ('seq', 'dp'), [(i, i ^ move) for i in range(here)])]
    ppermute x3 -> x10, waiting for transfers between devices: 3.97 us -> 19.2 us  [hop(): return lax.ppermute(a, ('seq', 'dp'), pairs)]
    ppermute x3 -> x10, starting transfers between devices: 4.45 us -> 15.7 us  [hop(): return lax.ppermute(a, ('seq', 'dp'), pairs)]
    all_to_all x1 -> x0, starting transfers between devices: 7.4 us -> none  [towers(): weights = lax.all_to_all(sent, 'seq', 0, 0, tiled=True).reshape(width, wide)]
    ppermute x3 -> x4, starting transfers between devices: 3.61 us -> 6.49 us  [plane_hop(): return lax.ppermute(a, ('seq', 'dp'), [(i, i ^ move) for i in range(here)])]
    unnamed x14 -> x11, local copies, waits for them, and re-layouts: 3.73 us -> 1.16 us
    pallas_call x3 -> x4, Pallas kernels: 4.39 us -> 3.44 us  [the longest x1 1.42 us: towers(): call(project_kernel, (shape((2 * tokens, wide), bf16), shape((MESSAGE, HE...]
  transfers between devices with their start and end apart: 7 -> 14, of which waited for: 4 -> 8; matrix products, arithmetic and copies ran while one was open for 0% -> 0% of each run, Pallas kernels for 1% -> 3%
where the time goes in v7:
time: 63.6 us; the launch traced here: 63.4 us
  starting transfers between devices  22.2 us (35%)
  waiting for transfers between devices  21.4 us (34%)
  blocking collectives  11.7 us (18%)
  Pallas kernels  5.6 us (9%)
  between operations  1.4 us (2%)
  local copies, waits for them, and re-layouts  1.17 us (2%)
    ppermute x10, waiting for transfers between devices, hop(): return lax.ppermute(a, ('seq', 'dp'), pairs)  19.2 us
    ppermute x10, starting transfers between devices, hop(): return lax.ppermute(a, ('seq', 'dp'), pairs)  15.7 us
    all_to_all x1, blocking collectives, towers(): parts = lax.all_to_all(part, ('seq', 'dp', 'domain'), 0, 0, tiled=True)  11.7 us
    ppermute x4, starting transfers between devices, plane_hop(): return lax.ppermute(a, ('seq', 'dp'), [(i, i ^ move) for i in range(here)])  6.49 us
    ppermute x4, waiting for transfers between devices, plane_hop(): return lax.ppermute(a, ('seq', 'dp'), [(i, i ^ move) for i in range(here)])  2.15 us
    pallas_call x1, Pallas kernels, towers(): call(project_kernel, (shape((2 * tokens, wide), bf16), shape((MESSAGE, HE...  1.42 us
    pallas_call x1, Pallas kernels, towers(): call(loss_kernel, (shape((1, 1, width // 8), bf16), shape((1, 1), f32)),...  1.29 us
  transfers between devices with their start and end apart: 14, of which 8 were waited for; matrix products, arithmetic and copies ran while one was open for 0% of the time, Pallas kernels for 3%

profile of v7, /device:TPU:0, one launch (start us, length us, event | category | flops | bytes accessed | tf_op | source)
XLA Modules:
  0.0 63.4 jit_solution(1441942184000924532)
XLA Ops:
  0.6 1.1 %copy-done = bf16[1,128,3072]{2,1,0:T(8,128)(2,1)S(1)} copy-done((bf16[1,128,3072]{2,1,0:T(8,128)(2,1)S(1)}, bf16[1,128,3072]{2,1,0:T(8,128)(2,1)}, u32[]{:S(2)}) %copy-start) | copy-done | bytes 786456
  1.9 3.0 %collective-permute-start.3 = (bf16[128,768]{1,0:T(8,128)(2,1)S(1)}, bf16[128,768]{1,0:T(8,128)(2,1)S(1)}, u32[]{:S(2)}, u32[]{:S(2)}) collective-permute-start(bf16[128,768]{1,0:T(8,128)(2,1)S(1)} %get-tuple-element.12), channel_id=1, source_target_pairs={{0,4},{2,6},{4,0},{6,2},{8,12},{10,14},{12,8},{14,10},{16,20},{18,... | collective-permute-start | bytes 589832 | tf_op jit(solution)/shard_map/ppermute | solution.py:423
  4.9 2.6 %collective-permute-start.6 = (bf16[128,768]{1,0:T(8,128)(2,1)S(1)}, bf16[128,768]{1,0:T(8,128)(2,1)S(1)}, u32[]{:S(2)}, u32[]{:S(2)}) collective-permute-start(bf16[128,768]{1,0:T(8,128)(2,1)S(1)} %get-tuple-element.11), channel_id=1, source_target_pairs={{0,16},{2,18},{4,20},{6,22},{8,24},{10,26},{12,28},{14,30},{16,0},... | collective-permute-start | bytes 589832 | tf_op jit(solution)/shard_map/ppermute | solution.py:420
  7.5 1.5 %collective-permute-start.2 = (bf16[256,1024]{1,0:T(8,128)(2,1)}, bf16[256,1024]{1,0:T(8,128)(2,1)S(1)}, u32[]{:S(2)}, u32[]{:S(2)}) collective-permute-start(bf16[256,1024]{1,0:T(8,128)(2,1)} %bitcast.3), channel_id=1, source_target_pairs={{0,6},{2,4},{4,2},{6,0},{8,14},{10,12},{12,10},{14,8},{16,22},{18,... | collective-permute-start | bytes 1572872 | tf_op jit(solution)/shard_map/ppermute | solution.py:423
  9.0 1.6 %collective-permute-start.4 = (bf16[128,768]{1,0:T(8,128)(2,1)S(1)}, bf16[128,768]{1,0:T(8,128)(2,1)S(1)}, u32[]{:S(2)}, u32[]{:S(2)}) collective-permute-start(bf16[128,768]{1,0:T(8,128)(2,1)S(1)} %get-tuple-element.11), channel_id=1, source_target_pairs={{0,8},{2,10},{4,12},{6,14},{8,0},{10,2},{12,4},{14,6},{16,24},{18,... | collective-permute-start | bytes 589832 | tf_op jit(solution)/shard_map/ppermute | solution.py:420
  11.1 1.5 %collective-permute-start = (bf16[256,1024]{1,0:T(8,128)(2,1)}, bf16[256,1024]{1,0:T(8,128)(2,1)S(1)}, u32[]{:S(2)}, u32[]{:S(2)}) collective-permute-start(bf16[256,1024]{1,0:T(8,128)(2,1)} %bitcast.5), channel_id=1, source_target_pairs={{0,4},{2,6},{4,0},{6,2},{8,12},{10,14},{12,8},{14,10},{16,20},{18,... | collective-permute-start | bytes 1572872 | tf_op jit(solution)/shard_map/ppermute | solution.py:423
  12.6 3.9 %collective-permute-done.6.two_own = bf16[128,768]{1,0:T(8,128)(2,1)S(1)} collective-permute-done((bf16[128,768]{1,0:T(8,128)(2,1)S(1)}, bf16[128,768]{1,0:T(8,128)(2,1)S(1)}, u32[]{:S(2)}, u32[]{:S(2)}) %collective-permute-start.6) | collective-permute-done | bytes 196640 | tf_op jit(solution)/shard_map/ppermute | solution.py:420
  16.5 1.4 %collective-permute-done.4 = bf16[128,768]{1,0:T(8,128)(2,1)S(1)} collective-permute-done((bf16[128,768]{1,0:T(8,128)(2,1)S(1)}, bf16[128,768]{1,0:T(8,128)(2,1)S(1)}, u32[]{:S(2)}, u32[]{:S(2)}) %collective-permute-start.4) | collective-permute-done | bytes 196640 | tf_op jit(solution)/shard_map/ppermute | solution.py:420
  17.9 2.7 %collective-permute-start.5 = (bf16[128,768]{1,0:T(8,128)(2,1)S(1)}, bf16[128,768]{1,0:T(8,128)(2,1)S(1)}, u32[]{:S(2)}, u32[]{:S(2)}) collective-permute-start(bf16[128,768]{1,0:T(8,128)(2,1)S(1)} %collective-permute-done.3), channel_id=1, source_target_pairs={{0,8},{2,10},{4,12},{6,14},{8,0},{10,2},{12,4},{14,6},{16,24},{18,... | collective-permute-start | bytes 589832 | tf_op jit(solution)/shard_map/ppermute | solution.py:420
  20.6 6.7 %collective-permute-done.7.two_near = bf16[128,768]{1,0:T(8,128)(2,1)S(1)} collective-permute-done((bf16[128,768]{1,0:T(8,128)(2,1)S(1)}, bf16[128,768]{1,0:T(8,128)(2,1)S(1)}, u32[]{:S(2)}, u32[]{:S(2)}) %collective-permute-start.7) | collective-permute-done | bytes 196640 | tf_op jit(solution)/shard_map/ppermute | solution.py:420
  27.3 0.7 %collective-permute-start.8 = (bf16[256,768]{1,0:T(8,128)(2,1)S(1)}, bf16[256,768]{1,0:T(8,128)(2,1)S(1)}, u32[]{:S(2)}, u32[]{:S(2)}) collective-permute-start(bf16[256,768]{1,0:T(8,128)(2,1)S(1)} %constant_dynamic-update-slice_fusion.both), channel_id=1, source_target_pairs={{8,16},{10,18},{12,20},{14,22},{16,8},{18,10},{20,12},{22,14},{9,1... | collective-permute-start | bytes 1179656 | tf_op jit(solution)/shard_map/ppermute | solution.py:420
  28.0 1.3 %collective-permute-start.9 = (bf16[128,768]{1,0:T(8,128)(2,1)S(1)}, bf16[128,768]{1,0:T(8,128)(2,1)S(1)}, u32[]{:S(2)}, u32[]{:S(2)}) collective-permute-start(bf16[128,768]{1,0:T(8,128)(2,1)S(1)} %collective-permute-done.6.two_own), channel_id=1, source_target_pairs={{8,0},{10,2},{12,4},{14,6},{16,24},{18,26},{20,28},{22,30},{9,1},{... | collective-permute-start | bytes 589832 | tf_op jit(solution)/shard_map/ppermute | solution.py:420
  29.4 1.3 %collective-permute-start.10 = (bf16[128,768]{1,0:T(8,128)(2,1)S(1)}, bf16[128,768]{1,0:T(8,128)(2,1)S(1)}, u32[]{:S(2)}, u32[]{:S(2)}) collective-permute-start(bf16[128,768]{1,0:T(8,128)(2,1)S(1)} %collective-permute-done.7.two_near), channel_id=1, source_target_pairs={{8,0},{10,2},{12,4},{14,6},{16,24},{18,26},{20,28},{22,30},{9,1},{... | collective-permute-start | bytes 589832 | tf_op jit(solution)/shard_map/ppermute | solution.py:420
  31.3 2.1 %collective-permute-done.1.across = bf16[256,1024]{1,0:T(8,128)(2,1)S(1)} collective-permute-done((bf16[256,1024]{1,0:T(8,128)(2,1)}, bf16[256,1024]{1,0:T(8,128)(2,1)S(1)}, u32[]{:S(2)}, u32[]{:S(2)}) %collective-permute-start.1) | collective-permute-done | bytes 524320 | tf_op jit(solution)/shard_map/ppermute | solution.py:423
  33.5 0.7 %shard_map.77 = (bf16[512,1024]{1,0:T(8,128)(2,1)S(1)}, f32[1,256]{1,0:T(1,128)S(1)}, bf16[256,1024]{1,0:T(8,128)(2,1)S(1)}) custom-call(s32[1,1]{1,0:T(1,128)S(6)} %copy.9.lengths, bf16[256,1024]{1,0:T(8,128)(2,1)S(1)} %bitcast.6, bf16[256,1024]{1,0:T(8,128)(2,1)S(1)} %collective-permute-done.near, bf16[256,1024]{1,0:T(8,128)(2,1)S(1)} %collective-permute-done.1.across, ...), custom_call_target="tpu_custom_call" | custom-call | flops 1572864 | bytes 2097152 | tf_op jit(solution)/shard_map/pallas_call | solution.py:446
  34.2 1.7 %collective-permute-done.9.far_own = bf16[128,768]{1,0:T(8,128)(2,1)S(1)} collective-permute-done((bf16[128,768]{1,0:T(8,128)(2,1)S(1)}, bf16[128,768]{1,0:T(8,128)(2,1)S(1)}, u32[]{:S(2)}, u32[]{:S(2)}) %collective-permute-start.9) | collective-permute-done | bytes 196640 | tf_op jit(solution)/shard_map/ppermute | solution.py:420
  35.9 2.1 %collective-permute-done.10.far_near = bf16[128,768]{1,0:T(8,128)(2,1)S(1)} collective-permute-done((bf16[128,768]{1,0:T(8,128)(2,1)S(1)}, bf16[128,768]{1,0:T(8,128)(2,1)S(1)}, u32[]{:S(2)}, u32[]{:S(2)}) %collective-permute-start.10) | collective-permute-done | bytes 196640 | tf_op jit(solution)/shard_map/ppermute | solution.py:420
  38.0 1.4 %shard_map.79 = (bf16[512,768]{1,0:T(8,128)(2,1)S(1)}, bf16[272,128]{1,0:T(8,128)(2,1)S(1)}, bf16[1024,768]{1,0:T(8,128)(2,1)S(1)}) custom-call(bf16[512,1024]{1,0:T(8,128)(2,1)S(1)} %get-tuple-element.10.normed, bf16[256,768]{1,0:T(8,128)(2,1)S(1)} %constant_dynamic-update-slice_fusion.both, bf16[256,768]{1,0:T(8,128)(2,1)S(1)} %pad_maximum_fusion.one, ...), custom_call_target="tpu_custom_call" | custom-call | flops 805306368 | bytes 2097152 | tf_op jit(solution)/shard_map/pallas_call | solution.py:453
  39.5 4.8 %collective-permute-start.13 = (bf16[272,128]{1,0:T(8,128)(2,1)S(1)}, bf16[272,128]{1,0:T(8,128)(2,1)S(1)}, u32[]{:S(2)}, u32[]{:S(2)}) collective-permute-start(bf16[272,128]{1,0:T(8,128)(2,1)S(1)} %get-tuple-element.13), channel_id=1, source_target_pairs={{0,24},{2,26},{4,28},{6,30},{8,16},{10,18},{12,20},{14,22},{16,8},... | collective-permute-start | bytes 208904 | tf_op jit(solution)/shard_map/ppermute | solution.py:420
  45.0 1.2 %shard_map.80.short = f32[1,256]{1,0:T(1,128)S(1)} custom-call(bf16[256,1024]{1,0:T(8,128)(2,1)S(1)} %get-tuple-element.16.raw, bf16[1024,768]{1,0:T(8,128)(2,1)S(1)} %get-tuple-element.17.weights, f32[1,1024]{1,0:T(1,128)S(1)} %copy-done.2), custom_call_target="tpu_custom_call" | custom-call | flops 402653184 | bytes 2097152 | tf_op jit(solution)/shard_map/pallas_call | solution.py:460
  46.7 2.8 %collective-permute-done.12.state_2 = bf16[272,128]{1,0:T(8,128)(2,1)S(1)} collective-permute-done((bf16[272,128]{1,0:T(8,128)(2,1)S(1)}, bf16[272,128]{1,0:T(8,128)(2,1)S(1)}, u32[]{:S(2)}, u32[]{:S(2)}) %collective-permute-start.12) | collective-permute-done | bytes 69664 | tf_op jit(solution)/shard_map/ppermute | solution.py:420
  49.5 0.9 %shard_map.81 = f32[32,4,256]{2,1,0:T(4,128)S(1)} custom-call(s32[1,1]{1,0:T(1,128)S(6)} %copy.9.lengths, bf16[272,128]{1,0:T(8,128)(2,1)S(1)} %collective-permute-done.11.state_1, bf16[272,128]{1,0:T(8,128)(2,1)S(1)} %collective-permute-done.12.state_2, bf16[272,128]{1,0:T(8,128)(2,1)S(1)} %collective-permute-done.13.state_3, ...), custom_call_target="tpu_custom_call" | custom-call | flops 301989888 | bytes 2097152 | tf_op jit(solution)/shard_map/pallas_call | solution.py:463
  50.4 11.7 %all_to_all.5.parts = f32[32,4,256]{2,1,0:T(4,128)S(1)} all-to-all(f32[32,4,256]{2,1,0:T(4,128)S(1)} %shard_map.81), channel_id=1, replica_groups=mesh['seq'=8,'dp'=2,'domain'=2] {'seq','dp','domain'}, dimensions={0} | all-to-all | bytes 262144 | tf_op jit(solution)/shard_map/all_to_all | solution.py:470
  62.1 1.3 %shard_map.82 = (bf16[1,1,128]{2,1,0:T(2,128)(2,1)}, f32[1,1]{1,0:T(1,128)}) custom-call(s32[2]{0:T(128)S(1)} %copy-done.4, f32[32,4,256]{2,1,0:T(4,128)S(1)} %all_to_all.5.parts), custom_call_target="tpu_custom_call" | custom-call | flops 16384 | bytes 2097152 | tf_op jit(solution)/shard_map/pallas_call | solution.py:471
  (24 shorter events, 1.9 us)
Async XLA Ops:
  0.6 1.1 %copy-start = (bf16[1,128,3072]{2,1,0:T(8,128)(2,1)S(1)}, bf16[1,128,3072]{2,1,0:T(8,128)(2,1)}, u32[]{:S(2)}) copy-start(bf16[1,128,3072]{2,1,0:T(8,128)(2,1)} %param.7) | copy-start | bytes 2359300
  1.8 31.7 %copy-start.1 = (bf16[1,1,256,1024]{3,2,1,0:T(8,128)(2,1)S(1)}, bf16[1,1,256,1024]{3,2,1,0:T(8,128)(2,1)}, u32[]{:S(2)}) copy-start(bf16[1,1,256,1024]{3,2,1,0:T(8,128)(2,1)} %param.6) | copy-start | bytes 1572868
  1.8 31.7 %copy-start.2 = (f32[1,1024]{1,0:T(1,128)S(1)}, f32[1,1024]{1,0:T(1,128)}, u32[]{:S(2)}) copy-start(f32[1,1024]{1,0:T(1,128)} %gain.4) | copy-start | bytes 12292
  1.9 9.2 %collective-permute-start.3 = (bf16[128,768]{1,0:T(8,128)(2,1)S(1)}, bf16[128,768]{1,0:T(8,128)(2,1)S(1)}, u32[]{:S(2)}, u32[]{:S(2)}) collective-permute-start(bf16[128,768]{1,0:T(8,128)(2,1)S(1)} %get-tuple-element.12), channel_id=1, source_target_pairs={{0,4},{2,6},{4,0},{6,2},{8,12},{10,14},{12,8},{14,10},{16,20},{18,... | collective-permute-start | bytes 589832 | tf_op jit(solution)/shard_map/ppermute | solution.py:423
  4.9 11.6 %collective-permute-start.6 = (bf16[128,768]{1,0:T(8,128)(2,1)S(1)}, bf16[128,768]{1,0:T(8,128)(2,1)S(1)}, u32[]{:S(2)}, u32[]{:S(2)}) collective-permute-start(bf16[128,768]{1,0:T(8,128)(2,1)S(1)} %get-tuple-element.11), channel_id=1, source_target_pairs={{0,16},{2,18},{4,20},{6,22},{8,24},{10,26},{12,28},{14,30},{16,0},... | collective-permute-start | bytes 589832 | tf_op jit(solution)/shard_map/ppermute | solution.py:420
  7.5 21.9 %collective-permute-start.2 = (bf16[256,1024]{1,0:T(8,128)(2,1)}, bf16[256,1024]{1,0:T(8,128)(2,1)S(1)}, u32[]{:S(2)}, u32[]{:S(2)}) collective-permute-start(bf16[256,1024]{1,0:T(8,128)(2,1)} %bitcast.3), channel_id=1, source_target_pairs={{0,6},{2,4},{4,2},{6,0},{8,14},{10,12},{12,10},{14,8},{16,22},{18,... | collective-permute-start | bytes 1572872 | tf_op jit(solution)/shard_map/ppermute | solution.py:423
  9.0 8.9 %collective-permute-start.4 = (bf16[128,768]{1,0:T(8,128)(2,1)S(1)}, bf16[128,768]{1,0:T(8,128)(2,1)S(1)}, u32[]{:S(2)}, u32[]{:S(2)}) collective-permute-start(bf16[128,768]{1,0:T(8,128)(2,1)S(1)} %get-tuple-element.11), channel_id=1, source_target_pairs={{0,8},{2,10},{4,12},{6,14},{8,0},{10,2},{12,4},{14,6},{16,24},{18,... | collective-permute-start | bytes 589832 | tf_op jit(solution)/shard_map/ppermute | solution.py:420
  10.6 22.9 %collective-permute-start.1 = (bf16[256,1024]{1,0:T(8,128)(2,1)}, bf16[256,1024]{1,0:T(8,128)(2,1)S(1)}, u32[]{:S(2)}, u32[]{:S(2)}) collective-permute-start(bf16[256,1024]{1,0:T(8,128)(2,1)} %bitcast.4), channel_id=1, source_target_pairs={{0,2},{2,0},{4,6},{6,4},{8,10},{10,8},{12,14},{14,12},{16,18},{18,... | collective-permute-start | bytes 1572872 | tf_op jit(solution)/shard_map/ppermute | solution.py:423
  11.1 22.4 %collective-permute-start = (bf16[256,1024]{1,0:T(8,128)(2,1)}, bf16[256,1024]{1,0:T(8,128)(2,1)S(1)}, u32[]{:S(2)}, u32[]{:S(2)}) collective-permute-start(bf16[256,1024]{1,0:T(8,128)(2,1)} %bitcast.5), channel_id=1, source_target_pairs={{0,4},{2,6},{4,0},{6,2},{8,12},{10,14},{12,8},{14,10},{16,20},{18,... | collective-permute-start | bytes 1572872 | tf_op jit(solution)/shard_map/ppermute | solution.py:423
  16.5 10.9 %collective-permute-start.7 = (bf16[128,768]{1,0:T(8,128)(2,1)S(1)}, bf16[128,768]{1,0:T(8,128)(2,1)S(1)}, u32[]{:S(2)}, u32[]{:S(2)}) collective-permute-start(bf16[128,768]{1,0:T(8,128)(2,1)S(1)} %collective-permute-done.3), channel_id=1, source_target_pairs={{0,16},{2,18},{4,20},{6,22},{8,24},{10,26},{12,28},{14,30},{16,0},... | collective-permute-start | bytes 589832 | tf_op jit(solution)/shard_map/ppermute | solution.py:420
  17.9 10.1 %collective-permute-start.5 = (bf16[128,768]{1,0:T(8,128)(2,1)S(1)}, bf16[128,768]{1,0:T(8,128)(2,1)S(1)}, u32[]{:S(2)}, u32[]{:S(2)}) collective-permute-start(bf16[128,768]{1,0:T(8,128)(2,1)S(1)} %collective-permute-done.3), channel_id=1, source_target_pairs={{0,8},{2,10},{4,12},{6,14},{8,0},{10,2},{12,4},{14,6},{16,24},{18,... | collective-permute-start | bytes 589832 | tf_op jit(solution)/shard_map/ppermute | solution.py:420
  27.3 10.7 %collective-permute-start.8 = (bf16[256,768]{1,0:T(8,128)(2,1)S(1)}, bf16[256,768]{1,0:T(8,128)(2,1)S(1)}, u32[]{:S(2)}, u32[]{:S(2)}) collective-permute-start(bf16[256,768]{1,0:T(8,128)(2,1)S(1)} %constant_dynamic-update-slice_fusion.both), channel_id=1, source_target_pairs={{8,16},{10,18},{12,20},{14,22},{16,8},{18,10},{20,12},{22,14},{9,1... | collective-permute-start | bytes 1179656 | tf_op jit(solution)/shard_map/ppermute | solution.py:420
  28.0 7.9 %collective-permute-start.9 = (bf16[128,768]{1,0:T(8,128)(2,1)S(1)}, bf16[128,768]{1,0:T(8,128)(2,1)S(1)}, u32[]{:S(2)}, u32[]{:S(2)}) collective-permute-start(bf16[128,768]{1,0:T(8,128)(2,1)S(1)} %collective-permute-done.6.two_own), channel_id=1, source_target_pairs={{8,0},{10,2},{12,4},{14,6},{16,24},{18,26},{20,28},{22,30},{9,1},{... | collective-permute-start | bytes 589832 | tf_op jit(solution)/shard_map/ppermute | solution.py:420
  29.4 8.7 %collective-permute-start.10 = (bf16[128,768]{1,0:T(8,128)(2,1)S(1)}, bf16[128,768]{1,0:T(8,128)(2,1)S(1)}, u32[]{:S(2)}, u32[]{:S(2)}) collective-permute-start(bf16[128,768]{1,0:T(8,128)(2,1)S(1)} %collective-permute-done.7.two_near), channel_id=1, source_target_pairs={{8,0},{10,2},{12,4},{14,6},{16,24},{18,26},{20,28},{22,30},{9,1},{... | collective-permute-start | bytes 589832 | tf_op jit(solution)/shard_map/ppermute | solution.py:420
  39.5 10.1 %copy-start.3 = (f32[1,1024]{1,0:T(1,128)S(1)}, f32[1,1024]{1,0:T(1,128)}, u32[]{:S(2)}) copy-start(f32[1,1024]{1,0:T(1,128)} %gain.5) | copy-start | bytes 12292
  39.5 7.2 %collective-permute-start.13 = (bf16[272,128]{1,0:T(8,128)(2,1)S(1)}, bf16[272,128]{1,0:T(8,128)(2,1)S(1)}, u32[]{:S(2)}, u32[]{:S(2)}) collective-permute-start(bf16[272,128]{1,0:T(8,128)(2,1)S(1)} %get-tuple-element.13), channel_id=1, source_target_pairs={{0,24},{2,26},{4,28},{6,30},{8,16},{10,18},{12,20},{14,22},{16,8},... | collective-permute-start | bytes 208904 | tf_op jit(solution)/shard_map/ppermute | solution.py:420
  44.3 5.2 %collective-permute-start.12 = (bf16[272,128]{1,0:T(8,128)(2,1)S(1)}, bf16[272,128]{1,0:T(8,128)(2,1)S(1)}, u32[]{:S(2)}, u32[]{:S(2)}) collective-permute-start(bf16[272,128]{1,0:T(8,128)(2,1)S(1)} %get-tuple-element.13), channel_id=1, source_target_pairs={{0,16},{2,18},{4,20},{6,22},{8,24},{10,26},{12,28},{14,30},{16,0},... | collective-permute-start | bytes 208904 | tf_op jit(solution)/shard_map/ppermute | solution.py:420
  44.3 5.2 %collective-permute-start.11 = (bf16[272,128]{1,0:T(8,128)(2,1)S(1)}, bf16[272,128]{1,0:T(8,128)(2,1)S(1)}, u32[]{:S(2)}, u32[]{:S(2)}) collective-permute-start(bf16[272,128]{1,0:T(8,128)(2,1)S(1)} %get-tuple-element.13), channel_id=1, source_target_pairs={{0,8},{2,10},{4,12},{6,14},{8,0},{10,2},{12,4},{14,6},{16,24},{18,... | collective-permute-start | bytes 208904 | tf_op jit(solution)/shard_map/ppermute | solution.py:420
  45.0 17.1 %copy-start.4 = (s32[2]{0:T(128)S(1)}, s32[2]{0:T(128)}, u32[]{:S(2)}) copy-start(s32[2]{0:T(128)} %positives.1) | copy-start | bytes 28

commit v8 on v7

--- a/solution.py
+++ b/solution.py
@@ -181,9 +181,8 @@
         copy.wait()
 
 
-def gate_kernel(values, after, out):
-    del after
-    out[...] = values[...]
+def gate_kernel(values, *rest):
+    rest[-1][...] = values[...]
 
 
 def normalise(values, gain):
@@ -224,27 +223,30 @@
     pltpu.make_async_copy(own, short, sems.at[2]).wait()
 
 
-def project_kernel(normed, both, one, two_own, two_near, next_both, far_own, far_near, feats, message, weights):
+def project_kernel(normed, *refs):
+    own, near, one_own, one_near, next_own, next_near, then_own, then_near, far_own, far_near, last_own, last_near = refs[:12]
+    feats, message, weights = refs[12:]
     tokens = normed.shape[0]
-    rows = two_own.shape[0]
+    rows = own.shape[0]
     z, x, _ = places()
 
-    def put(plane, own, near):
-        for place, values in ((x, own), (1 - x, near)):
-            weights[pl.ds(pl.multiple_of((2 * plane + place) * rows, rows), rows), :] = values
-
-    put(z, both[:rows, :], both[rows:, :])
-    put(jnp.bitwise_xor(z, 1), one[:rows, :], one[rows:, :])
-    put(jnp.bitwise_xor(z, 2), two_own[...], two_near[...])
+    def put(plane, here, there):
+        for place, ref in ((x, here), (1 - x, there)):
+            weights[pl.ds(pl.multiple_of((2 * plane + place) * rows, rows), rows), :] = ref[...]
+
+    put(z, own, near)
+    put(jnp.bitwise_xor(z, 1), one_own, one_near)
     inner = jnp.logical_or(z == 1, z == 2)
 
     @pl.when(inner)
     def _():
-        put(3 - z, next_both[:rows, :], next_both[rows:, :])
+        put(3 - z, next_own, next_near)
+        put(jnp.bitwise_xor(z, 2), far_own, far_near)
 
     @pl.when(jnp.logical_not(inner))
     def _():
-        put(3 - z, far_own[...], far_near[...])
+        put(jnp.bitwise_xor(z, 2), then_own, then_near)
+        put(3 - z, last_own, last_near)
 
     half = tokens // 2
     total = jnp.zeros((1, GROUP), jnp.float32)
@@ -429,19 +431,27 @@
     w_own, w_sent = call(
         pack_kernel, (shape((rows, wide), bf16),) * 2, [hbm()], [pltpu.SemaphoreType.DMA((6,))], 0
     )(weight)
+
+    def between(p):
+        return 3 - p if p in (1, 2) else None
+
+    def outward(p):
+        return {1: 0, 2: 3}.get(p)
+
     near = plane_hop(events, 2)
     across = plane_hop(events, 1)
-    corner = plane_hop(events, 3)
     w_near = plane_hop(w_sent, 2)
-    two_own = hop(w_own, lambda p: p ^ 2)
-    two_near = hop(w_near, lambda p: p ^ 2)
-    both = jnp.concatenate([w_own, w_near], axis=0)
+    corner = plane_hop(call(gate_kernel, shape((tokens, width), bf16), [vmem()] + [anywhere()] * 1, [], 0)(events, w_near), 3)
+    next_own = hop(w_own, between)
+    then_own = hop(next_own, outward)
+    one_near = hop(call(gate_kernel, shape((rows, wide), bf16), [vmem()] + [anywhere()] * 1, [], 0)(w_near, then_own), lambda p: p ^ 1)
+    far_near = hop(one_near, between)
+    last_near = hop(call(gate_kernel, shape((rows, wide), bf16), [vmem()] + [anywhere()] * 1, [], 0)(far_near, corner), outward)
     one_own = hop(w_own, lambda p: p ^ 1)
-    one_near = hop(w_near, lambda p: p ^ 1)
-    one = jnp.concatenate([one_own, one_near], axis=0)
-    next_both = hop(both, lambda p: 3 - p if p in (1, 2) else None)
-    far_own = hop(two_own, lambda p: {1: 0, 2: 3}.get(p))
-    far_near = hop(two_near, lambda p: {1: 0, 2: 3}.get(p))
+    far_own = hop(one_own, between)
+    last_own = hop(far_own, outward)
+    next_near = hop(call(gate_kernel, shape((rows, wide), bf16), [vmem()] + [anywhere()] * 1, [], 0)(w_near, far_own), between)
+    then_near = hop(next_near, outward)
 
     normed, sums, raw_short = call(
         norm_kernel,
@@ -453,10 +463,10 @@
     feats, message, weights = call(
         project_kernel,
         (shape((2 * tokens, wide), bf16), shape((MESSAGE, HEAD_DIM), bf16), shape((width, wide), bf16)),
-        [vmem()] * 8,
+        [vmem()] * 13,
         [],
         2 * 2 * tokens * width * wide,
-    )(normed, both, one, two_own, two_near, next_both, far_own, far_near)
+    )(normed, w_own, w_near, one_own, one_near, next_own, next_near, then_own, then_near, far_own, far_near, last_own, last_near)
     short = call(
         short_kernel, shape((1, GROUP), f32), [vmem()] * 3, [], 2 * tokens * width * wide
     )(raw_short, weights, norm_gain)

time: 63.6 us -> 68 us (1.069)
  starting transfers between devices: 22.2 us -> 25.9 us
  blocking collectives: 11.7 us -> 9.93 us
  waiting for transfers between devices: 21.4 us -> 22.5 us
  local copies, waits for them, and re-layouts: 1.17 us -> 2.24 us
    ppermute x4, waiting for transfers between devices: 2.15 us -> 6.64 us  [plane_hop(): return lax.ppermute(a, ('seq', 'dp'), [(i, i ^ move) for i in range(here)])]
    ppermute x10 -> x13, starting transfers between devices: 15.7 us -> 19.8 us  [hop(): return lax.ppermute(a, ('seq', 'dp'), pairs)]
    ppermute x10 -> x13, waiting for transfers between devices: 19.2 us -> 15.9 us  [hop(): return lax.ppermute(a, ('seq', 'dp'), pairs)]
    all_to_all x1, blocking collectives: 11.7 us -> 9.93 us  [towers(): parts = lax.all_to_all(part, ('seq', 'dp', 'domain'), 0, 0, tiled=True)]
    unnamed x11 -> x12, local copies, waits for them, and re-layouts: 1.16 us -> 2.24 us
  transfers between devices with their start and end apart: 14 -> 17, of which waited for: 8 -> 10; matrix products, arithmetic and copies ran while one was open for 0% -> 0% of each run, Pallas kernels for 3% -> 3%
where the time goes in v8:
time: 68 us; the launch traced here: 67.7 us
  starting transfers between devices  25.9 us (38%)
  waiting for transfers between devices  22.5 us (33%)
  blocking collectives  9.93 us (15%)
  Pallas kernels  5.65 us (8%)
  local copies, waits for them, and re-layouts  2.24 us (3%)
  between operations  1.46 us (2%)
    ppermute x13, starting transfers between devices, hop(): return lax.ppermute(a, ('seq', 'dp'), pairs)  19.8 us
    ppermute x13, waiting for transfers between devices, hop(): return lax.ppermute(a, ('seq', 'dp'), pairs)  15.9 us
    all_to_all x1, blocking collectives, towers(): parts = lax.all_to_all(part, ('seq', 'dp', 'domain'), 0, 0, tiled=True)  9.93 us
    ppermute x4, waiting for transfers between devices, plane_hop(): return lax.ppermute(a, ('seq', 'dp'), [(i, i ^ move) for i in range(here)])  6.64 us
    ppermute x4, starting transfers between devices, plane_hop(): return lax.ppermute(a, ('seq', 'dp'), [(i, i ^ move) for i in range(here)])  6.01 us
    unnamed x12, local copies, waits for them, and re-layouts  2.24 us
    pallas_call x1, Pallas kernels, towers(): call(project_kernel, (shape((2 * tokens, wide), bf16), shape((MESSAGE, HE...  1.41 us
  transfers between devices with their start and end apart: 17, of which 10 were waited for; matrix products, arithmetic and copies ran while one was open for 0% of the time, Pallas kernels for 3%

profile of v8, /device:TPU:0, one launch (start us, length us, event | category | flops | bytes accessed | tf_op | source)
XLA Modules:
  0.0 67.7 jit_solution(1568868738385634368)
XLA Ops:
  0.7 1.2 %copy-done.2 = bf16[1,128,3072]{2,1,0:T(8,128)(2,1)S(1)} copy-done((bf16[1,128,3072]{2,1,0:T(8,128)(2,1)S(1)}, bf16[1,128,3072]{2,1,0:T(8,128)(2,1)}, u32[]{:S(2)}) %copy-start.2) | copy-done | bytes 786456
  2.6 3.0 %collective-permute-start.2 = (bf16[128,768]{1,0:T(8,128)(2,1)S(1)}, bf16[128,768]{1,0:T(8,128)(2,1)S(1)}, u32[]{:S(2)}, u32[]{:S(2)}) collective-permute-start(bf16[128,768]{1,0:T(8,128)(2,1)S(1)} %get-tuple-element.10), channel_id=1, source_target_pairs={{0,4},{2,6},{4,0},{6,2},{8,12},{10,14},{12,8},{14,10},{16,20},{18,... | collective-permute-start | bytes 589832 | tf_op jit(solution)/shard_map/ppermute | solution.py:425
  5.6 4.4 %collective-permute-start.4 = (bf16[128,768]{1,0:T(8,128)(2,1)S(1)}, bf16[128,768]{1,0:T(8,128)(2,1)S(1)}, u32[]{:S(2)}, u32[]{:S(2)}) collective-permute-start(bf16[128,768]{1,0:T(8,128)(2,1)S(1)} %get-tuple-element.12.refs_0_), channel_id=1, source_target_pairs={{0,8},{2,10},{4,12},{6,14},{8,0},{10,2},{12,4},{14,6},{16,24},{18,... | collective-permute-start | bytes 589832 | tf_op jit(solution)/shard_map/ppermute | solution.py:422
  10.0 1.3 %collective-permute-start.6 = (bf16[128,768]{1,0:T(8,128)(2,1)S(1)}, bf16[128,768]{1,0:T(8,128)(2,1)S(1)}, u32[]{:S(2)}, u32[]{:S(2)}) collective-permute-start(bf16[128,768]{1,0:T(8,128)(2,1)S(1)} %collective-permute-done.5.refs_4_), channel_id=1, source_target_pairs={{8,0},{10,2},{12,4},{14,6},{16,24},{18,26},{20,28},{22,30},{9,1},{... | collective-permute-start | bytes 589832 | tf_op jit(solution)/shard_map/ppermute | solution.py:422
  11.4 1.0 %copy-done = bf16[1,1,256,1024]{3,2,1,0:T(8,128)(2,1)S(1)} copy-done((bf16[1,1,256,1024]{3,2,1,0:T(8,128)(2,1)S(1)}, bf16[1,1,256,1024]{3,2,1,0:T(8,128)(2,1)}, u32[]{:S(2)}) %copy-start) | copy-done | bytes 524312
  12.4 2.0 %collective-permute-start.3 = (bf16[256,1024]{1,0:T(8,128)(2,1)S(1)}, bf16[256,1024]{1,0:T(8,128)(2,1)S(1)}, u32[]{:S(2)}, u32[]{:S(2)}) collective-permute-start(bf16[256,1024]{1,0:T(8,128)(2,1)S(1)} %shard_map.78), channel_id=1, source_target_pairs={{0,6},{2,4},{4,2},{6,0},{8,14},{10,12},{12,10},{14,8},{16,22},{18,... | collective-permute-start | bytes 1572872 | tf_op jit(solution)/shard_map/ppermute | solution.py:425
  15.1 3.7 %collective-permute-done.6.rest_0_.refs_6_ = bf16[128,768]{1,0:T(8,128)(2,1)S(1)} collective-permute-done((bf16[128,768]{1,0:T(8,128)(2,1)S(1)}, bf16[128,768]{1,0:T(8,128)(2,1)S(1)}, u32[]{:S(2)}, u32[]{:S(2)}) %collective-permute-start.6) | collective-permute-done | bytes 196640 | tf_op jit(solution)/shard_map/ppermute | solution.py:422
  18.8 3.2 %collective-permute-start.7 = (bf16[128,768]{1,0:T(8,128)(2,1)S(1)}, bf16[128,768]{1,0:T(8,128)(2,1)S(1)}, u32[]{:S(2)}, u32[]{:S(2)}) collective-permute-start(bf16[128,768]{1,0:T(8,128)(2,1)S(1)} %shard_map.80), channel_id=1, source_target_pairs={{0,8},{2,10},{4,12},{6,14},{8,0},{10,2},{12,4},{14,6},{16,24},{18,... | collective-permute-start | bytes 589832 | tf_op jit(solution)/shard_map/ppermute | solution.py:422
  23.8 1.9 %collective-permute-done.7.refs_3_ = bf16[128,768]{1,0:T(8,128)(2,1)S(1)} collective-permute-done((bf16[128,768]{1,0:T(8,128)(2,1)S(1)}, bf16[128,768]{1,0:T(8,128)(2,1)S(1)}, u32[]{:S(2)}, u32[]{:S(2)}) %collective-permute-start.7) | collective-permute-done | bytes 196640 | tf_op jit(solution)/shard_map/ppermute | solution.py:422
  26.3 1.3 %collective-permute-start.12 = (bf16[128,768]{1,0:T(8,128)(2,1)S(1)}, bf16[128,768]{1,0:T(8,128)(2,1)S(1)}, u32[]{:S(2)}, u32[]{:S(2)}) collective-permute-start(bf16[128,768]{1,0:T(8,128)(2,1)S(1)} %collective-permute-done.8.rest_0_.refs_8_), channel_id=1, source_target_pairs={{8,0},{10,2},{12,4},{14,6},{16,24},{18,26},{20,28},{22,30},{9,1},{... | collective-permute-start | bytes 589832 | tf_op jit(solution)/shard_map/ppermute | solution.py:422
  28.3 1.3 %collective-permute-start.10 = (bf16[128,768]{1,0:T(8,128)(2,1)S(1)}, bf16[128,768]{1,0:T(8,128)(2,1)S(1)}, u32[]{:S(2)}, u32[]{:S(2)}) collective-permute-start(bf16[128,768]{1,0:T(8,128)(2,1)S(1)} %collective-permute-done.9.refs_5_), channel_id=1, source_target_pairs={{8,0},{10,2},{12,4},{14,6},{16,24},{18,26},{20,28},{22,30},{9,1},{... | collective-permute-start | bytes 589832 | tf_op jit(solution)/shard_map/ppermute | solution.py:422
  29.6 1.3 %collective-permute-start.13 = (bf16[128,768]{1,0:T(8,128)(2,1)S(1)}, bf16[128,768]{1,0:T(8,128)(2,1)S(1)}, u32[]{:S(2)}, u32[]{:S(2)}) collective-permute-start(bf16[128,768]{1,0:T(8,128)(2,1)S(1)} %shard_map.82), channel_id=1, source_target_pairs={{8,0},{10,2},{12,4},{14,6},{16,24},{18,26},{20,28},{22,30},{9,1},{... | collective-permute-start | bytes 589832 | tf_op jit(solution)/shard_map/ppermute | solution.py:422
  31.5 5.9 %collective-permute-done.1.across = bf16[256,1024]{1,0:T(8,128)(2,1)S(1)} collective-permute-done((bf16[256,1024]{1,0:T(8,128)(2,1)S(1)}, bf16[256,1024]{1,0:T(8,128)(2,1)S(1)}, u32[]{:S(2)}, u32[]{:S(2)}) %collective-permute-start.1) | collective-permute-done | bytes 524320 | tf_op jit(solution)/shard_map/ppermute | solution.py:425
  38.2 4.0 %collective-permute-done.12.refs_10_ = bf16[128,768]{1,0:T(8,128)(2,1)S(1)} collective-permute-done((bf16[128,768]{1,0:T(8,128)(2,1)S(1)}, bf16[128,768]{1,0:T(8,128)(2,1)S(1)}, u32[]{:S(2)}, u32[]{:S(2)}) %collective-permute-start.12) | collective-permute-done | bytes 196640 | tf_op jit(solution)/shard_map/ppermute | solution.py:422
  42.2 2.1 %collective-permute-done.10.refs_7_ = bf16[128,768]{1,0:T(8,128)(2,1)S(1)} collective-permute-done((bf16[128,768]{1,0:T(8,128)(2,1)S(1)}, bf16[128,768]{1,0:T(8,128)(2,1)S(1)}, u32[]{:S(2)}, u32[]{:S(2)}) %collective-permute-start.10) | collective-permute-done | bytes 196640 | tf_op jit(solution)/shard_map/ppermute | solution.py:422
  44.3 2.1 %collective-permute-done.13.refs_11_ = bf16[128,768]{1,0:T(8,128)(2,1)S(1)} collective-permute-done((bf16[128,768]{1,0:T(8,128)(2,1)S(1)}, bf16[128,768]{1,0:T(8,128)(2,1)S(1)}, u32[]{:S(2)}, u32[]{:S(2)}) %collective-permute-start.13) | collective-permute-done | bytes 196640 | tf_op jit(solution)/shard_map/ppermute | solution.py:422
  46.4 1.4 %shard_map.83 = (bf16[512,768]{1,0:T(8,128)(2,1)S(1)}, bf16[272,128]{1,0:T(8,128)(2,1)S(1)}, bf16[1024,768]{1,0:T(8,128)(2,1)S(1)}) custom-call(bf16[512,1024]{1,0:T(8,128)(2,1)S(1)} %get-tuple-element.11.normed, bf16[128,768]{1,0:T(8,128)(2,1)S(1)} %get-tuple-element.12.refs_0_, bf16[128,768]{1,0:T(8,128)(2,1)S(1)} %collective-permute-done.2.rest_0_.values.refs_1_, ...), custom_call_target="tpu_custom_call" | custom-call | flops 805306368 | bytes 2097152 | tf_op jit(solution)/shard_map/pallas_call | solution.py:463
  47.9 1.4 %collective-permute-start.16 = (bf16[272,128]{1,0:T(8,128)(2,1)S(1)}, bf16[272,128]{1,0:T(8,128)(2,1)S(1)}, u32[]{:S(2)}, u32[]{:S(2)}) collective-permute-start(bf16[272,128]{1,0:T(8,128)(2,1)S(1)} %get-tuple-element.13), channel_id=1, source_target_pairs={{0,24},{2,26},{4,28},{6,30},{8,16},{10,18},{12,20},{14,22},{16,8},... | collective-permute-start | bytes 208904 | tf_op jit(solution)/shard_map/ppermute | solution.py:422
  49.3 3.1 %collective-permute-start.14 = (bf16[272,128]{1,0:T(8,128)(2,1)S(1)}, bf16[272,128]{1,0:T(8,128)(2,1)S(1)}, u32[]{:S(2)}, u32[]{:S(2)}) collective-permute-start(bf16[272,128]{1,0:T(8,128)(2,1)S(1)} %get-tuple-element.13), channel_id=1, source_target_pairs={{0,8},{2,10},{4,12},{6,14},{8,0},{10,2},{12,4},{14,6},{16,24},{18,... | collective-permute-start | bytes 208904 | tf_op jit(solution)/shard_map/ppermute | solution.py:422
  52.3 1.2 %shard_map.84.short = f32[1,256]{1,0:T(1,128)S(1)} custom-call(bf16[256,1024]{1,0:T(8,128)(2,1)S(1)} %get-tuple-element.16.raw, bf16[1024,768]{1,0:T(8,128)(2,1)S(1)} %get-tuple-element.17.weights, f32[1,1024]{1,0:T(1,128)S(1)} %copy-done.3), custom_call_target="tpu_custom_call" | custom-call | flops 402653184 | bytes 2097152 | tf_op jit(solution)/shard_map/pallas_call | solution.py:470
  54.1 1.4 %collective-permute-done.15.state_2 = bf16[272,128]{1,0:T(8,128)(2,1)S(1)} collective-permute-done((bf16[272,128]{1,0:T(8,128)(2,1)S(1)}, bf16[272,128]{1,0:T(8,128)(2,1)S(1)}, u32[]{:S(2)}, u32[]{:S(2)}) %collective-permute-start.15) | collective-permute-done | bytes 69664 | tf_op jit(solution)/shard_map/ppermute | solution.py:422
  55.5 0.9 %shard_map.85 = f32[32,4,256]{2,1,0:T(4,128)S(1)} custom-call(s32[1,1]{1,0:T(1,128)S(6)} %copy.8.lengths, bf16[272,128]{1,0:T(8,128)(2,1)S(1)} %collective-permute-done.14.state_1, bf16[272,128]{1,0:T(8,128)(2,1)S(1)} %collective-permute-done.15.state_2, bf16[272,128]{1,0:T(8,128)(2,1)S(1)} %collective-permute-done.16.state_3, ...), custom_call_target="tpu_custom_call" | custom-call | flops 301989888 | bytes 2097152 | tf_op jit(solution)/shard_map/pallas_call | solution.py:473
  56.4 9.9 %all_to_all.5.parts = f32[32,4,256]{2,1,0:T(4,128)S(1)} all-to-all(f32[32,4,256]{2,1,0:T(4,128)S(1)} %shard_map.85), channel_id=1, replica_groups=mesh['seq'=8,'dp'=2,'domain'=2] {'seq','dp','domain'}, dimensions={0} | all-to-all | bytes 262144 | tf_op jit(solution)/shard_map/all_to_all | solution.py:480
  66.4 1.3 %shard_map.86 = (bf16[1,1,128]{2,1,0:T(2,128)(2,1)}, f32[1,1]{1,0:T(1,128)}) custom-call(s32[2]{0:T(128)S(1)} %copy-done.5, f32[32,4,256]{2,1,0:T(4,128)S(1)} %all_to_all.5.parts), custom_call_target="tpu_custom_call" | custom-call | flops 16384 | bytes 2097152 | tf_op jit(solution)/shard_map/pallas_call | solution.py:481
  (33 shorter events, 5.9 us)
Async XLA Ops:
  0.6 21.4 %copy-start.1 = (bf16[1,1,256,1024]{3,2,1,0:T(8,128)(2,1)S(1)}, bf16[1,1,256,1024]{3,2,1,0:T(8,128)(2,1)}, u32[]{:S(2)}) copy-start(bf16[1,1,256,1024]{3,2,1,0:T(8,128)(2,1)} %param.6) | copy-start | bytes 1572868
  0.6 1.2 %copy-start.2 = (bf16[1,128,3072]{2,1,0:T(8,128)(2,1)S(1)}, bf16[1,128,3072]{2,1,0:T(8,128)(2,1)}, u32[]{:S(2)}) copy-start(bf16[1,128,3072]{2,1,0:T(8,128)(2,1)} %param.7) | copy-start | bytes 2359300
  2.0 8.1 %collective-permute-start.5 = (bf16[128,768]{1,0:T(8,128)(2,1)S(1)}, bf16[128,768]{1,0:T(8,128)(2,1)S(1)}, u32[]{:S(2)}, u32[]{:S(2)}) collective-permute-start(bf16[128,768]{1,0:T(8,128)(2,1)S(1)} %get-tuple-element.12.refs_0_), channel_id=1, source_target_pairs={{8,16},{10,18},{12,20},{14,22},{16,8},{18,10},{20,12},{22,14},{9,1... | collective-permute-start | bytes 589832 | tf_op jit(solution)/shard_map/ppermute | solution.py:422
  2.6 8.7 %collective-permute-start.2 = (bf16[128,768]{1,0:T(8,128)(2,1)S(1)}, bf16[128,768]{1,0:T(8,128)(2,1)S(1)}, u32[]{:S(2)}, u32[]{:S(2)}) collective-permute-start(bf16[128,768]{1,0:T(8,128)(2,1)S(1)} %get-tuple-element.10), channel_id=1, source_target_pairs={{0,4},{2,6},{4,0},{6,2},{8,12},{10,14},{12,8},{14,10},{16,20},{18,... | collective-permute-start | bytes 589832 | tf_op jit(solution)/shard_map/ppermute | solution.py:425
  5.6 8.7 %collective-permute-start.4 = (bf16[128,768]{1,0:T(8,128)(2,1)S(1)}, bf16[128,768]{1,0:T(8,128)(2,1)S(1)}, u32[]{:S(2)}, u32[]{:S(2)}) collective-permute-start(bf16[128,768]{1,0:T(8,128)(2,1)S(1)} %get-tuple-element.12.refs_0_), channel_id=1, source_target_pairs={{0,8},{2,10},{4,12},{6,14},{8,0},{10,2},{12,4},{14,6},{16,24},{18,... | collective-permute-start | bytes 589832 | tf_op jit(solution)/shard_map/ppermute | solution.py:422
  10.0 8.8 %collective-permute-start.6 = (bf16[128,768]{1,0:T(8,128)(2,1)S(1)}, bf16[128,768]{1,0:T(8,128)(2,1)S(1)}, u32[]{:S(2)}, u32[]{:S(2)}) collective-permute-start(bf16[128,768]{1,0:T(8,128)(2,1)S(1)} %collective-permute-done.5.refs_4_), channel_id=1, source_target_pairs={{8,0},{10,2},{12,4},{14,6},{16,24},{18,26},{20,28},{22,30},{9,1},{... | collective-permute-start | bytes 589832 | tf_op jit(solution)/shard_map/ppermute | solution.py:422
  11.3 1.0 %copy-start = (bf16[1,1,256,1024]{3,2,1,0:T(8,128)(2,1)S(1)}, bf16[1,1,256,1024]{3,2,1,0:T(8,128)(2,1)}, u32[]{:S(2)}) copy-start(bf16[1,1,256,1024]{3,2,1,0:T(8,128)(2,1)} %param.6) | copy-start | bytes 1572868
  12.4 25.2 %copy-start.3 = (f32[1,1024]{1,0:T(1,128)S(1)}, f32[1,1024]{1,0:T(1,128)}, u32[]{:S(2)}) copy-start(f32[1,1024]{1,0:T(1,128)} %gain.4) | copy-start | bytes 12292
  12.4 15.8 %collective-permute-start.3 = (bf16[256,1024]{1,0:T(8,128)(2,1)S(1)}, bf16[256,1024]{1,0:T(8,128)(2,1)S(1)}, u32[]{:S(2)}, u32[]{:S(2)}) collective-permute-start(bf16[256,1024]{1,0:T(8,128)(2,1)S(1)} %shard_map.78), channel_id=1, source_target_pairs={{0,6},{2,4},{4,2},{6,0},{8,14},{10,12},{12,10},{14,8},{16,22},{18,... | collective-permute-start | bytes 1572872 | tf_op jit(solution)/shard_map/ppermute | solution.py:425
  14.4 8.7 %collective-permute-start.8 = (bf16[128,768]{1,0:T(8,128)(2,1)S(1)}, bf16[128,768]{1,0:T(8,128)(2,1)S(1)}, u32[]{:S(2)}, u32[]{:S(2)}) collective-permute-start(bf16[128,768]{1,0:T(8,128)(2,1)S(1)} %collective-permute-done.4.refs_2_), channel_id=1, source_target_pairs={{8,16},{10,18},{12,20},{14,22},{16,8},{18,10},{20,12},{22,14},{9,1... | collective-permute-start | bytes 589832 | tf_op jit(solution)/shard_map/ppermute | solution.py:422
  18.8 6.8 %collective-permute-start.7 = (bf16[128,768]{1,0:T(8,128)(2,1)S(1)}, bf16[128,768]{1,0:T(8,128)(2,1)S(1)}, u32[]{:S(2)}, u32[]{:S(2)}) collective-permute-start(bf16[128,768]{1,0:T(8,128)(2,1)S(1)} %shard_map.80), channel_id=1, source_target_pairs={{0,8},{2,10},{4,12},{6,14},{8,0},{10,2},{12,4},{14,6},{16,24},{18,... | collective-permute-start | bytes 589832 | tf_op jit(solution)/shard_map/ppermute | solution.py:422
  22.0 15.4 %collective-permute-start.1 = (bf16[256,1024]{1,0:T(8,128)(2,1)S(1)}, bf16[256,1024]{1,0:T(8,128)(2,1)S(1)}, u32[]{:S(2)}, u32[]{:S(2)}) collective-permute-start(bf16[256,1024]{1,0:T(8,128)(2,1)S(1)} %bitcast.3), channel_id=1, source_target_pairs={{0,2},{2,0},{4,6},{6,4},{8,10},{10,8},{12,14},{14,12},{16,18},{18,... | collective-permute-start | bytes 1572872 | tf_op jit(solution)/shard_map/ppermute | solution.py:425
  22.5 15.0 %collective-permute-start = (bf16[256,1024]{1,0:T(8,128)(2,1)S(1)}, bf16[256,1024]{1,0:T(8,128)(2,1)S(1)}, u32[]{:S(2)}, u32[]{:S(2)}) collective-permute-start(bf16[256,1024]{1,0:T(8,128)(2,1)S(1)} %bitcast.4), channel_id=1, source_target_pairs={{0,4},{2,6},{4,0},{6,2},{8,12},{10,14},{12,8},{14,10},{16,20},{18,... | collective-permute-start | bytes 1572872 | tf_op jit(solution)/shard_map/ppermute | solution.py:425
  23.1 3.3 %collective-permute-start.9 = (bf16[128,768]{1,0:T(8,128)(2,1)S(1)}, bf16[128,768]{1,0:T(8,128)(2,1)S(1)}, u32[]{:S(2)}, u32[]{:S(2)}) collective-permute-start(bf16[128,768]{1,0:T(8,128)(2,1)S(1)} %shard_map.81), channel_id=1, source_target_pairs={{8,16},{10,18},{12,20},{14,22},{16,8},{18,10},{20,12},{22,14},{9,1... | collective-permute-start | bytes 589832 | tf_op jit(solution)/shard_map/ppermute | solution.py:422
  25.7 3.9 %collective-permute-start.11 = (bf16[128,768]{1,0:T(8,128)(2,1)S(1)}, bf16[128,768]{1,0:T(8,128)(2,1)S(1)}, u32[]{:S(2)}, u32[]{:S(2)}) collective-permute-start(bf16[128,768]{1,0:T(8,128)(2,1)S(1)} %collective-permute-done.7.refs_3_), channel_id=1, source_target_pairs={{8,16},{10,18},{12,20},{14,22},{16,8},{18,10},{20,12},{22,14},{9,1... | collective-permute-start | bytes 589832 | tf_op jit(solution)/shard_map/ppermute | solution.py:422
  26.3 15.9 %collective-permute-start.12 = (bf16[128,768]{1,0:T(8,128)(2,1)S(1)}, bf16[128,768]{1,0:T(8,128)(2,1)S(1)}, u32[]{:S(2)}, u32[]{:S(2)}) collective-permute-start(bf16[128,768]{1,0:T(8,128)(2,1)S(1)} %collective-permute-done.8.rest_0_.refs_8_), channel_id=1, source_target_pairs={{8,0},{10,2},{12,4},{14,6},{16,24},{18,26},{20,28},{22,30},{9,1},{... | collective-permute-start | bytes 589832 | tf_op jit(solution)/shard_map/ppermute | solution.py:422
  28.3 16.1 %collective-permute-start.10 = (bf16[128,768]{1,0:T(8,128)(2,1)S(1)}, bf16[128,768]{1,0:T(8,128)(2,1)S(1)}, u32[]{:S(2)}, u32[]{:S(2)}) collective-permute-start(bf16[128,768]{1,0:T(8,128)(2,1)S(1)} %collective-permute-done.9.refs_5_), channel_id=1, source_target_pairs={{8,0},{10,2},{12,4},{14,6},{16,24},{18,26},{20,28},{22,30},{9,1},{... | collective-permute-start | bytes 589832 | tf_op jit(solution)/shard_map/ppermute | solution.py:422
  29.6 16.9 %collective-permute-start.13 = (bf16[128,768]{1,0:T(8,128)(2,1)S(1)}, bf16[128,768]{1,0:T(8,128)(2,1)S(1)}, u32[]{:S(2)}, u32[]{:S(2)}) collective-permute-start(bf16[128,768]{1,0:T(8,128)(2,1)S(1)} %shard_map.82), channel_id=1, source_target_pairs={{8,0},{10,2},{12,4},{14,6},{16,24},{18,26},{20,28},{22,30},{9,1},{... | collective-permute-start | bytes 589832 | tf_op jit(solution)/shard_map/ppermute | solution.py:422
  47.9 7.7 %copy-start.4 = (f32[1,1024]{1,0:T(1,128)S(1)}, f32[1,1024]{1,0:T(1,128)}, u32[]{:S(2)}) copy-start(f32[1,1024]{1,0:T(1,128)} %gain.5) | copy-start | bytes 12292
  47.9 6.2 %collective-permute-start.16 = (bf16[272,128]{1,0:T(8,128)(2,1)S(1)}, bf16[272,128]{1,0:T(8,128)(2,1)S(1)}, u32[]{:S(2)}, u32[]{:S(2)}) collective-permute-start(bf16[272,128]{1,0:T(8,128)(2,1)S(1)} %get-tuple-element.13), channel_id=1, source_target_pairs={{0,24},{2,26},{4,28},{6,30},{8,16},{10,18},{12,20},{14,22},{16,8},... | collective-permute-start | bytes 208904 | tf_op jit(solution)/shard_map/ppermute | solution.py:422
  49.3 6.3 %collective-permute-start.15 = (bf16[272,128]{1,0:T(8,128)(2,1)S(1)}, bf16[272,128]{1,0:T(8,128)(2,1)S(1)}, u32[]{:S(2)}, u32[]{:S(2)}) collective-permute-start(bf16[272,128]{1,0:T(8,128)(2,1)S(1)} %get-tuple-element.13), channel_id=1, source_target_pairs={{0,16},{2,18},{4,20},{6,22},{8,24},{10,26},{12,28},{14,30},{16,0},... | collective-permute-start | bytes 208904 | tf_op jit(solution)/shard_map/ppermute | solution.py:422
  49.3 6.3 %collective-permute-start.14 = (bf16[272,128]{1,0:T(8,128)(2,1)S(1)}, bf16[272,128]{1,0:T(8,128)(2,1)S(1)}, u32[]{:S(2)}, u32[]{:S(2)}) collective-permute-start(bf16[272,128]{1,0:T(8,128)(2,1)S(1)} %get-tuple-element.13), channel_id=1, source_target_pairs={{0,8},{2,10},{4,12},{6,14},{8,0},{10,2},{12,4},{14,6},{16,24},{18,... | collective-permute-start | bytes 208904 | tf_op jit(solution)/shard_map/ppermute | solution.py:422
  52.3 14.0 %copy-start.5 = (s32[2]{0:T(128)S(1)}, s32[2]{0:T(128)}, u32[]{:S(2)}) copy-start(s32[2]{0:T(128)} %positives.1) | copy-start | bytes 28

commit v9 on v8

--- a/solution.py
+++ b/solution.py
@@ -433,10 +433,10 @@
     )(weight)
 
     def between(p):
-        return 3 - p if p in (1, 2) else None
+        return 3 - p if p in (1, 2) else p
 
     def outward(p):
-        return {1: 0, 2: 3}.get(p)
+        return p ^ 1
 
     near = plane_hop(events, 2)
     across = plane_hop(events, 1)

time: 68 us -> 66.7 us (0.981)
  waiting for transfers between devices: 22.5 us -> 10.7 us
  starting transfers between devices: 25.9 us -> 35.7 us
  blocking collectives: 9.93 us -> 10.7 us
    ppermute x13, starting transfers between devices: 19.8 us -> 28.7 us  [hop(): return lax.ppermute(a, ('seq', 'dp'), pairs)]
    ppermute x13, waiting for transfers between devices: 15.9 us -> 8.59 us  [hop(): return lax.ppermute(a, ('seq', 'dp'), pairs)]
    ppermute x4, waiting for transfers between devices: 6.64 us -> 2.13 us  [plane_hop(): return lax.ppermute(a, ('seq', 'dp'), [(i, i ^ move) for i in range(here)])]
    ppermute x4, starting transfers between devices: 6.01 us -> 7.03 us  [plane_hop(): return lax.ppermute(a, ('seq', 'dp'), [(i, i ^ move) for i in range(here)])]
    all_to_all x1, blocking collectives: 9.93 us -> 10.7 us  [towers(): parts = lax.all_to_all(part, ('seq', 'dp', 'domain'), 0, 0, tiled=True)]
  transfers between devices with their start and end apart: 17 -> 17, of which waited for: 10 -> 8; matrix products, arithmetic and copies ran while one was open for 0% -> 0% of each run, Pallas kernels for 3% -> 3%
where the time goes in v9:
time: 66.7 us; the launch traced here: 66.4 us
  starting transfers between devices  35.7 us (54%)
  waiting for transfers between devices  10.7 us (16%)
  blocking collectives  10.7 us (16%)
  Pallas kernels  5.65 us (8%)
  local copies, waits for them, and re-layouts  2.25 us (3%)
  between operations  1.42 us (2%)
    ppermute x13, starting transfers between devices, hop(): return lax.ppermute(a, ('seq', 'dp'), pairs)  28.7 us
    all_to_all x1, blocking collectives, towers(): parts = lax.all_to_all(part, ('seq', 'dp', 'domain'), 0, 0, tiled=True)  10.7 us
    ppermute x13, waiting for transfers between devices, hop(): return lax.ppermute(a, ('seq', 'dp'), pairs)  8.59 us
    ppermute x4, starting transfers between devices, plane_hop(): return lax.ppermute(a, ('seq', 'dp'), [(i, i ^ move) for i in range(here)])  7.03 us
    unnamed x12, local copies, waits for them, and re-layouts  2.25 us
    ppermute x4, waiting for transfers between devices, plane_hop(): return lax.ppermute(a, ('seq', 'dp'), [(i, i ^ move) for i in range(here)])  2.13 us
    pallas_call x1, Pallas kernels, towers(): call(project_kernel, (shape((2 * tokens, wide), bf16), shape((MESSAGE, HE...  1.41 us
  transfers between devices with their start and end apart: 17, of which 8 were waited for; matrix products, arithmetic and copies ran while one was open for 0% of the time, Pallas kernels for 3%

profile of v9, /device:TPU:0, one launch (start us, length us, event | category | flops | bytes accessed | tf_op | source)
XLA Modules:
  0.0 66.4 jit_solution(11796172405397684417)
XLA Ops:
  0.7 1.2 %copy-done.2 = bf16[1,128,3072]{2,1,0:T(8,128)(2,1)S(1)} copy-done((bf16[1,128,3072]{2,1,0:T(8,128)(2,1)S(1)}, bf16[1,128,3072]{2,1,0:T(8,128)(2,1)}, u32[]{:S(2)}) %copy-start.2) | copy-done | bytes 786456
  2.6 3.0 %collective-permute-start.2 = (bf16[128,768]{1,0:T(8,128)(2,1)S(1)}, bf16[128,768]{1,0:T(8,128)(2,1)S(1)}, u32[]{:S(2)}, u32[]{:S(2)}) collective-permute-start(bf16[128,768]{1,0:T(8,128)(2,1)S(1)} %get-tuple-element.10), channel_id=1, source_target_pairs={{0,4},{2,6},{4,0},{6,2},{8,12},{10,14},{12,8},{14,10},{16,20},{18,... | collective-permute-start | bytes 589832 | tf_op jit(solution)/shard_map/ppermute | solution.py:425
  5.6 4.4 %collective-permute-start.4 = (bf16[128,768]{1,0:T(8,128)(2,1)S(1)}, bf16[128,768]{1,0:T(8,128)(2,1)S(1)}, u32[]{:S(2)}, u32[]{:S(2)}) collective-permute-start(bf16[128,768]{1,0:T(8,128)(2,1)S(1)} %get-tuple-element.12.refs_0_), channel_id=1, source_target_pairs={{0,8},{2,10},{4,12},{6,14},{8,0},{10,2},{12,4},{14,6},{16,24},{18,... | collective-permute-start | bytes 589832 | tf_op jit(solution)/shard_map/ppermute | solution.py:422
  10.0 3.5 %collective-permute-start.6 = (bf16[128,768]{1,0:T(8,128)(2,1)S(1)}, bf16[128,768]{1,0:T(8,128)(2,1)S(1)}, u32[]{:S(2)}, u32[]{:S(2)}) collective-permute-start(bf16[128,768]{1,0:T(8,128)(2,1)S(1)} %collective-permute-done.5.refs_4_), channel_id=1, source_target_pairs={{0,8},{2,10},{4,12},{6,14},{8,0},{10,2},{12,4},{14,6},{16,24},{18,... | collective-permute-start | bytes 589832 | tf_op jit(solution)/shard_map/ppermute | solution.py:422
  13.5 1.0 %copy-done = bf16[1,1,256,1024]{3,2,1,0:T(8,128)(2,1)S(1)} copy-done((bf16[1,1,256,1024]{3,2,1,0:T(8,128)(2,1)S(1)}, bf16[1,1,256,1024]{3,2,1,0:T(8,128)(2,1)}, u32[]{:S(2)}) %copy-start) | copy-done | bytes 524312
  14.6 2.5 %collective-permute-start.3 = (bf16[256,1024]{1,0:T(8,128)(2,1)S(1)}, bf16[256,1024]{1,0:T(8,128)(2,1)S(1)}, u32[]{:S(2)}, u32[]{:S(2)}) collective-permute-start(bf16[256,1024]{1,0:T(8,128)(2,1)S(1)} %shard_map.78), channel_id=1, source_target_pairs={{0,6},{2,4},{4,2},{6,0},{8,14},{10,12},{12,10},{14,8},{16,22},{18,... | collective-permute-start | bytes 1572872 | tf_op jit(solution)/shard_map/ppermute | solution.py:425
  17.8 0.8 %collective-permute-done.6.rest_0_.refs_6_ = bf16[128,768]{1,0:T(8,128)(2,1)S(1)} collective-permute-done((bf16[128,768]{1,0:T(8,128)(2,1)S(1)}, bf16[128,768]{1,0:T(8,128)(2,1)S(1)}, u32[]{:S(2)}, u32[]{:S(2)}) %collective-permute-start.6) | collective-permute-done | bytes 196640 | tf_op jit(solution)/shard_map/ppermute | solution.py:422
  18.6 2.4 %collective-permute-start.7 = (bf16[128,768]{1,0:T(8,128)(2,1)S(1)}, bf16[128,768]{1,0:T(8,128)(2,1)S(1)}, u32[]{:S(2)}, u32[]{:S(2)}) collective-permute-start(bf16[128,768]{1,0:T(8,128)(2,1)S(1)} %shard_map.80), channel_id=1, source_target_pairs={{0,8},{2,10},{4,12},{6,14},{8,0},{10,2},{12,4},{14,6},{16,24},{18,... | collective-permute-start | bytes 589832 | tf_op jit(solution)/shard_map/ppermute | solution.py:422
  21.0 1.0 %collective-permute-start.1 = (bf16[256,1024]{1,0:T(8,128)(2,1)S(1)}, bf16[256,1024]{1,0:T(8,128)(2,1)S(1)}, u32[]{:S(2)}, u32[]{:S(2)}) collective-permute-start(bf16[256,1024]{1,0:T(8,128)(2,1)S(1)} %bitcast.3), channel_id=1, source_target_pairs={{0,2},{2,0},{4,6},{6,4},{8,10},{10,8},{12,14},{14,12},{16,18},{18,... | collective-permute-start | bytes 1572872 | tf_op jit(solution)/shard_map/ppermute | solution.py:425
  23.2 1.4 %collective-permute-done.7.refs_3_ = bf16[128,768]{1,0:T(8,128)(2,1)S(1)} collective-permute-done((bf16[128,768]{1,0:T(8,128)(2,1)S(1)}, bf16[128,768]{1,0:T(8,128)(2,1)S(1)}, u32[]{:S(2)}, u32[]{:S(2)}) %collective-permute-start.7) | collective-permute-done | bytes 196640 | tf_op jit(solution)/shard_map/ppermute | solution.py:422
  25.3 9.2 %collective-permute-start.12 = (bf16[128,768]{1,0:T(8,128)(2,1)S(1)}, bf16[128,768]{1,0:T(8,128)(2,1)S(1)}, u32[]{:S(2)}, u32[]{:S(2)}) collective-permute-start(bf16[128,768]{1,0:T(8,128)(2,1)S(1)} %collective-permute-done.8.rest_0_.refs_8_), channel_id=1, source_target_pairs={{0,8},{2,10},{4,12},{6,14},{8,0},{10,2},{12,4},{14,6},{16,24},{18,... | collective-permute-start | bytes 589832 | tf_op jit(solution)/shard_map/ppermute | solution.py:422
  34.5 2.1 %collective-permute-start.13 = (bf16[128,768]{1,0:T(8,128)(2,1)S(1)}, bf16[128,768]{1,0:T(8,128)(2,1)S(1)}, u32[]{:S(2)}, u32[]{:S(2)}) collective-permute-start(bf16[128,768]{1,0:T(8,128)(2,1)S(1)} %shard_map.82), channel_id=1, source_target_pairs={{0,8},{2,10},{4,12},{6,14},{8,0},{10,2},{12,4},{14,6},{16,24},{18,... | collective-permute-start | bytes 589832 | tf_op jit(solution)/shard_map/ppermute | solution.py:422
  37.3 2.0 %collective-permute-done.1.across = bf16[256,1024]{1,0:T(8,128)(2,1)S(1)} collective-permute-done((bf16[256,1024]{1,0:T(8,128)(2,1)S(1)}, bf16[256,1024]{1,0:T(8,128)(2,1)S(1)}, u32[]{:S(2)}, u32[]{:S(2)}) %collective-permute-start.1) | collective-permute-done | bytes 524320 | tf_op jit(solution)/shard_map/ppermute | solution.py:425
  40.1 1.6 %collective-permute-done.10.refs_7_ = bf16[128,768]{1,0:T(8,128)(2,1)S(1)} collective-permute-done((bf16[128,768]{1,0:T(8,128)(2,1)S(1)}, bf16[128,768]{1,0:T(8,128)(2,1)S(1)}, u32[]{:S(2)}, u32[]{:S(2)}) %collective-permute-start.10) | collective-permute-done | bytes 196640 | tf_op jit(solution)/shard_map/ppermute | solution.py:422
  41.7 2.1 %collective-permute-done.13.refs_11_ = bf16[128,768]{1,0:T(8,128)(2,1)S(1)} collective-permute-done((bf16[128,768]{1,0:T(8,128)(2,1)S(1)}, bf16[128,768]{1,0:T(8,128)(2,1)S(1)}, u32[]{:S(2)}, u32[]{:S(2)}) %collective-permute-start.13) | collective-permute-done | bytes 196640 | tf_op jit(solution)/shard_map/ppermute | solution.py:422
  43.8 1.4 %shard_map.83 = (bf16[512,768]{1,0:T(8,128)(2,1)S(1)}, bf16[272,128]{1,0:T(8,128)(2,1)S(1)}, bf16[1024,768]{1,0:T(8,128)(2,1)S(1)}) custom-call(bf16[512,1024]{1,0:T(8,128)(2,1)S(1)} %get-tuple-element.11.normed, bf16[128,768]{1,0:T(8,128)(2,1)S(1)} %get-tuple-element.12.refs_0_, bf16[128,768]{1,0:T(8,128)(2,1)S(1)} %collective-permute-done.2.rest_0_.values.refs_1_, ...), custom_call_target="tpu_custom_call" | custom-call | flops 805306368 | bytes 2097152 | tf_op jit(solution)/shard_map/pallas_call | solution.py:463
  45.2 2.4 %collective-permute-start.16 = (bf16[272,128]{1,0:T(8,128)(2,1)S(1)}, bf16[272,128]{1,0:T(8,128)(2,1)S(1)}, u32[]{:S(2)}, u32[]{:S(2)}) collective-permute-start(bf16[272,128]{1,0:T(8,128)(2,1)S(1)} %get-tuple-element.13), channel_id=1, source_target_pairs={{0,24},{2,26},{4,28},{6,30},{8,16},{10,18},{12,20},{14,22},{16,8},... | collective-permute-start | bytes 208904 | tf_op jit(solution)/shard_map/ppermute | solution.py:422
  47.6 0.9 %collective-permute-start.15 = (bf16[272,128]{1,0:T(8,128)(2,1)S(1)}, bf16[272,128]{1,0:T(8,128)(2,1)S(1)}, u32[]{:S(2)}, u32[]{:S(2)}) collective-permute-start(bf16[272,128]{1,0:T(8,128)(2,1)S(1)} %get-tuple-element.13), channel_id=1, source_target_pairs={{0,16},{2,18},{4,20},{6,22},{8,24},{10,26},{12,28},{14,30},{16,0},... | collective-permute-start | bytes 208904 | tf_op jit(solution)/shard_map/ppermute | solution.py:422
  48.5 1.2 %collective-permute-start.14 = (bf16[272,128]{1,0:T(8,128)(2,1)S(1)}, bf16[272,128]{1,0:T(8,128)(2,1)S(1)}, u32[]{:S(2)}, u32[]{:S(2)}) collective-permute-start(bf16[272,128]{1,0:T(8,128)(2,1)S(1)} %get-tuple-element.13), channel_id=1, source_target_pairs={{0,8},{2,10},{4,12},{6,14},{8,0},{10,2},{12,4},{14,6},{16,24},{18,... | collective-permute-start | bytes 208904 | tf_op jit(solution)/shard_map/ppermute | solution.py:422
  49.7 1.2 %shard_map.84.short = f32[1,256]{1,0:T(1,128)S(1)} custom-call(bf16[256,1024]{1,0:T(8,128)(2,1)S(1)} %get-tuple-element.16.raw, bf16[1024,768]{1,0:T(8,128)(2,1)S(1)} %get-tuple-element.17.weights, f32[1,1024]{1,0:T(1,128)S(1)} %copy-done.3), custom_call_target="tpu_custom_call" | custom-call | flops 402653184 | bytes 2097152 | tf_op jit(solution)/shard_map/pallas_call | solution.py:470
  51.5 2.0 %collective-permute-done.15.state_2 = bf16[272,128]{1,0:T(8,128)(2,1)S(1)} collective-permute-done((bf16[272,128]{1,0:T(8,128)(2,1)S(1)}, bf16[272,128]{1,0:T(8,128)(2,1)S(1)}, u32[]{:S(2)}, u32[]{:S(2)}) %collective-permute-start.15) | collective-permute-done | bytes 69664 | tf_op jit(solution)/shard_map/ppermute | solution.py:422
  53.6 0.9 %shard_map.85 = f32[32,4,256]{2,1,0:T(4,128)S(1)} custom-call(s32[1,1]{1,0:T(1,128)S(6)} %copy.8.lengths, bf16[272,128]{1,0:T(8,128)(2,1)S(1)} %collective-permute-done.14.state_1, bf16[272,128]{1,0:T(8,128)(2,1)S(1)} %collective-permute-done.15.state_2, bf16[272,128]{1,0:T(8,128)(2,1)S(1)} %collective-permute-done.16.state_3, ...), custom_call_target="tpu_custom_call" | custom-call | flops 301989888 | bytes 2097152 | tf_op jit(solution)/shard_map/pallas_call | solution.py:473
  54.4 10.7 %all_to_all.5.parts = f32[32,4,256]{2,1,0:T(4,128)S(1)} all-to-all(f32[32,4,256]{2,1,0:T(4,128)S(1)} %shard_map.85), channel_id=1, replica_groups=mesh['seq'=8,'dp'=2,'domain'=2] {'seq','dp','domain'}, dimensions={0} | all-to-all | bytes 262144 | tf_op jit(solution)/shard_map/all_to_all | solution.py:480
  65.1 1.3 %shard_map.86 = (bf16[1,1,128]{2,1,0:T(2,128)(2,1)}, f32[1,1]{1,0:T(1,128)}) custom-call(s32[2]{0:T(128)S(1)} %copy-done.5, f32[32,4,256]{2,1,0:T(4,128)S(1)} %all_to_all.5.parts), custom_call_target="tpu_custom_call" | custom-call | flops 16384 | bytes 2097152 | tf_op jit(solution)/shard_map/pallas_call | solution.py:481
  (33 shorter events, 4.9 us)
Async XLA Ops:
  0.6 20.3 %copy-start.1 = (bf16[1,1,256,1024]{3,2,1,0:T(8,128)(2,1)S(1)}, bf16[1,1,256,1024]{3,2,1,0:T(8,128)(2,1)}, u32[]{:S(2)}) copy-start(bf16[1,1,256,1024]{3,2,1,0:T(8,128)(2,1)} %param.6) | copy-start | bytes 1572868
  0.6 1.2 %copy-start.2 = (bf16[1,128,3072]{2,1,0:T(8,128)(2,1)S(1)}, bf16[1,128,3072]{2,1,0:T(8,128)(2,1)}, u32[]{:S(2)}) copy-start(bf16[1,128,3072]{2,1,0:T(8,128)(2,1)} %param.7) | copy-start | bytes 2359300
  2.0 8.1 %collective-permute-start.5 = (bf16[128,768]{1,0:T(8,128)(2,1)S(1)}, bf16[128,768]{1,0:T(8,128)(2,1)S(1)}, u32[]{:S(2)}, u32[]{:S(2)}) collective-permute-start(bf16[128,768]{1,0:T(8,128)(2,1)S(1)} %get-tuple-element.12.refs_0_), channel_id=1, source_target_pairs={{0,0},{2,2},{4,4},{6,6},{8,16},{10,18},{12,20},{14,22},{16,8},{18,... | collective-permute-start | bytes 589832 | tf_op jit(solution)/shard_map/ppermute | solution.py:422
  2.6 10.9 %collective-permute-start.2 = (bf16[128,768]{1,0:T(8,128)(2,1)S(1)}, bf16[128,768]{1,0:T(8,128)(2,1)S(1)}, u32[]{:S(2)}, u32[]{:S(2)}) collective-permute-start(bf16[128,768]{1,0:T(8,128)(2,1)S(1)} %get-tuple-element.10), channel_id=1, source_target_pairs={{0,4},{2,6},{4,0},{6,2},{8,12},{10,14},{12,8},{14,10},{16,20},{18,... | collective-permute-start | bytes 589832 | tf_op jit(solution)/shard_map/ppermute | solution.py:425
  5.6 11.5 %collective-permute-start.4 = (bf16[128,768]{1,0:T(8,128)(2,1)S(1)}, bf16[128,768]{1,0:T(8,128)(2,1)S(1)}, u32[]{:S(2)}, u32[]{:S(2)}) collective-permute-start(bf16[128,768]{1,0:T(8,128)(2,1)S(1)} %get-tuple-element.12.refs_0_), channel_id=1, source_target_pairs={{0,8},{2,10},{4,12},{6,14},{8,0},{10,2},{12,4},{14,6},{16,24},{18,... | collective-permute-start | bytes 589832 | tf_op jit(solution)/shard_map/ppermute | solution.py:422
  10.0 8.5 %collective-permute-start.6 = (bf16[128,768]{1,0:T(8,128)(2,1)S(1)}, bf16[128,768]{1,0:T(8,128)(2,1)S(1)}, u32[]{:S(2)}, u32[]{:S(2)}) collective-permute-start(bf16[128,768]{1,0:T(8,128)(2,1)S(1)} %collective-permute-done.5.refs_4_), channel_id=1, source_target_pairs={{0,8},{2,10},{4,12},{6,14},{8,0},{10,2},{12,4},{14,6},{16,24},{18,... | collective-permute-start | bytes 589832 | tf_op jit(solution)/shard_map/ppermute | solution.py:422
  13.5 1.0 %copy-start = (bf16[1,1,256,1024]{3,2,1,0:T(8,128)(2,1)S(1)}, bf16[1,1,256,1024]{3,2,1,0:T(8,128)(2,1)}, u32[]{:S(2)}) copy-start(bf16[1,1,256,1024]{3,2,1,0:T(8,128)(2,1)} %param.6) | copy-start | bytes 1572868
  14.6 24.9 %copy-start.3 = (f32[1,1024]{1,0:T(1,128)S(1)}, f32[1,1024]{1,0:T(1,128)}, u32[]{:S(2)}) copy-start(f32[1,1024]{1,0:T(1,128)} %gain.4) | copy-start | bytes 12292
  14.6 19.8 %collective-permute-start.3 = (bf16[256,1024]{1,0:T(8,128)(2,1)S(1)}, bf16[256,1024]{1,0:T(8,128)(2,1)S(1)}, u32[]{:S(2)}, u32[]{:S(2)}) collective-permute-start(bf16[256,1024]{1,0:T(8,128)(2,1)S(1)} %shard_map.78), channel_id=1, source_target_pairs={{0,6},{2,4},{4,2},{6,0},{8,14},{10,12},{12,10},{14,8},{16,22},{18,... | collective-permute-start | bytes 1572872 | tf_op jit(solution)/shard_map/ppermute | solution.py:425
  17.1 5.3 %collective-permute-start.8 = (bf16[128,768]{1,0:T(8,128)(2,1)S(1)}, bf16[128,768]{1,0:T(8,128)(2,1)S(1)}, u32[]{:S(2)}, u32[]{:S(2)}) collective-permute-start(bf16[128,768]{1,0:T(8,128)(2,1)S(1)} %collective-permute-done.4.refs_2_), channel_id=1, source_target_pairs={{0,0},{2,2},{4,4},{6,6},{8,16},{10,18},{12,20},{14,22},{16,8},{18,... | collective-permute-start | bytes 589832 | tf_op jit(solution)/shard_map/ppermute | solution.py:422
  18.6 6.0 %collective-permute-start.7 = (bf16[128,768]{1,0:T(8,128)(2,1)S(1)}, bf16[128,768]{1,0:T(8,128)(2,1)S(1)}, u32[]{:S(2)}, u32[]{:S(2)}) collective-permute-start(bf16[128,768]{1,0:T(8,128)(2,1)S(1)} %shard_map.80), channel_id=1, source_target_pairs={{0,8},{2,10},{4,12},{6,14},{8,0},{10,2},{12,4},{14,6},{16,24},{18,... | collective-permute-start | bytes 589832 | tf_op jit(solution)/shard_map/ppermute | solution.py:422
  21.0 18.4 %collective-permute-start.1 = (bf16[256,1024]{1,0:T(8,128)(2,1)S(1)}, bf16[256,1024]{1,0:T(8,128)(2,1)S(1)}, u32[]{:S(2)}, u32[]{:S(2)}) collective-permute-start(bf16[256,1024]{1,0:T(8,128)(2,1)S(1)} %bitcast.3), channel_id=1, source_target_pairs={{0,2},{2,0},{4,6},{6,4},{8,10},{10,8},{12,14},{14,12},{16,18},{18,... | collective-permute-start | bytes 1572872 | tf_op jit(solution)/shard_map/ppermute | solution.py:425
  21.9 17.5 %collective-permute-start = (bf16[256,1024]{1,0:T(8,128)(2,1)S(1)}, bf16[256,1024]{1,0:T(8,128)(2,1)S(1)}, u32[]{:S(2)}, u32[]{:S(2)}) collective-permute-start(bf16[256,1024]{1,0:T(8,128)(2,1)S(1)} %bitcast.4), channel_id=1, source_target_pairs={{0,4},{2,6},{4,0},{6,2},{8,12},{10,14},{12,8},{14,10},{16,20},{18,... | collective-permute-start | bytes 1572872 | tf_op jit(solution)/shard_map/ppermute | solution.py:425
  22.5 2.8 %collective-permute-start.9 = (bf16[128,768]{1,0:T(8,128)(2,1)S(1)}, bf16[128,768]{1,0:T(8,128)(2,1)S(1)}, u32[]{:S(2)}, u32[]{:S(2)}) collective-permute-start(bf16[128,768]{1,0:T(8,128)(2,1)S(1)} %shard_map.81), channel_id=1, source_target_pairs={{0,0},{2,2},{4,4},{6,6},{8,16},{10,18},{12,20},{14,22},{16,8},{18,... | collective-permute-start | bytes 589832 | tf_op jit(solution)/shard_map/ppermute | solution.py:422
  24.6 9.9 %collective-permute-start.11 = (bf16[128,768]{1,0:T(8,128)(2,1)S(1)}, bf16[128,768]{1,0:T(8,128)(2,1)S(1)}, u32[]{:S(2)}, u32[]{:S(2)}) collective-permute-start(bf16[128,768]{1,0:T(8,128)(2,1)S(1)} %collective-permute-done.7.refs_3_), channel_id=1, source_target_pairs={{0,0},{2,2},{4,4},{6,6},{8,16},{10,18},{12,20},{14,22},{16,8},{18,... | collective-permute-start | bytes 589832 | tf_op jit(solution)/shard_map/ppermute | solution.py:422
  25.3 14.8 %collective-permute-start.12 = (bf16[128,768]{1,0:T(8,128)(2,1)S(1)}, bf16[128,768]{1,0:T(8,128)(2,1)S(1)}, u32[]{:S(2)}, u32[]{:S(2)}) collective-permute-start(bf16[128,768]{1,0:T(8,128)(2,1)S(1)} %collective-permute-done.8.rest_0_.refs_8_), channel_id=1, source_target_pairs={{0,8},{2,10},{4,12},{6,14},{8,0},{10,2},{12,4},{14,6},{16,24},{18,... | collective-permute-start | bytes 589832 | tf_op jit(solution)/shard_map/ppermute | solution.py:422
  34.5 7.2 %collective-permute-start.10 = (bf16[128,768]{1,0:T(8,128)(2,1)S(1)}, bf16[128,768]{1,0:T(8,128)(2,1)S(1)}, u32[]{:S(2)}, u32[]{:S(2)}) collective-permute-start(bf16[128,768]{1,0:T(8,128)(2,1)S(1)} %collective-permute-done.9.refs_5_), channel_id=1, source_target_pairs={{0,8},{2,10},{4,12},{6,14},{8,0},{10,2},{12,4},{14,6},{16,24},{18,... | collective-permute-start | bytes 589832 | tf_op jit(solution)/shard_map/ppermute | solution.py:422
  34.5 9.3 %collective-permute-start.13 = (bf16[128,768]{1,0:T(8,128)(2,1)S(1)}, bf16[128,768]{1,0:T(8,128)(2,1)S(1)}, u32[]{:S(2)}, u32[]{:S(2)}) collective-permute-start(bf16[128,768]{1,0:T(8,128)(2,1)S(1)} %shard_map.82), channel_id=1, source_target_pairs={{0,8},{2,10},{4,12},{6,14},{8,0},{10,2},{12,4},{14,6},{16,24},{18,... | collective-permute-start | bytes 589832 | tf_op jit(solution)/shard_map/ppermute | solution.py:422
  45.2 8.3 %copy-start.4 = (f32[1,1024]{1,0:T(1,128)S(1)}, f32[1,1024]{1,0:T(1,128)}, u32[]{:S(2)}) copy-start(f32[1,1024]{1,0:T(1,128)} %gain.5) | copy-start | bytes 12292
  45.2 6.3 %collective-permute-start.16 = (bf16[272,128]{1,0:T(8,128)(2,1)S(1)}, bf16[272,128]{1,0:T(8,128)(2,1)S(1)}, u32[]{:S(2)}, u32[]{:S(2)}) collective-permute-start(bf16[272,128]{1,0:T(8,128)(2,1)S(1)} %get-tuple-element.13), channel_id=1, source_target_pairs={{0,24},{2,26},{4,28},{6,30},{8,16},{10,18},{12,20},{14,22},{16,8},... | collective-permute-start | bytes 208904 | tf_op jit(solution)/shard_map/ppermute | solution.py:422
  47.6 6.0 %collective-permute-start.15 = (bf16[272,128]{1,0:T(8,128)(2,1)S(1)}, bf16[272,128]{1,0:T(8,128)(2,1)S(1)}, u32[]{:S(2)}, u32[]{:S(2)}) collective-permute-start(bf16[272,128]{1,0:T(8,128)(2,1)S(1)} %get-tuple-element.13), channel_id=1, source_target_pairs={{0,16},{2,18},{4,20},{6,22},{8,24},{10,26},{12,28},{14,30},{16,0},... | collective-permute-start | bytes 208904 | tf_op jit(solution)/shard_map/ppermute | solution.py:422
  48.5 5.1 %collective-permute-start.14 = (bf16[272,128]{1,0:T(8,128)(2,1)S(1)}, bf16[272,128]{1,0:T(8,128)(2,1)S(1)}, u32[]{:S(2)}, u32[]{:S(2)}) collective-permute-start(bf16[272,128]{1,0:T(8,128)(2,1)S(1)} %get-tuple-element.13), channel_id=1, source_target_pairs={{0,8},{2,10},{4,12},{6,14},{8,0},{10,2},{12,4},{14,6},{16,24},{18,... | collective-permute-start | bytes 208904 | tf_op jit(solution)/shard_map/ppermute | solution.py:422
  49.7 15.4 %copy-start.5 = (s32[2]{0:T(128)S(1)}, s32[2]{0:T(128)}, u32[]{:S(2)}) copy-start(s32[2]{0:T(128)} %positives.1) | copy-start | bytes 28

commit v10 on v7

--- a/solution.py
+++ b/solution.py
@@ -181,9 +181,8 @@
         copy.wait()
 
 
-def gate_kernel(values, after, out):
-    del after
-    out[...] = values[...]
+def gate_kernel(values, *rest):
+    rest[-1][...] = values[...]
 
 
 def normalise(values, gain):
@@ -192,8 +191,7 @@
     return (wide * scale * gain).astype(jnp.bfloat16)
 
 
-def features(normed, weights):
-    out = jnp.dot(normed, weights, preferred_element_type=jnp.float32)
+def features(out):
     raw = out[:, : 2 * GROUP]
     low = jnp.where(raw > 0.0, raw + 1.0, jnp.exp(jnp.minimum(raw, 0.0))).astype(jnp.bfloat16)
     return low[:, :GROUP], low[:, GROUP:], out[:, 2 * GROUP :].astype(jnp.bfloat16)
@@ -224,33 +222,50 @@
     pltpu.make_async_copy(own, short, sems.at[2]).wait()
 
 
-def project_kernel(normed, both, one, two_own, two_near, next_both, far_own, far_near, feats, message, weights):
+def place_rows(dest, start, x, here, there):
+    rows = here.shape[0]
+    for place, values in ((x, here), (1 - x, there)):
+        dest[pl.ds(pl.multiple_of(start + place * rows, rows), rows), :] = values
+
+
+def partial_kernel(normed, own, near, one_own, one_near, two_own, two_near, partial, weights):
+    z, x, _ = places()
+    parts = ((own, near), (one_own, one_near), (two_own, two_near), None)
+    starts = [pl.multiple_of(jnp.bitwise_xor(z, j) * GROUP, GROUP) for j in range(PLANES)]
+    for start, refs in zip(starts, parts):
+        if refs is None:
+            weights[pl.ds(start, GROUP), :] = jnp.zeros((GROUP, weights.shape[1]), weights.dtype)
+        else:
+            place_rows(weights, start, x, refs[0][...], refs[1][...])
+    total = None
+    for start in starts[:3]:
+        rows = pl.ds(start, GROUP)
+        out = jnp.dot(normed[:, rows], weights[rows, :], preferred_element_type=jnp.float32)
+        total = out if total is None else total + out
+    partial[...] = total
+
+
+def project_kernel(normed, partial, next_both, far_own, far_near, feats, message, last):
     tokens = normed.shape[0]
-    rows = two_own.shape[0]
+    rows = far_own.shape[0]
     z, x, _ = places()
-
-    def put(plane, own, near):
-        for place, values in ((x, own), (1 - x, near)):
-            weights[pl.ds(pl.multiple_of((2 * plane + place) * rows, rows), rows), :] = values
-
-    put(z, both[:rows, :], both[rows:, :])
-    put(jnp.bitwise_xor(z, 1), one[:rows, :], one[rows:, :])
-    put(jnp.bitwise_xor(z, 2), two_own[...], two_near[...])
     inner = jnp.logical_or(z == 1, z == 2)
 
     @pl.when(inner)
     def _():
-        put(3 - z, next_both[:rows, :], next_both[rows:, :])
+        place_rows(last, 0, x, next_both[:rows, :], next_both[rows:, :])
 
     @pl.when(jnp.logical_not(inner))
     def _():
-        put(3 - z, far_own[...], far_near[...])
-
+        place_rows(last, 0, x, far_own[...], far_near[...])
+
+    columns = pl.ds(pl.multiple_of((3 - z) * GROUP, GROUP), GROUP)
     half = tokens // 2
     total = jnp.zeros((1, GROUP), jnp.float32)
     for part in range(2):
         at = pl.ds(part * half, half)
-        query, key, value = features(normed[at, :], weights[...])
+        out = partial[at, :] + jnp.dot(normed[at, columns], last[...], preferred_element_type=jnp.float32)
+        query, key, value = features(out)
         feats[at, :GROUP] = query
         feats[at, GROUP : 2 * GROUP] = key
         feats[at, 2 * GROUP :] = value
@@ -291,13 +306,16 @@
     return jnp.sum(weight * value.astype(jnp.float32), axis=0, keepdims=True)
 
 
-def short_kernel(raw, weights, gain, out):
+def short_kernel(raw, weights, last, gain, out):
     z, x, u = places()
     out[...] = jnp.zeros(out.shape, jnp.float32)
 
     @pl.when(z == 0)
     def _():
-        query, key, value = features(normalise(raw[...], gain[...]), weights[...])
+        low = normalise(raw[...], gain[...])
+        wide = jnp.dot(low, weights[...], preferred_element_type=jnp.float32)
+        wide = wide + jnp.dot(low[:, 3 * GROUP :], last[...], preferred_element_type=jnp.float32)
+        query, key, value = features(wide)
         share, _ = shares(query, key, jnp.zeros((1, GROUP), jnp.float32))
         columns = pl.ds(pl.multiple_of((2 * x + u) * GROUP, GROUP), GROUP)
         own = jnp.sum(raw[:, columns].astype(jnp.float32), axis=0, keepdims=True)
@@ -341,41 +359,48 @@
     first = jnp.where(long_u == 0, long_row, short_row)
     second = jnp.where(long_u == 0, short_row, long_row)
     own_gain = gain[:, pl.ds(pl.multiple_of((2 * x + u) * GROUP, GROUP), GROUP)]
-    rows = jnp.concatenate([first, second, own_gain, own_gain], axis=0)
-    part[...] = jnp.broadcast_to(rows[None], part.shape)
-
-
-def loss_kernel(positives, parts, vec, loss, mine, theirs):
+    half = jnp.where(lax.rem(z, 2) == 0, own_gain[:, :HEAD_DIM], own_gain[:, HEAD_DIM:])
+    part[...] = jnp.broadcast_to(jnp.concatenate([first, second, half], axis=1)[None], part.shape)
+
+
+def loss_kernel(positives, parts, vec, loss, mine):
     z, x, u = places()
     domain = lax.axis_index("domain")
     width = mine.shape[1]
     piece = vec.shape[2]
 
-    def collect(place, dest):
-        total = jnp.zeros((2, 1), jnp.float32)
+    def collect(place):
+        groups = []
         for group in range(PLANE):
-            blocks = [parts[2 * (PLANE * plane + group) + place] for plane in range(PLANES)]
-            values = (blocks[0][:2] + blocks[1][:2]) + (blocks[2][:2] + blocks[3][:2])
-            total = total + jnp.sum(values * values, axis=1, keepdims=True)
-            dest[:, group * GROUP : (group + 1) * GROUP] = values * blocks[0][2:3]
-        factor = lax.rsqrt(total / width + epsilon)
-        return (dest[...] * factor).astype(jnp.bfloat16).astype(jnp.float32)
-
-    own = collect(domain, mine)
-    other = collect(1 - domain, theirs)
-    mine[...] = own
+            at = [parts[2 * (PLANE * plane + group) + place] for plane in range(PLANES)]
+            total = (at[0][:, : 2 * GROUP] + at[1][:, : 2 * GROUP]) + (at[2][:, : 2 * GROUP] + at[3][:, : 2 * GROUP])
+            gain = jnp.concatenate([at[0][:, 2 * GROUP :], at[1][:, 2 * GROUP :]], axis=1)
+            groups.append((total[:, :GROUP], total[:, GROUP:], gain))
+        return groups
+
+    def reduced(terms):
+        total = (terms[0] + terms[1]) + (terms[2] + terms[3])
+        return jnp.sum(total, axis=1, keepdims=True)
+
+    own = [(jnp.where(u == 0, a, b), gain) for a, b, gain in collect(domain)]
+    other = collect(1 - domain)
+    scaled = [a * gain for a, gain in own]
+    for group in range(PLANE):
+        mine[:, group * GROUP : (group + 1) * GROUP] = scaled[group]
+    factor = lax.rsqrt(reduced([a * a for a, _ in own]) / width + epsilon)
+    logits = []
+    for user in range(2):
+        norm = reduced([o[user] * o[user] for o in other])
+        product = reduced([s * (o[user] * o[2]) for s, o in zip(scaled, other)])
+        logits.append(product * factor * lax.rsqrt(norm / width + epsilon) * (logit_scale / width))
     start = pl.multiple_of((2 * z + x) * piece, piece)
-    out = mine[:, pl.ds(start, piece)]
-    vec[0] = jnp.where(u == 0, out[0:1], out[1:2]).astype(jnp.bfloat16)
-    this = jnp.where(u == 0, own[0:1], own[1:2])
-    logits = jnp.sum(this * other, axis=1, keepdims=True) * (logit_scale / width)
-    top = jnp.max(logits, axis=0, keepdims=True)
-    spread = jnp.log(jnp.sum(jnp.exp(logits - top), axis=0, keepdims=True)) + top
+    vec[0] = (mine[:, pl.ds(start, piece)] * factor).astype(jnp.bfloat16)
     forward = jnp.where(u == 0, positives[0], positives[1])
     backward = jnp.where(positives[0] == u, 0, 1)
     partner = jnp.where(domain == 0, forward, backward)
-    rows = lax.broadcasted_iota(jnp.int32, (2, 1), 0)
-    loss[...] = spread - jnp.sum(jnp.where(rows == partner, logits, 0.0), axis=0, keepdims=True)
+    top = jnp.maximum(logits[0], logits[1])
+    spread = jnp.log(jnp.exp(logits[0] - top) + jnp.exp(logits[1] - top)) + top
+    loss[...] = spread - jnp.where(partner == 0, logits[0], logits[1])
 
 
 def vmem():
@@ -429,19 +454,18 @@
     w_own, w_sent = call(
         pack_kernel, (shape((rows, wide), bf16),) * 2, [hbm()], [pltpu.SemaphoreType.DMA((6,))], 0
     )(weight)
+    two_own = hop(w_own, lambda p: p ^ 2)
+    far_own = hop(two_own, lambda p: {1: 0, 2: 3}.get(p))
+    w_near = plane_hop(w_sent, 2)
+    two_near = hop(call(gate_kernel, shape((rows, wide), bf16), [vmem()] + [anywhere()] * 1, [], 0)(w_near, two_own), lambda p: p ^ 2)
+    one_near = hop(w_near, lambda p: p ^ 1)
+    far_near = hop(call(gate_kernel, shape((rows, wide), bf16), [vmem()] + [anywhere()] * 1, [], 0)(two_near, far_own), lambda p: {1: 0, 2: 3}.get(p))
+    both = jnp.concatenate([w_own, w_near], axis=0)
+    corner = plane_hop(events, 3)
     near = plane_hop(events, 2)
+    one_own = hop(w_own, lambda p: p ^ 1)
+    next_both = hop(call(gate_kernel, shape((2 * rows, wide), bf16), [vmem()] + [anywhere()] * 1, [], 0)(both, one_own), lambda p: 3 - p if p in (1, 2) else None)
     across = plane_hop(events, 1)
-    corner = plane_hop(events, 3)
-    w_near = plane_hop(w_sent, 2)
-    two_own = hop(w_own, lambda p: p ^ 2)
-    two_near = hop(w_near, lambda p: p ^ 2)
-    both = jnp.concatenate([w_own, w_near], axis=0)
-    one_own = hop(w_own, lambda p: p ^ 1)
-    one_near = hop(w_near, lambda p: p ^ 1)
-    one = jnp.concatenate([one_own, one_near], axis=0)
-    next_both = hop(both, lambda p: 3 - p if p in (1, 2) else None)
-    far_own = hop(two_own, lambda p: {1: 0, 2: 3}.get(p))
-    far_near = hop(two_near, lambda p: {1: 0, 2: 3}.get(p))
 
     normed, sums, raw_short = call(
         norm_kernel,
@@ -450,19 +474,26 @@
         [pltpu.VMEM((2, tokens, width), bf16), pltpu.SemaphoreType.DMA((3,))],
         2 * 3 * tokens * width,
     )(lengths, events, near, across, corner, norm_gain)
-    feats, message, weights = call(
+    partial, weights = call(
+        partial_kernel,
+        (shape((2 * tokens, wide), f32), shape((width, wide), bf16)),
+        [vmem()] * 7,
+        [],
+        2 * 2 * tokens * 3 * GROUP * wide,
+    )(normed, w_own, w_near, one_own, one_near, two_own, two_near)
+    feats, message, last = call(
         project_kernel,
-        (shape((2 * tokens, wide), bf16), shape((MESSAGE, HEAD_DIM), bf16), shape((width, wide), bf16)),
-        [vmem()] * 8,
+        (shape((2 * tokens, wide), bf16), shape((MESSAGE, HEAD_DIM), bf16), shape((GROUP, wide), bf16)),
+        [vmem()] * 5,
         [],
-        2 * 2 * tokens * width * wide,
-    )(normed, both, one, two_own, two_near, next_both, far_own, far_near)
+        2 * 2 * tokens * GROUP * wide,
+    )(normed, partial, next_both, far_own, far_near)
     short = call(
-        short_kernel, shape((1, GROUP), f32), [vmem()] * 3, [], 2 * tokens * width * wide
-    )(raw_short, weights, norm_gain)
+        short_kernel, shape((1, GROUP), f32), [vmem()] * 4, [], 2 * tokens * width * wide
+    )(raw_short, weights, last, norm_gain)
     part = call(
         pool_kernel,
-        shape((2 * here, 4, GROUP), f32),
+        shape((2 * here, 1, 2 * GROUP + HEAD_DIM), f32),
         [smem()] + [vmem()] * 7,
         [],
         2 * 9 * tokens * tokens * GROUP,
@@ -472,7 +503,7 @@
         loss_kernel,
         (shape((1, 1, width // 8), bf16), shape((1, 1), f32)),
         [smem(), vmem()],
-        [pltpu.VMEM((2, width), f32), pltpu.VMEM((2, width), f32)],
+        [pltpu.VMEM((1, width), f32)],
         2**14,
     )(positives, parts)
     return vec, loss

time: 63.6 us -> 63.5 us (level)
  waiting for transfers between devices: 21.4 us -> 25.2 us
  starting transfers between devices: 22.2 us -> 18.6 us
  blocking collectives: 11.7 us -> 10.9 us
    ppermute x10, waiting for transfers between devices: 19.2 us -> 23.9 us  [hop(): return lax.ppermute(a, ('seq', 'dp'), pairs)]
    ppermute x10, starting transfers between devices: 15.7 us -> 12 us  [hop(): return lax.ppermute(a, ('seq', 'dp'), pairs)]
    pallas_call x2 -> x6, Pallas kernels: 2.08 us -> 3.16 us  [the longest x1 1.31 us: towers(): call(short_kernel, shape((1, GROUP), f32), [vmem()] * 4, [], 2 * tokens *...]
    ppermute x4, waiting for transfers between devices: 2.15 us -> 1.24 us  [plane_hop(): return lax.ppermute(a, ('seq', 'dp'), [(i, i ^ move) for i in range(here)])]
    all_to_all x1, blocking collectives: 11.7 us -> 10.9 us  [towers(): parts = lax.all_to_all(part, ('seq', 'dp', 'domain'), 0, 0, tiled=True)]
  transfers between devices with their start and end apart: 14 -> 14, of which waited for: 8 -> 9; matrix products, arithmetic and copies ran while one was open for 0% -> 0% of each run, Pallas kernels for 3% -> 5%
where the time goes in v10:
time: 63.5 us; the launch traced here: 63.3 us
  waiting for transfers between devices  25.2 us (40%)
  starting transfers between devices  18.6 us (29%)
  blocking collectives  10.9 us (17%)
  Pallas kernels  5.99 us (9%)
  between operations  1.43 us (2%)
  local copies, waits for them, and re-layouts  1.15 us (2%)
    ppermute x10, waiting for transfers between devices, hop(): return lax.ppermute(a, ('seq', 'dp'), pairs)  23.9 us
    ppermute x10, starting transfers between devices, hop(): return lax.ppermute(a, ('seq', 'dp'), pairs)  12 us
    all_to_all x1, blocking collectives, towers(): parts = lax.all_to_all(part, ('seq', 'dp', 'domain'), 0, 0, tiled=True)  10.9 us
    ppermute x4, starting transfers between devices, plane_hop(): return lax.ppermute(a, ('seq', 'dp'), [(i, i ^ move) for i in range(here)])  6.61 us
    pallas_call x1, Pallas kernels, towers(): call(short_kernel, shape((1, GROUP), f32), [vmem()] * 4, [], 2 * tokens *...  1.31 us
  transfers between devices with their start and end apart: 14, of which 9 were waited for; matrix products, arithmetic and copies ran while one was open for 0% of the time, Pallas kernels for 5%

profile of v10, /device:TPU:0, one launch (start us, length us, event | category | flops | bytes accessed | tf_op | source)
XLA Modules:
  0.0 63.3 jit_solution(4919997131685268544)
XLA Ops:
  0.6 1.1 %copy-done = bf16[1,128,3072]{2,1,0:T(8,128)(2,1)S(1)} copy-done((bf16[1,128,3072]{2,1,0:T(8,128)(2,1)S(1)}, bf16[1,128,3072]{2,1,0:T(8,128)(2,1)}, u32[]{:S(2)}) %copy-start) | copy-done | bytes 786456
  1.9 3.0 %collective-permute-start.3 = (bf16[128,768]{1,0:T(8,128)(2,1)S(1)}, bf16[128,768]{1,0:T(8,128)(2,1)S(1)}, u32[]{:S(2)}, u32[]{:S(2)}) collective-permute-start(bf16[128,768]{1,0:T(8,128)(2,1)S(1)} %get-tuple-element.14), channel_id=1, source_target_pairs={{0,4},{2,6},{4,0},{6,2},{8,12},{10,14},{12,8},{14,10},{16,20},{18,... | collective-permute-start | bytes 589832 | tf_op jit(solution)/shard_map/ppermute | solution.py:448
  4.9 2.6 %collective-permute-start.6 = (bf16[128,768]{1,0:T(8,128)(2,1)S(1)}, bf16[128,768]{1,0:T(8,128)(2,1)S(1)}, u32[]{:S(2)}, u32[]{:S(2)}) collective-permute-start(bf16[128,768]{1,0:T(8,128)(2,1)S(1)} %get-tuple-element.13.own), channel_id=1, source_target_pairs={{0,16},{2,18},{4,20},{6,22},{8,24},{10,26},{12,28},{14,30},{16,0},... | collective-permute-start | bytes 589832 | tf_op jit(solution)/shard_map/ppermute | solution.py:445
  7.5 1.5 %collective-permute-start.2 = (bf16[256,1024]{1,0:T(8,128)(2,1)}, bf16[256,1024]{1,0:T(8,128)(2,1)S(1)}, u32[]{:S(2)}, u32[]{:S(2)}) collective-permute-start(bf16[256,1024]{1,0:T(8,128)(2,1)} %bitcast.3), channel_id=1, source_target_pairs={{0,6},{2,4},{4,2},{6,0},{8,14},{10,12},{12,10},{14,8},{16,22},{18,... | collective-permute-start | bytes 1572872 | tf_op jit(solution)/shard_map/ppermute | solution.py:448
  9.0 1.6 %collective-permute-start.4 = (bf16[128,768]{1,0:T(8,128)(2,1)S(1)}, bf16[128,768]{1,0:T(8,128)(2,1)S(1)}, u32[]{:S(2)}, u32[]{:S(2)}) collective-permute-start(bf16[128,768]{1,0:T(8,128)(2,1)S(1)} %get-tuple-element.13.own), channel_id=1, source_target_pairs={{0,8},{2,10},{4,12},{6,14},{8,0},{10,2},{12,4},{14,6},{16,24},{18,... | collective-permute-start | bytes 589832 | tf_op jit(solution)/shard_map/ppermute | solution.py:445
  10.6 5.9 %collective-permute-done.6.rest_0_.two_own = bf16[128,768]{1,0:T(8,128)(2,1)S(1)} collective-permute-done((bf16[128,768]{1,0:T(8,128)(2,1)S(1)}, bf16[128,768]{1,0:T(8,128)(2,1)S(1)}, u32[]{:S(2)}, u32[]{:S(2)}) %collective-permute-start.6) | collective-permute-done | bytes 196640 | tf_op jit(solution)/shard_map/ppermute | solution.py:445
  16.6 1.6 %collective-permute-start.1 = (bf16[256,1024]{1,0:T(8,128)(2,1)}, bf16[256,1024]{1,0:T(8,128)(2,1)S(1)}, u32[]{:S(2)}, u32[]{:S(2)}) collective-permute-start(bf16[256,1024]{1,0:T(8,128)(2,1)} %bitcast.4), channel_id=1, source_target_pairs={{0,2},{2,0},{4,6},{6,4},{8,10},{10,8},{12,14},{14,12},{16,18},{18,... | collective-permute-start | bytes 1572872 | tf_op jit(solution)/shard_map/ppermute | solution.py:448
  18.7 1.3 %collective-permute-start.9 = (bf16[128,768]{1,0:T(8,128)(2,1)S(1)}, bf16[128,768]{1,0:T(8,128)(2,1)S(1)}, u32[]{:S(2)}, u32[]{:S(2)}) collective-permute-start(bf16[128,768]{1,0:T(8,128)(2,1)S(1)} %collective-permute-done.6.rest_0_.two_own), channel_id=1, source_target_pairs={{8,0},{10,2},{12,4},{14,6},{16,24},{18,26},{20,28},{22,30},{9,1},{... | collective-permute-start | bytes 589832 | tf_op jit(solution)/shard_map/ppermute | solution.py:445
  20.1 7.4 %collective-permute-done.7.two_near.values = bf16[128,768]{1,0:T(8,128)(2,1)S(1)} collective-permute-done((bf16[128,768]{1,0:T(8,128)(2,1)S(1)}, bf16[128,768]{1,0:T(8,128)(2,1)S(1)}, u32[]{:S(2)}, u32[]{:S(2)}) %collective-permute-start.7) | collective-permute-done | bytes 196640 | tf_op jit(solution)/shard_map/ppermute | solution.py:445
  27.5 0.7 %collective-permute-start.8 = (bf16[256,768]{1,0:T(8,128)(2,1)S(1)}, bf16[256,768]{1,0:T(8,128)(2,1)S(1)}, u32[]{:S(2)}, u32[]{:S(2)}) collective-permute-start(bf16[256,768]{1,0:T(8,128)(2,1)S(1)} %shard_map.81), channel_id=1, source_target_pairs={{8,16},{10,18},{12,20},{14,22},{16,8},{18,10},{20,12},{22,14},{9,1... | collective-permute-start | bytes 1179656 | tf_op jit(solution)/shard_map/ppermute | solution.py:445
  28.1 2.2 %collective-permute-done.9.rest_0_.far_own = bf16[128,768]{1,0:T(8,128)(2,1)S(1)} collective-permute-done((bf16[128,768]{1,0:T(8,128)(2,1)S(1)}, bf16[128,768]{1,0:T(8,128)(2,1)S(1)}, u32[]{:S(2)}, u32[]{:S(2)}) %collective-permute-start.9) | collective-permute-done | bytes 196640 | tf_op jit(solution)/shard_map/ppermute | solution.py:445
  30.3 1.3 %collective-permute-start.10 = (bf16[128,768]{1,0:T(8,128)(2,1)S(1)}, bf16[128,768]{1,0:T(8,128)(2,1)S(1)}, u32[]{:S(2)}, u32[]{:S(2)}) collective-permute-start(bf16[128,768]{1,0:T(8,128)(2,1)S(1)} %shard_map.82), channel_id=1, source_target_pairs={{8,0},{10,2},{12,4},{14,6},{16,24},{18,26},{20,28},{22,30},{9,1},{... | collective-permute-start | bytes 589832 | tf_op jit(solution)/shard_map/ppermute | solution.py:445
  32.3 1.2 %collective-permute-done.1.across = bf16[256,1024]{1,0:T(8,128)(2,1)S(1)} collective-permute-done((bf16[256,1024]{1,0:T(8,128)(2,1)}, bf16[256,1024]{1,0:T(8,128)(2,1)S(1)}, u32[]{:S(2)}, u32[]{:S(2)}) %collective-permute-start.1) | collective-permute-done | bytes 524320 | tf_op jit(solution)/shard_map/ppermute | solution.py:448
  33.5 0.7 %shard_map.77 = (bf16[512,1024]{1,0:T(8,128)(2,1)S(1)}, f32[1,256]{1,0:T(1,128)S(1)}, bf16[256,1024]{1,0:T(8,128)(2,1)S(1)}) custom-call(s32[1,1]{1,0:T(1,128)S(6)} %copy.8.lengths, bf16[256,1024]{1,0:T(8,128)(2,1)S(1)} %bitcast.6, bf16[256,1024]{1,0:T(8,128)(2,1)S(1)} %collective-permute-done.near, bf16[256,1024]{1,0:T(8,128)(2,1)S(1)} %collective-permute-done.1.across, ...), custom_call_target="tpu_custom_call" | custom-call | flops 1572864 | bytes 2097152 | tf_op jit(solution)/shard_map/pallas_call | solution.py:470
  34.2 3.7 %collective-permute-done.5.one_near = bf16[128,768]{1,0:T(8,128)(2,1)S(1)} collective-permute-done((bf16[128,768]{1,0:T(8,128)(2,1)S(1)}, bf16[128,768]{1,0:T(8,128)(2,1)S(1)}, u32[]{:S(2)}, u32[]{:S(2)}) %collective-permute-start.5) | collective-permute-done | bytes 196640 | tf_op jit(solution)/shard_map/ppermute | solution.py:445
  37.9 0.9 %shard_map.80 = (f32[512,768]{1,0:T(8,128)S(1)}, bf16[1024,768]{1,0:T(8,128)(2,1)S(1)}) custom-call(bf16[512,1024]{1,0:T(8,128)(2,1)S(1)} %get-tuple-element.12.normed, bf16[128,768]{1,0:T(8,128)(2,1)S(1)} %get-tuple-element.13.own, bf16[128,768]{1,0:T(8,128)(2,1)S(1)} %collective-permute-done.3.values.near, ...), custom_call_target="tpu_custom_call" | custom-call | flops 603979776 | bytes 2097152 | tf_op jit(solution)/shard_map/pallas_call | solution.py:477
  38.8 1.2 %collective-permute-done.10.far_near = bf16[128,768]{1,0:T(8,128)(2,1)S(1)} collective-permute-done((bf16[128,768]{1,0:T(8,128)(2,1)S(1)}, bf16[128,768]{1,0:T(8,128)(2,1)S(1)}, u32[]{:S(2)}, u32[]{:S(2)}) %collective-permute-start.10) | collective-permute-done | bytes 196640 | tf_op jit(solution)/shard_map/ppermute | solution.py:445
  40.0 0.8 %shard_map.83 = (bf16[512,768]{1,0:T(8,128)(2,1)S(1)}, bf16[272,128]{1,0:T(8,128)(2,1)S(1)}, bf16[256,768]{1,0:T(8,128)(2,1)S(1)}) custom-call(bf16[512,1024]{1,0:T(8,128)(2,1)S(1)} %get-tuple-element.12.normed, f32[512,768]{1,0:T(8,128)S(1)} %get-tuple-element.15.partial, bf16[256,768]{1,0:T(8,128)(2,1)S(1)} %collective-permute-done.8.next_both, ...), custom_call_target="tpu_custom_call" | custom-call | flops 201326592 | bytes 2097152 | tf_op jit(solution)/shard_map/pallas_call | solution.py:484
  40.8 3.9 %collective-permute-start.13 = (bf16[272,128]{1,0:T(8,128)(2,1)S(1)}, bf16[272,128]{1,0:T(8,128)(2,1)S(1)}, u32[]{:S(2)}, u32[]{:S(2)}) collective-permute-start(bf16[272,128]{1,0:T(8,128)(2,1)S(1)} %get-tuple-element.16), channel_id=1, source_target_pairs={{0,24},{2,26},{4,28},{6,30},{8,16},{10,18},{12,20},{14,22},{16,8},... | collective-permute-start | bytes 208904 | tf_op jit(solution)/shard_map/ppermute | solution.py:445
  45.3 1.3 %shard_map.84.short = f32[1,256]{1,0:T(1,128)S(1)} custom-call(bf16[256,1024]{1,0:T(8,128)(2,1)S(1)} %get-tuple-element.19.raw, bf16[1024,768]{1,0:T(8,128)(2,1)S(1)} %get-tuple-element.20.weights, bf16[256,768]{1,0:T(8,128)(2,1)S(1)} %get-tuple-element.21.last, f32[1,1024]{1,0:T(1,128)S(1)} %copy-done.2), custom_call_target="tpu_custom_call" | custom-call | flops 402653184 | bytes 2097152 | tf_op jit(solution)/shard_map/pallas_call | solution.py:491
  47.2 2.8 %collective-permute-done.12.state_2 = bf16[272,128]{1,0:T(8,128)(2,1)S(1)} collective-permute-done((bf16[272,128]{1,0:T(8,128)(2,1)S(1)}, bf16[272,128]{1,0:T(8,128)(2,1)S(1)}, u32[]{:S(2)}, u32[]{:S(2)}) %collective-permute-start.12) | collective-permute-done | bytes 69664 | tf_op jit(solution)/shard_map/ppermute | solution.py:445
  50.3 0.9 %shard_map.85 = f32[32,1,640]{2,1,0:T(1,128)S(1)} custom-call(s32[1,1]{1,0:T(1,128)S(6)} %copy.8.lengths, bf16[272,128]{1,0:T(8,128)(2,1)S(1)} %collective-permute-done.11.state_1, bf16[272,128]{1,0:T(8,128)(2,1)S(1)} %collective-permute-done.12.state_2, bf16[272,128]{1,0:T(8,128)(2,1)S(1)} %collective-permute-done.13.state_3, ...), custom_call_target="tpu_custom_call" | custom-call | flops 301989888 | bytes 2097152 | tf_op jit(solution)/shard_map/pallas_call | solution.py:494
  51.2 10.9 %all_to_all.5.parts = f32[32,1,640]{2,1,0:T(1,128)S(1)} all-to-all(f32[32,1,640]{2,1,0:T(1,128)S(1)} %shard_map.85), channel_id=1, replica_groups=mesh['seq'=8,'dp'=2,'domain'=2] {'seq','dp','domain'}, dimensions={0} | all-to-all | bytes 163840 | tf_op jit(solution)/shard_map/all_to_all | solution.py:501
  62.1 1.2 %shard_map.86 = (bf16[1,1,128]{2,1,0:T(2,128)(2,1)}, f32[1,1]{1,0:T(1,128)}) custom-call(s32[2]{0:T(128)S(1)} %copy-done.3, f32[32,1,640]{2,1,0:T(1,128)S(1)} %all_to_all.5.parts), custom_call_target="tpu_custom_call" | custom-call | flops 16384 | bytes 2097152 | tf_op jit(solution)/shard_map/pallas_call | solution.py:502
  (26 shorter events, 2.3 us)
Async XLA Ops:
  0.6 1.1 %copy-start = (bf16[1,128,3072]{2,1,0:T(8,128)(2,1)S(1)}, bf16[1,128,3072]{2,1,0:T(8,128)(2,1)}, u32[]{:S(2)}) copy-start(bf16[1,128,3072]{2,1,0:T(8,128)(2,1)} %param.7) | copy-start | bytes 2359300
  1.9 31.6 %copy-start.1 = (bf16[1,1,256,1024]{3,2,1,0:T(8,128)(2,1)S(1)}, bf16[1,1,256,1024]{3,2,1,0:T(8,128)(2,1)}, u32[]{:S(2)}) copy-start(bf16[1,1,256,1024]{3,2,1,0:T(8,128)(2,1)} %param.6) | copy-start | bytes 1572868
  1.9 31.6 %copy-start.2 = (f32[1,1024]{1,0:T(1,128)S(1)}, f32[1,1024]{1,0:T(1,128)}, u32[]{:S(2)}) copy-start(f32[1,1024]{1,0:T(1,128)} %gain.4) | copy-start | bytes 12292
  1.9 8.7 %collective-permute-start.3 = (bf16[128,768]{1,0:T(8,128)(2,1)S(1)}, bf16[128,768]{1,0:T(8,128)(2,1)S(1)}, u32[]{:S(2)}, u32[]{:S(2)}) collective-permute-start(bf16[128,768]{1,0:T(8,128)(2,1)S(1)} %get-tuple-element.14), channel_id=1, source_target_pairs={{0,4},{2,6},{4,0},{6,2},{8,12},{10,14},{12,8},{14,10},{16,20},{18,... | collective-permute-start | bytes 589832 | tf_op jit(solution)/shard_map/ppermute | solution.py:448
  4.9 11.6 %collective-permute-start.6 = (bf16[128,768]{1,0:T(8,128)(2,1)S(1)}, bf16[128,768]{1,0:T(8,128)(2,1)S(1)}, u32[]{:S(2)}, u32[]{:S(2)}) collective-permute-start(bf16[128,768]{1,0:T(8,128)(2,1)S(1)} %get-tuple-element.13.own), channel_id=1, source_target_pairs={{0,16},{2,18},{4,20},{6,22},{8,24},{10,26},{12,28},{14,30},{16,0},... | collective-permute-start | bytes 589832 | tf_op jit(solution)/shard_map/ppermute | solution.py:445
  7.5 22.8 %collective-permute-start.2 = (bf16[256,1024]{1,0:T(8,128)(2,1)}, bf16[256,1024]{1,0:T(8,128)(2,1)S(1)}, u32[]{:S(2)}, u32[]{:S(2)}) collective-permute-start(bf16[256,1024]{1,0:T(8,128)(2,1)} %bitcast.3), channel_id=1, source_target_pairs={{0,6},{2,4},{4,2},{6,0},{8,14},{10,12},{12,10},{14,8},{16,22},{18,... | collective-permute-start | bytes 1572872 | tf_op jit(solution)/shard_map/ppermute | solution.py:448
  9.0 9.7 %collective-permute-start.4 = (bf16[128,768]{1,0:T(8,128)(2,1)S(1)}, bf16[128,768]{1,0:T(8,128)(2,1)S(1)}, u32[]{:S(2)}, u32[]{:S(2)}) collective-permute-start(bf16[128,768]{1,0:T(8,128)(2,1)S(1)} %get-tuple-element.13.own), channel_id=1, source_target_pairs={{0,8},{2,10},{4,12},{6,14},{8,0},{10,2},{12,4},{14,6},{16,24},{18,... | collective-permute-start | bytes 589832 | tf_op jit(solution)/shard_map/ppermute | solution.py:445
  16.5 10.9 %collective-permute-start.7 = (bf16[128,768]{1,0:T(8,128)(2,1)S(1)}, bf16[128,768]{1,0:T(8,128)(2,1)S(1)}, u32[]{:S(2)}, u32[]{:S(2)}) collective-permute-start(bf16[128,768]{1,0:T(8,128)(2,1)S(1)} %shard_map.79), channel_id=1, source_target_pairs={{0,16},{2,18},{4,20},{6,22},{8,24},{10,26},{12,28},{14,30},{16,0},... | collective-permute-start | bytes 589832 | tf_op jit(solution)/shard_map/ppermute | solution.py:445
  16.6 16.9 %collective-permute-start.1 = (bf16[256,1024]{1,0:T(8,128)(2,1)}, bf16[256,1024]{1,0:T(8,128)(2,1)S(1)}, u32[]{:S(2)}, u32[]{:S(2)}) collective-permute-start(bf16[256,1024]{1,0:T(8,128)(2,1)} %bitcast.4), channel_id=1, source_target_pairs={{0,2},{2,0},{4,6},{6,4},{8,10},{10,8},{12,14},{14,12},{16,18},{18,... | collective-permute-start | bytes 1572872 | tf_op jit(solution)/shard_map/ppermute | solution.py:448
  18.2 15.3 %collective-permute-start = (bf16[256,1024]{1,0:T(8,128)(2,1)}, bf16[256,1024]{1,0:T(8,128)(2,1)S(1)}, u32[]{:S(2)}, u32[]{:S(2)}) collective-permute-start(bf16[256,1024]{1,0:T(8,128)(2,1)} %bitcast.5), channel_id=1, source_target_pairs={{0,4},{2,6},{4,0},{6,2},{8,12},{10,14},{12,8},{14,10},{16,20},{18,... | collective-permute-start | bytes 1572872 | tf_op jit(solution)/shard_map/ppermute | solution.py:448
  18.7 11.6 %collective-permute-start.9 = (bf16[128,768]{1,0:T(8,128)(2,1)S(1)}, bf16[128,768]{1,0:T(8,128)(2,1)S(1)}, u32[]{:S(2)}, u32[]{:S(2)}) collective-permute-start(bf16[128,768]{1,0:T(8,128)(2,1)S(1)} %collective-permute-done.6.rest_0_.two_own), channel_id=1, source_target_pairs={{8,0},{10,2},{12,4},{14,6},{16,24},{18,26},{20,28},{22,30},{9,1},{... | collective-permute-start | bytes 589832 | tf_op jit(solution)/shard_map/ppermute | solution.py:445
  27.5 12.5 %collective-permute-start.8 = (bf16[256,768]{1,0:T(8,128)(2,1)S(1)}, bf16[256,768]{1,0:T(8,128)(2,1)S(1)}, u32[]{:S(2)}, u32[]{:S(2)}) collective-permute-start(bf16[256,768]{1,0:T(8,128)(2,1)S(1)} %shard_map.81), channel_id=1, source_target_pairs={{8,16},{10,18},{12,20},{14,22},{16,8},{18,10},{20,12},{22,14},{9,1... | collective-permute-start | bytes 1179656 | tf_op jit(solution)/shard_map/ppermute | solution.py:445
  30.3 7.6 %collective-permute-start.5 = (bf16[128,768]{1,0:T(8,128)(2,1)S(1)}, bf16[128,768]{1,0:T(8,128)(2,1)S(1)}, u32[]{:S(2)}, u32[]{:S(2)}) collective-permute-start(bf16[128,768]{1,0:T(8,128)(2,1)S(1)} %collective-permute-done.3.values.near), channel_id=1, source_target_pairs={{0,8},{2,10},{4,12},{6,14},{8,0},{10,2},{12,4},{14,6},{16,24},{18,... | collective-permute-start | bytes 589832 | tf_op jit(solution)/shard_map/ppermute | solution.py:445
  30.3 9.7 %collective-permute-start.10 = (bf16[128,768]{1,0:T(8,128)(2,1)S(1)}, bf16[128,768]{1,0:T(8,128)(2,1)S(1)}, u32[]{:S(2)}, u32[]{:S(2)}) collective-permute-start(bf16[128,768]{1,0:T(8,128)(2,1)S(1)} %shard_map.82), channel_id=1, source_target_pairs={{8,0},{10,2},{12,4},{14,6},{16,24},{18,26},{20,28},{22,30},{9,1},{... | collective-permute-start | bytes 589832 | tf_op jit(solution)/shard_map/ppermute | solution.py:445
  40.8 9.5 %copy-start.4 = (f32[1,1024]{1,0:T(1,128)S(1)}, f32[1,1024]{1,0:T(1,128)}, u32[]{:S(2)}) copy-start(f32[1,1024]{1,0:T(1,128)} %gain.5) | copy-start | bytes 12292
  40.8 6.3 %collective-permute-start.13 = (bf16[272,128]{1,0:T(8,128)(2,1)S(1)}, bf16[272,128]{1,0:T(8,128)(2,1)S(1)}, u32[]{:S(2)}, u32[]{:S(2)}) collective-permute-start(bf16[272,128]{1,0:T(8,128)(2,1)S(1)} %get-tuple-element.16), channel_id=1, source_target_pairs={{0,24},{2,26},{4,28},{6,30},{8,16},{10,18},{12,20},{14,22},{16,8},... | collective-permute-start | bytes 208904 | tf_op jit(solution)/shard_map/ppermute | solution.py:445
  44.7 5.3 %collective-permute-start.12 = (bf16[272,128]{1,0:T(8,128)(2,1)S(1)}, bf16[272,128]{1,0:T(8,128)(2,1)S(1)}, u32[]{:S(2)}, u32[]{:S(2)}) collective-permute-start(bf16[272,128]{1,0:T(8,128)(2,1)S(1)} %get-tuple-element.16), channel_id=1, source_target_pairs={{0,16},{2,18},{4,20},{6,22},{8,24},{10,26},{12,28},{14,30},{16,0},... | collective-permute-start | bytes 208904 | tf_op jit(solution)/shard_map/ppermute | solution.py:445
  44.7 5.6 %collective-permute-start.11 = (bf16[272,128]{1,0:T(8,128)(2,1)S(1)}, bf16[272,128]{1,0:T(8,128)(2,1)S(1)}, u32[]{:S(2)}, u32[]{:S(2)}) collective-permute-start(bf16[272,128]{1,0:T(8,128)(2,1)S(1)} %get-tuple-element.16), channel_id=1, source_target_pairs={{0,8},{2,10},{4,12},{6,14},{8,0},{10,2},{12,4},{14,6},{16,24},{18,... | collective-permute-start | bytes 208904 | tf_op jit(solution)/shard_map/ppermute | solution.py:445
  45.3 16.7 %copy-start.3 = (s32[2]{0:T(128)S(1)}, s32[2]{0:T(128)}, u32[]{:S(2)}) copy-start(s32[2]{0:T(128)} %positives.1) | copy-start | bytes 28

commit v11 on v10

--- a/solution.py
+++ b/solution.py
@@ -245,20 +245,10 @@
     partial[...] = total
 
 
-def project_kernel(normed, partial, next_both, far_own, far_near, feats, message, last):
+def project_kernel(normed, partial, far_own, far_near, feats, message, last):
     tokens = normed.shape[0]
-    rows = far_own.shape[0]
     z, x, _ = places()
-    inner = jnp.logical_or(z == 1, z == 2)
-
-    @pl.when(inner)
-    def _():
-        place_rows(last, 0, x, next_both[:rows, :], next_both[rows:, :])
-
-    @pl.when(jnp.logical_not(inner))
-    def _():
-        place_rows(last, 0, x, far_own[...], far_near[...])
-
+    place_rows(last, 0, x, far_own[...], far_near[...])
     columns = pl.ds(pl.multiple_of((3 - z) * GROUP, GROUP), GROUP)
     half = tokens // 2
     total = jnp.zeros((1, GROUP), jnp.float32)
@@ -454,18 +444,16 @@
     w_own, w_sent = call(
         pack_kernel, (shape((rows, wide), bf16),) * 2, [hbm()], [pltpu.SemaphoreType.DMA((6,))], 0
     )(weight)
+    across = plane_hop(events, 1)
     two_own = hop(w_own, lambda p: p ^ 2)
-    far_own = hop(two_own, lambda p: {1: 0, 2: 3}.get(p))
+    one_own = hop(w_own, lambda p: p ^ 1)
+    near = plane_hop(events, 2)
+    corner = plane_hop(events, 3)
     w_near = plane_hop(w_sent, 2)
-    two_near = hop(call(gate_kernel, shape((rows, wide), bf16), [vmem()] + [anywhere()] * 1, [], 0)(w_near, two_own), lambda p: p ^ 2)
-    one_near = hop(w_near, lambda p: p ^ 1)
-    far_near = hop(call(gate_kernel, shape((rows, wide), bf16), [vmem()] + [anywhere()] * 1, [], 0)(two_near, far_own), lambda p: {1: 0, 2: 3}.get(p))
-    both = jnp.concatenate([w_own, w_near], axis=0)
-    corner = plane_hop(events, 3)
-    near = plane_hop(events, 2)
-    one_own = hop(w_own, lambda p: p ^ 1)
-    next_both = hop(call(gate_kernel, shape((2 * rows, wide), bf16), [vmem()] + [anywhere()] * 1, [], 0)(both, one_own), lambda p: 3 - p if p in (1, 2) else None)
-    across = plane_hop(events, 1)
+    one_near = hop(call(gate_kernel, shape((rows, wide), bf16), [vmem()] + [anywhere()] * 1, [], 0)(w_near, one_own), lambda p: p ^ 1)
+    far_own = hop(call(gate_kernel, shape((rows, wide), bf16), [vmem()] + [anywhere()] * 1, [], 0)(two_own, one_near), lambda p: p ^ 1)
+    two_near = hop(w_near, lambda p: p ^ 2)
+    far_near = hop(call(gate_kernel, shape((rows, wide), bf16), [vmem()] + [anywhere()] * 1, [], 0)(two_near, one_near), lambda p: p ^ 1)
 
     normed, sums, raw_short = call(
         norm_kernel,
@@ -484,10 +472,10 @@
     feats, message, last = call(
         project_kernel,
         (shape((2 * tokens, wide), bf16), shape((MESSAGE, HEAD_DIM), bf16), shape((GROUP, wide), bf16)),
-        [vmem()] * 5,
+        [vmem()] * 4,
         [],
         2 * 2 * tokens * GROUP * wide,
-    )(normed, partial, next_both, far_own, far_near)
+    )(normed, partial, far_own, far_near)
     short = call(
         short_kernel, shape((1, GROUP), f32), [vmem()] * 4, [], 2 * tokens * width * wide
     )(raw_short, weights, last, norm_gain)

time: 63.5 us -> 59.2 us (0.932)
  waiting for transfers between devices: 25.2 us -> 22.6 us
  starting transfers between devices: 18.6 us -> 16.6 us
    ppermute x10 -> x9, waiting for transfers between devices: 23.9 us -> 16.6 us  [hop(): return lax.ppermute(a, ('seq', 'dp'), pairs)]
    ppermute x4, waiting for transfers between devices: 1.24 us -> 6.01 us  [plane_hop(): return lax.ppermute(a, ('seq', 'dp'), [(i, i ^ move) for i in range(here)])]
    ppermute x10 -> x9, starting transfers between devices: 12 us -> 10.1 us  [hop(): return lax.ppermute(a, ('seq', 'dp'), pairs)]
  transfers between devices with their start and end apart: 14 -> 13, of which waited for: 9 -> 8; matrix products, arithmetic and copies ran while one was open for 0% -> 0% of each run, Pallas kernels for 5% -> 5%
where the time goes in v11:
time: 59.2 us; the launch traced here: 59 us
  waiting for transfers between devices  22.6 us (38%)
  starting transfers between devices  16.6 us (28%)
  blocking collectives  11.3 us (19%)
  Pallas kernels  5.95 us (10%)
  between operations  1.41 us (2%)
  local copies, waits for them, and re-layouts  1.14 us (2%)
    ppermute x9, waiting for transfers between devices, hop(): return lax.ppermute(a, ('seq', 'dp'), pairs)  16.6 us
    all_to_all x1, blocking collectives, towers(): parts = lax.all_to_all(part, ('seq', 'dp', 'domain'), 0, 0, tiled=True)  11.3 us
    ppermute x9, starting transfers between devices, hop(): return lax.ppermute(a, ('seq', 'dp'), pairs)  10.1 us
    ppermute x4, starting transfers between devices, plane_hop(): return lax.ppermute(a, ('seq', 'dp'), [(i, i ^ move) for i in range(here)])  6.49 us
    ppermute x4, waiting for transfers between devices, plane_hop(): return lax.ppermute(a, ('seq', 'dp'), [(i, i ^ move) for i in range(here)])  6.01 us
    pallas_call x1, Pallas kernels, towers(): call(short_kernel, shape((1, GROUP), f32), [vmem()] * 4, [], 2 * tokens *...  1.31 us
    pallas_call x1, Pallas kernels, towers(): call(loss_kernel, (shape((1, 1, width // 8), bf16), shape((1, 1), f32)),...  1.19 us
  transfers between devices with their start and end apart: 13, of which 8 were waited for; matrix products, arithmetic and copies ran while one was open for 0% of the time, Pallas kernels for 5%

profile of v11, /device:TPU:0, one launch (start us, length us, event | category | flops | bytes accessed | tf_op | source)
XLA Modules:
  0.0 59.0 jit_solution(7496092430174991204)
XLA Ops:
  0.6 1.1 %copy-done = bf16[1,128,3072]{2,1,0:T(8,128)(2,1)S(1)} copy-done((bf16[1,128,3072]{2,1,0:T(8,128)(2,1)S(1)}, bf16[1,128,3072]{2,1,0:T(8,128)(2,1)}, u32[]{:S(2)}) %copy-start) | copy-done | bytes 786456
  1.9 3.0 %collective-permute-start.3 = (bf16[128,768]{1,0:T(8,128)(2,1)S(1)}, bf16[128,768]{1,0:T(8,128)(2,1)S(1)}, u32[]{:S(2)}, u32[]{:S(2)}) collective-permute-start(bf16[128,768]{1,0:T(8,128)(2,1)S(1)} %get-tuple-element.14), channel_id=1, source_target_pairs={{0,4},{2,6},{4,0},{6,2},{8,12},{10,14},{12,8},{14,10},{16,20},{18,... | collective-permute-start | bytes 589832 | tf_op jit(solution)/shard_map/ppermute | solution.py:438
  4.9 1.6 %collective-permute-start.4 = (bf16[128,768]{1,0:T(8,128)(2,1)S(1)}, bf16[128,768]{1,0:T(8,128)(2,1)S(1)}, u32[]{:S(2)}, u32[]{:S(2)}) collective-permute-start(bf16[128,768]{1,0:T(8,128)(2,1)S(1)} %get-tuple-element.13.own), channel_id=1, source_target_pairs={{0,8},{2,10},{4,12},{6,14},{8,0},{10,2},{12,4},{14,6},{16,24},{18,... | collective-permute-start | bytes 589832 | tf_op jit(solution)/shard_map/ppermute | solution.py:435
  6.5 2.6 %collective-permute-start.6 = (bf16[128,768]{1,0:T(8,128)(2,1)S(1)}, bf16[128,768]{1,0:T(8,128)(2,1)S(1)}, u32[]{:S(2)}, u32[]{:S(2)}) collective-permute-start(bf16[128,768]{1,0:T(8,128)(2,1)S(1)} %get-tuple-element.13.own), channel_id=1, source_target_pairs={{0,16},{2,18},{4,20},{6,22},{8,24},{10,26},{12,28},{14,30},{16,0},... | collective-permute-start | bytes 589832 | tf_op jit(solution)/shard_map/ppermute | solution.py:435
  9.1 1.5 %collective-permute-start.2 = (bf16[256,1024]{1,0:T(8,128)(2,1)}, bf16[256,1024]{1,0:T(8,128)(2,1)S(1)}, u32[]{:S(2)}, u32[]{:S(2)}) collective-permute-start(bf16[256,1024]{1,0:T(8,128)(2,1)} %bitcast.3), channel_id=1, source_target_pairs={{0,6},{2,4},{4,2},{6,0},{8,14},{10,12},{12,10},{14,8},{16,22},{18,... | collective-permute-start | bytes 1572872 | tf_op jit(solution)/shard_map/ppermute | solution.py:438
  10.6 0.5 collective-permute-start.1
  11.1 1.5 %collective-permute-start = (bf16[256,1024]{1,0:T(8,128)(2,1)}, bf16[256,1024]{1,0:T(8,128)(2,1)S(1)}, u32[]{:S(2)}, u32[]{:S(2)}) collective-permute-start(bf16[256,1024]{1,0:T(8,128)(2,1)} %bitcast.5), channel_id=1, source_target_pairs={{0,4},{2,6},{4,0},{6,2},{8,12},{10,14},{12,8},{14,10},{16,20},{18,... | collective-permute-start | bytes 1572872 | tf_op jit(solution)/shard_map/ppermute | solution.py:438
  12.6 2.8 %collective-permute-done.4.rest_0_.one_own = bf16[128,768]{1,0:T(8,128)(2,1)S(1)} collective-permute-done((bf16[128,768]{1,0:T(8,128)(2,1)S(1)}, bf16[128,768]{1,0:T(8,128)(2,1)S(1)}, u32[]{:S(2)}, u32[]{:S(2)}) %collective-permute-start.4) | collective-permute-done | bytes 196640 | tf_op jit(solution)/shard_map/ppermute | solution.py:435
  15.5 2.4 %collective-permute-done.6.two_own.values = bf16[128,768]{1,0:T(8,128)(2,1)S(1)} collective-permute-done((bf16[128,768]{1,0:T(8,128)(2,1)S(1)}, bf16[128,768]{1,0:T(8,128)(2,1)S(1)}, u32[]{:S(2)}, u32[]{:S(2)}) %collective-permute-start.6) | collective-permute-done | bytes 196640 | tf_op jit(solution)/shard_map/ppermute | solution.py:435
  17.8 1.3 %collective-permute-start.7 = (bf16[128,768]{1,0:T(8,128)(2,1)S(1)}, bf16[128,768]{1,0:T(8,128)(2,1)S(1)}, u32[]{:S(2)}, u32[]{:S(2)}) collective-permute-start(bf16[128,768]{1,0:T(8,128)(2,1)S(1)} %collective-permute-done.3.values.near), channel_id=1, source_target_pairs={{0,16},{2,18},{4,20},{6,22},{8,24},{10,26},{12,28},{14,30},{16,0},... | collective-permute-start | bytes 589832 | tf_op jit(solution)/shard_map/ppermute | solution.py:435
  19.1 5.3 %collective-permute-done.5.one_near.rest_0_ = bf16[128,768]{1,0:T(8,128)(2,1)S(1)} collective-permute-done((bf16[128,768]{1,0:T(8,128)(2,1)S(1)}, bf16[128,768]{1,0:T(8,128)(2,1)S(1)}, u32[]{:S(2)}, u32[]{:S(2)}) %collective-permute-start.5) | collective-permute-done | bytes 196640 | tf_op jit(solution)/shard_map/ppermute | solution.py:435
  24.6 3.0 %collective-permute-done.7.two_near.values = bf16[128,768]{1,0:T(8,128)(2,1)S(1)} collective-permute-done((bf16[128,768]{1,0:T(8,128)(2,1)S(1)}, bf16[128,768]{1,0:T(8,128)(2,1)S(1)}, u32[]{:S(2)}, u32[]{:S(2)}) %collective-permute-start.7) | collective-permute-done | bytes 196640 | tf_op jit(solution)/shard_map/ppermute | solution.py:435
  28.3 5.9 %collective-permute-done.1.across = bf16[256,1024]{1,0:T(8,128)(2,1)S(1)} collective-permute-done((bf16[256,1024]{1,0:T(8,128)(2,1)}, bf16[256,1024]{1,0:T(8,128)(2,1)S(1)}, u32[]{:S(2)}, u32[]{:S(2)}) %collective-permute-start.1) | collective-permute-done | bytes 524320 | tf_op jit(solution)/shard_map/ppermute | solution.py:438
  34.3 0.7 %shard_map.77 = (bf16[512,1024]{1,0:T(8,128)(2,1)S(1)}, f32[1,256]{1,0:T(1,128)S(1)}, bf16[256,1024]{1,0:T(8,128)(2,1)S(1)}) custom-call(s32[1,1]{1,0:T(1,128)S(6)} %copy.8.lengths, bf16[256,1024]{1,0:T(8,128)(2,1)S(1)} %bitcast.6, bf16[256,1024]{1,0:T(8,128)(2,1)S(1)} %collective-permute-done.near, bf16[256,1024]{1,0:T(8,128)(2,1)S(1)} %collective-permute-done.1.across, ...), custom_call_target="tpu_custom_call" | custom-call | flops 1572864 | bytes 2097152 | tf_op jit(solution)/shard_map/pallas_call | solution.py:458
  35.0 0.9 %shard_map.80 = (f32[512,768]{1,0:T(8,128)S(1)}, bf16[1024,768]{1,0:T(8,128)(2,1)S(1)}) custom-call(bf16[512,1024]{1,0:T(8,128)(2,1)S(1)} %get-tuple-element.12.normed, bf16[128,768]{1,0:T(8,128)(2,1)S(1)} %get-tuple-element.13.own, bf16[128,768]{1,0:T(8,128)(2,1)S(1)} %collective-permute-done.3.values.near, ...), custom_call_target="tpu_custom_call" | custom-call | flops 603979776 | bytes 2097152 | tf_op jit(solution)/shard_map/pallas_call | solution.py:465
  35.9 0.8 %shard_map.83 = (bf16[512,768]{1,0:T(8,128)(2,1)S(1)}, bf16[272,128]{1,0:T(8,128)(2,1)S(1)}, bf16[256,768]{1,0:T(8,128)(2,1)S(1)}) custom-call(bf16[512,1024]{1,0:T(8,128)(2,1)S(1)} %get-tuple-element.12.normed, f32[512,768]{1,0:T(8,128)S(1)} %get-tuple-element.15.partial, bf16[128,768]{1,0:T(8,128)(2,1)S(1)} %collective-permute-done.8.far_own, ...), custom_call_target="tpu_custom_call" | custom-call | flops 201326592 | bytes 2097152 | tf_op jit(solution)/shard_map/pallas_call | solution.py:472
  36.8 1.9 %collective-permute-start.12 = (bf16[272,128]{1,0:T(8,128)(2,1)S(1)}, bf16[272,128]{1,0:T(8,128)(2,1)S(1)}, u32[]{:S(2)}, u32[]{:S(2)}) collective-permute-start(bf16[272,128]{1,0:T(8,128)(2,1)S(1)} %get-tuple-element.16), channel_id=1, source_target_pairs={{0,24},{2,26},{4,28},{6,30},{8,16},{10,18},{12,20},{14,22},{16,8},... | collective-permute-start | bytes 208904 | tf_op jit(solution)/shard_map/ppermute | solution.py:435
  38.9 2.4 %collective-permute-start.10 = (bf16[272,128]{1,0:T(8,128)(2,1)S(1)}, bf16[272,128]{1,0:T(8,128)(2,1)S(1)}, u32[]{:S(2)}, u32[]{:S(2)}) collective-permute-start(bf16[272,128]{1,0:T(8,128)(2,1)S(1)} %get-tuple-element.16), channel_id=1, source_target_pairs={{0,8},{2,10},{4,12},{6,14},{8,0},{10,2},{12,4},{14,6},{16,24},{18,... | collective-permute-start | bytes 208904 | tf_op jit(solution)/shard_map/ppermute | solution.py:435
  41.3 1.3 %shard_map.84.short = f32[1,256]{1,0:T(1,128)S(1)} custom-call(bf16[256,1024]{1,0:T(8,128)(2,1)S(1)} %get-tuple-element.19.raw, bf16[1024,768]{1,0:T(8,128)(2,1)S(1)} %get-tuple-element.20.weights, bf16[256,768]{1,0:T(8,128)(2,1)S(1)} %get-tuple-element.21.last, f32[1,1024]{1,0:T(1,128)S(1)} %copy-done.2), custom_call_target="tpu_custom_call" | custom-call | flops 402653184 | bytes 2097152 | tf_op jit(solution)/shard_map/pallas_call | solution.py:479
  42.6 1.1 %collective-permute-done.12.state_3 = bf16[272,128]{1,0:T(8,128)(2,1)S(1)} collective-permute-done((bf16[272,128]{1,0:T(8,128)(2,1)S(1)}, bf16[272,128]{1,0:T(8,128)(2,1)S(1)}, u32[]{:S(2)}, u32[]{:S(2)}) %collective-permute-start.12) | collective-permute-done | bytes 69664 | tf_op jit(solution)/shard_map/ppermute | solution.py:435
  43.7 1.9 %collective-permute-done.11.state_2 = bf16[272,128]{1,0:T(8,128)(2,1)S(1)} collective-permute-done((bf16[272,128]{1,0:T(8,128)(2,1)S(1)}, bf16[272,128]{1,0:T(8,128)(2,1)S(1)}, u32[]{:S(2)}, u32[]{:S(2)}) %collective-permute-start.11) | collective-permute-done | bytes 69664 | tf_op jit(solution)/shard_map/ppermute | solution.py:435
  45.7 0.9 %shard_map.85 = f32[32,1,640]{2,1,0:T(1,128)S(1)} custom-call(s32[1,1]{1,0:T(1,128)S(6)} %copy.8.lengths, bf16[272,128]{1,0:T(8,128)(2,1)S(1)} %collective-permute-done.10.state_1, bf16[272,128]{1,0:T(8,128)(2,1)S(1)} %collective-permute-done.11.state_2, bf16[272,128]{1,0:T(8,128)(2,1)S(1)} %collective-permute-done.12.state_3, ...), custom_call_target="tpu_custom_call" | custom-call | flops 301989888 | bytes 2097152 | tf_op jit(solution)/shard_map/pallas_call | solution.py:482
  46.6 11.3 %all_to_all.5.parts = f32[32,1,640]{2,1,0:T(1,128)S(1)} all-to-all(f32[32,1,640]{2,1,0:T(1,128)S(1)} %shard_map.85), channel_id=1, replica_groups=mesh['seq'=8,'dp'=2,'domain'=2] {'seq','dp','domain'}, dimensions={0} | all-to-all | bytes 163840 | tf_op jit(solution)/shard_map/all_to_all | solution.py:489
  57.9 1.2 %shard_map.86 = (bf16[1,1,128]{2,1,0:T(2,128)(2,1)}, f32[1,1]{1,0:T(1,128)}) custom-call(s32[2]{0:T(128)S(1)} %copy-done.3, f32[32,1,640]{2,1,0:T(1,128)S(1)} %all_to_all.5.parts), custom_call_target="tpu_custom_call" | custom-call | flops 16384 | bytes 2097152 | tf_op jit(solution)/shard_map/pallas_call | solution.py:490
  (23 shorter events, 0.7 us)
Async XLA Ops:
  0.6 1.1 %copy-start = (bf16[1,128,3072]{2,1,0:T(8,128)(2,1)S(1)}, bf16[1,128,3072]{2,1,0:T(8,128)(2,1)}, u32[]{:S(2)}) copy-start(bf16[1,128,3072]{2,1,0:T(8,128)(2,1)} %param.7) | copy-start | bytes 2359300
  1.8 32.6 %copy-start.1 = (bf16[1,1,256,1024]{3,2,1,0:T(8,128)(2,1)S(1)}, bf16[1,1,256,1024]{3,2,1,0:T(8,128)(2,1)}, u32[]{:S(2)}) copy-start(bf16[1,1,256,1024]{3,2,1,0:T(8,128)(2,1)} %param.6) | copy-start | bytes 1572868
  1.8 32.6 %copy-start.2 = (f32[1,1024]{1,0:T(1,128)S(1)}, f32[1,1024]{1,0:T(1,128)}, u32[]{:S(2)}) copy-start(f32[1,1024]{1,0:T(1,128)} %gain.4) | copy-start | bytes 12292
  1.9 9.2 %collective-permute-start.3 = (bf16[128,768]{1,0:T(8,128)(2,1)S(1)}, bf16[128,768]{1,0:T(8,128)(2,1)S(1)}, u32[]{:S(2)}, u32[]{:S(2)}) collective-permute-start(bf16[128,768]{1,0:T(8,128)(2,1)S(1)} %get-tuple-element.14), channel_id=1, source_target_pairs={{0,4},{2,6},{4,0},{6,2},{8,12},{10,14},{12,8},{14,10},{16,20},{18,... | collective-permute-start | bytes 589832 | tf_op jit(solution)/shard_map/ppermute | solution.py:438
  4.9 10.5 %collective-permute-start.4 = (bf16[128,768]{1,0:T(8,128)(2,1)S(1)}, bf16[128,768]{1,0:T(8,128)(2,1)S(1)}, u32[]{:S(2)}, u32[]{:S(2)}) collective-permute-start(bf16[128,768]{1,0:T(8,128)(2,1)S(1)} %get-tuple-element.13.own), channel_id=1, source_target_pairs={{0,8},{2,10},{4,12},{6,14},{8,0},{10,2},{12,4},{14,6},{16,24},{18,... | collective-permute-start | bytes 589832 | tf_op jit(solution)/shard_map/ppermute | solution.py:435
  6.5 11.3 %collective-permute-start.6 = (bf16[128,768]{1,0:T(8,128)(2,1)S(1)}, bf16[128,768]{1,0:T(8,128)(2,1)S(1)}, u32[]{:S(2)}, u32[]{:S(2)}) collective-permute-start(bf16[128,768]{1,0:T(8,128)(2,1)S(1)} %get-tuple-element.13.own), channel_id=1, source_target_pairs={{0,16},{2,18},{4,20},{6,22},{8,24},{10,26},{12,28},{14,30},{16,0},... | collective-permute-start | bytes 589832 | tf_op jit(solution)/shard_map/ppermute | solution.py:435
  9.1 19.3 %collective-permute-start.2 = (bf16[256,1024]{1,0:T(8,128)(2,1)}, bf16[256,1024]{1,0:T(8,128)(2,1)S(1)}, u32[]{:S(2)}, u32[]{:S(2)}) collective-permute-start(bf16[256,1024]{1,0:T(8,128)(2,1)} %bitcast.3), channel_id=1, source_target_pairs={{0,6},{2,4},{4,2},{6,0},{8,14},{10,12},{12,10},{14,8},{16,22},{18,... | collective-permute-start | bytes 1572872 | tf_op jit(solution)/shard_map/ppermute | solution.py:438
  10.6 23.7 %collective-permute-start.1 = (bf16[256,1024]{1,0:T(8,128)(2,1)}, bf16[256,1024]{1,0:T(8,128)(2,1)S(1)}, u32[]{:S(2)}, u32[]{:S(2)}) collective-permute-start(bf16[256,1024]{1,0:T(8,128)(2,1)} %bitcast.4), channel_id=1, source_target_pairs={{0,2},{2,0},{4,6},{6,4},{8,10},{10,8},{12,14},{14,12},{16,18},{18,... | collective-permute-start | bytes 1572872 | tf_op jit(solution)/shard_map/ppermute | solution.py:438
  11.1 23.3 %collective-permute-start = (bf16[256,1024]{1,0:T(8,128)(2,1)}, bf16[256,1024]{1,0:T(8,128)(2,1)S(1)}, u32[]{:S(2)}, u32[]{:S(2)}) collective-permute-start(bf16[256,1024]{1,0:T(8,128)(2,1)} %bitcast.5), channel_id=1, source_target_pairs={{0,4},{2,6},{4,0},{6,2},{8,12},{10,14},{12,8},{14,10},{16,20},{18,... | collective-permute-start | bytes 1572872 | tf_op jit(solution)/shard_map/ppermute | solution.py:438
  15.4 9.1 %collective-permute-start.5 = (bf16[128,768]{1,0:T(8,128)(2,1)S(1)}, bf16[128,768]{1,0:T(8,128)(2,1)S(1)}, u32[]{:S(2)}, u32[]{:S(2)}) collective-permute-start(bf16[128,768]{1,0:T(8,128)(2,1)S(1)} %shard_map.79), channel_id=1, source_target_pairs={{0,8},{2,10},{4,12},{6,14},{8,0},{10,2},{12,4},{14,6},{16,24},{18,... | collective-permute-start | bytes 589832 | tf_op jit(solution)/shard_map/ppermute | solution.py:435
  17.8 9.8 %collective-permute-start.7 = (bf16[128,768]{1,0:T(8,128)(2,1)S(1)}, bf16[128,768]{1,0:T(8,128)(2,1)S(1)}, u32[]{:S(2)}, u32[]{:S(2)}) collective-permute-start(bf16[128,768]{1,0:T(8,128)(2,1)S(1)} %collective-permute-done.3.values.near), channel_id=1, source_target_pairs={{0,16},{2,18},{4,20},{6,22},{8,24},{10,26},{12,28},{14,30},{16,0},... | collective-permute-start | bytes 589832 | tf_op jit(solution)/shard_map/ppermute | solution.py:435
  24.5 11.4 %collective-permute-start.8 = (bf16[128,768]{1,0:T(8,128)(2,1)S(1)}, bf16[128,768]{1,0:T(8,128)(2,1)S(1)}, u32[]{:S(2)}, u32[]{:S(2)}) collective-permute-start(bf16[128,768]{1,0:T(8,128)(2,1)S(1)} %shard_map.81), channel_id=1, source_target_pairs={{0,8},{2,10},{4,12},{6,14},{8,0},{10,2},{12,4},{14,6},{16,24},{18,... | collective-permute-start | bytes 589832 | tf_op jit(solution)/shard_map/ppermute | solution.py:435
  27.6 8.3 %collective-permute-start.9 = (bf16[128,768]{1,0:T(8,128)(2,1)S(1)}, bf16[128,768]{1,0:T(8,128)(2,1)S(1)}, u32[]{:S(2)}, u32[]{:S(2)}) collective-permute-start(bf16[128,768]{1,0:T(8,128)(2,1)S(1)} %shard_map.82), channel_id=1, source_target_pairs={{0,8},{2,10},{4,12},{6,14},{8,0},{10,2},{12,4},{14,6},{16,24},{18,... | collective-permute-start | bytes 589832 | tf_op jit(solution)/shard_map/ppermute | solution.py:435
  36.8 8.9 %copy-start.4 = (f32[1,1024]{1,0:T(1,128)S(1)}, f32[1,1024]{1,0:T(1,128)}, u32[]{:S(2)}) copy-start(f32[1,1024]{1,0:T(1,128)} %gain.5) | copy-start | bytes 12292
  36.8 6.9 %collective-permute-start.12 = (bf16[272,128]{1,0:T(8,128)(2,1)S(1)}, bf16[272,128]{1,0:T(8,128)(2,1)S(1)}, u32[]{:S(2)}, u32[]{:S(2)}) collective-permute-start(bf16[272,128]{1,0:T(8,128)(2,1)S(1)} %get-tuple-element.16), channel_id=1, source_target_pairs={{0,24},{2,26},{4,28},{6,30},{8,16},{10,18},{12,20},{14,22},{16,8},... | collective-permute-start | bytes 208904 | tf_op jit(solution)/shard_map/ppermute | solution.py:435
  38.7 7.0 %collective-permute-start.11 = (bf16[272,128]{1,0:T(8,128)(2,1)S(1)}, bf16[272,128]{1,0:T(8,128)(2,1)S(1)}, u32[]{:S(2)}, u32[]{:S(2)}) collective-permute-start(bf16[272,128]{1,0:T(8,128)(2,1)S(1)} %get-tuple-element.16), channel_id=1, source_target_pairs={{0,16},{2,18},{4,20},{6,22},{8,24},{10,26},{12,28},{14,30},{16,0},... | collective-permute-start | bytes 208904 | tf_op jit(solution)/shard_map/ppermute | solution.py:435
  38.9 6.8 %collective-permute-start.10 = (bf16[272,128]{1,0:T(8,128)(2,1)S(1)}, bf16[272,128]{1,0:T(8,128)(2,1)S(1)}, u32[]{:S(2)}, u32[]{:S(2)}) collective-permute-start(bf16[272,128]{1,0:T(8,128)(2,1)S(1)} %get-tuple-element.16), channel_id=1, source_target_pairs={{0,8},{2,10},{4,12},{6,14},{8,0},{10,2},{12,4},{14,6},{16,24},{18,... | collective-permute-start | bytes 208904 | tf_op jit(solution)/shard_map/ppermute | solution.py:435
  41.3 16.6 %copy-start.3 = (s32[2]{0:T(128)S(1)}, s32[2]{0:T(128)}, u32[]{:S(2)}) copy-start(s32[2]{0:T(128)} %positives.1) | copy-start | bytes 28

commit v12 on v11

--- a/solution.py
+++ b/solution.py
@@ -444,16 +444,16 @@
     w_own, w_sent = call(
         pack_kernel, (shape((rows, wide), bf16),) * 2, [hbm()], [pltpu.SemaphoreType.DMA((6,))], 0
     )(weight)
-    across = plane_hop(events, 1)
+    w_near = plane_hop(w_sent, 2)
+    two_near = hop(w_near, lambda p: p ^ 2)
+    corner = plane_hop(events, 3)
+    across = plane_hop(call(gate_kernel, shape((tokens, width), bf16), [vmem()] + [anywhere()] * 1, [], 0)(events, w_sent), 1)
     two_own = hop(w_own, lambda p: p ^ 2)
     one_own = hop(w_own, lambda p: p ^ 1)
-    near = plane_hop(events, 2)
-    corner = plane_hop(events, 3)
-    w_near = plane_hop(w_sent, 2)
+    near = plane_hop(call(gate_kernel, shape((tokens, width), bf16), [vmem()] + [anywhere()] * 1, [], 0)(events, one_own), 2)
     one_near = hop(call(gate_kernel, shape((rows, wide), bf16), [vmem()] + [anywhere()] * 1, [], 0)(w_near, one_own), lambda p: p ^ 1)
+    far_near = hop(call(gate_kernel, shape((rows, wide), bf16), [vmem()] + [anywhere()] * 1, [], 0)(two_near, one_near), lambda p: p ^ 1)
     far_own = hop(call(gate_kernel, shape((rows, wide), bf16), [vmem()] + [anywhere()] * 1, [], 0)(two_own, one_near), lambda p: p ^ 1)
-    two_near = hop(w_near, lambda p: p ^ 2)
-    far_near = hop(call(gate_kernel, shape((rows, wide), bf16), [vmem()] + [anywhere()] * 1, [], 0)(two_near, one_near), lambda p: p ^ 1)
 
     normed, sums, raw_short = call(
         norm_kernel,

time: 59.2 us -> 59.2 us (level)
  waiting for transfers between devices: 22.6 us -> 19.7 us
  starting transfers between devices: 16.6 us -> 18.7 us
  local copies, waits for them, and re-layouts: 1.14 us -> 2.28 us
    ppermute x9, waiting for transfers between devices: 16.6 us -> 13.7 us  [hop(): return lax.ppermute(a, ('seq', 'dp'), pairs)]
    ppermute x9, starting transfers between devices: 10.1 us -> 12 us  [hop(): return lax.ppermute(a, ('seq', 'dp'), pairs)]
    unnamed x10 -> x12, local copies, waits for them, and re-layouts: 1.14 us -> 2.28 us
  transfers between devices with their start and end apart: 13 -> 13, of which waited for: 8 -> 6; matrix products, arithmetic and copies ran while one was open for 0% -> 0% of each run, Pallas kernels for 5% -> 5%
where the time goes in v12:
time: 59.2 us; the launch traced here: 58.9 us
  waiting for transfers between devices  19.7 us (33%)
  starting transfers between devices  18.7 us (32%)
  blocking collectives  10.8 us (18%)
  Pallas kernels  6.05 us (10%)
  local copies, waits for them, and re-layouts  2.28 us (4%)
  between operations  1.42 us (2%)
    ppermute x9, waiting for transfers between devices, hop(): return lax.ppermute(a, ('seq', 'dp'), pairs)  13.7 us
    ppermute x9, starting transfers between devices, hop(): return lax.ppermute(a, ('seq', 'dp'), pairs)  12 us
    all_to_all x1, blocking collectives, towers(): parts = lax.all_to_all(part, ('seq', 'dp', 'domain'), 0, 0, tiled=True)  10.8 us
    ppermute x4, starting transfers between devices, plane_hop(): return lax.ppermute(a, ('seq', 'dp'), [(i, i ^ move) for i in range(here)])  6.75 us
    ppermute x4, waiting for transfers between devices, plane_hop(): return lax.ppermute(a, ('seq', 'dp'), [(i, i ^ move) for i in range(here)])  6 us
    unnamed x12, local copies, waits for them, and re-layouts  2.28 us
    pallas_call x1, Pallas kernels, towers(): call(short_kernel, shape((1, GROUP), f32), [vmem()] * 4, [], 2 * tokens *...  1.31 us
    pallas_call x1, Pallas kernels, towers(): call(loss_kernel, (shape((1, 1, width // 8), bf16), shape((1, 1), f32)),...  1.19 us
  transfers between devices with their start and end apart: 13, of which 6 were waited for; matrix products, arithmetic and copies ran while one was open for 0% of the time, Pallas kernels for 5%

profile of v12, /device:TPU:0, one launch (start us, length us, event | category | flops | bytes accessed | tf_op | source)
XLA Modules:
  0.0 58.9 jit_solution(12011662076474864425)
XLA Ops:
  0.7 1.2 %copy-done.2 = bf16[1,128,3072]{2,1,0:T(8,128)(2,1)S(1)} copy-done((bf16[1,128,3072]{2,1,0:T(8,128)(2,1)S(1)}, bf16[1,128,3072]{2,1,0:T(8,128)(2,1)}, u32[]{:S(2)}) %copy-start.2) | copy-done | bytes 786456
  2.0 3.1 %collective-permute-start = (bf16[128,768]{1,0:T(8,128)(2,1)S(1)}, bf16[128,768]{1,0:T(8,128)(2,1)S(1)}, u32[]{:S(2)}, u32[]{:S(2)}) collective-permute-start(bf16[128,768]{1,0:T(8,128)(2,1)S(1)} %get-tuple-element.12.own), channel_id=1, source_target_pairs={{0,8},{2,10},{4,12},{6,14},{8,0},{10,2},{12,4},{14,6},{16,24},{18,... | collective-permute-start | bytes 589832 | tf_op jit(solution)/shard_map/ppermute | solution.py:435
  5.1 1.5 %collective-permute-start.4 = (bf16[128,768]{1,0:T(8,128)(2,1)S(1)}, bf16[128,768]{1,0:T(8,128)(2,1)S(1)}, u32[]{:S(2)}, u32[]{:S(2)}) collective-permute-start(bf16[128,768]{1,0:T(8,128)(2,1)S(1)} %get-tuple-element.13.rest_0_), channel_id=1, source_target_pairs={{0,4},{2,6},{4,0},{6,2},{8,12},{10,14},{12,8},{14,10},{16,20},{18,... | collective-permute-start | bytes 589832 | tf_op jit(solution)/shard_map/ppermute | solution.py:438
  6.5 2.6 %collective-permute-start.6 = (bf16[128,768]{1,0:T(8,128)(2,1)S(1)}, bf16[128,768]{1,0:T(8,128)(2,1)S(1)}, u32[]{:S(2)}, u32[]{:S(2)}) collective-permute-start(bf16[128,768]{1,0:T(8,128)(2,1)S(1)} %get-tuple-element.12.own), channel_id=1, source_target_pairs={{0,16},{2,18},{4,20},{6,22},{8,24},{10,26},{12,28},{14,30},{16,0},... | collective-permute-start | bytes 589832 | tf_op jit(solution)/shard_map/ppermute | solution.py:435
  9.1 1.5 %collective-permute-start.3 = (bf16[256,1024]{1,0:T(8,128)(2,1)}, bf16[256,1024]{1,0:T(8,128)(2,1)S(1)}, u32[]{:S(2)}, u32[]{:S(2)}) collective-permute-start(bf16[256,1024]{1,0:T(8,128)(2,1)} %bitcast.2), channel_id=1, source_target_pairs={{0,6},{2,4},{4,2},{6,0},{8,14},{10,12},{12,10},{14,8},{16,22},{18,... | collective-permute-start | bytes 1572872 | tf_op jit(solution)/shard_map/ppermute | solution.py:438
  10.6 1.1 %copy-done = bf16[1,1,256,1024]{3,2,1,0:T(8,128)(2,1)S(1)} copy-done((bf16[1,1,256,1024]{3,2,1,0:T(8,128)(2,1)S(1)}, bf16[1,1,256,1024]{3,2,1,0:T(8,128)(2,1)}, u32[]{:S(2)}) %copy-start) | copy-done | bytes 524312
  12.4 3.2 %collective-permute-start.1 = (bf16[256,1024]{1,0:T(8,128)(2,1)S(1)}, bf16[256,1024]{1,0:T(8,128)(2,1)S(1)}, u32[]{:S(2)}, u32[]{:S(2)}) collective-permute-start(bf16[256,1024]{1,0:T(8,128)(2,1)S(1)} %shard_map.78), channel_id=1, source_target_pairs={{0,4},{2,6},{4,0},{6,2},{8,12},{10,14},{12,8},{14,10},{16,20},{18,... | collective-permute-start | bytes 1572872 | tf_op jit(solution)/shard_map/ppermute | solution.py:438
  15.7 2.2 %collective-permute-done.6.two_own.values = bf16[128,768]{1,0:T(8,128)(2,1)S(1)} collective-permute-done((bf16[128,768]{1,0:T(8,128)(2,1)S(1)}, bf16[128,768]{1,0:T(8,128)(2,1)S(1)}, u32[]{:S(2)}, u32[]{:S(2)}) %collective-permute-start.6) | collective-permute-done | bytes 196640 | tf_op jit(solution)/shard_map/ppermute | solution.py:435
  17.9 0.8 %collective-permute-start.7 = (bf16[128,768]{1,0:T(8,128)(2,1)S(1)}, bf16[128,768]{1,0:T(8,128)(2,1)S(1)}, u32[]{:S(2)}, u32[]{:S(2)}) collective-permute-start(bf16[128,768]{1,0:T(8,128)(2,1)S(1)} %collective-permute-done.4.values.near), channel_id=1, source_target_pairs={{0,16},{2,18},{4,20},{6,22},{8,24},{10,26},{12,28},{14,30},{16,0},... | collective-permute-start | bytes 589832 | tf_op jit(solution)/shard_map/ppermute | solution.py:435
  18.7 6.1 %collective-permute-done.5.one_near.rest_0_ = bf16[128,768]{1,0:T(8,128)(2,1)S(1)} collective-permute-done((bf16[128,768]{1,0:T(8,128)(2,1)S(1)}, bf16[128,768]{1,0:T(8,128)(2,1)S(1)}, u32[]{:S(2)}, u32[]{:S(2)}) %collective-permute-start.5) | collective-permute-done | bytes 196640 | tf_op jit(solution)/shard_map/ppermute | solution.py:435
  24.9 2.4 %collective-permute-done.7.two_near.values = bf16[128,768]{1,0:T(8,128)(2,1)S(1)} collective-permute-done((bf16[128,768]{1,0:T(8,128)(2,1)S(1)}, bf16[128,768]{1,0:T(8,128)(2,1)S(1)}, u32[]{:S(2)}, u32[]{:S(2)}) %collective-permute-start.7) | collective-permute-done | bytes 196640 | tf_op jit(solution)/shard_map/ppermute | solution.py:435
  27.3 0.9 %collective-permute-start.9 = (bf16[128,768]{1,0:T(8,128)(2,1)S(1)}, bf16[128,768]{1,0:T(8,128)(2,1)S(1)}, u32[]{:S(2)}, u32[]{:S(2)}) collective-permute-start(bf16[128,768]{1,0:T(8,128)(2,1)S(1)} %shard_map.84), channel_id=1, source_target_pairs={{0,8},{2,10},{4,12},{6,14},{8,0},{10,2},{12,4},{14,6},{16,24},{18,... | collective-permute-start | bytes 589832 | tf_op jit(solution)/shard_map/ppermute | solution.py:435
  28.9 6.0 %collective-permute-done.2.across = bf16[256,1024]{1,0:T(8,128)(2,1)S(1)} collective-permute-done((bf16[256,1024]{1,0:T(8,128)(2,1)S(1)}, bf16[256,1024]{1,0:T(8,128)(2,1)S(1)}, u32[]{:S(2)}, u32[]{:S(2)}) %collective-permute-start.2) | collective-permute-done | bytes 524320 | tf_op jit(solution)/shard_map/ppermute | solution.py:438
  34.9 0.7 %shard_map.80 = (bf16[512,1024]{1,0:T(8,128)(2,1)S(1)}, f32[1,256]{1,0:T(1,128)S(1)}, bf16[256,1024]{1,0:T(8,128)(2,1)S(1)}) custom-call(s32[1,1]{1,0:T(1,128)S(6)} %copy.8.lengths, bf16[256,1024]{1,0:T(8,128)(2,1)S(1)} %bitcast.5, bf16[256,1024]{1,0:T(8,128)(2,1)S(1)} %collective-permute-done.1.near, bf16[256,1024]{1,0:T(8,128)(2,1)S(1)} %collective-permute-done.2.across, ...), custom_call_target="tpu_custom_call" | custom-call | flops 1572864 | bytes 2097152 | tf_op jit(solution)/shard_map/pallas_call | solution.py:458
  35.6 0.9 %shard_map.82 = (f32[512,768]{1,0:T(8,128)S(1)}, bf16[1024,768]{1,0:T(8,128)(2,1)S(1)}) custom-call(bf16[512,1024]{1,0:T(8,128)(2,1)S(1)} %get-tuple-element.14.normed, bf16[128,768]{1,0:T(8,128)(2,1)S(1)} %get-tuple-element.12.own, bf16[128,768]{1,0:T(8,128)(2,1)S(1)} %collective-permute-done.4.values.near, ...), custom_call_target="tpu_custom_call" | custom-call | flops 603979776 | bytes 2097152 | tf_op jit(solution)/shard_map/pallas_call | solution.py:465
  36.5 0.8 %shard_map.85 = (bf16[512,768]{1,0:T(8,128)(2,1)S(1)}, bf16[272,128]{1,0:T(8,128)(2,1)S(1)}, bf16[256,768]{1,0:T(8,128)(2,1)S(1)}) custom-call(bf16[512,1024]{1,0:T(8,128)(2,1)S(1)} %get-tuple-element.14.normed, f32[512,768]{1,0:T(8,128)S(1)} %get-tuple-element.15.partial, bf16[128,768]{1,0:T(8,128)(2,1)S(1)} %collective-permute-done.8.far_own, ...), custom_call_target="tpu_custom_call" | custom-call | flops 201326592 | bytes 2097152 | tf_op jit(solution)/shard_map/pallas_call | solution.py:472
  37.3 1.6 %collective-permute-start.12 = (bf16[272,128]{1,0:T(8,128)(2,1)S(1)}, bf16[272,128]{1,0:T(8,128)(2,1)S(1)}, u32[]{:S(2)}, u32[]{:S(2)}) collective-permute-start(bf16[272,128]{1,0:T(8,128)(2,1)S(1)} %get-tuple-element.16), channel_id=1, source_target_pairs={{0,24},{2,26},{4,28},{6,30},{8,16},{10,18},{12,20},{14,22},{16,8},... | collective-permute-start | bytes 208904 | tf_op jit(solution)/shard_map/ppermute | solution.py:435
  39.3 2.5 %collective-permute-start.10 = (bf16[272,128]{1,0:T(8,128)(2,1)S(1)}, bf16[272,128]{1,0:T(8,128)(2,1)S(1)}, u32[]{:S(2)}, u32[]{:S(2)}) collective-permute-start(bf16[272,128]{1,0:T(8,128)(2,1)S(1)} %get-tuple-element.16), channel_id=1, source_target_pairs={{0,8},{2,10},{4,12},{6,14},{8,0},{10,2},{12,4},{14,6},{16,24},{18,... | collective-permute-start | bytes 208904 | tf_op jit(solution)/shard_map/ppermute | solution.py:435
  41.8 1.3 %shard_map.86.short = f32[1,256]{1,0:T(1,128)S(1)} custom-call(bf16[256,1024]{1,0:T(8,128)(2,1)S(1)} %get-tuple-element.19.raw, bf16[1024,768]{1,0:T(8,128)(2,1)S(1)} %get-tuple-element.20.weights, bf16[256,768]{1,0:T(8,128)(2,1)S(1)} %get-tuple-element.21.last, f32[1,1024]{1,0:T(1,128)S(1)} %copy-done.3), custom_call_target="tpu_custom_call" | custom-call | flops 402653184 | bytes 2097152 | tf_op jit(solution)/shard_map/pallas_call | solution.py:479
  43.1 1.2 %collective-permute-done.12.state_3 = bf16[272,128]{1,0:T(8,128)(2,1)S(1)} collective-permute-done((bf16[272,128]{1,0:T(8,128)(2,1)S(1)}, bf16[272,128]{1,0:T(8,128)(2,1)S(1)}, u32[]{:S(2)}, u32[]{:S(2)}) %collective-permute-start.12) | collective-permute-done | bytes 69664 | tf_op jit(solution)/shard_map/ppermute | solution.py:435
  44.3 1.8 %collective-permute-done.11.state_2 = bf16[272,128]{1,0:T(8,128)(2,1)S(1)} collective-permute-done((bf16[272,128]{1,0:T(8,128)(2,1)S(1)}, bf16[272,128]{1,0:T(8,128)(2,1)S(1)}, u32[]{:S(2)}, u32[]{:S(2)}) %collective-permute-start.11) | collective-permute-done | bytes 69664 | tf_op jit(solution)/shard_map/ppermute | solution.py:435
  46.1 0.9 %shard_map.87 = f32[32,1,640]{2,1,0:T(1,128)S(1)} custom-call(s32[1,1]{1,0:T(1,128)S(6)} %copy.8.lengths, bf16[272,128]{1,0:T(8,128)(2,1)S(1)} %collective-permute-done.10.state_1, bf16[272,128]{1,0:T(8,128)(2,1)S(1)} %collective-permute-done.11.state_2, bf16[272,128]{1,0:T(8,128)(2,1)S(1)} %collective-permute-done.12.state_3, ...), custom_call_target="tpu_custom_call" | custom-call | flops 301989888 | bytes 2097152 | tf_op jit(solution)/shard_map/pallas_call | solution.py:482
  47.0 10.8 %all_to_all.5.parts = f32[32,1,640]{2,1,0:T(1,128)S(1)} all-to-all(f32[32,1,640]{2,1,0:T(1,128)S(1)} %shard_map.87), channel_id=1, replica_groups=mesh['seq'=8,'dp'=2,'domain'=2] {'seq','dp','domain'}, dimensions={0} | all-to-all | bytes 163840 | tf_op jit(solution)/shard_map/all_to_all | solution.py:489
  57.8 1.2 %shard_map.88 = (bf16[1,1,128]{2,1,0:T(2,128)(2,1)}, f32[1,1]{1,0:T(1,128)}) custom-call(s32[2]{0:T(128)S(1)} %copy-done.4, f32[32,1,640]{2,1,0:T(1,128)S(1)} %all_to_all.5.parts), custom_call_target="tpu_custom_call" | custom-call | flops 16384 | bytes 2097152 | tf_op jit(solution)/shard_map/pallas_call | solution.py:490
  (27 shorter events, 1.4 us)
Async XLA Ops:
  0.6 11.7 %copy-start.1 = (bf16[1,1,256,1024]{3,2,1,0:T(8,128)(2,1)S(1)}, bf16[1,1,256,1024]{3,2,1,0:T(8,128)(2,1)}, u32[]{:S(2)}) copy-start(bf16[1,1,256,1024]{3,2,1,0:T(8,128)(2,1)} %param.6) | copy-start | bytes 1572868
  0.6 1.2 %copy-start.2 = (bf16[1,128,3072]{2,1,0:T(8,128)(2,1)S(1)}, bf16[1,128,3072]{2,1,0:T(8,128)(2,1)}, u32[]{:S(2)}) copy-start(bf16[1,128,3072]{2,1,0:T(8,128)(2,1)} %param.7) | copy-start | bytes 2359300
  2.0 10.4 %collective-permute-start = (bf16[128,768]{1,0:T(8,128)(2,1)S(1)}, bf16[128,768]{1,0:T(8,128)(2,1)S(1)}, u32[]{:S(2)}, u32[]{:S(2)}) collective-permute-start(bf16[128,768]{1,0:T(8,128)(2,1)S(1)} %get-tuple-element.12.own), channel_id=1, source_target_pairs={{0,8},{2,10},{4,12},{6,14},{8,0},{10,2},{12,4},{14,6},{16,24},{18,... | collective-permute-start | bytes 589832 | tf_op jit(solution)/shard_map/ppermute | solution.py:435
  5.1 10.5 %collective-permute-start.4 = (bf16[128,768]{1,0:T(8,128)(2,1)S(1)}, bf16[128,768]{1,0:T(8,128)(2,1)S(1)}, u32[]{:S(2)}, u32[]{:S(2)}) collective-permute-start(bf16[128,768]{1,0:T(8,128)(2,1)S(1)} %get-tuple-element.13.rest_0_), channel_id=1, source_target_pairs={{0,4},{2,6},{4,0},{6,2},{8,12},{10,14},{12,8},{14,10},{16,20},{18,... | collective-permute-start | bytes 589832 | tf_op jit(solution)/shard_map/ppermute | solution.py:438
  6.5 11.3 %collective-permute-start.6 = (bf16[128,768]{1,0:T(8,128)(2,1)S(1)}, bf16[128,768]{1,0:T(8,128)(2,1)S(1)}, u32[]{:S(2)}, u32[]{:S(2)}) collective-permute-start(bf16[128,768]{1,0:T(8,128)(2,1)S(1)} %get-tuple-element.12.own), channel_id=1, source_target_pairs={{0,16},{2,18},{4,20},{6,22},{8,24},{10,26},{12,28},{14,30},{16,0},... | collective-permute-start | bytes 589832 | tf_op jit(solution)/shard_map/ppermute | solution.py:435
  9.1 25.7 %collective-permute-start.3 = (bf16[256,1024]{1,0:T(8,128)(2,1)}, bf16[256,1024]{1,0:T(8,128)(2,1)S(1)}, u32[]{:S(2)}, u32[]{:S(2)}) collective-permute-start(bf16[256,1024]{1,0:T(8,128)(2,1)} %bitcast.2), channel_id=1, source_target_pairs={{0,6},{2,4},{4,2},{6,0},{8,14},{10,12},{12,10},{14,8},{16,22},{18,... | collective-permute-start | bytes 1572872 | tf_op jit(solution)/shard_map/ppermute | solution.py:438
  10.6 1.1 %copy-start = (bf16[1,1,256,1024]{3,2,1,0:T(8,128)(2,1)S(1)}, bf16[1,1,256,1024]{3,2,1,0:T(8,128)(2,1)}, u32[]{:S(2)}) copy-start(bf16[1,1,256,1024]{3,2,1,0:T(8,128)(2,1)} %param.6) | copy-start | bytes 1572868
  11.7 23.1 %copy-start.3 = (f32[1,1024]{1,0:T(1,128)S(1)}, f32[1,1024]{1,0:T(1,128)}, u32[]{:S(2)}) copy-start(f32[1,1024]{1,0:T(1,128)} %gain.4) | copy-start | bytes 12292
  11.8 23.1 %collective-permute-start.2 = (bf16[256,1024]{1,0:T(8,128)(2,1)S(1)}, bf16[256,1024]{1,0:T(8,128)(2,1)S(1)}, u32[]{:S(2)}, u32[]{:S(2)}) collective-permute-start(bf16[256,1024]{1,0:T(8,128)(2,1)S(1)} %shard_map.79), channel_id=1, source_target_pairs={{0,2},{2,0},{4,6},{6,4},{8,10},{10,8},{12,14},{14,12},{16,18},{18,... | collective-permute-start | bytes 1572872 | tf_op jit(solution)/shard_map/ppermute | solution.py:438
  12.4 22.5 %collective-permute-start.1 = (bf16[256,1024]{1,0:T(8,128)(2,1)S(1)}, bf16[256,1024]{1,0:T(8,128)(2,1)S(1)}, u32[]{:S(2)}, u32[]{:S(2)}) collective-permute-start(bf16[256,1024]{1,0:T(8,128)(2,1)S(1)} %shard_map.78), channel_id=1, source_target_pairs={{0,4},{2,6},{4,0},{6,2},{8,12},{10,14},{12,8},{14,10},{16,20},{18,... | collective-permute-start | bytes 1572872 | tf_op jit(solution)/shard_map/ppermute | solution.py:438
  15.6 9.2 %collective-permute-start.5 = (bf16[128,768]{1,0:T(8,128)(2,1)S(1)}, bf16[128,768]{1,0:T(8,128)(2,1)S(1)}, u32[]{:S(2)}, u32[]{:S(2)}) collective-permute-start(bf16[128,768]{1,0:T(8,128)(2,1)S(1)} %shard_map.81), channel_id=1, source_target_pairs={{0,8},{2,10},{4,12},{6,14},{8,0},{10,2},{12,4},{14,6},{16,24},{18,... | collective-permute-start | bytes 589832 | tf_op jit(solution)/shard_map/ppermute | solution.py:435
  17.9 9.4 %collective-permute-start.7 = (bf16[128,768]{1,0:T(8,128)(2,1)S(1)}, bf16[128,768]{1,0:T(8,128)(2,1)S(1)}, u32[]{:S(2)}, u32[]{:S(2)}) collective-permute-start(bf16[128,768]{1,0:T(8,128)(2,1)S(1)} %collective-permute-done.4.values.near), channel_id=1, source_target_pairs={{0,16},{2,18},{4,20},{6,22},{8,24},{10,26},{12,28},{14,30},{16,0},... | collective-permute-start | bytes 589832 | tf_op jit(solution)/shard_map/ppermute | solution.py:435
  24.8 11.7 %collective-permute-start.8 = (bf16[128,768]{1,0:T(8,128)(2,1)S(1)}, bf16[128,768]{1,0:T(8,128)(2,1)S(1)}, u32[]{:S(2)}, u32[]{:S(2)}) collective-permute-start(bf16[128,768]{1,0:T(8,128)(2,1)S(1)} %shard_map.83), channel_id=1, source_target_pairs={{0,8},{2,10},{4,12},{6,14},{8,0},{10,2},{12,4},{14,6},{16,24},{18,... | collective-permute-start | bytes 589832 | tf_op jit(solution)/shard_map/ppermute | solution.py:435
  27.3 9.2 %collective-permute-start.9 = (bf16[128,768]{1,0:T(8,128)(2,1)S(1)}, bf16[128,768]{1,0:T(8,128)(2,1)S(1)}, u32[]{:S(2)}, u32[]{:S(2)}) collective-permute-start(bf16[128,768]{1,0:T(8,128)(2,1)S(1)} %shard_map.84), channel_id=1, source_target_pairs={{0,8},{2,10},{4,12},{6,14},{8,0},{10,2},{12,4},{14,6},{16,24},{18,... | collective-permute-start | bytes 589832 | tf_op jit(solution)/shard_map/ppermute | solution.py:435
  37.3 8.8 %copy-start.5 = (f32[1,1024]{1,0:T(1,128)S(1)}, f32[1,1024]{1,0:T(1,128)}, u32[]{:S(2)}) copy-start(f32[1,1024]{1,0:T(1,128)} %gain.5) | copy-start | bytes 12292
  37.3 7.0 %collective-permute-start.12 = (bf16[272,128]{1,0:T(8,128)(2,1)S(1)}, bf16[272,128]{1,0:T(8,128)(2,1)S(1)}, u32[]{:S(2)}, u32[]{:S(2)}) collective-permute-start(bf16[272,128]{1,0:T(8,128)(2,1)S(1)} %get-tuple-element.16), channel_id=1, source_target_pairs={{0,24},{2,26},{4,28},{6,30},{8,16},{10,18},{12,20},{14,22},{16,8},... | collective-permute-start | bytes 208904 | tf_op jit(solution)/shard_map/ppermute | solution.py:435
  38.9 7.2 %collective-permute-start.11 = (bf16[272,128]{1,0:T(8,128)(2,1)S(1)}, bf16[272,128]{1,0:T(8,128)(2,1)S(1)}, u32[]{:S(2)}, u32[]{:S(2)}) collective-permute-start(bf16[272,128]{1,0:T(8,128)(2,1)S(1)} %get-tuple-element.16), channel_id=1, source_target_pairs={{0,16},{2,18},{4,20},{6,22},{8,24},{10,26},{12,28},{14,30},{16,0},... | collective-permute-start | bytes 208904 | tf_op jit(solution)/shard_map/ppermute | solution.py:435
  39.3 6.8 %collective-permute-start.10 = (bf16[272,128]{1,0:T(8,128)(2,1)S(1)}, bf16[272,128]{1,0:T(8,128)(2,1)S(1)}, u32[]{:S(2)}, u32[]{:S(2)}) collective-permute-start(bf16[272,128]{1,0:T(8,128)(2,1)S(1)} %get-tuple-element.16), channel_id=1, source_target_pairs={{0,8},{2,10},{4,12},{6,14},{8,0},{10,2},{12,4},{14,6},{16,24},{18,... | collective-permute-start | bytes 208904 | tf_op jit(solution)/shard_map/ppermute | solution.py:435
  41.8 15.9 %copy-start.4 = (s32[2]{0:T(128)S(1)}, s32[2]{0:T(128)}, u32[]{:S(2)}) copy-start(s32[2]{0:T(128)} %positives.1) | copy-start | bytes 28

commit v13 on v12

--- a/solution.py
+++ b/solution.py
@@ -197,69 +197,53 @@
     return low[:, :GROUP], low[:, GROUP:], out[:, 2 * GROUP :].astype(jnp.bfloat16)
 
 
-def norm_kernel(lengths, own, near, across, corner, gain, normed, sums, short, raw, sems):
-    tokens = own.shape[0]
-    _, x, u = places()
-    long_u = jnp.where(lengths[0, 0] > tokens, u, 1 - u)
-    for slot in range(3):
-        from_x = 1 if slot == 1 else 0
-        from_u = 1 - long_u if slot == 2 else long_u
-        pick = jnp.bitwise_xor(x, from_x) + 2 * jnp.bitwise_xor(u, from_u)
-        dest = short if slot == 2 else raw.at[slot]
-        for j, ref in enumerate((own, near, across, corner)):
-
-            @pl.when(pick == j)
-            def _():
-                pltpu.make_async_copy(ref, dest, sems.at[slot]).start()
-
-    columns = pl.ds(pl.multiple_of((2 * x + u) * GROUP, GROUP), GROUP)
-    total = jnp.zeros((1, GROUP), jnp.float32)
-    for slot in range(2):
-        pltpu.make_async_copy(own, raw.at[slot], sems.at[slot]).wait()
-        normed[pl.ds(slot * tokens, tokens), :] = normalise(raw[slot], gain[...])
-        total = total + jnp.sum(raw[slot, :, columns].astype(jnp.float32), axis=0, keepdims=True)
-    sums[...] = total
-    pltpu.make_async_copy(own, short, sems.at[2]).wait()
-
-
 def place_rows(dest, start, x, here, there):
     rows = here.shape[0]
     for place, values in ((x, here), (1 - x, there)):
         dest[pl.ds(pl.multiple_of(start + place * rows, rows), rows), :] = values
 
 
-def partial_kernel(normed, own, near, one_own, one_near, two_own, two_near, partial, weights):
+def choose(pick, first, second, dest):
+    @pl.when(pick)
+    def _():
+        dest[...] = first[...]
+
+    @pl.when(jnp.logical_not(pick))
+    def _():
+        dest[...] = second[...]
+
+
+def project(raw, gain, weights, feats, at):
+    _, x, u = places()
+    tokens = raw.shape[0]
+    query, key, value = features(
+        jnp.dot(normalise(raw[...], gain[...]), weights[...], preferred_element_type=jnp.float32)
+    )
+    rows = pl.ds(at, tokens)
+    feats[rows, :GROUP] = query
+    feats[rows, GROUP : 2 * GROUP] = key
+    feats[rows, 2 * GROUP :] = value
+    columns = pl.ds(pl.multiple_of((2 * x + u) * GROUP, GROUP), GROUP)
+    return jnp.sum(raw[:, columns].astype(jnp.float32), axis=0, keepdims=True)
+
+
+def first_kernel(lengths, own, across, gain, *refs):
+    feats, sums, weights, raw = refs[2 * PLANES :]
     z, x, _ = places()
-    parts = ((own, near), (one_own, one_near), (two_own, two_near), None)
-    starts = [pl.multiple_of(jnp.bitwise_xor(z, j) * GROUP, GROUP) for j in range(PLANES)]
-    for start, refs in zip(starts, parts):
-        if refs is None:
-            weights[pl.ds(start, GROUP), :] = jnp.zeros((GROUP, weights.shape[1]), weights.dtype)
-        else:
-            place_rows(weights, start, x, refs[0][...], refs[1][...])
-    total = None
-    for start in starts[:3]:
-        rows = pl.ds(start, GROUP)
-        out = jnp.dot(normed[:, rows], weights[rows, :], preferred_element_type=jnp.float32)
-        total = out if total is None else total + out
-    partial[...] = total
-
-
-def project_kernel(normed, partial, far_own, far_near, feats, message, last):
-    tokens = normed.shape[0]
-    z, x, _ = places()
-    place_rows(last, 0, x, far_own[...], far_near[...])
-    columns = pl.ds(pl.multiple_of((3 - z) * GROUP, GROUP), GROUP)
-    half = tokens // 2
-    total = jnp.zeros((1, GROUP), jnp.float32)
-    for part in range(2):
-        at = pl.ds(part * half, half)
-        out = partial[at, :] + jnp.dot(normed[at, columns], last[...], preferred_element_type=jnp.float32)
-        query, key, value = features(out)
-        feats[at, :GROUP] = query
-        feats[at, GROUP : 2 * GROUP] = key
-        feats[at, 2 * GROUP :] = value
-        total = total + jnp.sum(key.astype(jnp.float32), axis=0, keepdims=True)
+    for j in range(PLANES):
+        start = pl.multiple_of(jnp.bitwise_xor(z, j) * GROUP, GROUP)
+        place_rows(weights, start, x, refs[2 * j][...], refs[2 * j + 1][...])
+    choose(lengths[0, 0] > own.shape[0], own, across, raw)
+    sums[...] = project(raw, gain, weights, feats, 0)
+
+
+def second_kernel(lengths, near, corner, gain, weights, first, first_sums, feats, message, sums, raw):
+    tokens = near.shape[0]
+    _, x, _ = places()
+    choose(lengths[0, 0] > tokens, near, corner, raw)
+    feats[pl.ds(pl.multiple_of(x * tokens, tokens), tokens), :] = first[...]
+    sums[...] = first_sums[...] + project(raw, gain, weights, feats, pl.multiple_of((1 - x) * tokens, tokens))
+    total = jnp.sum(feats[:, GROUP : 2 * GROUP].astype(jnp.float32), axis=0, keepdims=True)
     high, low = split_two(total)
     for h in range(GROUP // HEAD_DIM):
         at = h * HEAD_DIM
@@ -296,23 +280,32 @@
     return jnp.sum(weight * value.astype(jnp.float32), axis=0, keepdims=True)
 
 
-def short_kernel(raw, weights, last, gain, out):
+def short_kernel(lengths, own, near, across, corner, weights, gain, out, raw):
+    tokens = own.shape[0]
     z, x, u = places()
     out[...] = jnp.zeros(out.shape, jnp.float32)
 
     @pl.when(z == 0)
     def _():
-        low = normalise(raw[...], gain[...])
-        wide = jnp.dot(low, weights[...], preferred_element_type=jnp.float32)
-        wide = wide + jnp.dot(low[:, 3 * GROUP :], last[...], preferred_element_type=jnp.float32)
+        own_long = lengths[0, 0] > tokens
+
+        @pl.when(x == 0)
+        def _():
+            choose(own_long, across, own, raw)
+
+        @pl.when(x != 0)
+        def _():
+            choose(own_long, corner, near, raw)
+
+        wide = jnp.dot(normalise(raw[...], gain[...]), weights[...], preferred_element_type=jnp.float32)
         query, key, value = features(wide)
         share, _ = shares(query, key, jnp.zeros((1, GROUP), jnp.float32))
         columns = pl.ds(pl.multiple_of((2 * x + u) * GROUP, GROUP), GROUP)
-        own = jnp.sum(raw[:, columns].astype(jnp.float32), axis=0, keepdims=True)
-        out[...] = own + weighted(key, value, suffix(share))
-
-
-def pool_kernel(lengths, state_1, state_2, state_3, feats, sums, short, gain, part):
+        total = jnp.sum(raw[:, columns].astype(jnp.float32), axis=0, keepdims=True)
+        out[...] = total + weighted(key, value, suffix(share))
+
+
+def pool_kernel(lengths, state_3, state_2, state_1, feats, sums, short, gain, part):
     tokens = feats.shape[0] // 2
     z, x, u = places()
     long_u = jnp.where(lengths[0, 0] > tokens, u, 1 - u)
@@ -444,48 +437,45 @@
     w_own, w_sent = call(
         pack_kernel, (shape((rows, wide), bf16),) * 2, [hbm()], [pltpu.SemaphoreType.DMA((6,))], 0
     )(weight)
+    near = plane_hop(events, 2)
+    across = plane_hop(events, 1)
     w_near = plane_hop(w_sent, 2)
+    two_own = hop(call(gate_kernel, shape((rows, wide), bf16), [vmem()] + [anywhere()] * 1, [], 0)(w_own, w_sent), lambda p: p ^ 2)
     two_near = hop(w_near, lambda p: p ^ 2)
-    corner = plane_hop(events, 3)
-    across = plane_hop(call(gate_kernel, shape((tokens, width), bf16), [vmem()] + [anywhere()] * 1, [], 0)(events, w_sent), 1)
-    two_own = hop(w_own, lambda p: p ^ 2)
     one_own = hop(w_own, lambda p: p ^ 1)
-    near = plane_hop(call(gate_kernel, shape((tokens, width), bf16), [vmem()] + [anywhere()] * 1, [], 0)(events, one_own), 2)
     one_near = hop(call(gate_kernel, shape((rows, wide), bf16), [vmem()] + [anywhere()] * 1, [], 0)(w_near, one_own), lambda p: p ^ 1)
+    far_own = hop(call(gate_kernel, shape((rows, wide), bf16), [vmem()] + [anywhere()] * 1, [], 0)(two_own, one_near), lambda p: p ^ 1)
     far_near = hop(call(gate_kernel, shape((rows, wide), bf16), [vmem()] + [anywhere()] * 1, [], 0)(two_near, one_near), lambda p: p ^ 1)
-    far_own = hop(call(gate_kernel, shape((rows, wide), bf16), [vmem()] + [anywhere()] * 1, [], 0)(two_own, one_near), lambda p: p ^ 1)
-
-    normed, sums, raw_short = call(
-        norm_kernel,
-        (shape((2 * tokens, width), bf16), shape((1, GROUP), f32), shape((tokens, width), bf16)),
-        [smem()] + [anywhere()] * 4 + [vmem()],
-        [pltpu.VMEM((2, tokens, width), bf16), pltpu.SemaphoreType.DMA((3,))],
-        2 * 3 * tokens * width,
-    )(lengths, events, near, across, corner, norm_gain)
-    partial, weights = call(
-        partial_kernel,
-        (shape((2 * tokens, wide), f32), shape((width, wide), bf16)),
-        [vmem()] * 7,
-        [],
-        2 * 2 * tokens * 3 * GROUP * wide,
-    )(normed, w_own, w_near, one_own, one_near, two_own, two_near)
-    feats, message, last = call(
-        project_kernel,
-        (shape((2 * tokens, wide), bf16), shape((MESSAGE, HEAD_DIM), bf16), shape((GROUP, wide), bf16)),
-        [vmem()] * 4,
-        [],
-        2 * 2 * tokens * GROUP * wide,
-    )(normed, partial, far_own, far_near)
+    corner = plane_hop(call(gate_kernel, shape((tokens, width), bf16), [vmem()] + [anywhere()] * 2, [], 0)(events, one_own, w_near), 3)
+
+    first, first_sums, weights = call(
+        first_kernel,
+        (shape((tokens, wide), bf16), shape((1, GROUP), f32), shape((width, wide), bf16)),
+        [smem()] + [vmem()] * (3 + 2 * PLANES),
+        [pltpu.VMEM((tokens, width), bf16)],
+        2 * tokens * width * wide,
+    )(lengths, events, across, norm_gain, w_own, w_near, one_own, one_near, two_own, two_near, far_own, far_near)
+    feats, message, sums = call(
+        second_kernel,
+        (shape((2 * tokens, wide), bf16), shape((MESSAGE, HEAD_DIM), bf16), shape((1, GROUP), f32)),
+        [smem()] + [vmem()] * 6,
+        [pltpu.VMEM((tokens, width), bf16)],
+        2 * tokens * width * wide,
+    )(lengths, near, corner, norm_gain, weights, first, first_sums)
     short = call(
-        short_kernel, shape((1, GROUP), f32), [vmem()] * 4, [], 2 * tokens * width * wide
-    )(raw_short, weights, last, norm_gain)
+        short_kernel,
+        shape((1, GROUP), f32),
+        [smem()] + [vmem()] * 6,
+        [pltpu.VMEM((tokens, width), bf16)],
+        2 * tokens * width * wide,
+    )(lengths, events, near, across, corner, weights, norm_gain)
     part = call(
         pool_kernel,
         shape((2 * here, 1, 2 * GROUP + HEAD_DIM), f32),
         [smem()] + [vmem()] * 7,
         [],
         2 * 9 * tokens * tokens * GROUP,
-    )(lengths, *each(message), feats, sums, short, pool_gain)
+    )(lengths, *each(message)[::-1], feats, sums, short, pool_gain)
     parts = lax.all_to_all(part, ("seq", "dp", "domain"), 0, 0, tiled=True)
     vec, loss = call(
         loss_kernel,

time: 59.2 us -> 59.1 us (level)
  starting transfers between devices: 18.7 us -> 23.1 us
  waiting for transfers between devices: 19.7 us -> 16.1 us
  local copies, waits for them, and re-layouts: 2.28 us -> 1.21 us
  blocking collectives: 10.8 us -> 11.6 us
  Pallas kernels: 6.05 us -> 5.43 us
    ppermute x4, waiting for transfers between devices: 6 us -> 0.01 us  [plane_hop(): return lax.ppermute(a, ('seq', 'dp'), [(i, i ^ move) for i in range(here)])]
    ppermute x9, starting transfers between devices: 12 us -> 15.2 us  [hop(): return lax.ppermute(a, ('seq', 'dp'), pairs)]
    ppermute x9, waiting for transfers between devices: 13.7 us -> 16.1 us  [hop(): return lax.ppermute(a, ('seq', 'dp'), pairs)]
    ppermute x4, starting transfers between devices: 6.75 us -> 7.91 us  [plane_hop(): return lax.ppermute(a, ('seq', 'dp'), [(i, i ^ move) for i in range(here)])]
    unnamed x12 -> x10, local copies, waits for them, and re-layouts: 2.28 us -> 1.21 us
    all_to_all x1, blocking collectives: 10.8 us -> 11.6 us  [towers(): parts = lax.all_to_all(part, ('seq', 'dp', 'domain'), 0, 0, tiled=True)]
    pallas_call x4 -> x3, Pallas kernels: 3.75 us -> 3.15 us  [the longest x1 1.22 us: towers(): call(short_kernel, shape((1, GROUP), f32), [smem()] + [vmem()] * 6, [pltp...]
  transfers between devices with their start and end apart: 13 -> 13, of which waited for: 6 -> 7; matrix products, arithmetic and copies ran while one was open for 0% -> 0% of each run, Pallas kernels for 5% -> 4%
where the time goes in v13:
time: 59.1 us; the launch traced here: 58.9 us
  starting transfers between devices  23.1 us (39%)
  waiting for transfers between devices  16.1 us (27%)
  blocking collectives  11.6 us (20%)
  Pallas kernels  5.43 us (9%)
  between operations  1.43 us (2%)
  local copies, waits for them, and re-layouts  1.21 us (2%)
    ppermute x9, waiting for transfers between devices, hop(): return lax.ppermute(a, ('seq', 'dp'), pairs)  16.1 us
    ppermute x9, starting transfers between devices, hop(): return lax.ppermute(a, ('seq', 'dp'), pairs)  15.2 us
    all_to_all x1, blocking collectives, towers(): parts = lax.all_to_all(part, ('seq', 'dp', 'domain'), 0, 0, tiled=True)  11.6 us
    ppermute x4, starting transfers between devices, plane_hop(): return lax.ppermute(a, ('seq', 'dp'), [(i, i ^ move) for i in range(here)])  7.91 us
    pallas_call x1, Pallas kernels, towers(): call(short_kernel, shape((1, GROUP), f32), [smem()] + [vmem()] * 6, [pltp...  1.22 us
    unnamed x10, local copies, waits for them, and re-layouts  1.21 us
    pallas_call x1, Pallas kernels, towers(): call(loss_kernel, (shape((1, 1, width // 8), bf16), shape((1, 1), f32)),...  1.19 us
  transfers between devices with their start and end apart: 13, of which 7 were waited for; matrix products, arithmetic and copies ran while one was open for 0% of the time, Pallas kernels for 4%

profile of v13, /device:TPU:0, one launch (start us, length us, event | category | flops | bytes accessed | tf_op | source)
XLA Modules:
  0.0 58.9 jit_solution(7177854862015303058)
XLA Ops:
  0.7 1.2 %copy-done.1 = bf16[1,128,3072]{2,1,0:T(8,128)(2,1)S(1)} copy-done((bf16[1,128,3072]{2,1,0:T(8,128)(2,1)S(1)}, bf16[1,128,3072]{2,1,0:T(8,128)(2,1)}, u32[]{:S(2)}) %copy-start.1) | copy-done | bytes 786456
  2.0 3.1 %collective-permute-start.1 = (bf16[128,768]{1,0:T(8,128)(2,1)S(1)}, bf16[128,768]{1,0:T(8,128)(2,1)S(1)}, u32[]{:S(2)}, u32[]{:S(2)}) collective-permute-start(bf16[128,768]{1,0:T(8,128)(2,1)S(1)} %get-tuple-element.10.values.refs_0_), channel_id=1, source_target_pairs={{0,8},{2,10},{4,12},{6,14},{8,0},{10,2},{12,4},{14,6},{16,24},{18,... | collective-permute-start | bytes 589832 | tf_op jit(solution)/shard_map/ppermute | solution.py:428
  5.1 1.5 %collective-permute-start.2 = (bf16[128,768]{1,0:T(8,128)(2,1)S(1)}, bf16[128,768]{1,0:T(8,128)(2,1)S(1)}, u32[]{:S(2)}, u32[]{:S(2)}) collective-permute-start(bf16[128,768]{1,0:T(8,128)(2,1)S(1)} %get-tuple-element.11.rest_0_), channel_id=1, source_target_pairs={{0,4},{2,6},{4,0},{6,2},{8,12},{10,14},{12,8},{14,10},{16,20},{18,... | collective-permute-start | bytes 589832 | tf_op jit(solution)/shard_map/ppermute | solution.py:431
  6.6 2.7 %collective-permute-start.6 = (bf16[128,768]{1,0:T(8,128)(2,1)S(1)}, bf16[128,768]{1,0:T(8,128)(2,1)S(1)}, u32[]{:S(2)}, u32[]{:S(2)}) collective-permute-start(bf16[128,768]{1,0:T(8,128)(2,1)S(1)} %shard_map.80), channel_id=1, source_target_pairs={{0,16},{2,18},{4,20},{6,22},{8,24},{10,26},{12,28},{14,30},{16,0},... | collective-permute-start | bytes 589832 | tf_op jit(solution)/shard_map/ppermute | solution.py:428
  9.2 1.5 %collective-permute-start.4 = (bf16[256,1024]{1,0:T(8,128)(2,1)}, bf16[256,1024]{1,0:T(8,128)(2,1)S(1)}, u32[]{:S(2)}, u32[]{:S(2)}) collective-permute-start(bf16[256,1024]{1,0:T(8,128)(2,1)} %bitcast.2), channel_id=1, source_target_pairs={{0,2},{2,0},{4,6},{6,4},{8,10},{10,8},{12,14},{14,12},{16,18},{18,... | collective-permute-start | bytes 1572872 | tf_op jit(solution)/shard_map/ppermute | solution.py:431
  10.7 0.5 collective-permute-start
  11.3 0.8 %collective-permute-done.1.rest_0_.refs_2_ = bf16[128,768]{1,0:T(8,128)(2,1)S(1)} collective-permute-done((bf16[128,768]{1,0:T(8,128)(2,1)S(1)}, bf16[128,768]{1,0:T(8,128)(2,1)S(1)}, u32[]{:S(2)}, u32[]{:S(2)}) %collective-permute-start.1) | collective-permute-done | bytes 196640 | tf_op jit(solution)/shard_map/ppermute | solution.py:428
  12.1 4.4 %collective-permute-start.3 = (bf16[256,1024]{1,0:T(8,128)(2,1)S(1)}, bf16[256,1024]{1,0:T(8,128)(2,1)S(1)}, u32[]{:S(2)}, u32[]{:S(2)}) collective-permute-start(bf16[256,1024]{1,0:T(8,128)(2,1)S(1)} %shard_map.78), channel_id=1, source_target_pairs={{0,6},{2,4},{4,2},{6,0},{8,14},{10,12},{12,10},{14,8},{16,22},{18,... | collective-permute-start | bytes 1572872 | tf_op jit(solution)/shard_map/ppermute | solution.py:431
  16.5 1.4 %collective-permute-done.6.values.refs_4_ = bf16[128,768]{1,0:T(8,128)(2,1)S(1)} collective-permute-done((bf16[128,768]{1,0:T(8,128)(2,1)S(1)}, bf16[128,768]{1,0:T(8,128)(2,1)S(1)}, u32[]{:S(2)}, u32[]{:S(2)}) %collective-permute-start.6) | collective-permute-done | bytes 196640 | tf_op jit(solution)/shard_map/ppermute | solution.py:428
  18.0 1.6 %collective-permute-start.7 = (bf16[128,768]{1,0:T(8,128)(2,1)S(1)}, bf16[128,768]{1,0:T(8,128)(2,1)S(1)}, u32[]{:S(2)}, u32[]{:S(2)}) collective-permute-start(bf16[128,768]{1,0:T(8,128)(2,1)S(1)} %collective-permute-done.2.rest_1_.values.refs_1_), channel_id=1, source_target_pairs={{0,16},{2,18},{4,20},{6,22},{8,24},{10,26},{12,28},{14,30},{16,0},... | collective-permute-start | bytes 589832 | tf_op jit(solution)/shard_map/ppermute | solution.py:428
  19.6 6.7 %collective-permute-done.5.rest_0_.refs_3_ = bf16[128,768]{1,0:T(8,128)(2,1)S(1)} collective-permute-done((bf16[128,768]{1,0:T(8,128)(2,1)S(1)}, bf16[128,768]{1,0:T(8,128)(2,1)S(1)}, u32[]{:S(2)}, u32[]{:S(2)}) %collective-permute-start.5) | collective-permute-done | bytes 196640 | tf_op jit(solution)/shard_map/ppermute | solution.py:428
  26.4 3.3 %collective-permute-start.9 = (bf16[128,768]{1,0:T(8,128)(2,1)S(1)}, bf16[128,768]{1,0:T(8,128)(2,1)S(1)}, u32[]{:S(2)}, u32[]{:S(2)}) collective-permute-start(bf16[128,768]{1,0:T(8,128)(2,1)S(1)} %shard_map.82), channel_id=1, source_target_pairs={{0,8},{2,10},{4,12},{6,14},{8,0},{10,2},{12,4},{14,6},{16,24},{18,... | collective-permute-start | bytes 589832 | tf_op jit(solution)/shard_map/ppermute | solution.py:428
  30.4 2.5 %collective-permute-done.8.refs_6_ = bf16[128,768]{1,0:T(8,128)(2,1)S(1)} collective-permute-done((bf16[128,768]{1,0:T(8,128)(2,1)S(1)}, bf16[128,768]{1,0:T(8,128)(2,1)S(1)}, u32[]{:S(2)}, u32[]{:S(2)}) %collective-permute-start.8) | collective-permute-done | bytes 196640 | tf_op jit(solution)/shard_map/ppermute | solution.py:428
  32.8 2.1 %collective-permute-done.9.refs_7_ = bf16[128,768]{1,0:T(8,128)(2,1)S(1)} collective-permute-done((bf16[128,768]{1,0:T(8,128)(2,1)S(1)}, bf16[128,768]{1,0:T(8,128)(2,1)S(1)}, u32[]{:S(2)}, u32[]{:S(2)}) %collective-permute-start.9) | collective-permute-done | bytes 196640 | tf_op jit(solution)/shard_map/ppermute | solution.py:428
  34.9 0.8 %shard_map.83 = (bf16[256,768]{1,0:T(8,128)(2,1)S(1)}, f32[1,256]{1,0:T(1,128)S(1)}, bf16[1024,768]{1,0:T(8,128)(2,1)S(1)}) custom-call(s32[1,1]{1,0:T(1,128)S(6)} %copy.8.lengths, bf16[256,1024]{1,0:T(8,128)(2,1)S(1)} %bitcast.5, bf16[256,1024]{1,0:T(8,128)(2,1)S(1)} %collective-permute-done.4.across, f32[1,1024]{1,0:T(1,128)S(1)} %copy-done.2, ...), custom_call_target="tpu_custom_call" | custom-call | flops 402653184 | bytes 2097152 | tf_op jit(solution)/shard_map/pallas_call | solution.py:451
  35.8 1.1 %shard_map.84 = (bf16[512,768]{1,0:T(8,128)(2,1)S(1)}, bf16[272,128]{1,0:T(8,128)(2,1)S(1)}, f32[1,256]{1,0:T(1,128)S(1)}) custom-call(s32[1,1]{1,0:T(1,128)S(6)} %copy.8.lengths, bf16[256,1024]{1,0:T(8,128)(2,1)S(1)} %collective-permute-done.near, bf16[256,1024]{1,0:T(8,128)(2,1)S(1)} %collective-permute-done.3.corner, f32[1,1024]{1,0:T(1,128)S(1)} %copy-done.2, ...), custom_call_target="tpu_custom_call" | custom-call | flops 402653184 | bytes 2097152 | tf_op jit(solution)/shard_map/pallas_call | solution.py:458
  36.9 2.4 %collective-permute-start.10 = (bf16[272,128]{1,0:T(8,128)(2,1)S(1)}, bf16[272,128]{1,0:T(8,128)(2,1)S(1)}, u32[]{:S(2)}, u32[]{:S(2)}) collective-permute-start(bf16[272,128]{1,0:T(8,128)(2,1)S(1)} %get-tuple-element.15), channel_id=1, source_target_pairs={{0,24},{2,26},{4,28},{6,30},{8,16},{10,18},{12,20},{14,22},{16,8},... | collective-permute-start | bytes 208904 | tf_op jit(solution)/shard_map/ppermute | solution.py:428
  39.5 1.9 %collective-permute-start.12 = (bf16[272,128]{1,0:T(8,128)(2,1)S(1)}, bf16[272,128]{1,0:T(8,128)(2,1)S(1)}, u32[]{:S(2)}, u32[]{:S(2)}) collective-permute-start(bf16[272,128]{1,0:T(8,128)(2,1)S(1)} %get-tuple-element.15), channel_id=1, source_target_pairs={{0,8},{2,10},{4,12},{6,14},{8,0},{10,2},{12,4},{14,6},{16,24},{18,... | collective-permute-start | bytes 208904 | tf_op jit(solution)/shard_map/ppermute | solution.py:428
  41.4 1.2 %shard_map.85.short = f32[1,256]{1,0:T(1,128)S(1)} custom-call(s32[1,1]{1,0:T(1,128)S(6)} %copy.8.lengths, bf16[256,1024]{1,0:T(8,128)(2,1)S(1)} %bitcast.6, bf16[256,1024]{1,0:T(8,128)(2,1)S(1)} %collective-permute-done.near, bf16[256,1024]{1,0:T(8,128)(2,1)S(1)} %collective-permute-done.4.across, bf16[256,1024]{1,0:T(8,128)(2,1)S(1)} %collective-permute-done.3.corner, ...), custom_call_target="tpu_custom_call" | custom-call | flops 402653184 | bytes 2097152 | tf_op jit(solution)/shard_map/pallas_call | solution.py:465
  42.6 1.3 %collective-permute-done.10.state_3 = bf16[272,128]{1,0:T(8,128)(2,1)S(1)} collective-permute-done((bf16[272,128]{1,0:T(8,128)(2,1)S(1)}, bf16[272,128]{1,0:T(8,128)(2,1)S(1)}, u32[]{:S(2)}, u32[]{:S(2)}) %collective-permute-start.10) | collective-permute-done | bytes 69664 | tf_op jit(solution)/shard_map/ppermute | solution.py:428
  43.9 1.4 %collective-permute-done.11.state_2 = bf16[272,128]{1,0:T(8,128)(2,1)S(1)} collective-permute-done((bf16[272,128]{1,0:T(8,128)(2,1)S(1)}, bf16[272,128]{1,0:T(8,128)(2,1)S(1)}, u32[]{:S(2)}, u32[]{:S(2)}) %collective-permute-start.11) | collective-permute-done | bytes 69664 | tf_op jit(solution)/shard_map/ppermute | solution.py:428
  45.3 0.9 %shard_map.86 = f32[32,1,640]{2,1,0:T(1,128)S(1)} custom-call(s32[1,1]{1,0:T(1,128)S(6)} %copy.8.lengths, bf16[272,128]{1,0:T(8,128)(2,1)S(1)} %collective-permute-done.10.state_3, bf16[272,128]{1,0:T(8,128)(2,1)S(1)} %collective-permute-done.11.state_2, bf16[272,128]{1,0:T(8,128)(2,1)S(1)} %collective-permute-done.12.state_1, ...), custom_call_target="tpu_custom_call" | custom-call | flops 301989888 | bytes 2097152 | tf_op jit(solution)/shard_map/pallas_call | solution.py:472
  46.1 11.6 %all_to_all.5.parts = f32[32,1,640]{2,1,0:T(1,128)S(1)} all-to-all(f32[32,1,640]{2,1,0:T(1,128)S(1)} %shard_map.86), channel_id=1, replica_groups=mesh['seq'=8,'dp'=2,'domain'=2] {'seq','dp','domain'}, dimensions={0} | all-to-all | bytes 163840 | tf_op jit(solution)/shard_map/all_to_all | solution.py:479
  57.7 1.2 %shard_map.87 = (bf16[1,1,128]{2,1,0:T(2,128)(2,1)}, f32[1,1]{1,0:T(1,128)}) custom-call(s32[2]{0:T(128)S(1)} %copy-done.3, f32[32,1,640]{2,1,0:T(1,128)S(1)} %all_to_all.5.parts), custom_call_target="tpu_custom_call" | custom-call | flops 16384 | bytes 2097152 | tf_op jit(solution)/shard_map/pallas_call | solution.py:480
  (24 shorter events, 0.5 us)
Async XLA Ops:
  0.6 11.4 %copy-start = (bf16[1,1,256,1024]{3,2,1,0:T(8,128)(2,1)S(1)}, bf16[1,1,256,1024]{3,2,1,0:T(8,128)(2,1)}, u32[]{:S(2)}) copy-start(bf16[1,1,256,1024]{3,2,1,0:T(8,128)(2,1)} %param.6) | copy-start | bytes 1572868
  0.6 1.2 %copy-start.1 = (bf16[1,128,3072]{2,1,0:T(8,128)(2,1)S(1)}, bf16[1,128,3072]{2,1,0:T(8,128)(2,1)}, u32[]{:S(2)}) copy-start(bf16[1,128,3072]{2,1,0:T(8,128)(2,1)} %param.7) | copy-start | bytes 2359300
  2.0 10.1 %collective-permute-start.1 = (bf16[128,768]{1,0:T(8,128)(2,1)S(1)}, bf16[128,768]{1,0:T(8,128)(2,1)S(1)}, u32[]{:S(2)}, u32[]{:S(2)}) collective-permute-start(bf16[128,768]{1,0:T(8,128)(2,1)S(1)} %get-tuple-element.10.values.refs_0_), channel_id=1, source_target_pairs={{0,8},{2,10},{4,12},{6,14},{8,0},{10,2},{12,4},{14,6},{16,24},{18,... | collective-permute-start | bytes 589832 | tf_op jit(solution)/shard_map/ppermute | solution.py:428
  5.1 7.0 %collective-permute-start.2 = (bf16[128,768]{1,0:T(8,128)(2,1)S(1)}, bf16[128,768]{1,0:T(8,128)(2,1)S(1)}, u32[]{:S(2)}, u32[]{:S(2)}) collective-permute-start(bf16[128,768]{1,0:T(8,128)(2,1)S(1)} %get-tuple-element.11.rest_0_), channel_id=1, source_target_pairs={{0,4},{2,6},{4,0},{6,2},{8,12},{10,14},{12,8},{14,10},{16,20},{18,... | collective-permute-start | bytes 589832 | tf_op jit(solution)/shard_map/ppermute | solution.py:431
  6.6 11.4 %collective-permute-start.6 = (bf16[128,768]{1,0:T(8,128)(2,1)S(1)}, bf16[128,768]{1,0:T(8,128)(2,1)S(1)}, u32[]{:S(2)}, u32[]{:S(2)}) collective-permute-start(bf16[128,768]{1,0:T(8,128)(2,1)S(1)} %shard_map.80), channel_id=1, source_target_pairs={{0,16},{2,18},{4,20},{6,22},{8,24},{10,26},{12,28},{14,30},{16,0},... | collective-permute-start | bytes 589832 | tf_op jit(solution)/shard_map/ppermute | solution.py:428
  9.2 25.7 %copy-start.2 = (f32[1,1024]{1,0:T(1,128)S(1)}, f32[1,1024]{1,0:T(1,128)}, u32[]{:S(2)}) copy-start(f32[1,1024]{1,0:T(1,128)} %gain.6) | copy-start | bytes 12292
  9.2 21.1 %collective-permute-start.4 = (bf16[256,1024]{1,0:T(8,128)(2,1)}, bf16[256,1024]{1,0:T(8,128)(2,1)S(1)}, u32[]{:S(2)}, u32[]{:S(2)}) collective-permute-start(bf16[256,1024]{1,0:T(8,128)(2,1)} %bitcast.2), channel_id=1, source_target_pairs={{0,2},{2,0},{4,6},{6,4},{8,10},{10,8},{12,14},{14,12},{16,18},{18,... | collective-permute-start | bytes 1572872 | tf_op jit(solution)/shard_map/ppermute | solution.py:431
  10.7 25.0 %collective-permute-start = (bf16[256,1024]{1,0:T(8,128)(2,1)}, bf16[256,1024]{1,0:T(8,128)(2,1)S(1)}, u32[]{:S(2)}, u32[]{:S(2)}) collective-permute-start(bf16[256,1024]{1,0:T(8,128)(2,1)} %bitcast.3), channel_id=1, source_target_pairs={{0,4},{2,6},{4,0},{6,2},{8,12},{10,14},{12,8},{14,10},{16,20},{18,... | collective-permute-start | bytes 1572872 | tf_op jit(solution)/shard_map/ppermute | solution.py:431
  12.1 23.7 %collective-permute-start.3 = (bf16[256,1024]{1,0:T(8,128)(2,1)S(1)}, bf16[256,1024]{1,0:T(8,128)(2,1)S(1)}, u32[]{:S(2)}, u32[]{:S(2)}) collective-permute-start(bf16[256,1024]{1,0:T(8,128)(2,1)S(1)} %shard_map.78), channel_id=1, source_target_pairs={{0,6},{2,4},{4,2},{6,0},{8,14},{10,12},{12,10},{14,8},{16,22},{18,... | collective-permute-start | bytes 1572872 | tf_op jit(solution)/shard_map/ppermute | solution.py:431
  16.5 9.8 %collective-permute-start.5 = (bf16[128,768]{1,0:T(8,128)(2,1)S(1)}, bf16[128,768]{1,0:T(8,128)(2,1)S(1)}, u32[]{:S(2)}, u32[]{:S(2)}) collective-permute-start(bf16[128,768]{1,0:T(8,128)(2,1)S(1)} %shard_map.79), channel_id=1, source_target_pairs={{0,8},{2,10},{4,12},{6,14},{8,0},{10,2},{12,4},{14,6},{16,24},{18,... | collective-permute-start | bytes 589832 | tf_op jit(solution)/shard_map/ppermute | solution.py:428
  18.0 8.4 %collective-permute-start.7 = (bf16[128,768]{1,0:T(8,128)(2,1)S(1)}, bf16[128,768]{1,0:T(8,128)(2,1)S(1)}, u32[]{:S(2)}, u32[]{:S(2)}) collective-permute-start(bf16[128,768]{1,0:T(8,128)(2,1)S(1)} %collective-permute-done.2.rest_1_.values.refs_1_), channel_id=1, source_target_pairs={{0,16},{2,18},{4,20},{6,22},{8,24},{10,26},{12,28},{14,30},{16,0},... | collective-permute-start | bytes 589832 | tf_op jit(solution)/shard_map/ppermute | solution.py:428
  26.3 6.5 %collective-permute-start.8 = (bf16[128,768]{1,0:T(8,128)(2,1)S(1)}, bf16[128,768]{1,0:T(8,128)(2,1)S(1)}, u32[]{:S(2)}, u32[]{:S(2)}) collective-permute-start(bf16[128,768]{1,0:T(8,128)(2,1)S(1)} %shard_map.81), channel_id=1, source_target_pairs={{0,8},{2,10},{4,12},{6,14},{8,0},{10,2},{12,4},{14,6},{16,24},{18,... | collective-permute-start | bytes 589832 | tf_op jit(solution)/shard_map/ppermute | solution.py:428
  26.4 8.5 %collective-permute-start.9 = (bf16[128,768]{1,0:T(8,128)(2,1)S(1)}, bf16[128,768]{1,0:T(8,128)(2,1)S(1)}, u32[]{:S(2)}, u32[]{:S(2)}) collective-permute-start(bf16[128,768]{1,0:T(8,128)(2,1)S(1)} %shard_map.82), channel_id=1, source_target_pairs={{0,8},{2,10},{4,12},{6,14},{8,0},{10,2},{12,4},{14,6},{16,24},{18,... | collective-permute-start | bytes 589832 | tf_op jit(solution)/shard_map/ppermute | solution.py:428
  36.9 8.4 %copy-start.4 = (f32[1,1024]{1,0:T(1,128)S(1)}, f32[1,1024]{1,0:T(1,128)}, u32[]{:S(2)}) copy-start(f32[1,1024]{1,0:T(1,128)} %gain.7) | copy-start | bytes 12292
  36.9 20.8 %copy-start.3 = (s32[2]{0:T(128)S(1)}, s32[2]{0:T(128)}, u32[]{:S(2)}) copy-start(s32[2]{0:T(128)} %positives.1) | copy-start | bytes 28
  36.9 7.0 %collective-permute-start.10 = (bf16[272,128]{1,0:T(8,128)(2,1)S(1)}, bf16[272,128]{1,0:T(8,128)(2,1)S(1)}, u32[]{:S(2)}, u32[]{:S(2)}) collective-permute-start(bf16[272,128]{1,0:T(8,128)(2,1)S(1)} %get-tuple-element.15), channel_id=1, source_target_pairs={{0,24},{2,26},{4,28},{6,30},{8,16},{10,18},{12,20},{14,22},{16,8},... | collective-permute-start | bytes 208904 | tf_op jit(solution)/shard_map/ppermute | solution.py:428
  39.3 5.9 %collective-permute-start.11 = (bf16[272,128]{1,0:T(8,128)(2,1)S(1)}, bf16[272,128]{1,0:T(8,128)(2,1)S(1)}, u32[]{:S(2)}, u32[]{:S(2)}) collective-permute-start(bf16[272,128]{1,0:T(8,128)(2,1)S(1)} %get-tuple-element.15), channel_id=1, source_target_pairs={{0,16},{2,18},{4,20},{6,22},{8,24},{10,26},{12,28},{14,30},{16,0},... | collective-permute-start | bytes 208904 | tf_op jit(solution)/shard_map/ppermute | solution.py:428
  39.5 5.8 %collective-permute-start.12 = (bf16[272,128]{1,0:T(8,128)(2,1)S(1)}, bf16[272,128]{1,0:T(8,128)(2,1)S(1)}, u32[]{:S(2)}, u32[]{:S(2)}) collective-permute-start(bf16[272,128]{1,0:T(8,128)(2,1)S(1)} %get-tuple-element.15), channel_id=1, source_target_pairs={{0,8},{2,10},{4,12},{6,14},{8,0},{10,2},{12,4},{14,6},{16,24},{18,... | collective-permute-start | bytes 208904 | tf_op jit(solution)/shard_map/ppermute | solution.py:428

commit v14 on v13

--- a/solution.py
+++ b/solution.py
@@ -137,6 +137,7 @@
 PLANES = 4
 GROUP = 256
 DOT_T = (((0,), (0,)), ((), ()))
+DOT_NT = (((1,), (1,)), ((), ()))
 MESSAGE = GROUP + 16
 
 
@@ -280,6 +281,17 @@
     return jnp.sum(weight * value.astype(jnp.float32), axis=0, keepdims=True)
 
 
+def local_kernel(feats, local):
+    tokens = feats.shape[0] // 2
+    lower = triangle(tokens, False)
+    carry = jnp.zeros((1, GROUP), jnp.float32)
+    for slot in range(2):
+        at = pl.ds(slot * tokens, tokens)
+        prefix = jnp.dot(lower, feats[at, GROUP : 2 * GROUP], preferred_element_type=jnp.float32) + carry
+        local[at, :] = by_head(head_sums(feats[at, :GROUP].astype(jnp.float32) * prefix))
+        carry = prefix[tokens - 1 :, :]
+
+
 def short_kernel(lengths, own, near, across, corner, weights, gain, out, raw):
     tokens = own.shape[0]
     z, x, u = places()
@@ -305,7 +317,7 @@
         out[...] = total + weighted(key, value, suffix(share))
 
 
-def pool_kernel(lengths, state_3, state_2, state_1, feats, sums, short, gain, part):
+def pool_kernel(lengths, state_3, state_2, state_1, feats, local, sums, short, gain, part):
     tokens = feats.shape[0] // 2
     z, x, u = places()
     long_u = jnp.where(lengths[0, 0] > tokens, u, 1 - u)
@@ -322,8 +334,19 @@
 
     query_one, key_one, value_one = block(0)
     query_two, key_two, value_two = block(1)
-    share_one, carry = shares(query_one, key_one, before)
-    share_two, _ = shares(query_two, key_two, carry)
+    row = lax.broadcasted_iota(jnp.int32, (GROUP, GROUP), 0) < HEAD_DIM
+    col = lax.broadcasted_iota(jnp.int32, (GROUP, GROUP), 1) < HEAD_DIM
+    same_head = jnp.where(row == col, jnp.broadcast_to(before, (GROUP, GROUP)), 0.0)
+    high, low = split_two(same_head)
+
+    def share(query, at):
+        total = local[at : at + tokens, :]
+        for table in (high, low):
+            total = total + lax.dot_general(query, table, DOT_NT, preferred_element_type=jnp.float32)
+        return query.astype(jnp.float32) / total
+
+    share_one = share(query_one, 0)
+    share_two = share(query_two, tokens)
     after_two = suffix(share_two)
     after_one = suffix(share_one) + after_two[0:1, :]
     long_row = weighted(key_one, value_one, after_one) + weighted(key_two, value_two, after_two) + sums[...]
@@ -436,7 +459,7 @@
     wide = 3 * GROUP
     w_own, w_sent = call(
         pack_kernel, (shape((rows, wide), bf16),) * 2, [hbm()], [pltpu.SemaphoreType.DMA((6,))], 0
-    )(weight)
+    )(pltpu.with_memory_space_constraint(weight, pltpu.HBM))
     near = plane_hop(events, 2)
     across = plane_hop(events, 1)
     w_near = plane_hop(w_sent, 2)
@@ -469,13 +492,16 @@
         [pltpu.VMEM((tokens, width), bf16)],
         2 * tokens * width * wide,
     )(lengths, events, near, across, corner, weights, norm_gain)
+    local = call(
+        local_kernel, shape((2 * tokens, GROUP), f32), [vmem()], [], 2 * 2 * tokens * tokens * GROUP
+    )(feats)
     part = call(
         pool_kernel,
         shape((2 * here, 1, 2 * GROUP + HEAD_DIM), f32),
-        [smem()] + [vmem()] * 7,
+        [smem()] + [vmem()] * 8,
         [],
         2 * 9 * tokens * tokens * GROUP,
-    )(lengths, *each(message)[::-1], feats, sums, short, pool_gain)
+    )(lengths, *each(message)[::-1], feats, local, sums, short, pool_gain)
     parts = lax.all_to_all(part, ("seq", "dp", "domain"), 0, 0, tiled=True)
     vec, loss = call(
         loss_kernel,

time: 59.1 us -> 58.9 us (level)
  Pallas kernels: 5.43 us -> 6.84 us
  local copies, waits for them, and re-layouts: 1.21 us -> 0.02 us
    unnamed x10 -> x8, local copies, waits for them, and re-layouts: 1.21 us -> 0.02 us
    pallas_call x1, Pallas kernels: 0.12 us -> 1.12 us  [towers(): call(pack_kernel, (shape((rows, wide), bf16),) * 2, [hbm()], [pltpu.Semap...]
where the time goes in v14:
time: 58.9 us; the launch traced here: 58.7 us
  starting transfers between devices  23.1 us (39%)
  waiting for transfers between devices  15.7 us (27%)
  blocking collectives  11.6 us (20%)
  Pallas kernels  6.84 us (12%)
  between operations  1.43 us (2%)
    ppermute x9, waiting for transfers between devices, hop(): return lax.ppermute(a, ('seq', 'dp'), pairs)  15.7 us
    ppermute x9, starting transfers between devices, hop(): return lax.ppermute(a, ('seq', 'dp'), pairs)  15.2 us
    all_to_all x1, blocking collectives, towers(): parts = lax.all_to_all(part, ('seq', 'dp', 'domain'), 0, 0, tiled=True)  11.6 us
    ppermute x4, starting transfers between devices, plane_hop(): return lax.ppermute(a, ('seq', 'dp'), [(i, i ^ move) for i in range(here)])  7.91 us
    pallas_call x1, Pallas kernels, towers(): call(short_kernel, shape((1, GROUP), f32), [smem()] + [vmem()] * 6, [pltp...  1.25 us
    pallas_call x1, Pallas kernels, towers(): call(loss_kernel, (shape((1, 1, width // 8), bf16), shape((1, 1), f32)),...  1.19 us
  transfers between devices with their start and end apart: 13, of which 7 were waited for; matrix products, arithmetic and copies ran while one was open for 0% of the time, Pallas kernels for 4%

profile of v14, /device:TPU:0, one launch (start us, length us, event | category | flops | bytes accessed | tf_op | source)
XLA Modules:
  0.0 58.7 jit_solution(8944037626423198054)
XLA Ops:
  0.6 1.1 %shard_map.77 = (bf16[128,768]{1,0:T(8,128)(2,1)S(1)}, bf16[128,768]{1,0:T(8,128)(2,1)S(1)}) custom-call(bf16[128,3072]{1,0:T(8,128)(2,1)} %bitcast.7), custom_call_target="tpu_custom_call" | custom-call | bytes 2097152 | tf_op jit(solution)/shard_map/pallas_call | solution.py:460
  1.8 3.1 %collective-permute-start.1 = (bf16[128,768]{1,0:T(8,128)(2,1)S(1)}, bf16[128,768]{1,0:T(8,128)(2,1)S(1)}, u32[]{:S(2)}, u32[]{:S(2)}) collective-permute-start(bf16[128,768]{1,0:T(8,128)(2,1)S(1)} %get-tuple-element.10.values.refs_0_), channel_id=1, source_target_pairs={{0,8},{2,10},{4,12},{6,14},{8,0},{10,2},{12,4},{14,6},{16,24},{18,... | collective-permute-start | bytes 589832 | tf_op jit(solution)/shard_map/ppermute | solution.py:451
  4.9 1.5 %collective-permute-start.2 = (bf16[128,768]{1,0:T(8,128)(2,1)S(1)}, bf16[128,768]{1,0:T(8,128)(2,1)S(1)}, u32[]{:S(2)}, u32[]{:S(2)}) collective-permute-start(bf16[128,768]{1,0:T(8,128)(2,1)S(1)} %get-tuple-element.11.rest_0_), channel_id=1, source_target_pairs={{0,4},{2,6},{4,0},{6,2},{8,12},{10,14},{12,8},{14,10},{16,20},{18,... | collective-permute-start | bytes 589832 | tf_op jit(solution)/shard_map/ppermute | solution.py:454
  6.4 2.7 %collective-permute-start.6 = (bf16[128,768]{1,0:T(8,128)(2,1)S(1)}, bf16[128,768]{1,0:T(8,128)(2,1)S(1)}, u32[]{:S(2)}, u32[]{:S(2)}) collective-permute-start(bf16[128,768]{1,0:T(8,128)(2,1)S(1)} %shard_map.80), channel_id=1, source_target_pairs={{0,16},{2,18},{4,20},{6,22},{8,24},{10,26},{12,28},{14,30},{16,0},... | collective-permute-start | bytes 589832 | tf_op jit(solution)/shard_map/ppermute | solution.py:451
  9.0 1.5 %collective-permute-start.4 = (bf16[256,1024]{1,0:T(8,128)(2,1)}, bf16[256,1024]{1,0:T(8,128)(2,1)S(1)}, u32[]{:S(2)}, u32[]{:S(2)}) collective-permute-start(bf16[256,1024]{1,0:T(8,128)(2,1)} %bitcast.2), channel_id=1, source_target_pairs={{0,2},{2,0},{4,6},{6,4},{8,10},{10,8},{12,14},{14,12},{16,18},{18,... | collective-permute-start | bytes 1572872 | tf_op jit(solution)/shard_map/ppermute | solution.py:454
  10.5 0.5 collective-permute-start
  11.1 0.8 %collective-permute-done.1.rest_0_.refs_2_ = bf16[128,768]{1,0:T(8,128)(2,1)S(1)} collective-permute-done((bf16[128,768]{1,0:T(8,128)(2,1)S(1)}, bf16[128,768]{1,0:T(8,128)(2,1)S(1)}, u32[]{:S(2)}, u32[]{:S(2)}) %collective-permute-start.1) | collective-permute-done | bytes 196640 | tf_op jit(solution)/shard_map/ppermute | solution.py:451
  11.9 4.4 %collective-permute-start.3 = (bf16[256,1024]{1,0:T(8,128)(2,1)S(1)}, bf16[256,1024]{1,0:T(8,128)(2,1)S(1)}, u32[]{:S(2)}, u32[]{:S(2)}) collective-permute-start(bf16[256,1024]{1,0:T(8,128)(2,1)S(1)} %shard_map.78), channel_id=1, source_target_pairs={{0,6},{2,4},{4,2},{6,0},{8,14},{10,12},{12,10},{14,8},{16,22},{18,... | collective-permute-start | bytes 1572872 | tf_op jit(solution)/shard_map/ppermute | solution.py:454
  16.3 1.4 %collective-permute-done.6.values.refs_4_ = bf16[128,768]{1,0:T(8,128)(2,1)S(1)} collective-permute-done((bf16[128,768]{1,0:T(8,128)(2,1)S(1)}, bf16[128,768]{1,0:T(8,128)(2,1)S(1)}, u32[]{:S(2)}, u32[]{:S(2)}) %collective-permute-start.6) | collective-permute-done | bytes 196640 | tf_op jit(solution)/shard_map/ppermute | solution.py:451
  17.8 1.6 %collective-permute-start.7 = (bf16[128,768]{1,0:T(8,128)(2,1)S(1)}, bf16[128,768]{1,0:T(8,128)(2,1)S(1)}, u32[]{:S(2)}, u32[]{:S(2)}) collective-permute-start(bf16[128,768]{1,0:T(8,128)(2,1)S(1)} %collective-permute-done.2.rest_1_.values.refs_1_), channel_id=1, source_target_pairs={{0,16},{2,18},{4,20},{6,22},{8,24},{10,26},{12,28},{14,30},{16,0},... | collective-permute-start | bytes 589832 | tf_op jit(solution)/shard_map/ppermute | solution.py:451
  19.4 6.7 %collective-permute-done.5.rest_0_.refs_3_ = bf16[128,768]{1,0:T(8,128)(2,1)S(1)} collective-permute-done((bf16[128,768]{1,0:T(8,128)(2,1)S(1)}, bf16[128,768]{1,0:T(8,128)(2,1)S(1)}, u32[]{:S(2)}, u32[]{:S(2)}) %collective-permute-start.5) | collective-permute-done | bytes 196640 | tf_op jit(solution)/shard_map/ppermute | solution.py:451
  26.2 3.3 %collective-permute-start.9 = (bf16[128,768]{1,0:T(8,128)(2,1)S(1)}, bf16[128,768]{1,0:T(8,128)(2,1)S(1)}, u32[]{:S(2)}, u32[]{:S(2)}) collective-permute-start(bf16[128,768]{1,0:T(8,128)(2,1)S(1)} %shard_map.82), channel_id=1, source_target_pairs={{0,8},{2,10},{4,12},{6,14},{8,0},{10,2},{12,4},{14,6},{16,24},{18,... | collective-permute-start | bytes 589832 | tf_op jit(solution)/shard_map/ppermute | solution.py:451
  30.2 2.5 %collective-permute-done.8.refs_6_ = bf16[128,768]{1,0:T(8,128)(2,1)S(1)} collective-permute-done((bf16[128,768]{1,0:T(8,128)(2,1)S(1)}, bf16[128,768]{1,0:T(8,128)(2,1)S(1)}, u32[]{:S(2)}, u32[]{:S(2)}) %collective-permute-start.8) | collective-permute-done | bytes 196640 | tf_op jit(solution)/shard_map/ppermute | solution.py:451
  32.6 2.1 %collective-permute-done.9.refs_7_ = bf16[128,768]{1,0:T(8,128)(2,1)S(1)} collective-permute-done((bf16[128,768]{1,0:T(8,128)(2,1)S(1)}, bf16[128,768]{1,0:T(8,128)(2,1)S(1)}, u32[]{:S(2)}, u32[]{:S(2)}) %collective-permute-start.9) | collective-permute-done | bytes 196640 | tf_op jit(solution)/shard_map/ppermute | solution.py:451
  34.7 0.8 %shard_map.83 = (bf16[256,768]{1,0:T(8,128)(2,1)S(1)}, f32[1,256]{1,0:T(1,128)S(1)}, bf16[1024,768]{1,0:T(8,128)(2,1)S(1)}) custom-call(s32[1,1]{1,0:T(1,128)S(6)} %copy.8.lengths, bf16[256,1024]{1,0:T(8,128)(2,1)S(1)} %bitcast.5, bf16[256,1024]{1,0:T(8,128)(2,1)S(1)} %collective-permute-done.4.across, f32[1,1024]{1,0:T(1,128)S(1)} %copy-done.1, ...), custom_call_target="tpu_custom_call" | custom-call | flops 402653184 | bytes 2097152 | tf_op jit(solution)/shard_map/pallas_call | solution.py:474
  35.6 1.1 %shard_map.84 = (bf16[512,768]{1,0:T(8,128)(2,1)S(1)}, bf16[272,128]{1,0:T(8,128)(2,1)S(1)}, f32[1,256]{1,0:T(1,128)S(1)}) custom-call(s32[1,1]{1,0:T(1,128)S(6)} %copy.8.lengths, bf16[256,1024]{1,0:T(8,128)(2,1)S(1)} %collective-permute-done.near, bf16[256,1024]{1,0:T(8,128)(2,1)S(1)} %collective-permute-done.3.corner, f32[1,1024]{1,0:T(1,128)S(1)} %copy-done.1, ...), custom_call_target="tpu_custom_call" | custom-call | flops 402653184 | bytes 2097152 | tf_op jit(solution)/shard_map/pallas_call | solution.py:481
  36.7 2.4 %collective-permute-start.10 = (bf16[272,128]{1,0:T(8,128)(2,1)S(1)}, bf16[272,128]{1,0:T(8,128)(2,1)S(1)}, u32[]{:S(2)}, u32[]{:S(2)}) collective-permute-start(bf16[272,128]{1,0:T(8,128)(2,1)S(1)} %get-tuple-element.15), channel_id=1, source_target_pairs={{0,24},{2,26},{4,28},{6,30},{8,16},{10,18},{12,20},{14,22},{16,8},... | collective-permute-start | bytes 208904 | tf_op jit(solution)/shard_map/ppermute | solution.py:451
  39.3 1.9 %collective-permute-start.12 = (bf16[272,128]{1,0:T(8,128)(2,1)S(1)}, bf16[272,128]{1,0:T(8,128)(2,1)S(1)}, u32[]{:S(2)}, u32[]{:S(2)}) collective-permute-start(bf16[272,128]{1,0:T(8,128)(2,1)S(1)} %get-tuple-element.15), channel_id=1, source_target_pairs={{0,8},{2,10},{4,12},{6,14},{8,0},{10,2},{12,4},{14,6},{16,24},{18,... | collective-permute-start | bytes 208904 | tf_op jit(solution)/shard_map/ppermute | solution.py:451
  41.6 1.2 %shard_map.86.short = f32[1,256]{1,0:T(1,128)S(1)} custom-call(s32[1,1]{1,0:T(1,128)S(6)} %copy.8.lengths, bf16[256,1024]{1,0:T(8,128)(2,1)S(1)} %bitcast.6, bf16[256,1024]{1,0:T(8,128)(2,1)S(1)} %collective-permute-done.near, bf16[256,1024]{1,0:T(8,128)(2,1)S(1)} %collective-permute-done.4.across, bf16[256,1024]{1,0:T(8,128)(2,1)S(1)} %collective-permute-done.3.corner, ...), custom_call_target="tpu_custom_call" | custom-call | flops 402653184 | bytes 2097152 | tf_op jit(solution)/shard_map/pallas_call | solution.py:488
  42.8 0.8 %collective-permute-done.10.state_3 = bf16[272,128]{1,0:T(8,128)(2,1)S(1)} collective-permute-done((bf16[272,128]{1,0:T(8,128)(2,1)S(1)}, bf16[272,128]{1,0:T(8,128)(2,1)S(1)}, u32[]{:S(2)}, u32[]{:S(2)}) %collective-permute-start.10) | collective-permute-done | bytes 69664 | tf_op jit(solution)/shard_map/ppermute | solution.py:451
  43.7 1.4 %collective-permute-done.11.state_2 = bf16[272,128]{1,0:T(8,128)(2,1)S(1)} collective-permute-done((bf16[272,128]{1,0:T(8,128)(2,1)S(1)}, bf16[272,128]{1,0:T(8,128)(2,1)S(1)}, u32[]{:S(2)}, u32[]{:S(2)}) %collective-permute-start.11) | collective-permute-done | bytes 69664 | tf_op jit(solution)/shard_map/ppermute | solution.py:451
  45.1 0.9 %shard_map.87 = f32[32,1,640]{2,1,0:T(1,128)S(1)} custom-call(s32[1,1]{1,0:T(1,128)S(6)} %copy.8.lengths, bf16[272,128]{1,0:T(8,128)(2,1)S(1)} %collective-permute-done.10.state_3, bf16[272,128]{1,0:T(8,128)(2,1)S(1)} %collective-permute-done.11.state_2, bf16[272,128]{1,0:T(8,128)(2,1)S(1)} %collective-permute-done.12.state_1, ...), custom_call_target="tpu_custom_call" | custom-call | flops 301989888 | bytes 2097152 | tf_op jit(solution)/shard_map/pallas_call | solution.py:498
  45.9 11.6 %all_to_all.5.parts = f32[32,1,640]{2,1,0:T(1,128)S(1)} all-to-all(f32[32,1,640]{2,1,0:T(1,128)S(1)} %shard_map.87), channel_id=1, replica_groups=mesh['seq'=8,'dp'=2,'domain'=2] {'seq','dp','domain'}, dimensions={0} | all-to-all | bytes 163840 | tf_op jit(solution)/shard_map/all_to_all | solution.py:505
  57.5 1.2 %shard_map.88 = (bf16[1,1,128]{2,1,0:T(2,128)(2,1)}, f32[1,1]{1,0:T(1,128)}) custom-call(s32[2]{0:T(128)S(1)} %copy-done.3, f32[32,1,640]{2,1,0:T(1,128)S(1)} %all_to_all.5.parts), custom_call_target="tpu_custom_call" | custom-call | flops 16384 | bytes 2097152 | tf_op jit(solution)/shard_map/pallas_call | solution.py:506
  (23 shorter events, 0.8 us)
Async XLA Ops:
  0.6 11.2 %copy-start = (bf16[1,1,256,1024]{3,2,1,0:T(8,128)(2,1)S(1)}, bf16[1,1,256,1024]{3,2,1,0:T(8,128)(2,1)}, u32[]{:S(2)}) copy-start(bf16[1,1,256,1024]{3,2,1,0:T(8,128)(2,1)} %param.6) | copy-start | bytes 1572868
  1.8 10.1 %collective-permute-start.1 = (bf16[128,768]{1,0:T(8,128)(2,1)S(1)}, bf16[128,768]{1,0:T(8,128)(2,1)S(1)}, u32[]{:S(2)}, u32[]{:S(2)}) collective-permute-start(bf16[128,768]{1,0:T(8,128)(2,1)S(1)} %get-tuple-element.10.values.refs_0_), channel_id=1, source_target_pairs={{0,8},{2,10},{4,12},{6,14},{8,0},{10,2},{12,4},{14,6},{16,24},{18,... | collective-permute-start | bytes 589832 | tf_op jit(solution)/shard_map/ppermute | solution.py:451
  4.9 7.0 %collective-permute-start.2 = (bf16[128,768]{1,0:T(8,128)(2,1)S(1)}, bf16[128,768]{1,0:T(8,128)(2,1)S(1)}, u32[]{:S(2)}, u32[]{:S(2)}) collective-permute-start(bf16[128,768]{1,0:T(8,128)(2,1)S(1)} %get-tuple-element.11.rest_0_), channel_id=1, source_target_pairs={{0,4},{2,6},{4,0},{6,2},{8,12},{10,14},{12,8},{14,10},{16,20},{18,... | collective-permute-start | bytes 589832 | tf_op jit(solution)/shard_map/ppermute | solution.py:454
  6.4 11.4 %collective-permute-start.6 = (bf16[128,768]{1,0:T(8,128)(2,1)S(1)}, bf16[128,768]{1,0:T(8,128)(2,1)S(1)}, u32[]{:S(2)}, u32[]{:S(2)}) collective-permute-start(bf16[128,768]{1,0:T(8,128)(2,1)S(1)} %shard_map.80), channel_id=1, source_target_pairs={{0,16},{2,18},{4,20},{6,22},{8,24},{10,26},{12,28},{14,30},{16,0},... | collective-permute-start | bytes 589832 | tf_op jit(solution)/shard_map/ppermute | solution.py:451
  9.0 25.7 %copy-start.1 = (f32[1,1024]{1,0:T(1,128)S(1)}, f32[1,1024]{1,0:T(1,128)}, u32[]{:S(2)}) copy-start(f32[1,1024]{1,0:T(1,128)} %gain.6) | copy-start | bytes 12292
  9.0 21.1 %collective-permute-start.4 = (bf16[256,1024]{1,0:T(8,128)(2,1)}, bf16[256,1024]{1,0:T(8,128)(2,1)S(1)}, u32[]{:S(2)}, u32[]{:S(2)}) collective-permute-start(bf16[256,1024]{1,0:T(8,128)(2,1)} %bitcast.2), channel_id=1, source_target_pairs={{0,2},{2,0},{4,6},{6,4},{8,10},{10,8},{12,14},{14,12},{16,18},{18,... | collective-permute-start | bytes 1572872 | tf_op jit(solution)/shard_map/ppermute | solution.py:454
  10.5 25.0 %collective-permute-start = (bf16[256,1024]{1,0:T(8,128)(2,1)}, bf16[256,1024]{1,0:T(8,128)(2,1)S(1)}, u32[]{:S(2)}, u32[]{:S(2)}) collective-permute-start(bf16[256,1024]{1,0:T(8,128)(2,1)} %bitcast.3), channel_id=1, source_target_pairs={{0,4},{2,6},{4,0},{6,2},{8,12},{10,14},{12,8},{14,10},{16,20},{18,... | collective-permute-start | bytes 1572872 | tf_op jit(solution)/shard_map/ppermute | solution.py:454
  11.9 23.7 %collective-permute-start.3 = (bf16[256,1024]{1,0:T(8,128)(2,1)S(1)}, bf16[256,1024]{1,0:T(8,128)(2,1)S(1)}, u32[]{:S(2)}, u32[]{:S(2)}) collective-permute-start(bf16[256,1024]{1,0:T(8,128)(2,1)S(1)} %shard_map.78), channel_id=1, source_target_pairs={{0,6},{2,4},{4,2},{6,0},{8,14},{10,12},{12,10},{14,8},{16,22},{18,... | collective-permute-start | bytes 1572872 | tf_op jit(solution)/shard_map/ppermute | solution.py:454
  16.3 9.8 %collective-permute-start.5 = (bf16[128,768]{1,0:T(8,128)(2,1)S(1)}, bf16[128,768]{1,0:T(8,128)(2,1)S(1)}, u32[]{:S(2)}, u32[]{:S(2)}) collective-permute-start(bf16[128,768]{1,0:T(8,128)(2,1)S(1)} %shard_map.79), channel_id=1, source_target_pairs={{0,8},{2,10},{4,12},{6,14},{8,0},{10,2},{12,4},{14,6},{16,24},{18,... | collective-permute-start | bytes 589832 | tf_op jit(solution)/shard_map/ppermute | solution.py:451
  17.8 8.4 %collective-permute-start.7 = (bf16[128,768]{1,0:T(8,128)(2,1)S(1)}, bf16[128,768]{1,0:T(8,128)(2,1)S(1)}, u32[]{:S(2)}, u32[]{:S(2)}) collective-permute-start(bf16[128,768]{1,0:T(8,128)(2,1)S(1)} %collective-permute-done.2.rest_1_.values.refs_1_), channel_id=1, source_target_pairs={{0,16},{2,18},{4,20},{6,22},{8,24},{10,26},{12,28},{14,30},{16,0},... | collective-permute-start | bytes 589832 | tf_op jit(solution)/shard_map/ppermute | solution.py:451
  26.1 6.5 %collective-permute-start.8 = (bf16[128,768]{1,0:T(8,128)(2,1)S(1)}, bf16[128,768]{1,0:T(8,128)(2,1)S(1)}, u32[]{:S(2)}, u32[]{:S(2)}) collective-permute-start(bf16[128,768]{1,0:T(8,128)(2,1)S(1)} %shard_map.81), channel_id=1, source_target_pairs={{0,8},{2,10},{4,12},{6,14},{8,0},{10,2},{12,4},{14,6},{16,24},{18,... | collective-permute-start | bytes 589832 | tf_op jit(solution)/shard_map/ppermute | solution.py:451
  26.2 8.5 %collective-permute-start.9 = (bf16[128,768]{1,0:T(8,128)(2,1)S(1)}, bf16[128,768]{1,0:T(8,128)(2,1)S(1)}, u32[]{:S(2)}, u32[]{:S(2)}) collective-permute-start(bf16[128,768]{1,0:T(8,128)(2,1)S(1)} %shard_map.82), channel_id=1, source_target_pairs={{0,8},{2,10},{4,12},{6,14},{8,0},{10,2},{12,4},{14,6},{16,24},{18,... | collective-permute-start | bytes 589832 | tf_op jit(solution)/shard_map/ppermute | solution.py:451
  36.7 7.0 %collective-permute-start.10 = (bf16[272,128]{1,0:T(8,128)(2,1)S(1)}, bf16[272,128]{1,0:T(8,128)(2,1)S(1)}, u32[]{:S(2)}, u32[]{:S(2)}) collective-permute-start(bf16[272,128]{1,0:T(8,128)(2,1)S(1)} %get-tuple-element.15), channel_id=1, source_target_pairs={{0,24},{2,26},{4,28},{6,30},{8,16},{10,18},{12,20},{14,22},{16,8},... | collective-permute-start | bytes 208904 | tf_op jit(solution)/shard_map/ppermute | solution.py:451
  39.1 5.9 %collective-permute-start.11 = (bf16[272,128]{1,0:T(8,128)(2,1)S(1)}, bf16[272,128]{1,0:T(8,128)(2,1)S(1)}, u32[]{:S(2)}, u32[]{:S(2)}) collective-permute-start(bf16[272,128]{1,0:T(8,128)(2,1)S(1)} %get-tuple-element.15), channel_id=1, source_target_pairs={{0,16},{2,18},{4,20},{6,22},{8,24},{10,26},{12,28},{14,30},{16,0},... | collective-permute-start | bytes 208904 | tf_op jit(solution)/shard_map/ppermute | solution.py:451
  39.3 5.8 %collective-permute-start.12 = (bf16[272,128]{1,0:T(8,128)(2,1)S(1)}, bf16[272,128]{1,0:T(8,128)(2,1)S(1)}, u32[]{:S(2)}, u32[]{:S(2)}) collective-permute-start(bf16[272,128]{1,0:T(8,128)(2,1)S(1)} %get-tuple-element.15), channel_id=1, source_target_pairs={{0,8},{2,10},{4,12},{6,14},{8,0},{10,2},{12,4},{14,6},{16,24},{18,... | collective-permute-start | bytes 208904 | tf_op jit(solution)/shard_map/ppermute | solution.py:451
  41.6 3.5 %copy-start.2 = (f32[1,1024]{1,0:T(1,128)S(1)}, f32[1,1024]{1,0:T(1,128)}, u32[]{:S(2)}) copy-start(f32[1,1024]{1,0:T(1,128)} %gain.7) | copy-start | bytes 12292
  42.8 14.7 %copy-start.3 = (s32[2]{0:T(128)S(1)}, s32[2]{0:T(128)}, u32[]{:S(2)}) copy-start(s32[2]{0:T(128)} %positives.1) | copy-start | bytes 28

commit v15 on v14

--- a/solution.py
+++ b/solution.py
@@ -214,36 +214,55 @@
         dest[...] = second[...]
 
 
-def project(raw, gain, weights, feats, at):
+def column_sum(raw):
     _, x, u = places()
-    tokens = raw.shape[0]
-    query, key, value = features(
-        jnp.dot(normalise(raw[...], gain[...]), weights[...], preferred_element_type=jnp.float32)
-    )
-    rows = pl.ds(at, tokens)
+    columns = pl.ds(pl.multiple_of((2 * x + u) * GROUP, GROUP), GROUP)
+    return jnp.sum(raw[:, columns].astype(jnp.float32), axis=0, keepdims=True)
+
+
+def store(out, feats, at):
+    query, key, value = features(out)
+    rows = pl.ds(at, out.shape[0])
     feats[rows, :GROUP] = query
     feats[rows, GROUP : 2 * GROUP] = key
     feats[rows, 2 * GROUP :] = value
-    columns = pl.ds(pl.multiple_of((2 * x + u) * GROUP, GROUP), GROUP)
-    return jnp.sum(raw[:, columns].astype(jnp.float32), axis=0, keepdims=True)
-
-
-def first_kernel(lengths, own, across, gain, *refs):
-    feats, sums, weights, raw = refs[2 * PLANES :]
+
+
+def early_kernel(lengths, own, across, gain, *refs):
+    normed, partial, sums, weights, raw = refs[2 * PLANES - 2 :]
     z, x, _ = places()
-    for j in range(PLANES):
+    choose(lengths[0, 0] > own.shape[0], own, across, raw)
+    normed[...] = normalise(raw[...], gain[...])
+    sums[...] = column_sum(raw)
+    total = jnp.zeros(partial.shape, jnp.float32)
+    for j in range(PLANES - 1):
         start = pl.multiple_of(jnp.bitwise_xor(z, j) * GROUP, GROUP)
         place_rows(weights, start, x, refs[2 * j][...], refs[2 * j + 1][...])
-    choose(lengths[0, 0] > own.shape[0], own, across, raw)
-    sums[...] = project(raw, gain, weights, feats, 0)
-
-
-def second_kernel(lengths, near, corner, gain, weights, first, first_sums, feats, message, sums, raw):
+        rows = pl.ds(start, GROUP)
+        total = total + jnp.dot(normed[:, rows], weights[rows, :], preferred_element_type=jnp.float32)
+    weights[pl.ds(pl.multiple_of((PLANES - 1 - z) * GROUP, GROUP), GROUP), :] = jnp.zeros(
+        (GROUP, weights.shape[1]), weights.dtype
+    )
+    partial[...] = total
+
+
+def first_kernel(normed, partial, far_own, far_near, feats, last):
+    z, x, _ = places()
+    place_rows(last, 0, x, far_own[...], far_near[...])
+    columns = pl.ds(pl.multiple_of((PLANES - 1 - z) * GROUP, GROUP), GROUP)
+    store(partial[...] + jnp.dot(normed[:, columns], last[...], preferred_element_type=jnp.float32), feats, 0)
+
+
+def second_kernel(lengths, near, corner, gain, early, last, first, first_sums, feats, message, sums, weights, raw):
     tokens = near.shape[0]
-    _, x, _ = places()
+    z, x, _ = places()
+    weights[...] = early[...]
+    weights[pl.ds(pl.multiple_of((PLANES - 1 - z) * GROUP, GROUP), GROUP), :] = last[...]
     choose(lengths[0, 0] > tokens, near, corner, raw)
     feats[pl.ds(pl.multiple_of(x * tokens, tokens), tokens), :] = first[...]
-    sums[...] = first_sums[...] + project(raw, gain, weights, feats, pl.multiple_of((1 - x) * tokens, tokens))
+    out = jnp.dot(normalise(raw[...], gain[...]), weights[...], preferred_element_type=jnp.float32)
+    store(out, feats, pl.multiple_of((1 - x) * tokens, tokens))
+    sums[...] = first_sums[...] + column_sum(raw)
     total = jnp.sum(feats[:, GROUP : 2 * GROUP].astype(jnp.float32), axis=0, keepdims=True)
     high, low = split_two(total)
     for h in range(GROUP // HEAD_DIM):
@@ -317,7 +336,7 @@
         out[...] = total + weighted(key, value, suffix(share))
 
 
-def pool_kernel(lengths, state_3, state_2, state_1, feats, local, sums, short, gain, part):
+def pool_kernel(lengths, state_1, state_2, state_3, feats, local, sums, short, gain, part):
     tokens = feats.shape[0] // 2
     z, x, u = places()
     long_u = jnp.where(lengths[0, 0] > tokens, u, 1 - u)
@@ -471,20 +490,32 @@
     far_near = hop(call(gate_kernel, shape((rows, wide), bf16), [vmem()] + [anywhere()] * 1, [], 0)(two_near, one_near), lambda p: p ^ 1)
     corner = plane_hop(call(gate_kernel, shape((tokens, width), bf16), [vmem()] + [anywhere()] * 2, [], 0)(events, one_own, w_near), 3)
 
-    first, first_sums, weights = call(
+    normed, partial, first_sums, early = call(
+        early_kernel,
+        (shape((tokens, width), bf16), shape((tokens, wide), f32), shape((1, GROUP), f32), shape((width, wide), bf16)),
+        [smem()] + [vmem()] * (1 + 2 * PLANES),
+        [pltpu.VMEM((tokens, width), bf16)],
+        2 * tokens * 3 * GROUP * wide,
+    )(lengths, events, across, norm_gain, w_own, w_near, one_own, one_near, two_own, two_near)
+    first, last = call(
         first_kernel,
-        (shape((tokens, wide), bf16), shape((1, GROUP), f32), shape((width, wide), bf16)),
-        [smem()] + [vmem()] * (3 + 2 * PLANES),
+        (shape((tokens, wide), bf16), shape((GROUP, wide), bf16)),
+        [vmem()] * 4,
+        [],
+        2 * tokens * GROUP * wide,
+    )(normed, partial, far_own, far_near)
+    feats, message, sums, weights = call(
+        second_kernel,
+        (
+            shape((2 * tokens, wide), bf16),
+            shape((MESSAGE, HEAD_DIM), bf16),
+            shape((1, GROUP), f32),
+            shape((width, wide), bf16),
+        ),
+        [smem()] + [vmem()] * 7,
         [pltpu.VMEM((tokens, width), bf16)],
         2 * tokens * width * wide,
-    )(lengths, events, across, norm_gain, w_own, w_near, one_own, one_near, two_own, two_near, far_own, far_near)
-    feats, message, sums = call(
-        second_kernel,
-        (shape((2 * tokens, wide), bf16), shape((MESSAGE, HEAD_DIM), bf16), shape((1, GROUP), f32)),
-        [smem()] + [vmem()] * 6,
-        [pltpu.VMEM((tokens, width), bf16)],
-        2 * tokens * width * wide,
-    )(lengths, near, corner, norm_gain, weights, first, first_sums)
+    )(lengths, near, corner, norm_gain, early, last, first, first_sums)
     short = call(
         short_kernel,
         shape((1, GROUP), f32),
@@ -501,7 +532,7 @@
         [smem()] + [vmem()] * 8,
         [],
         2 * 9 * tokens * tokens * GROUP,
-    )(lengths, *each(message)[::-1], feats, local, sums, short, pool_gain)
+    )(lengths, *each(message), feats, local, sums, short, pool_gain)
     parts = lax.all_to_all(part, ("seq", "dp", "domain"), 0, 0, tiled=True)
     vec, loss = call(
         loss_kernel,

time: 58.9 us -> 57.8 us (0.981)
  starting transfers between devices: 23.1 us -> 17.9 us
  waiting for transfers between devices: 15.7 us -> 20 us
  blocking collectives: 11.6 us -> 10.9 us
    ppermute x9, waiting for transfers between devices: 15.7 us -> 19.8 us  [hop(): return lax.ppermute(a, ('seq', 'dp'), pairs)]
    ppermute x9, starting transfers between devices: 15.2 us -> 11.3 us  [hop(): return lax.ppermute(a, ('seq', 'dp'), pairs)]
    ppermute x4, starting transfers between devices: 7.91 us -> 6.61 us  [plane_hop(): return lax.ppermute(a, ('seq', 'dp'), [(i, i ^ move) for i in range(here)])]
    all_to_all x1, blocking collectives: 11.6 us -> 10.9 us  [towers(): parts = lax.all_to_all(part, ('seq', 'dp', 'domain'), 0, 0, tiled=True)]
    pallas_call x1 -> x2, Pallas kernels: 0.84 us -> 1.23 us  [the longest x1 0.87 us: towers(): call(early_kernel, (shape((tokens, width), bf16), shape((tokens, wide), f...]
  transfers between devices with their start and end apart: 13 -> 13, of which waited for: 7 -> 9; matrix products, arithmetic and copies ran while one was open for 0% -> 0% of each run, Pallas kernels for 4% -> 5%
where the time goes in v15:
time: 57.8 us; the launch traced here: 57.6 us
  waiting for transfers between devices  20 us (35%)
  starting transfers between devices  17.9 us (31%)
  blocking collectives  10.9 us (19%)
  Pallas kernels  7.34 us (13%)
  between operations  1.42 us (2%)
    ppermute x9, waiting for transfers between devices, hop(): return lax.ppermute(a, ('seq', 'dp'), pairs)  19.8 us
    ppermute x9, starting transfers between devices, hop(): return lax.ppermute(a, ('seq', 'dp'), pairs)  11.3 us
    all_to_all x1, blocking collectives, towers(): parts = lax.all_to_all(part, ('seq', 'dp', 'domain'), 0, 0, tiled=True)  10.9 us
    ppermute x4, starting transfers between devices, plane_hop(): return lax.ppermute(a, ('seq', 'dp'), [(i, i ^ move) for i in range(here)])  6.61 us
    pallas_call x1, Pallas kernels, towers(): call(short_kernel, shape((1, GROUP), f32), [smem()] + [vmem()] * 6, [pltp...  1.25 us
    pallas_call x1, Pallas kernels, towers(): call(second_kernel, (shape((2 * tokens, wide), bf16), shape((MESSAGE, HEA...  1.2 us
    pallas_call x1, Pallas kernels, towers(): call(loss_kernel, (shape((1, 1, width // 8), bf16), shape((1, 1), f32)),...  1.19 us
  transfers between devices with their start and end apart: 13, of which 9 were waited for; matrix products, arithmetic and copies ran while one was open for 0% of the time, Pallas kernels for 5%

profile of v15, /device:TPU:0, one launch (start us, length us, event | category | flops | bytes accessed | tf_op | source)
XLA Modules:
  0.0 57.6 jit_solution(2953312877505458572)
XLA Ops:
  0.6 1.1 %shard_map.77 = (bf16[128,768]{1,0:T(8,128)(2,1)S(1)}, bf16[128,768]{1,0:T(8,128)(2,1)S(1)}) custom-call(bf16[128,3072]{1,0:T(8,128)(2,1)} %bitcast.7), custom_call_target="tpu_custom_call" | custom-call | bytes 2097152 | tf_op jit(solution)/shard_map/pallas_call | solution.py:479
  1.8 3.0 %collective-permute-start.2 = (bf16[128,768]{1,0:T(8,128)(2,1)S(1)}, bf16[128,768]{1,0:T(8,128)(2,1)S(1)}, u32[]{:S(2)}, u32[]{:S(2)}) collective-permute-start(bf16[128,768]{1,0:T(8,128)(2,1)S(1)} %get-tuple-element.15.rest_0_), channel_id=1, source_target_pairs={{0,4},{2,6},{4,0},{6,2},{8,12},{10,14},{12,8},{14,10},{16,20},{18,... | collective-permute-start | bytes 589832 | tf_op jit(solution)/shard_map/ppermute | solution.py:473
  4.8 1.6 %collective-permute-start.1 = (bf16[128,768]{1,0:T(8,128)(2,1)S(1)}, bf16[128,768]{1,0:T(8,128)(2,1)S(1)}, u32[]{:S(2)}, u32[]{:S(2)}) collective-permute-start(bf16[128,768]{1,0:T(8,128)(2,1)S(1)} %get-tuple-element.14.values.refs_0_), channel_id=1, source_target_pairs={{0,8},{2,10},{4,12},{6,14},{8,0},{10,2},{12,4},{14,6},{16,24},{18,... | collective-permute-start | bytes 589832 | tf_op jit(solution)/shard_map/ppermute | solution.py:470
  6.4 2.7 %collective-permute-start.6 = (bf16[128,768]{1,0:T(8,128)(2,1)S(1)}, bf16[128,768]{1,0:T(8,128)(2,1)S(1)}, u32[]{:S(2)}, u32[]{:S(2)}) collective-permute-start(bf16[128,768]{1,0:T(8,128)(2,1)S(1)} %shard_map.80), channel_id=1, source_target_pairs={{0,16},{2,18},{4,20},{6,22},{8,24},{10,26},{12,28},{14,30},{16,0},... | collective-permute-start | bytes 589832 | tf_op jit(solution)/shard_map/ppermute | solution.py:470
  9.0 1.5 %collective-permute-start.4 = (bf16[256,1024]{1,0:T(8,128)(2,1)}, bf16[256,1024]{1,0:T(8,128)(2,1)S(1)}, u32[]{:S(2)}, u32[]{:S(2)}) collective-permute-start(bf16[256,1024]{1,0:T(8,128)(2,1)} %bitcast.2), channel_id=1, source_target_pairs={{0,2},{2,0},{4,6},{6,4},{8,10},{10,8},{12,14},{14,12},{16,18},{18,... | collective-permute-start | bytes 1572872 | tf_op jit(solution)/shard_map/ppermute | solution.py:473
  10.5 0.5 collective-permute-start
  11.1 4.1 %collective-permute-done.1.rest_0_.refs_2_ = bf16[128,768]{1,0:T(8,128)(2,1)S(1)} collective-permute-done((bf16[128,768]{1,0:T(8,128)(2,1)S(1)}, bf16[128,768]{1,0:T(8,128)(2,1)S(1)}, u32[]{:S(2)}, u32[]{:S(2)}) %collective-permute-start.1) | collective-permute-done | bytes 196640 | tf_op jit(solution)/shard_map/ppermute | solution.py:470
  15.2 1.6 %collective-permute-start.3 = (bf16[256,1024]{1,0:T(8,128)(2,1)S(1)}, bf16[256,1024]{1,0:T(8,128)(2,1)S(1)}, u32[]{:S(2)}, u32[]{:S(2)}) collective-permute-start(bf16[256,1024]{1,0:T(8,128)(2,1)S(1)} %shard_map.78), channel_id=1, source_target_pairs={{0,6},{2,4},{4,2},{6,0},{8,14},{10,12},{12,10},{14,8},{16,22},{18,... | collective-permute-start | bytes 1572872 | tf_op jit(solution)/shard_map/ppermute | solution.py:473
  16.8 0.9 %collective-permute-done.6.refs_4_.values = bf16[128,768]{1,0:T(8,128)(2,1)S(1)} collective-permute-done((bf16[128,768]{1,0:T(8,128)(2,1)S(1)}, bf16[128,768]{1,0:T(8,128)(2,1)S(1)}, u32[]{:S(2)}, u32[]{:S(2)}) %collective-permute-start.6) | collective-permute-done | bytes 196640 | tf_op jit(solution)/shard_map/ppermute | solution.py:470
  17.8 2.1 %collective-permute-start.7 = (bf16[128,768]{1,0:T(8,128)(2,1)S(1)}, bf16[128,768]{1,0:T(8,128)(2,1)S(1)}, u32[]{:S(2)}, u32[]{:S(2)}) collective-permute-start(bf16[128,768]{1,0:T(8,128)(2,1)S(1)} %collective-permute-done.2.rest_1_.values.refs_1_), channel_id=1, source_target_pairs={{0,16},{2,18},{4,20},{6,22},{8,24},{10,26},{12,28},{14,30},{16,0},... | collective-permute-start | bytes 589832 | tf_op jit(solution)/shard_map/ppermute | solution.py:470
  19.9 6.2 %collective-permute-done.5.refs_3_.rest_0_ = bf16[128,768]{1,0:T(8,128)(2,1)S(1)} collective-permute-done((bf16[128,768]{1,0:T(8,128)(2,1)S(1)}, bf16[128,768]{1,0:T(8,128)(2,1)S(1)}, u32[]{:S(2)}, u32[]{:S(2)}) %collective-permute-start.5) | collective-permute-done | bytes 196640 | tf_op jit(solution)/shard_map/ppermute | solution.py:470
  26.1 1.8 %collective-permute-done.7.refs_5_.values = bf16[128,768]{1,0:T(8,128)(2,1)S(1)} collective-permute-done((bf16[128,768]{1,0:T(8,128)(2,1)S(1)}, bf16[128,768]{1,0:T(8,128)(2,1)S(1)}, u32[]{:S(2)}, u32[]{:S(2)}) %collective-permute-start.7) | collective-permute-done | bytes 196640 | tf_op jit(solution)/shard_map/ppermute | solution.py:470
  28.9 0.9 %shard_map.81 = (bf16[256,1024]{1,0:T(8,128)(2,1)S(1)}, f32[256,768]{1,0:T(8,128)S(1)}, f32[1,256]{1,0:T(1,128)S(1)}, bf16[1024,768]{1,0:T(8,128)(2,1)S(1)}) custom-call(s32[1,1]{1,0:T(1,128)S(6)} %copy.8.lengths, bf16[256,1024]{1,0:T(8,128)(2,1)S(1)} %bitcast.5, bf16[256,1024]{1,0:T(8,128)(2,1)S(1)} %collective-permute-done.4.across, ...), custom_call_target="tpu_custom_call" | custom-call | flops 301989888 | bytes 2097152 | tf_op jit(solution)/shard_map/pallas_call | solution.py:493
  29.8 2.0 %collective-permute-done.8.far_own = bf16[128,768]{1,0:T(8,128)(2,1)S(1)} collective-permute-done((bf16[128,768]{1,0:T(8,128)(2,1)S(1)}, bf16[128,768]{1,0:T(8,128)(2,1)S(1)}, u32[]{:S(2)}, u32[]{:S(2)}) %collective-permute-start.8) | collective-permute-done | bytes 196640 | tf_op jit(solution)/shard_map/ppermute | solution.py:470
  31.8 2.1 %collective-permute-done.9.far_near = bf16[128,768]{1,0:T(8,128)(2,1)S(1)} collective-permute-done((bf16[128,768]{1,0:T(8,128)(2,1)S(1)}, bf16[128,768]{1,0:T(8,128)(2,1)S(1)}, u32[]{:S(2)}, u32[]{:S(2)}) %collective-permute-start.9) | collective-permute-done | bytes 196640 | tf_op jit(solution)/shard_map/ppermute | solution.py:470
  34.5 1.2 %shard_map.85 = (bf16[512,768]{1,0:T(8,128)(2,1)S(1)}, bf16[272,128]{1,0:T(8,128)(2,1)S(1)}, f32[1,256]{1,0:T(1,128)S(1)}, bf16[1024,768]{1,0:T(8,128)(2,1)S(1)}) custom-call(s32[1,1]{1,0:T(1,128)S(6)} %copy.8.lengths, bf16[256,1024]{1,0:T(8,128)(2,1)S(1)} %collective-permute-done.near, bf16[256,1024]{1,0:T(8,128)(2,1)S(1)} %collective-permute-done.3.corner, ...), custom_call_target="tpu_custom_call" | custom-call | flops 402653184 | bytes 2097152 | tf_op jit(solution)/shard_map/pallas_call | solution.py:507
  35.7 3.7 %collective-permute-start.12 = (bf16[272,128]{1,0:T(8,128)(2,1)S(1)}, bf16[272,128]{1,0:T(8,128)(2,1)S(1)}, u32[]{:S(2)}, u32[]{:S(2)}) collective-permute-start(bf16[272,128]{1,0:T(8,128)(2,1)S(1)} %get-tuple-element.22), channel_id=1, source_target_pairs={{0,24},{2,26},{4,28},{6,30},{8,16},{10,18},{12,20},{14,22},{16,8},... | collective-permute-start | bytes 208904 | tf_op jit(solution)/shard_map/ppermute | solution.py:470
  39.4 0.7 %collective-permute-start.10 = (bf16[272,128]{1,0:T(8,128)(2,1)S(1)}, bf16[272,128]{1,0:T(8,128)(2,1)S(1)}, u32[]{:S(2)}, u32[]{:S(2)}) collective-permute-start(bf16[272,128]{1,0:T(8,128)(2,1)S(1)} %get-tuple-element.22), channel_id=1, source_target_pairs={{0,8},{2,10},{4,12},{6,14},{8,0},{10,2},{12,4},{14,6},{16,24},{18,... | collective-permute-start | bytes 208904 | tf_op jit(solution)/shard_map/ppermute | solution.py:470
  40.5 1.2 %shard_map.87.short = f32[1,256]{1,0:T(1,128)S(1)} custom-call(s32[1,1]{1,0:T(1,128)S(6)} %copy.8.lengths, bf16[256,1024]{1,0:T(8,128)(2,1)S(1)} %bitcast.6, bf16[256,1024]{1,0:T(8,128)(2,1)S(1)} %collective-permute-done.near, bf16[256,1024]{1,0:T(8,128)(2,1)S(1)} %collective-permute-done.4.across, bf16[256,1024]{1,0:T(8,128)(2,1)S(1)} %collective-permute-done.3.corner, ...), custom_call_target="tpu_custom_call" | custom-call | flops 402653184 | bytes 2097152 | tf_op jit(solution)/shard_map/pallas_call | solution.py:519
  41.8 0.4 collective-permute-done.12.state_3
  42.2 2.4 %collective-permute-done.11.state_2 = bf16[272,128]{1,0:T(8,128)(2,1)S(1)} collective-permute-done((bf16[272,128]{1,0:T(8,128)(2,1)S(1)}, bf16[272,128]{1,0:T(8,128)(2,1)S(1)}, u32[]{:S(2)}, u32[]{:S(2)}) %collective-permute-start.11) | collective-permute-done | bytes 69664 | tf_op jit(solution)/shard_map/ppermute | solution.py:470
  44.6 0.9 %shard_map.88 = f32[32,1,640]{2,1,0:T(1,128)S(1)} custom-call(s32[1,1]{1,0:T(1,128)S(6)} %copy.8.lengths, bf16[272,128]{1,0:T(8,128)(2,1)S(1)} %collective-permute-done.10.state_1, bf16[272,128]{1,0:T(8,128)(2,1)S(1)} %collective-permute-done.11.state_2, bf16[272,128]{1,0:T(8,128)(2,1)S(1)} %collective-permute-done.12.state_3, ...), custom_call_target="tpu_custom_call" | custom-call | flops 301989888 | bytes 2097152 | tf_op jit(solution)/shard_map/pallas_call | solution.py:529
  45.5 10.9 %all_to_all.5.parts = f32[32,1,640]{2,1,0:T(1,128)S(1)} all-to-all(f32[32,1,640]{2,1,0:T(1,128)S(1)} %shard_map.88), channel_id=1, replica_groups=mesh['seq'=8,'dp'=2,'domain'=2] {'seq','dp','domain'}, dimensions={0} | all-to-all | bytes 163840 | tf_op jit(solution)/shard_map/all_to_all | solution.py:536
  56.4 1.2 %shard_map.89 = (bf16[1,1,128]{2,1,0:T(2,128)(2,1)}, f32[1,1]{1,0:T(1,128)}) custom-call(s32[2]{0:T(128)S(1)} %copy-done.3, f32[32,1,640]{2,1,0:T(1,128)S(1)} %all_to_all.5.parts), custom_call_target="tpu_custom_call" | custom-call | flops 16384 | bytes 2097152 | tf_op jit(solution)/shard_map/pallas_call | solution.py:537
  (24 shorter events, 1.5 us)
Async XLA Ops:
  0.6 14.5 %copy-start = (bf16[1,1,256,1024]{3,2,1,0:T(8,128)(2,1)S(1)}, bf16[1,1,256,1024]{3,2,1,0:T(8,128)(2,1)}, u32[]{:S(2)}) copy-start(bf16[1,1,256,1024]{3,2,1,0:T(8,128)(2,1)} %param.6) | copy-start | bytes 1572868
  1.8 9.3 %collective-permute-start.2 = (bf16[128,768]{1,0:T(8,128)(2,1)S(1)}, bf16[128,768]{1,0:T(8,128)(2,1)S(1)}, u32[]{:S(2)}, u32[]{:S(2)}) collective-permute-start(bf16[128,768]{1,0:T(8,128)(2,1)S(1)} %get-tuple-element.15.rest_0_), channel_id=1, source_target_pairs={{0,4},{2,6},{4,0},{6,2},{8,12},{10,14},{12,8},{14,10},{16,20},{18,... | collective-permute-start | bytes 589832 | tf_op jit(solution)/shard_map/ppermute | solution.py:473
  4.8 10.4 %collective-permute-start.1 = (bf16[128,768]{1,0:T(8,128)(2,1)S(1)}, bf16[128,768]{1,0:T(8,128)(2,1)S(1)}, u32[]{:S(2)}, u32[]{:S(2)}) collective-permute-start(bf16[128,768]{1,0:T(8,128)(2,1)S(1)} %get-tuple-element.14.values.refs_0_), channel_id=1, source_target_pairs={{0,8},{2,10},{4,12},{6,14},{8,0},{10,2},{12,4},{14,6},{16,24},{18,... | collective-permute-start | bytes 589832 | tf_op jit(solution)/shard_map/ppermute | solution.py:470
  6.4 11.4 %collective-permute-start.6 = (bf16[128,768]{1,0:T(8,128)(2,1)S(1)}, bf16[128,768]{1,0:T(8,128)(2,1)S(1)}, u32[]{:S(2)}, u32[]{:S(2)}) collective-permute-start(bf16[128,768]{1,0:T(8,128)(2,1)S(1)} %shard_map.80), channel_id=1, source_target_pairs={{0,16},{2,18},{4,20},{6,22},{8,24},{10,26},{12,28},{14,30},{16,0},... | collective-permute-start | bytes 589832 | tf_op jit(solution)/shard_map/ppermute | solution.py:470
  9.0 19.9 %copy-start.1 = (f32[1,1024]{1,0:T(1,128)S(1)}, f32[1,1024]{1,0:T(1,128)}, u32[]{:S(2)}) copy-start(f32[1,1024]{1,0:T(1,128)} %gain.6) | copy-start | bytes 12292
  9.0 19.9 %collective-permute-start.4 = (bf16[256,1024]{1,0:T(8,128)(2,1)}, bf16[256,1024]{1,0:T(8,128)(2,1)S(1)}, u32[]{:S(2)}, u32[]{:S(2)}) collective-permute-start(bf16[256,1024]{1,0:T(8,128)(2,1)} %bitcast.2), channel_id=1, source_target_pairs={{0,2},{2,0},{4,6},{6,4},{8,10},{10,8},{12,14},{14,12},{16,18},{18,... | collective-permute-start | bytes 1572872 | tf_op jit(solution)/shard_map/ppermute | solution.py:473
  10.5 23.7 %collective-permute-start = (bf16[256,1024]{1,0:T(8,128)(2,1)}, bf16[256,1024]{1,0:T(8,128)(2,1)S(1)}, u32[]{:S(2)}, u32[]{:S(2)}) collective-permute-start(bf16[256,1024]{1,0:T(8,128)(2,1)} %bitcast.3), channel_id=1, source_target_pairs={{0,4},{2,6},{4,0},{6,2},{8,12},{10,14},{12,8},{14,10},{16,20},{18,... | collective-permute-start | bytes 1572872 | tf_op jit(solution)/shard_map/ppermute | solution.py:473
  15.2 19.3 %collective-permute-start.3 = (bf16[256,1024]{1,0:T(8,128)(2,1)S(1)}, bf16[256,1024]{1,0:T(8,128)(2,1)S(1)}, u32[]{:S(2)}, u32[]{:S(2)}) collective-permute-start(bf16[256,1024]{1,0:T(8,128)(2,1)S(1)} %shard_map.78), channel_id=1, source_target_pairs={{0,6},{2,4},{4,2},{6,0},{8,14},{10,12},{12,10},{14,8},{16,22},{18,... | collective-permute-start | bytes 1572872 | tf_op jit(solution)/shard_map/ppermute | solution.py:473
  16.8 9.3 %collective-permute-start.5 = (bf16[128,768]{1,0:T(8,128)(2,1)S(1)}, bf16[128,768]{1,0:T(8,128)(2,1)S(1)}, u32[]{:S(2)}, u32[]{:S(2)}) collective-permute-start(bf16[128,768]{1,0:T(8,128)(2,1)S(1)} %shard_map.79), channel_id=1, source_target_pairs={{0,8},{2,10},{4,12},{6,14},{8,0},{10,2},{12,4},{14,6},{16,24},{18,... | collective-permute-start | bytes 589832 | tf_op jit(solution)/shard_map/ppermute | solution.py:470
  17.8 10.1 %collective-permute-start.7 = (bf16[128,768]{1,0:T(8,128)(2,1)S(1)}, bf16[128,768]{1,0:T(8,128)(2,1)S(1)}, u32[]{:S(2)}, u32[]{:S(2)}) collective-permute-start(bf16[128,768]{1,0:T(8,128)(2,1)S(1)} %collective-permute-done.2.rest_1_.values.refs_1_), channel_id=1, source_target_pairs={{0,16},{2,18},{4,20},{6,22},{8,24},{10,26},{12,28},{14,30},{16,0},... | collective-permute-start | bytes 589832 | tf_op jit(solution)/shard_map/ppermute | solution.py:470
  26.1 5.7 %collective-permute-start.8 = (bf16[128,768]{1,0:T(8,128)(2,1)S(1)}, bf16[128,768]{1,0:T(8,128)(2,1)S(1)}, u32[]{:S(2)}, u32[]{:S(2)}) collective-permute-start(bf16[128,768]{1,0:T(8,128)(2,1)S(1)} %shard_map.82), channel_id=1, source_target_pairs={{0,8},{2,10},{4,12},{6,14},{8,0},{10,2},{12,4},{14,6},{16,24},{18,... | collective-permute-start | bytes 589832 | tf_op jit(solution)/shard_map/ppermute | solution.py:470
  27.9 6.0 %collective-permute-start.9 = (bf16[128,768]{1,0:T(8,128)(2,1)S(1)}, bf16[128,768]{1,0:T(8,128)(2,1)S(1)}, u32[]{:S(2)}, u32[]{:S(2)}) collective-permute-start(bf16[128,768]{1,0:T(8,128)(2,1)S(1)} %shard_map.83), channel_id=1, source_target_pairs={{0,8},{2,10},{4,12},{6,14},{8,0},{10,2},{12,4},{14,6},{16,24},{18,... | collective-permute-start | bytes 589832 | tf_op jit(solution)/shard_map/ppermute | solution.py:470
  35.7 6.5 %collective-permute-start.12 = (bf16[272,128]{1,0:T(8,128)(2,1)S(1)}, bf16[272,128]{1,0:T(8,128)(2,1)S(1)}, u32[]{:S(2)}, u32[]{:S(2)}) collective-permute-start(bf16[272,128]{1,0:T(8,128)(2,1)S(1)} %get-tuple-element.22), channel_id=1, source_target_pairs={{0,24},{2,26},{4,28},{6,30},{8,16},{10,18},{12,20},{14,22},{16,8},... | collective-permute-start | bytes 208904 | tf_op jit(solution)/shard_map/ppermute | solution.py:470
  39.4 5.2 %collective-permute-start.11 = (bf16[272,128]{1,0:T(8,128)(2,1)S(1)}, bf16[272,128]{1,0:T(8,128)(2,1)S(1)}, u32[]{:S(2)}, u32[]{:S(2)}) collective-permute-start(bf16[272,128]{1,0:T(8,128)(2,1)S(1)} %get-tuple-element.22), channel_id=1, source_target_pairs={{0,16},{2,18},{4,20},{6,22},{8,24},{10,26},{12,28},{14,30},{16,0},... | collective-permute-start | bytes 208904 | tf_op jit(solution)/shard_map/ppermute | solution.py:470
  39.4 5.2 %collective-permute-start.10 = (bf16[272,128]{1,0:T(8,128)(2,1)S(1)}, bf16[272,128]{1,0:T(8,128)(2,1)S(1)}, u32[]{:S(2)}, u32[]{:S(2)}) collective-permute-start(bf16[272,128]{1,0:T(8,128)(2,1)S(1)} %get-tuple-element.22), channel_id=1, source_target_pairs={{0,8},{2,10},{4,12},{6,14},{8,0},{10,2},{12,4},{14,6},{16,24},{18,... | collective-permute-start | bytes 208904 | tf_op jit(solution)/shard_map/ppermute | solution.py:470
  40.5 4.1 %copy-start.2 = (f32[1,1024]{1,0:T(1,128)S(1)}, f32[1,1024]{1,0:T(1,128)}, u32[]{:S(2)}) copy-start(f32[1,1024]{1,0:T(1,128)} %gain.7) | copy-start | bytes 12292
  41.8 14.6 %copy-start.3 = (s32[2]{0:T(128)S(1)}, s32[2]{0:T(128)}, u32[]{:S(2)}) copy-start(s32[2]{0:T(128)} %positives.1) | copy-start | bytes 28

commit v16 on v15

--- a/solution.py
+++ b/solution.py
@@ -253,14 +253,17 @@
     store(partial[...] + jnp.dot(normed[:, columns], last[...], preferred_element_type=jnp.float32), feats, 0)
 
 
-def second_kernel(lengths, near, corner, gain, early, last, first, first_sums, feats, message, sums, weights, raw):
+def second_kernel(lengths, near, corner, gain, early, last, first, first_sums, feats, message, sums, raw, normed):
     tokens = near.shape[0]
     z, x, _ = places()
-    weights[...] = early[...]
-    weights[pl.ds(pl.multiple_of((PLANES - 1 - z) * GROUP, GROUP), GROUP), :] = last[...]
     choose(lengths[0, 0] > tokens, near, corner, raw)
     feats[pl.ds(pl.multiple_of(x * tokens, tokens), tokens), :] = first[...]
-    out = jnp.dot(normalise(raw[...], gain[...]), weights[...], preferred_element_type=jnp.float32)
+    normed[...] = normalise(raw[...], gain[...])
+    columns = pl.ds(pl.multiple_of((PLANES - 1 - z) * GROUP, GROUP), GROUP)
+    out = jnp.dot(normed[:, columns], last[...], preferred_element_type=jnp.float32)
+    for j in range(PLANES - 1):
+        rows = pl.ds(pl.multiple_of(jnp.bitwise_xor(z, j) * GROUP, GROUP), GROUP)
+        out = out + jnp.dot(normed[:, rows], early[rows, :], preferred_element_type=jnp.float32)
     store(out, feats, pl.multiple_of((1 - x) * tokens, tokens))
     sums[...] = first_sums[...] + column_sum(raw)
     total = jnp.sum(feats[:, GROUP : 2 * GROUP].astype(jnp.float32), axis=0, keepdims=True)
@@ -311,7 +314,7 @@
         carry = prefix[tokens - 1 :, :]
 
 
-def short_kernel(lengths, own, near, across, corner, weights, gain, out, raw):
+def short_kernel(lengths, own, near, across, corner, early, last, gain, out, raw):
     tokens = own.shape[0]
     z, x, u = places()
     out[...] = jnp.zeros(out.shape, jnp.float32)
@@ -328,7 +331,9 @@
         def _():
             choose(own_long, corner, near, raw)
 
-        wide = jnp.dot(normalise(raw[...], gain[...]), weights[...], preferred_element_type=jnp.float32)
+        low = normalise(raw[...], gain[...])
+        wide = jnp.dot(low, early[...], preferred_element_type=jnp.float32)
+        wide = wide + jnp.dot(low[:, 3 * GROUP :], last[...], preferred_element_type=jnp.float32)
         query, key, value = features(wide)
         share, _ = shares(query, key, jnp.zeros((1, GROUP), jnp.float32))
         columns = pl.ds(pl.multiple_of((2 * x + u) * GROUP, GROUP), GROUP)
@@ -336,7 +341,7 @@
         out[...] = total + weighted(key, value, suffix(share))
 
 
-def pool_kernel(lengths, state_1, state_2, state_3, feats, local, sums, short, gain, part):
+def pool_kernel(lengths, state_3, state_2, state_1, feats, local, sums, short, gain, part):
     tokens = feats.shape[0] // 2
     z, x, u = places()
     long_u = jnp.where(lengths[0, 0] > tokens, u, 1 - u)
@@ -504,25 +509,24 @@
         [],
         2 * tokens * GROUP * wide,
     )(normed, partial, far_own, far_near)
-    feats, message, sums, weights = call(
+    feats, message, sums = call(
         second_kernel,
         (
             shape((2 * tokens, wide), bf16),
             shape((MESSAGE, HEAD_DIM), bf16),
             shape((1, GROUP), f32),
-            shape((width, wide), bf16),
         ),
         [smem()] + [vmem()] * 7,
-        [pltpu.VMEM((tokens, width), bf16)],
+        [pltpu.VMEM((tokens, width), bf16)] * 2,
         2 * tokens * width * wide,
     )(lengths, near, corner, norm_gain, early, last, first, first_sums)
     short = call(
         short_kernel,
         shape((1, GROUP), f32),
-        [smem()] + [vmem()] * 6,
+        [smem()] + [vmem()] * 7,
         [pltpu.VMEM((tokens, width), bf16)],
         2 * tokens * width * wide,
-    )(lengths, events, near, across, corner, weights, norm_gain)
+    )(lengths, events, near, across, corner, early, last, norm_gain)
     local = call(
         local_kernel, shape((2 * tokens, GROUP), f32), [vmem()], [], 2 * 2 * tokens * tokens * GROUP
     )(feats)
@@ -532,7 +536,7 @@
         [smem()] + [vmem()] * 8,
         [],
         2 * 9 * tokens * tokens * GROUP,
-    )(lengths, *each(message), feats, local, sums, short, pool_gain)
+    )(lengths, *each(message)[::-1], feats, local, sums, short, pool_gain)
     parts = lax.all_to_all(part, ("seq", "dp", "domain"), 0, 0, tiled=True)
     vec, loss = call(
         loss_kernel,

time: 57.8 us -> 58.6 us (1.014)
  starting transfers between devices: 17.9 us -> 23.1 us
  waiting for transfers between devices: 20 us -> 14.9 us
    ppermute x9, waiting for transfers between devices: 19.8 us -> 14.9 us  [hop(): return lax.ppermute(a, ('seq', 'dp'), pairs)]
    ppermute x9, starting transfers between devices: 11.3 us -> 15.2 us  [hop(): return lax.ppermute(a, ('seq', 'dp'), pairs)]
    ppermute x4, starting transfers between devices: 6.61 us -> 7.91 us  [plane_hop(): return lax.ppermute(a, ('seq', 'dp'), [(i, i ^ move) for i in range(here)])]
  transfers between devices with their start and end apart: 13 -> 13, of which waited for: 9 -> 7; matrix products, arithmetic and copies ran while one was open for 0% -> 0% of each run, Pallas kernels for 5% -> 5%
where the time goes in v16:
time: 58.6 us; the launch traced here: 58.4 us
  starting transfers between devices  23.1 us (39%)
  waiting for transfers between devices  14.9 us (25%)
  blocking collectives  11.4 us (19%)
  Pallas kernels  7.55 us (13%)
  between operations  1.44 us (2%)
    ppermute x9, starting transfers between devices, hop(): return lax.ppermute(a, ('seq', 'dp'), pairs)  15.2 us
    ppermute x9, waiting for transfers between devices, hop(): return lax.ppermute(a, ('seq', 'dp'), pairs)  14.9 us
    all_to_all x1, blocking collectives, towers(): parts = lax.all_to_all(part, ('seq', 'dp', 'domain'), 0, 0, tiled=True)  11.4 us
    ppermute x4, starting transfers between devices, plane_hop(): return lax.ppermute(a, ('seq', 'dp'), [(i, i ^ move) for i in range(here)])  7.91 us
    pallas_call x1, Pallas kernels, towers(): call(short_kernel, shape((1, GROUP), f32), [smem()] + [vmem()] * 7, [pltp...  1.36 us
    pallas_call x1, Pallas kernels, towers(): call(second_kernel, (shape((2 * tokens, wide), bf16), shape((MESSAGE, HEA...  1.3 us
    pallas_call x1, Pallas kernels, towers(): call(loss_kernel, (shape((1, 1, width // 8), bf16), shape((1, 1), f32)),...  1.19 us
  transfers between devices with their start and end apart: 13, of which 7 were waited for; matrix products, arithmetic and copies ran while one was open for 0% of the time, Pallas kernels for 5%

profile of v16, /device:TPU:0, one launch (start us, length us, event | category | flops | bytes accessed | tf_op | source)
XLA Modules:
  0.0 58.4 jit_solution(7353776704880825580)
XLA Ops:
  0.6 1.1 %shard_map.77 = (bf16[128,768]{1,0:T(8,128)(2,1)S(1)}, bf16[128,768]{1,0:T(8,128)(2,1)S(1)}) custom-call(bf16[128,3072]{1,0:T(8,128)(2,1)} %bitcast.7), custom_call_target="tpu_custom_call" | custom-call | bytes 2097152 | tf_op jit(solution)/shard_map/pallas_call | solution.py:484
  1.8 3.1 %collective-permute-start.1 = (bf16[128,768]{1,0:T(8,128)(2,1)S(1)}, bf16[128,768]{1,0:T(8,128)(2,1)S(1)}, u32[]{:S(2)}, u32[]{:S(2)}) collective-permute-start(bf16[128,768]{1,0:T(8,128)(2,1)S(1)} %get-tuple-element.13.values.refs_0_), channel_id=1, source_target_pairs={{0,8},{2,10},{4,12},{6,14},{8,0},{10,2},{12,4},{14,6},{16,24},{18,... | collective-permute-start | bytes 589832 | tf_op jit(solution)/shard_map/ppermute | solution.py:475
  4.9 1.5 %collective-permute-start.2 = (bf16[128,768]{1,0:T(8,128)(2,1)S(1)}, bf16[128,768]{1,0:T(8,128)(2,1)S(1)}, u32[]{:S(2)}, u32[]{:S(2)}) collective-permute-start(bf16[128,768]{1,0:T(8,128)(2,1)S(1)} %get-tuple-element.14.rest_0_), channel_id=1, source_target_pairs={{0,4},{2,6},{4,0},{6,2},{8,12},{10,14},{12,8},{14,10},{16,20},{18,... | collective-permute-start | bytes 589832 | tf_op jit(solution)/shard_map/ppermute | solution.py:478
  6.4 2.7 %collective-permute-start.6 = (bf16[128,768]{1,0:T(8,128)(2,1)S(1)}, bf16[128,768]{1,0:T(8,128)(2,1)S(1)}, u32[]{:S(2)}, u32[]{:S(2)}) collective-permute-start(bf16[128,768]{1,0:T(8,128)(2,1)S(1)} %shard_map.80), channel_id=1, source_target_pairs={{0,16},{2,18},{4,20},{6,22},{8,24},{10,26},{12,28},{14,30},{16,0},... | collective-permute-start | bytes 589832 | tf_op jit(solution)/shard_map/ppermute | solution.py:475
  9.0 1.5 %collective-permute-start.4 = (bf16[256,1024]{1,0:T(8,128)(2,1)}, bf16[256,1024]{1,0:T(8,128)(2,1)S(1)}, u32[]{:S(2)}, u32[]{:S(2)}) collective-permute-start(bf16[256,1024]{1,0:T(8,128)(2,1)} %bitcast.2), channel_id=1, source_target_pairs={{0,2},{2,0},{4,6},{6,4},{8,10},{10,8},{12,14},{14,12},{16,18},{18,... | collective-permute-start | bytes 1572872 | tf_op jit(solution)/shard_map/ppermute | solution.py:478
  10.5 0.5 collective-permute-start
  11.1 0.8 %collective-permute-done.1.rest_0_.refs_2_ = bf16[128,768]{1,0:T(8,128)(2,1)S(1)} collective-permute-done((bf16[128,768]{1,0:T(8,128)(2,1)S(1)}, bf16[128,768]{1,0:T(8,128)(2,1)S(1)}, u32[]{:S(2)}, u32[]{:S(2)}) %collective-permute-start.1) | collective-permute-done | bytes 196640 | tf_op jit(solution)/shard_map/ppermute | solution.py:475
  11.9 4.4 %collective-permute-start.3 = (bf16[256,1024]{1,0:T(8,128)(2,1)S(1)}, bf16[256,1024]{1,0:T(8,128)(2,1)S(1)}, u32[]{:S(2)}, u32[]{:S(2)}) collective-permute-start(bf16[256,1024]{1,0:T(8,128)(2,1)S(1)} %shard_map.78), channel_id=1, source_target_pairs={{0,6},{2,4},{4,2},{6,0},{8,14},{10,12},{12,10},{14,8},{16,22},{18,... | collective-permute-start | bytes 1572872 | tf_op jit(solution)/shard_map/ppermute | solution.py:478
  16.3 1.4 %collective-permute-done.6.refs_4_.values = bf16[128,768]{1,0:T(8,128)(2,1)S(1)} collective-permute-done((bf16[128,768]{1,0:T(8,128)(2,1)S(1)}, bf16[128,768]{1,0:T(8,128)(2,1)S(1)}, u32[]{:S(2)}, u32[]{:S(2)}) %collective-permute-start.6) | collective-permute-done | bytes 196640 | tf_op jit(solution)/shard_map/ppermute | solution.py:475
  17.8 1.6 %collective-permute-start.7 = (bf16[128,768]{1,0:T(8,128)(2,1)S(1)}, bf16[128,768]{1,0:T(8,128)(2,1)S(1)}, u32[]{:S(2)}, u32[]{:S(2)}) collective-permute-start(bf16[128,768]{1,0:T(8,128)(2,1)S(1)} %collective-permute-done.2.rest_1_.values.refs_1_), channel_id=1, source_target_pairs={{0,16},{2,18},{4,20},{6,22},{8,24},{10,26},{12,28},{14,30},{16,0},... | collective-permute-start | bytes 589832 | tf_op jit(solution)/shard_map/ppermute | solution.py:475
  19.4 6.7 %collective-permute-done.5.refs_3_.rest_0_ = bf16[128,768]{1,0:T(8,128)(2,1)S(1)} collective-permute-done((bf16[128,768]{1,0:T(8,128)(2,1)S(1)}, bf16[128,768]{1,0:T(8,128)(2,1)S(1)}, u32[]{:S(2)}, u32[]{:S(2)}) %collective-permute-start.5) | collective-permute-done | bytes 196640 | tf_op jit(solution)/shard_map/ppermute | solution.py:475
  26.2 3.3 %collective-permute-start.9 = (bf16[128,768]{1,0:T(8,128)(2,1)S(1)}, bf16[128,768]{1,0:T(8,128)(2,1)S(1)}, u32[]{:S(2)}, u32[]{:S(2)}) collective-permute-start(bf16[128,768]{1,0:T(8,128)(2,1)S(1)} %shard_map.83), channel_id=1, source_target_pairs={{0,8},{2,10},{4,12},{6,14},{8,0},{10,2},{12,4},{14,6},{16,24},{18,... | collective-permute-start | bytes 589832 | tf_op jit(solution)/shard_map/ppermute | solution.py:475
  30.2 0.9 %shard_map.81 = (bf16[256,1024]{1,0:T(8,128)(2,1)S(1)}, f32[256,768]{1,0:T(8,128)S(1)}, f32[1,256]{1,0:T(1,128)S(1)}, bf16[1024,768]{1,0:T(8,128)(2,1)S(1)}) custom-call(s32[1,1]{1,0:T(1,128)S(6)} %copy.8.lengths, bf16[256,1024]{1,0:T(8,128)(2,1)S(1)} %bitcast.5, bf16[256,1024]{1,0:T(8,128)(2,1)S(1)} %collective-permute-done.4.across, ...), custom_call_target="tpu_custom_call" | custom-call | flops 301989888 | bytes 2097152 | tf_op jit(solution)/shard_map/pallas_call | solution.py:498
  31.1 1.6 %collective-permute-done.8.far_own = bf16[128,768]{1,0:T(8,128)(2,1)S(1)} collective-permute-done((bf16[128,768]{1,0:T(8,128)(2,1)S(1)}, bf16[128,768]{1,0:T(8,128)(2,1)S(1)}, u32[]{:S(2)}, u32[]{:S(2)}) %collective-permute-start.8) | collective-permute-done | bytes 196640 | tf_op jit(solution)/shard_map/ppermute | solution.py:475
  32.6 2.1 %collective-permute-done.9.far_near = bf16[128,768]{1,0:T(8,128)(2,1)S(1)} collective-permute-done((bf16[128,768]{1,0:T(8,128)(2,1)S(1)}, bf16[128,768]{1,0:T(8,128)(2,1)S(1)}, u32[]{:S(2)}, u32[]{:S(2)}) %collective-permute-start.9) | collective-permute-done | bytes 196640 | tf_op jit(solution)/shard_map/ppermute | solution.py:475
  35.1 1.3 %shard_map.85 = (bf16[512,768]{1,0:T(8,128)(2,1)S(1)}, bf16[272,128]{1,0:T(8,128)(2,1)S(1)}, f32[1,256]{1,0:T(1,128)S(1)}) custom-call(s32[1,1]{1,0:T(1,128)S(6)} %copy.8.lengths, bf16[256,1024]{1,0:T(8,128)(2,1)S(1)} %collective-permute-done.near, bf16[256,1024]{1,0:T(8,128)(2,1)S(1)} %collective-permute-done.3.corner, f32[1,1024]{1,0:T(1,128)S(1)} %copy-done.1, ...), custom_call_target="tpu_custom_call" | custom-call | flops 402653184 | bytes 2097152 | tf_op jit(solution)/shard_map/pallas_call | solution.py:512
  36.4 2.4 %collective-permute-start.10 = (bf16[272,128]{1,0:T(8,128)(2,1)S(1)}, bf16[272,128]{1,0:T(8,128)(2,1)S(1)}, u32[]{:S(2)}, u32[]{:S(2)}) collective-permute-start(bf16[272,128]{1,0:T(8,128)(2,1)S(1)} %get-tuple-element.21), channel_id=1, source_target_pairs={{0,24},{2,26},{4,28},{6,30},{8,16},{10,18},{12,20},{14,22},{16,8},... | collective-permute-start | bytes 208904 | tf_op jit(solution)/shard_map/ppermute | solution.py:475
  39.0 1.9 %collective-permute-start.12 = (bf16[272,128]{1,0:T(8,128)(2,1)S(1)}, bf16[272,128]{1,0:T(8,128)(2,1)S(1)}, u32[]{:S(2)}, u32[]{:S(2)}) collective-permute-start(bf16[272,128]{1,0:T(8,128)(2,1)S(1)} %get-tuple-element.21), channel_id=1, source_target_pairs={{0,8},{2,10},{4,12},{6,14},{8,0},{10,2},{12,4},{14,6},{16,24},{18,... | collective-permute-start | bytes 208904 | tf_op jit(solution)/shard_map/ppermute | solution.py:475
  41.3 1.4 %shard_map.87.short = f32[1,256]{1,0:T(1,128)S(1)} custom-call(s32[1,1]{1,0:T(1,128)S(6)} %copy.8.lengths, bf16[256,1024]{1,0:T(8,128)(2,1)S(1)} %bitcast.6, bf16[256,1024]{1,0:T(8,128)(2,1)S(1)} %collective-permute-done.near, bf16[256,1024]{1,0:T(8,128)(2,1)S(1)} %collective-permute-done.4.across, bf16[256,1024]{1,0:T(8,128)(2,1)S(1)} %collective-permute-done.3.corner, ...), custom_call_target="tpu_custom_call" | custom-call | flops 402653184 | bytes 2097152 | tf_op jit(solution)/shard_map/pallas_call | solution.py:523
  42.7 0.7 %collective-permute-done.10.state_3 = bf16[272,128]{1,0:T(8,128)(2,1)S(1)} collective-permute-done((bf16[272,128]{1,0:T(8,128)(2,1)S(1)}, bf16[272,128]{1,0:T(8,128)(2,1)S(1)}, u32[]{:S(2)}, u32[]{:S(2)}) %collective-permute-start.10) | collective-permute-done | bytes 69664 | tf_op jit(solution)/shard_map/ppermute | solution.py:475
  43.4 1.5 %collective-permute-done.11.state_2 = bf16[272,128]{1,0:T(8,128)(2,1)S(1)} collective-permute-done((bf16[272,128]{1,0:T(8,128)(2,1)S(1)}, bf16[272,128]{1,0:T(8,128)(2,1)S(1)}, u32[]{:S(2)}, u32[]{:S(2)}) %collective-permute-start.11) | collective-permute-done | bytes 69664 | tf_op jit(solution)/shard_map/ppermute | solution.py:475
  44.9 0.9 %shard_map.88 = f32[32,1,640]{2,1,0:T(1,128)S(1)} custom-call(s32[1,1]{1,0:T(1,128)S(6)} %copy.8.lengths, bf16[272,128]{1,0:T(8,128)(2,1)S(1)} %collective-permute-done.10.state_3, bf16[272,128]{1,0:T(8,128)(2,1)S(1)} %collective-permute-done.11.state_2, bf16[272,128]{1,0:T(8,128)(2,1)S(1)} %collective-permute-done.12.state_1, ...), custom_call_target="tpu_custom_call" | custom-call | flops 301989888 | bytes 2097152 | tf_op jit(solution)/shard_map/pallas_call | solution.py:533
  45.8 11.4 %all_to_all.5.parts = f32[32,1,640]{2,1,0:T(1,128)S(1)} all-to-all(f32[32,1,640]{2,1,0:T(1,128)S(1)} %shard_map.88), channel_id=1, replica_groups=mesh['seq'=8,'dp'=2,'domain'=2] {'seq','dp','domain'}, dimensions={0} | all-to-all | bytes 163840 | tf_op jit(solution)/shard_map/all_to_all | solution.py:540
  57.2 1.2 %shard_map.89 = (bf16[1,1,128]{2,1,0:T(2,128)(2,1)}, f32[1,1]{1,0:T(1,128)}) custom-call(s32[2]{0:T(128)S(1)} %copy-done.3, f32[32,1,640]{2,1,0:T(1,128)S(1)} %all_to_all.5.parts), custom_call_target="tpu_custom_call" | custom-call | flops 16384 | bytes 2097152 | tf_op jit(solution)/shard_map/pallas_call | solution.py:541
  (24 shorter events, 1.2 us)
Async XLA Ops:
  0.6 11.2 %copy-start = (bf16[1,1,256,1024]{3,2,1,0:T(8,128)(2,1)S(1)}, bf16[1,1,256,1024]{3,2,1,0:T(8,128)(2,1)}, u32[]{:S(2)}) copy-start(bf16[1,1,256,1024]{3,2,1,0:T(8,128)(2,1)} %param.6) | copy-start | bytes 1572868
  1.8 10.1 %collective-permute-start.1 = (bf16[128,768]{1,0:T(8,128)(2,1)S(1)}, bf16[128,768]{1,0:T(8,128)(2,1)S(1)}, u32[]{:S(2)}, u32[]{:S(2)}) collective-permute-start(bf16[128,768]{1,0:T(8,128)(2,1)S(1)} %get-tuple-element.13.values.refs_0_), channel_id=1, source_target_pairs={{0,8},{2,10},{4,12},{6,14},{8,0},{10,2},{12,4},{14,6},{16,24},{18,... | collective-permute-start | bytes 589832 | tf_op jit(solution)/shard_map/ppermute | solution.py:475
  4.9 7.0 %collective-permute-start.2 = (bf16[128,768]{1,0:T(8,128)(2,1)S(1)}, bf16[128,768]{1,0:T(8,128)(2,1)S(1)}, u32[]{:S(2)}, u32[]{:S(2)}) collective-permute-start(bf16[128,768]{1,0:T(8,128)(2,1)S(1)} %get-tuple-element.14.rest_0_), channel_id=1, source_target_pairs={{0,4},{2,6},{4,0},{6,2},{8,12},{10,14},{12,8},{14,10},{16,20},{18,... | collective-permute-start | bytes 589832 | tf_op jit(solution)/shard_map/ppermute | solution.py:478
  6.4 11.4 %collective-permute-start.6 = (bf16[128,768]{1,0:T(8,128)(2,1)S(1)}, bf16[128,768]{1,0:T(8,128)(2,1)S(1)}, u32[]{:S(2)}, u32[]{:S(2)}) collective-permute-start(bf16[128,768]{1,0:T(8,128)(2,1)S(1)} %shard_map.80), channel_id=1, source_target_pairs={{0,16},{2,18},{4,20},{6,22},{8,24},{10,26},{12,28},{14,30},{16,0},... | collective-permute-start | bytes 589832 | tf_op jit(solution)/shard_map/ppermute | solution.py:475
  9.0 21.2 %copy-start.1 = (f32[1,1024]{1,0:T(1,128)S(1)}, f32[1,1024]{1,0:T(1,128)}, u32[]{:S(2)}) copy-start(f32[1,1024]{1,0:T(1,128)} %gain.6) | copy-start | bytes 12292
  9.0 21.1 %collective-permute-start.4 = (bf16[256,1024]{1,0:T(8,128)(2,1)}, bf16[256,1024]{1,0:T(8,128)(2,1)S(1)}, u32[]{:S(2)}, u32[]{:S(2)}) collective-permute-start(bf16[256,1024]{1,0:T(8,128)(2,1)} %bitcast.2), channel_id=1, source_target_pairs={{0,2},{2,0},{4,6},{6,4},{8,10},{10,8},{12,14},{14,12},{16,18},{18,... | collective-permute-start | bytes 1572872 | tf_op jit(solution)/shard_map/ppermute | solution.py:478
  10.5 24.6 %collective-permute-start = (bf16[256,1024]{1,0:T(8,128)(2,1)}, bf16[256,1024]{1,0:T(8,128)(2,1)S(1)}, u32[]{:S(2)}, u32[]{:S(2)}) collective-permute-start(bf16[256,1024]{1,0:T(8,128)(2,1)} %bitcast.3), channel_id=1, source_target_pairs={{0,4},{2,6},{4,0},{6,2},{8,12},{10,14},{12,8},{14,10},{16,20},{18,... | collective-permute-start | bytes 1572872 | tf_op jit(solution)/shard_map/ppermute | solution.py:478
  11.9 23.2 %collective-permute-start.3 = (bf16[256,1024]{1,0:T(8,128)(2,1)S(1)}, bf16[256,1024]{1,0:T(8,128)(2,1)S(1)}, u32[]{:S(2)}, u32[]{:S(2)}) collective-permute-start(bf16[256,1024]{1,0:T(8,128)(2,1)S(1)} %shard_map.78), channel_id=1, source_target_pairs={{0,6},{2,4},{4,2},{6,0},{8,14},{10,12},{12,10},{14,8},{16,22},{18,... | collective-permute-start | bytes 1572872 | tf_op jit(solution)/shard_map/ppermute | solution.py:478
  16.3 9.8 %collective-permute-start.5 = (bf16[128,768]{1,0:T(8,128)(2,1)S(1)}, bf16[128,768]{1,0:T(8,128)(2,1)S(1)}, u32[]{:S(2)}, u32[]{:S(2)}) collective-permute-start(bf16[128,768]{1,0:T(8,128)(2,1)S(1)} %shard_map.79), channel_id=1, source_target_pairs={{0,8},{2,10},{4,12},{6,14},{8,0},{10,2},{12,4},{14,6},{16,24},{18,... | collective-permute-start | bytes 589832 | tf_op jit(solution)/shard_map/ppermute | solution.py:475
  17.8 8.4 %collective-permute-start.7 = (bf16[128,768]{1,0:T(8,128)(2,1)S(1)}, bf16[128,768]{1,0:T(8,128)(2,1)S(1)}, u32[]{:S(2)}, u32[]{:S(2)}) collective-permute-start(bf16[128,768]{1,0:T(8,128)(2,1)S(1)} %collective-permute-done.2.rest_1_.values.refs_1_), channel_id=1, source_target_pairs={{0,16},{2,18},{4,20},{6,22},{8,24},{10,26},{12,28},{14,30},{16,0},... | collective-permute-start | bytes 589832 | tf_op jit(solution)/shard_map/ppermute | solution.py:475
  26.1 6.5 %collective-permute-start.8 = (bf16[128,768]{1,0:T(8,128)(2,1)S(1)}, bf16[128,768]{1,0:T(8,128)(2,1)S(1)}, u32[]{:S(2)}, u32[]{:S(2)}) collective-permute-start(bf16[128,768]{1,0:T(8,128)(2,1)S(1)} %shard_map.82), channel_id=1, source_target_pairs={{0,8},{2,10},{4,12},{6,14},{8,0},{10,2},{12,4},{14,6},{16,24},{18,... | collective-permute-start | bytes 589832 | tf_op jit(solution)/shard_map/ppermute | solution.py:475
  26.2 8.5 %collective-permute-start.9 = (bf16[128,768]{1,0:T(8,128)(2,1)S(1)}, bf16[128,768]{1,0:T(8,128)(2,1)S(1)}, u32[]{:S(2)}, u32[]{:S(2)}) collective-permute-start(bf16[128,768]{1,0:T(8,128)(2,1)S(1)} %shard_map.83), channel_id=1, source_target_pairs={{0,8},{2,10},{4,12},{6,14},{8,0},{10,2},{12,4},{14,6},{16,24},{18,... | collective-permute-start | bytes 589832 | tf_op jit(solution)/shard_map/ppermute | solution.py:475
  36.4 7.0 %collective-permute-start.10 = (bf16[272,128]{1,0:T(8,128)(2,1)S(1)}, bf16[272,128]{1,0:T(8,128)(2,1)S(1)}, u32[]{:S(2)}, u32[]{:S(2)}) collective-permute-start(bf16[272,128]{1,0:T(8,128)(2,1)S(1)} %get-tuple-element.21), channel_id=1, source_target_pairs={{0,24},{2,26},{4,28},{6,30},{8,16},{10,18},{12,20},{14,22},{16,8},... | collective-permute-start | bytes 208904 | tf_op jit(solution)/shard_map/ppermute | solution.py:475
  38.9 6.1 %collective-permute-start.11 = (bf16[272,128]{1,0:T(8,128)(2,1)S(1)}, bf16[272,128]{1,0:T(8,128)(2,1)S(1)}, u32[]{:S(2)}, u32[]{:S(2)}) collective-permute-start(bf16[272,128]{1,0:T(8,128)(2,1)S(1)} %get-tuple-element.21), channel_id=1, source_target_pairs={{0,16},{2,18},{4,20},{6,22},{8,24},{10,26},{12,28},{14,30},{16,0},... | collective-permute-start | bytes 208904 | tf_op jit(solution)/shard_map/ppermute | solution.py:475
  39.0 5.9 %collective-permute-start.12 = (bf16[272,128]{1,0:T(8,128)(2,1)S(1)}, bf16[272,128]{1,0:T(8,128)(2,1)S(1)}, u32[]{:S(2)}, u32[]{:S(2)}) collective-permute-start(bf16[272,128]{1,0:T(8,128)(2,1)S(1)} %get-tuple-element.21), channel_id=1, source_target_pairs={{0,8},{2,10},{4,12},{6,14},{8,0},{10,2},{12,4},{14,6},{16,24},{18,... | collective-permute-start | bytes 208904 | tf_op jit(solution)/shard_map/ppermute | solution.py:475
  41.3 3.7 %copy-start.2 = (f32[1,1024]{1,0:T(1,128)S(1)}, f32[1,1024]{1,0:T(1,128)}, u32[]{:S(2)}) copy-start(f32[1,1024]{1,0:T(1,128)} %gain.7) | copy-start | bytes 12292
  42.7 14.6 %copy-start.3 = (s32[2]{0:T(128)S(1)}, s32[2]{0:T(128)}, u32[]{:S(2)}) copy-start(s32[2]{0:T(128)} %positives.1) | copy-start | bytes 28

commit v17 on v15

--- a/solution.py
+++ b/solution.py
@@ -256,7 +256,7 @@
 def second_kernel(lengths, near, corner, gain, early, last, first, first_sums, feats, message, sums, weights, raw):
     tokens = near.shape[0]
     z, x, _ = places()
-    weights[...] = early[...]
+    del early
     weights[pl.ds(pl.multiple_of((PLANES - 1 - z) * GROUP, GROUP), GROUP), :] = last[...]
     choose(lengths[0, 0] > tokens, near, corner, raw)
     feats[pl.ds(pl.multiple_of(x * tokens, tokens), tokens), :] = first[...]
@@ -444,13 +444,14 @@
     return pl.BlockSpec(memory_space=pltpu.SMEM)
 
 
-def call(kernel, outs, in_specs, scratch, flops):
+def call(kernel, outs, in_specs, scratch, flops, aliases=None):
     return pl.pallas_call(
         kernel,
         out_shape=outs,
         in_specs=in_specs,
         out_specs=jax.tree.map(lambda _: vmem(), outs),
         scratch_shapes=scratch,
+        input_output_aliases=aliases or {},
         compiler_params=pltpu.CompilerParams(vmem_limit_bytes=40 * 1024 * 1024),
         cost_estimate=pl.CostEstimate(flops=flops, bytes_accessed=2**21, transcendentals=0),
     )
@@ -515,6 +516,7 @@
         [smem()] + [vmem()] * 7,
         [pltpu.VMEM((tokens, width), bf16)],
         2 * tokens * width * wide,
+        {4: 3},
     )(lengths, near, corner, norm_gain, early, last, first, first_sums)
     short = call(
         short_kernel,

time: 57.8 us -> 57.7 us (level)
  no operation moved by 1% of the time
where the time goes in v17:
time: 57.7 us; the launch traced here: 57.5 us
  waiting for transfers between devices  20 us (35%)
  starting transfers between devices  17.9 us (31%)
  blocking collectives  10.9 us (19%)
  Pallas kernels  7.28 us (13%)
  between operations  1.42 us (2%)
    ppermute x9, waiting for transfers between devices, hop(): return lax.ppermute(a, ('seq', 'dp'), pairs)  19.8 us
    ppermute x9, starting transfers between devices, hop(): return lax.ppermute(a, ('seq', 'dp'), pairs)  11.3 us
    all_to_all x1, blocking collectives, towers(): parts = lax.all_to_all(part, ('seq', 'dp', 'domain'), 0, 0, tiled=True)  10.9 us
    ppermute x4, starting transfers between devices, plane_hop(): return lax.ppermute(a, ('seq', 'dp'), [(i, i ^ move) for i in range(here)])  6.61 us
    pallas_call x1, Pallas kernels, towers(): call(short_kernel, shape((1, GROUP), f32), [smem()] + [vmem()] * 6, [pltp...  1.25 us
    pallas_call x1, Pallas kernels, towers(): call(loss_kernel, (shape((1, 1, width // 8), bf16), shape((1, 1), f32)),...  1.19 us
  transfers between devices with their start and end apart: 13, of which 9 were waited for; matrix products, arithmetic and copies ran while one was open for 0% of the time, Pallas kernels for 5%

profile of v17, /device:TPU:0, one launch (start us, length us, event | category | flops | bytes accessed | tf_op | source)
XLA Modules:
  0.0 57.5 jit_solution(17016770036303295231)
XLA Ops:
  0.6 1.1 %shard_map.77 = (bf16[128,768]{1,0:T(8,128)(2,1)S(1)}, bf16[128,768]{1,0:T(8,128)(2,1)S(1)}) custom-call(bf16[128,3072]{1,0:T(8,128)(2,1)} %bitcast.7), custom_call_target="tpu_custom_call" | custom-call | bytes 2097152 | tf_op jit(solution)/shard_map/pallas_call | solution.py:480
  1.8 3.0 %collective-permute-start.2 = (bf16[128,768]{1,0:T(8,128)(2,1)S(1)}, bf16[128,768]{1,0:T(8,128)(2,1)S(1)}, u32[]{:S(2)}, u32[]{:S(2)}) collective-permute-start(bf16[128,768]{1,0:T(8,128)(2,1)S(1)} %get-tuple-element.15.rest_0_), channel_id=1, source_target_pairs={{0,4},{2,6},{4,0},{6,2},{8,12},{10,14},{12,8},{14,10},{16,20},{18,... | collective-permute-start | bytes 589832 | tf_op jit(solution)/shard_map/ppermute | solution.py:474
  4.8 1.6 %collective-permute-start.1 = (bf16[128,768]{1,0:T(8,128)(2,1)S(1)}, bf16[128,768]{1,0:T(8,128)(2,1)S(1)}, u32[]{:S(2)}, u32[]{:S(2)}) collective-permute-start(bf16[128,768]{1,0:T(8,128)(2,1)S(1)} %get-tuple-element.14.values.refs_0_), channel_id=1, source_target_pairs={{0,8},{2,10},{4,12},{6,14},{8,0},{10,2},{12,4},{14,6},{16,24},{18,... | collective-permute-start | bytes 589832 | tf_op jit(solution)/shard_map/ppermute | solution.py:471
  6.4 2.7 %collective-permute-start.6 = (bf16[128,768]{1,0:T(8,128)(2,1)S(1)}, bf16[128,768]{1,0:T(8,128)(2,1)S(1)}, u32[]{:S(2)}, u32[]{:S(2)}) collective-permute-start(bf16[128,768]{1,0:T(8,128)(2,1)S(1)} %shard_map.80), channel_id=1, source_target_pairs={{0,16},{2,18},{4,20},{6,22},{8,24},{10,26},{12,28},{14,30},{16,0},... | collective-permute-start | bytes 589832 | tf_op jit(solution)/shard_map/ppermute | solution.py:471
  9.0 1.5 %collective-permute-start.4 = (bf16[256,1024]{1,0:T(8,128)(2,1)}, bf16[256,1024]{1,0:T(8,128)(2,1)S(1)}, u32[]{:S(2)}, u32[]{:S(2)}) collective-permute-start(bf16[256,1024]{1,0:T(8,128)(2,1)} %bitcast.2), channel_id=1, source_target_pairs={{0,2},{2,0},{4,6},{6,4},{8,10},{10,8},{12,14},{14,12},{16,18},{18,... | collective-permute-start | bytes 1572872 | tf_op jit(solution)/shard_map/ppermute | solution.py:474
  10.5 0.5 collective-permute-start
  11.1 4.1 %collective-permute-done.1.rest_0_.refs_2_ = bf16[128,768]{1,0:T(8,128)(2,1)S(1)} collective-permute-done((bf16[128,768]{1,0:T(8,128)(2,1)S(1)}, bf16[128,768]{1,0:T(8,128)(2,1)S(1)}, u32[]{:S(2)}, u32[]{:S(2)}) %collective-permute-start.1) | collective-permute-done | bytes 196640 | tf_op jit(solution)/shard_map/ppermute | solution.py:471
  15.2 1.6 %collective-permute-start.3 = (bf16[256,1024]{1,0:T(8,128)(2,1)S(1)}, bf16[256,1024]{1,0:T(8,128)(2,1)S(1)}, u32[]{:S(2)}, u32[]{:S(2)}) collective-permute-start(bf16[256,1024]{1,0:T(8,128)(2,1)S(1)} %shard_map.78), channel_id=1, source_target_pairs={{0,6},{2,4},{4,2},{6,0},{8,14},{10,12},{12,10},{14,8},{16,22},{18,... | collective-permute-start | bytes 1572872 | tf_op jit(solution)/shard_map/ppermute | solution.py:474
  16.8 0.9 %collective-permute-done.6.refs_4_.values = bf16[128,768]{1,0:T(8,128)(2,1)S(1)} collective-permute-done((bf16[128,768]{1,0:T(8,128)(2,1)S(1)}, bf16[128,768]{1,0:T(8,128)(2,1)S(1)}, u32[]{:S(2)}, u32[]{:S(2)}) %collective-permute-start.6) | collective-permute-done | bytes 196640 | tf_op jit(solution)/shard_map/ppermute | solution.py:471
  17.8 2.1 %collective-permute-start.7 = (bf16[128,768]{1,0:T(8,128)(2,1)S(1)}, bf16[128,768]{1,0:T(8,128)(2,1)S(1)}, u32[]{:S(2)}, u32[]{:S(2)}) collective-permute-start(bf16[128,768]{1,0:T(8,128)(2,1)S(1)} %collective-permute-done.2.rest_1_.values.refs_1_), channel_id=1, source_target_pairs={{0,16},{2,18},{4,20},{6,22},{8,24},{10,26},{12,28},{14,30},{16,0},... | collective-permute-start | bytes 589832 | tf_op jit(solution)/shard_map/ppermute | solution.py:471
  19.9 6.2 %collective-permute-done.5.refs_3_.rest_0_ = bf16[128,768]{1,0:T(8,128)(2,1)S(1)} collective-permute-done((bf16[128,768]{1,0:T(8,128)(2,1)S(1)}, bf16[128,768]{1,0:T(8,128)(2,1)S(1)}, u32[]{:S(2)}, u32[]{:S(2)}) %collective-permute-start.5) | collective-permute-done | bytes 196640 | tf_op jit(solution)/shard_map/ppermute | solution.py:471
  26.1 1.8 %collective-permute-done.7.refs_5_.values = bf16[128,768]{1,0:T(8,128)(2,1)S(1)} collective-permute-done((bf16[128,768]{1,0:T(8,128)(2,1)S(1)}, bf16[128,768]{1,0:T(8,128)(2,1)S(1)}, u32[]{:S(2)}, u32[]{:S(2)}) %collective-permute-start.7) | collective-permute-done | bytes 196640 | tf_op jit(solution)/shard_map/ppermute | solution.py:471
  28.9 0.9 %shard_map.81 = (bf16[256,1024]{1,0:T(8,128)(2,1)S(1)}, f32[256,768]{1,0:T(8,128)S(1)}, f32[1,256]{1,0:T(1,128)S(1)}, bf16[1024,768]{1,0:T(8,128)(2,1)S(1)}) custom-call(s32[1,1]{1,0:T(1,128)S(6)} %copy.10.lengths, bf16[256,1024]{1,0:T(8,128)(2,1)S(1)} %bitcast.5, bf16[256,1024]{1,0:T(8,128)(2,1)S(1)} %collective-permute-done.4.across, ...), custom_call_target="tpu_custom_call" | custom-call | flops 301989888 | bytes 2097152 | tf_op jit(solution)/shard_map/pallas_call | solution.py:494
  29.8 2.0 %collective-permute-done.8.far_own = bf16[128,768]{1,0:T(8,128)(2,1)S(1)} collective-permute-done((bf16[128,768]{1,0:T(8,128)(2,1)S(1)}, bf16[128,768]{1,0:T(8,128)(2,1)S(1)}, u32[]{:S(2)}, u32[]{:S(2)}) %collective-permute-start.8) | collective-permute-done | bytes 196640 | tf_op jit(solution)/shard_map/ppermute | solution.py:471
  31.8 2.1 %collective-permute-done.9.far_near = bf16[128,768]{1,0:T(8,128)(2,1)S(1)} collective-permute-done((bf16[128,768]{1,0:T(8,128)(2,1)S(1)}, bf16[128,768]{1,0:T(8,128)(2,1)S(1)}, u32[]{:S(2)}, u32[]{:S(2)}) %collective-permute-start.9) | collective-permute-done | bytes 196640 | tf_op jit(solution)/shard_map/ppermute | solution.py:471
  34.5 1.1 %shard_map.85 = (bf16[512,768]{1,0:T(8,128)(2,1)S(1)}, bf16[272,128]{1,0:T(8,128)(2,1)S(1)}, f32[1,256]{1,0:T(1,128)S(1)}, bf16[1024,768]{1,0:T(8,128)(2,1)S(1)}) custom-call(s32[1,1]{1,0:T(1,128)S(6)} %copy.10.lengths, bf16[256,1024]{1,0:T(8,128)(2,1)S(1)} %collective-permute-done.near, ...), custom_call_target="tpu_custom_call", output_to_operand_aliasing={{3}: (4, {})} | custom-call | flops 402653184 | bytes 2097152 | tf_op jit(solution)/shard_map/pallas_call | solution.py:508
  35.6 3.7 %collective-permute-start.12 = (bf16[272,128]{1,0:T(8,128)(2,1)S(1)}, bf16[272,128]{1,0:T(8,128)(2,1)S(1)}, u32[]{:S(2)}, u32[]{:S(2)}) collective-permute-start(bf16[272,128]{1,0:T(8,128)(2,1)S(1)} %get-tuple-element.22), channel_id=1, source_target_pairs={{0,24},{2,26},{4,28},{6,30},{8,16},{10,18},{12,20},{14,22},{16,8},... | collective-permute-start | bytes 208904 | tf_op jit(solution)/shard_map/ppermute | solution.py:471
  39.3 0.8 %collective-permute-start.10 = (bf16[272,128]{1,0:T(8,128)(2,1)S(1)}, bf16[272,128]{1,0:T(8,128)(2,1)S(1)}, u32[]{:S(2)}, u32[]{:S(2)}) collective-permute-start(bf16[272,128]{1,0:T(8,128)(2,1)S(1)} %get-tuple-element.22), channel_id=1, source_target_pairs={{0,8},{2,10},{4,12},{6,14},{8,0},{10,2},{12,4},{14,6},{16,24},{18,... | collective-permute-start | bytes 208904 | tf_op jit(solution)/shard_map/ppermute | solution.py:471
  40.5 1.2 %shard_map.87.short = f32[1,256]{1,0:T(1,128)S(1)} custom-call(s32[1,1]{1,0:T(1,128)S(6)} %copy.10.lengths, bf16[256,1024]{1,0:T(8,128)(2,1)S(1)} %bitcast.6, bf16[256,1024]{1,0:T(8,128)(2,1)S(1)} %collective-permute-done.near, bf16[256,1024]{1,0:T(8,128)(2,1)S(1)} %collective-permute-done.4.across, bf16[256,1024]{1,0:T(8,128)(2,1)S(1)} %collective-permute-done.3.corner, ...), custom_call_target="tpu_custom_call" | custom-call | flops 402653184 | bytes 2097152 | tf_op jit(solution)/shard_map/pallas_call | solution.py:521
  41.7 0.4 collective-permute-done.12.state_3
  42.1 2.4 %collective-permute-done.11.state_2 = bf16[272,128]{1,0:T(8,128)(2,1)S(1)} collective-permute-done((bf16[272,128]{1,0:T(8,128)(2,1)S(1)}, bf16[272,128]{1,0:T(8,128)(2,1)S(1)}, u32[]{:S(2)}, u32[]{:S(2)}) %collective-permute-start.11) | collective-permute-done | bytes 69664 | tf_op jit(solution)/shard_map/ppermute | solution.py:471
  44.5 0.9 %shard_map.88 = f32[32,1,640]{2,1,0:T(1,128)S(1)} custom-call(s32[1,1]{1,0:T(1,128)S(6)} %copy.10.lengths, bf16[272,128]{1,0:T(8,128)(2,1)S(1)} %collective-permute-done.10.state_1, bf16[272,128]{1,0:T(8,128)(2,1)S(1)} %collective-permute-done.11.state_2, bf16[272,128]{1,0:T(8,128)(2,1)S(1)} %collective-permute-done.12.state_3, ...), custom_call_target="tpu_custom_call" | custom-call | flops 301989888 | bytes 2097152 | tf_op jit(solution)/shard_map/pallas_call | solution.py:531
  45.4 10.9 %all_to_all.5.parts = f32[32,1,640]{2,1,0:T(1,128)S(1)} all-to-all(f32[32,1,640]{2,1,0:T(1,128)S(1)} %shard_map.88), channel_id=1, replica_groups=mesh['seq'=8,'dp'=2,'domain'=2] {'seq','dp','domain'}, dimensions={0} | all-to-all | bytes 163840 | tf_op jit(solution)/shard_map/all_to_all | solution.py:538
  56.3 1.2 %shard_map.89 = (bf16[1,1,128]{2,1,0:T(2,128)(2,1)}, f32[1,1]{1,0:T(1,128)}) custom-call(s32[2]{0:T(128)S(1)} %copy-done.3, f32[32,1,640]{2,1,0:T(1,128)S(1)} %all_to_all.5.parts), custom_call_target="tpu_custom_call" | custom-call | flops 16384 | bytes 2097152 | tf_op jit(solution)/shard_map/pallas_call | solution.py:539
  (24 shorter events, 1.5 us)
Async XLA Ops:
  0.6 14.5 %copy-start = (bf16[1,1,256,1024]{3,2,1,0:T(8,128)(2,1)S(1)}, bf16[1,1,256,1024]{3,2,1,0:T(8,128)(2,1)}, u32[]{:S(2)}) copy-start(bf16[1,1,256,1024]{3,2,1,0:T(8,128)(2,1)} %param.6) | copy-start | bytes 1572868
  1.8 9.3 %collective-permute-start.2 = (bf16[128,768]{1,0:T(8,128)(2,1)S(1)}, bf16[128,768]{1,0:T(8,128)(2,1)S(1)}, u32[]{:S(2)}, u32[]{:S(2)}) collective-permute-start(bf16[128,768]{1,0:T(8,128)(2,1)S(1)} %get-tuple-element.15.rest_0_), channel_id=1, source_target_pairs={{0,4},{2,6},{4,0},{6,2},{8,12},{10,14},{12,8},{14,10},{16,20},{18,... | collective-permute-start | bytes 589832 | tf_op jit(solution)/shard_map/ppermute | solution.py:474
  4.8 10.4 %collective-permute-start.1 = (bf16[128,768]{1,0:T(8,128)(2,1)S(1)}, bf16[128,768]{1,0:T(8,128)(2,1)S(1)}, u32[]{:S(2)}, u32[]{:S(2)}) collective-permute-start(bf16[128,768]{1,0:T(8,128)(2,1)S(1)} %get-tuple-element.14.values.refs_0_), channel_id=1, source_target_pairs={{0,8},{2,10},{4,12},{6,14},{8,0},{10,2},{12,4},{14,6},{16,24},{18,... | collective-permute-start | bytes 589832 | tf_op jit(solution)/shard_map/ppermute | solution.py:471
  6.4 11.4 %collective-permute-start.6 = (bf16[128,768]{1,0:T(8,128)(2,1)S(1)}, bf16[128,768]{1,0:T(8,128)(2,1)S(1)}, u32[]{:S(2)}, u32[]{:S(2)}) collective-permute-start(bf16[128,768]{1,0:T(8,128)(2,1)S(1)} %shard_map.80), channel_id=1, source_target_pairs={{0,16},{2,18},{4,20},{6,22},{8,24},{10,26},{12,28},{14,30},{16,0},... | collective-permute-start | bytes 589832 | tf_op jit(solution)/shard_map/ppermute | solution.py:471
  9.0 19.9 %copy-start.1 = (f32[1,1024]{1,0:T(1,128)S(1)}, f32[1,1024]{1,0:T(1,128)}, u32[]{:S(2)}) copy-start(f32[1,1024]{1,0:T(1,128)} %gain.6) | copy-start | bytes 12292
  9.0 19.9 %collective-permute-start.4 = (bf16[256,1024]{1,0:T(8,128)(2,1)}, bf16[256,1024]{1,0:T(8,128)(2,1)S(1)}, u32[]{:S(2)}, u32[]{:S(2)}) collective-permute-start(bf16[256,1024]{1,0:T(8,128)(2,1)} %bitcast.2), channel_id=1, source_target_pairs={{0,2},{2,0},{4,6},{6,4},{8,10},{10,8},{12,14},{14,12},{16,18},{18,... | collective-permute-start | bytes 1572872 | tf_op jit(solution)/shard_map/ppermute | solution.py:474
  10.5 23.7 %collective-permute-start = (bf16[256,1024]{1,0:T(8,128)(2,1)}, bf16[256,1024]{1,0:T(8,128)(2,1)S(1)}, u32[]{:S(2)}, u32[]{:S(2)}) collective-permute-start(bf16[256,1024]{1,0:T(8,128)(2,1)} %bitcast.3), channel_id=1, source_target_pairs={{0,4},{2,6},{4,0},{6,2},{8,12},{10,14},{12,8},{14,10},{16,20},{18,... | collective-permute-start | bytes 1572872 | tf_op jit(solution)/shard_map/ppermute | solution.py:474
  15.2 19.3 %collective-permute-start.3 = (bf16[256,1024]{1,0:T(8,128)(2,1)S(1)}, bf16[256,1024]{1,0:T(8,128)(2,1)S(1)}, u32[]{:S(2)}, u32[]{:S(2)}) collective-permute-start(bf16[256,1024]{1,0:T(8,128)(2,1)S(1)} %shard_map.78), channel_id=1, source_target_pairs={{0,6},{2,4},{4,2},{6,0},{8,14},{10,12},{12,10},{14,8},{16,22},{18,... | collective-permute-start | bytes 1572872 | tf_op jit(solution)/shard_map/ppermute | solution.py:474
  16.8 9.3 %collective-permute-start.5 = (bf16[128,768]{1,0:T(8,128)(2,1)S(1)}, bf16[128,768]{1,0:T(8,128)(2,1)S(1)}, u32[]{:S(2)}, u32[]{:S(2)}) collective-permute-start(bf16[128,768]{1,0:T(8,128)(2,1)S(1)} %shard_map.79), channel_id=1, source_target_pairs={{0,8},{2,10},{4,12},{6,14},{8,0},{10,2},{12,4},{14,6},{16,24},{18,... | collective-permute-start | bytes 589832 | tf_op jit(solution)/shard_map/ppermute | solution.py:471
  17.8 10.1 %collective-permute-start.7 = (bf16[128,768]{1,0:T(8,128)(2,1)S(1)}, bf16[128,768]{1,0:T(8,128)(2,1)S(1)}, u32[]{:S(2)}, u32[]{:S(2)}) collective-permute-start(bf16[128,768]{1,0:T(8,128)(2,1)S(1)} %collective-permute-done.2.rest_1_.values.refs_1_), channel_id=1, source_target_pairs={{0,16},{2,18},{4,20},{6,22},{8,24},{10,26},{12,28},{14,30},{16,0},... | collective-permute-start | bytes 589832 | tf_op jit(solution)/shard_map/ppermute | solution.py:471
  26.1 5.7 %collective-permute-start.8 = (bf16[128,768]{1,0:T(8,128)(2,1)S(1)}, bf16[128,768]{1,0:T(8,128)(2,1)S(1)}, u32[]{:S(2)}, u32[]{:S(2)}) collective-permute-start(bf16[128,768]{1,0:T(8,128)(2,1)S(1)} %shard_map.82), channel_id=1, source_target_pairs={{0,8},{2,10},{4,12},{6,14},{8,0},{10,2},{12,4},{14,6},{16,24},{18,... | collective-permute-start | bytes 589832 | tf_op jit(solution)/shard_map/ppermute | solution.py:471
  27.9 6.0 %collective-permute-start.9 = (bf16[128,768]{1,0:T(8,128)(2,1)S(1)}, bf16[128,768]{1,0:T(8,128)(2,1)S(1)}, u32[]{:S(2)}, u32[]{:S(2)}) collective-permute-start(bf16[128,768]{1,0:T(8,128)(2,1)S(1)} %shard_map.83), channel_id=1, source_target_pairs={{0,8},{2,10},{4,12},{6,14},{8,0},{10,2},{12,4},{14,6},{16,24},{18,... | collective-permute-start | bytes 589832 | tf_op jit(solution)/shard_map/ppermute | solution.py:471
  35.6 6.5 %collective-permute-start.12 = (bf16[272,128]{1,0:T(8,128)(2,1)S(1)}, bf16[272,128]{1,0:T(8,128)(2,1)S(1)}, u32[]{:S(2)}, u32[]{:S(2)}) collective-permute-start(bf16[272,128]{1,0:T(8,128)(2,1)S(1)} %get-tuple-element.22), channel_id=1, source_target_pairs={{0,24},{2,26},{4,28},{6,30},{8,16},{10,18},{12,20},{14,22},{16,8},... | collective-permute-start | bytes 208904 | tf_op jit(solution)/shard_map/ppermute | solution.py:471
  39.3 5.2 %collective-permute-start.11 = (bf16[272,128]{1,0:T(8,128)(2,1)S(1)}, bf16[272,128]{1,0:T(8,128)(2,1)S(1)}, u32[]{:S(2)}, u32[]{:S(2)}) collective-permute-start(bf16[272,128]{1,0:T(8,128)(2,1)S(1)} %get-tuple-element.22), channel_id=1, source_target_pairs={{0,16},{2,18},{4,20},{6,22},{8,24},{10,26},{12,28},{14,30},{16,0},... | collective-permute-start | bytes 208904 | tf_op jit(solution)/shard_map/ppermute | solution.py:471
  39.3 5.2 %collective-permute-start.10 = (bf16[272,128]{1,0:T(8,128)(2,1)S(1)}, bf16[272,128]{1,0:T(8,128)(2,1)S(1)}, u32[]{:S(2)}, u32[]{:S(2)}) collective-permute-start(bf16[272,128]{1,0:T(8,128)(2,1)S(1)} %get-tuple-element.22), channel_id=1, source_target_pairs={{0,8},{2,10},{4,12},{6,14},{8,0},{10,2},{12,4},{14,6},{16,24},{18,... | collective-permute-start | bytes 208904 | tf_op jit(solution)/shard_map/ppermute | solution.py:471
  40.5 4.1 %copy-start.2 = (f32[1,1024]{1,0:T(1,128)S(1)}, f32[1,1024]{1,0:T(1,128)}, u32[]{:S(2)}) copy-start(f32[1,1024]{1,0:T(1,128)} %gain.7) | copy-start | bytes 12292
  41.7 14.6 %copy-start.3 = (s32[2]{0:T(128)S(1)}, s32[2]{0:T(128)}, u32[]{:S(2)}) copy-start(s32[2]{0:T(128)} %positives.1) | copy-start | bytes 28
